TPU v7x, 256 devices: a whole 4x4x8 slice. The times are simulated.
256 devices in a mesh: dp: 16 (over y, x), owner: 16 (over z, core).
Axes of the slice: x: 4, y: 4, z: 8, core: 2. Of those that a mesh axis runs over, the one named last changes fastest.
Arguments:
- acts: bfloat16 [2, 4096, 6144], P(None, 'dp'), may hold values from -6 to 6
- grads_out: bfloat16 [2, 4096, 24576], P(None, 'dp', 'owner'), may hold values from -6 to 6
- weight_grad: bfloat16 [2, 24576, 6144], P(None, 'owner', 'dp'), may hold values from -6 to 6
Outputs:
- preconditioned: bfloat16 [2, 24576, 6144], P(None, 'owner', 'dp')
All inputs are finite; a program needn't handle non-finite values. Where the computation divides by a largest or mean magnitude, that divisor is 1e-20 or more.
Results may differ from a plain program's by a relative error of at most 0.0098.
Values may be sent and summed in bfloat16 or wider, within the bound.
No kernel may reach another device: no remote copies, remote signals or barrier semaphores. Data moves between devices by JAX's collectives and lax.ppermute only.
A program may use at most 128 MiB of HBM per device.

v0:
```python
import jax
import jax.numpy as jnp
import numpy as np
from jax import lax
from jax.sharding import PartitionSpec as P

BLK = 512
ITERS = 2


damping = 0.1


def newton(matrix):
    eye = jnp.eye(matrix.shape[1], dtype=jnp.float32)
    alpha = 1.0 / jnp.max(jnp.sum(jnp.abs(matrix), axis=2), axis=1)
    low = matrix.astype(jnp.bfloat16)
    iterate = (alpha[:, None, None] * eye).astype(jnp.bfloat16)
    for step in range(ITERS):
        image = jnp.einsum("bij,bjk->bik", low, iterate, preferred_element_type=jnp.float32)
        residue = (2.0 * eye - image).astype(jnp.bfloat16)
        iterate = jnp.einsum(
            "bij,bjk->bik", iterate, residue, preferred_element_type=jnp.float32
        ).astype(jnp.bfloat16)
    return iterate


def body(acts, grads_out, weight_grad):
    n_data = lax.axis_size("dp")
    n_owners = lax.axis_size("owner")
    owner_id = lax.axis_index("owner")
    layers, tok_dev, width = acts.shape
    ff_dev = grads_out.shape[2]
    blocks_a = width // BLK
    blocks_g = ff_dev // BLK
    slots_a = (blocks_a + n_owners - 1) // n_owners
    tokens_all = tok_dev * n_data
    eye = jnp.eye(BLK, dtype=jnp.float32)
    results = []
    for layer in range(layers):
        rotation = layer * blocks_a % n_owners
        rows = acts[layer]
        first = (owner_id - rotation) % n_owners
        block = jnp.minimum(first + 0, blocks_a - 1)
        columns = lax.dynamic_slice_in_dim(rows, block * BLK, BLK, 1)
        partial_a = [
            lax.dot_general(
                columns, columns, (((0,), (0,)), ((), ())), preferred_element_type=jnp.float32
            )
        ]
        hidden_grad = grads_out[layer].reshape(tok_dev, blocks_g, BLK)
        partial_g = jnp.einsum(
            "tai,taj->aij", hidden_grad, hidden_grad, preferred_element_type=jnp.float32
        )
        partial_value = jnp.concatenate([jnp.stack(partial_a), partial_g], axis=0)
        summed = lax.psum(partial_value, "dp")
        matrix = summed / tokens_all + damping * eye
        inverse = newton(matrix)
        inverse_a = inverse[:slots_a]
        inverse_g = inverse[slots_a:]
        every_a = lax.all_gather(inverse_a, "owner", axis=0, tiled=True)
        order = np.array(
            [
                (block + rotation) % n_owners * slots_a + block // n_owners
                for block in range(blocks_a)
            ],
            dtype=np.int32,
        )
        full_a = every_a[order]
        gradient = weight_grad[layer]
        width_dev = gradient.shape[1]
        left = jnp.einsum(
            "gij,gjc->gic",
            inverse_g,
            gradient.reshape(blocks_g, BLK, width_dev),
            preferred_element_type=jnp.float32,
        )
        left = left.astype(jnp.bfloat16).reshape(ff_dev, width_dev)
        spread = lax.all_to_all(left, "dp", split_axis=0, concat_axis=1, tiled=True)
        count = spread.shape[0]
        right = jnp.einsum(
            "rab,abc->rac",
            spread.reshape(count, blocks_a, BLK),
            full_a,
            preferred_element_type=jnp.float32,
        )
        right = right.astype(jnp.bfloat16).reshape(count, width)
        results.append(lax.all_to_all(right, "dp", split_axis=1, concat_axis=0, tiled=True))
    return jnp.stack(results)


def solution(mesh):
    in_specs = (P(None, "dp", None), P(None, "dp", "owner"), P(None, "owner", "dp"))
    out_specs = P(None, "owner", "dp")
    return jax.shard_map(body, mesh=mesh, in_specs=in_specs, out_specs=out_specs, check_vma=False)
```

profile of v0, /device:TPU:1, one launch (start us, length us, event | category | flops | bytes accessed | tf_op | source)
XLA Modules:
  0.0 369.5 jit_solution(3679676072642577704)
XLA Ops:
  6.5 0.0 all-reduce.3.cloned.1.call-start
  6.5 0.0 copy-start.1
  6.5 6.3 %fusion.47 = (bf16[1,256,6144]{2,1,0:T(8,128)(2,1)}, bf16[1,256,6144]{2,1,0:T(8,128)(2,1)}) fusion(bf16[2,256,6144]{2,1,0:T(8,128)(2,1)} %param.7), kind=kLoop, calls=%fused_computation.59 | loop fusion | bytes 12582912 | tf_op jit(solution)/shard_map/slice | solution.py:42
  12.9 0.0 copy-done.1
  12.9 1.0 fusion.49
  13.9 1.2 copy.58
  15.0 2.1 fusion.50
  17.1 2.3 copy.59
  19.4 3.7 %fusion.51 = f32[3,512,512]{2,1,0:T(8,128)} fusion(bf16[256,3,512]{0,2,1:T(8,128)(2,1)} %bitcast.43), kind=kOutput, calls=%fused_computation.63 | convolution fusion | flops 402653184 | bytes 3932160 | tf_op jit(solution)/shard_map/tai,taj->aij/dot_general | solution.py:52
  23.2 2.3 convolution_bitcast_fusion
  25.5 1.4 convolution_bitcast_fusion.1
  26.8 6.7 %pad_maximum_fusion = (f32[4,512,512]{2,1,0:T(8,128)}, f32[4,512,512]{2,1,0:T(8,128)}) fusion(f32[3,512,512]{2,1,0:T(8,128)S(1)} %fusion.50, f32[1,512,512]{2,1,0:T(8,128)S(1)} %convolution_bitcast_fusion.1, f32[3,512,512]{2,1,0:T(8,128)} %fusion.51, f32[1,512,512]{2,1,0:T(8,128)} %convolution_bitcast_fusion), kind=kLoop, calls=%fused_computation.2 | loop fusion | flops 2097152 | bytes 16777216 | tf_op jit(solution)/shard_map/concatenate | solution.py:55
  33.6 0.0 all-reduce.3.cloned.1.call-update
  33.6 0.0 all-gather.3.cloned.1.call-start
  33.7 0.1 fusion.23
  33.8 0.2 fusion.22
  34.0 0.0 copy-start.3
  34.0 155.1 %all-reduce.3.cloned.1.call-done = (f32[4,512,512]{2,1,0:T(8,128)}, f32[4,512,512]{2,1,0:T(8,128)}) async-done(((f32[4,512,512]{2,1,0:T(8,128)}, f32[4,512,512]{2,1,0:T(8,128)}), (f32[4,512,512]{2,1,0:T(8,128)}, f32[4,512,512]{2,1,0:T(8,128)})) %all-reduce.3.cloned.1.call-update) | async-done | bytes 8388624 | tf_op jit(solution)/shard_map/psum | solution.py:56
  189.1 4.6 %abs_reduce_fusion.1 = (f32[4,512]{1,0:T(4,128)S(1)}, f32[4,512]{1,0:T(4,128)S(1)}) fusion(f32[4,512,512]{2,1,0:T(8,128)} %get-tuple-element.7, f32[512,512]{1,0:T(8,128)S(1)} %get-tuple-element.18, f32[4,512,512]{2,1,0:T(8,128)} %get-tuple-element.8), kind=kLoop, calls=%fused_computation.12 | loop fusion | flops 8384512 | bytes 9453568 | tf_op jit(solution)/shard_map/reduce_sum | solution.py:16
  193.8 0.1 reduce_max.18
  193.9 6.1 %fusion.17 = bf16[4,512,512]{2,1,0:T(8,128)(2,1)} fusion(f32[512,512]{1,0:T(8,128)S(1)} %get-tuple-element.17, f32[512,512]{1,0:T(8,128)S(1)} %fusion.23, f32[4]{0:T(128)S(1)} %broadcast_divide_fusion.1, f32[4,512,512]{2,1,0:T(8,128)} %get-tuple-element.7, f32[512,512]{1,0:T(8,128)S(1)} %get-tuple-element.18), kind=kOutput, calls=%fused_computation.30 | convolution fusion | flops 2157969408 | bytes 9437200 | tf_op jit(solution)/shard_map/bij,bjk->bik/dot_general | solution.py:22
  200.0 7.2 %convolution_convert_fusion.1 = bf16[4,512,512]{2,1,0:T(8,128)(2,1)} fusion(bf16[4,512,512]{2,1,0:T(8,128)(2,1)} %fusion.17, f32[512,512]{1,0:T(8,128)S(1)} %get-tuple-element.17, f32[4,512,512]{2,1,0:T(8,128)} %get-tuple-element.7, f32[512,512]{1,0:T(8,128)S(1)} %get-tuple-element.18), kind=kOutput, calls=%fused_computation.28 | convolution fusion | flops 2153775104 | bytes 10485760 | tf_op jit(solution)/shard_map/bij,bjk->bik/dot_general | solution.py:22
  207.2 1.9 slice.44
  209.1 0.0 all-gather.3.cloned.1.call-update
  209.1 0.2 all-gather.5.cloned.1.call-start
  209.3 0.1 reduce_max.19
  209.5 0.0 copy-done.3
  209.5 6.1 %fusion.16 = bf16[4,512,512]{2,1,0:T(8,128)(2,1)} fusion(f32[4]{0:T(128)S(1)} %broadcast_divide_fusion, f32[512,512]{1,0:T(8,128)S(1)} %get-tuple-element.17, f32[512,512]{1,0:T(8,128)S(1)} %fusion.23, f32[4,512,512]{2,1,0:T(8,128)} %get-tuple-element.8, f32[512,512]{1,0:T(8,128)S(1)} %get-tuple-element.18), kind=kOutput, calls=%fused_computation.29 | convolution fusion | flops 2157969408 | bytes 9437200 | tf_op jit(solution)/shard_map/bij,bjk->bik/dot_general | solution.py:22
  215.6 7.5 %convolution_convert_fusion = bf16[4,512,512]{2,1,0:T(8,128)(2,1)} fusion(bf16[4,512,512]{2,1,0:T(8,128)(2,1)} %fusion.16, f32[512,512]{1,0:T(8,128)} %copy-done.3, f32[4,512,512]{2,1,0:T(8,128)} %get-tuple-element.8, f32[512,512]{1,0:T(8,128)S(1)} %get-tuple-element.18), kind=kOutput, calls=%fused_computation.27 | convolution fusion | flops 2153775104 | bytes 10485760 | tf_op jit(solution)/shard_map/bij,bjk->bik/dot_general | solution.py:22
  223.1 1.9 slice.45
  225.0 0.0 all-gather.5.cloned.1.call-update
  225.0 0.0 copy-done
  225.0 0.0 copy-start.4
  225.0 1.3 fusion.48
  226.3 0.8 copy-done.4
  227.0 2.0 convolution_convert_fusion.3
  229.1 4.2 %all-to-all-start = ((bf16[16,96,384]{2,1,0:T(8,128)(2,1)}), bf16[16,96,384]{2,1,0:T(8,128)(2,1)S(1)}, u32[]{:S(2)}, u32[]{:S(2)}) async-start(bf16[16,96,384]{2,1,0:T(8,128)(2,1)} %bitcast.4), calls=%async_computation | async-start | bytes 2359296 | tf_op jit(solution)/shard_map/all_to_all | solution.py:79
  233.3 0.0 copy-done.2
  233.3 3.4 convolution_convert_fusion.2
  236.7 13.5 %all-to-all-done = bf16[16,96,384]{2,1,0:T(8,128)(2,1)S(1)} async-done(((bf16[16,96,384]{2,1,0:T(8,128)(2,1)}), bf16[16,96,384]{2,1,0:T(8,128)(2,1)S(1)}, u32[]{:S(2)}, u32[]{:S(2)}) %all-to-all-start) | async-done | bytes 1179680 | tf_op jit(solution)/shard_map/all_to_all | solution.py:79
  250.2 4.4 %all-to-all-start.2 = ((bf16[16,96,384]{2,1,0:T(8,128)(2,1)}), bf16[16,96,384]{2,1,0:T(8,128)(2,1)S(1)}, u32[]{:S(2)}, u32[]{:S(2)}) async-start(bf16[16,96,384]{2,1,0:T(8,128)(2,1)} %bitcast.47), calls=%async_computation.2 | async-start | bytes 2359296 | tf_op jit(solution)/shard_map/all_to_all | solution.py:79
  254.6 1.4 copy.46
  256.1 2.6 reshape.56
  258.6 6.4 %all-gather.3.cloned.1.call-done = bf16[16,512,512]{2,1,0:T(8,128)(2,1)} async-done(((bf16[1,512,512]{2,1,0:T(8,128)(2,1)}), bf16[16,512,512]{2,1,0:T(8,128)(2,1)}) %all-gather.3.cloned.1.call-update) | async-done | bytes 8388624 | tf_op jit(solution)/shard_map/all_gather | solution.py:61
  265.0 7.6 %gather_fusion = bf16[12,512,512]{2,1,0:T(8,128)(2,1)} fusion(bf16[16,512,512]{2,1,0:T(8,128)(2,1)} %all-gather.3.cloned.1.call-done, s32[1024]{0:T(1024)S(1)} %pad_clamp_fusion.1), kind=kCustom, calls=%fused_computation | custom fusion | bytes 12582960 | tf_op jit(solution)/shard_map/gather | solution.py:69
  272.6 4.5 %fusion.18 = bf16[96,12,512]{2,0,1:T(8,128)(2,1)S(1)} fusion(bf16[12,512,512]{2,1,0:T(8,128)(2,1)} %gather_fusion, bf16[96,12,512]{2,1,0:T(8,128)(2,1)S(1)} %reshape.56), kind=kOutput, calls=%fused_computation.35 | convolution fusion | flops 604569600 | bytes 8650752 | tf_op jit(solution)/shard_map/rab,abc->rac/dot_general | solution.py:81
  277.1 0.7 copy.48
  277.8 0.0 copy-start.5
  277.8 1.8 all_to_all.51
  279.6 2.6 copy.49
  282.1 0.0 all-to-all-done.2
  282.1 6.6 %all-to-all-start.1 = ((bf16[96,16,384]{2,0,1:T(8,128)(2,1)}), bf16[96,16,384]{2,0,1:T(8,128)(2,1)}, u32[]{:S(2)}, u32[]{:S(2)}) async-start(bf16[96,16,384]{2,0,1:T(8,128)(2,1)} %copy.49), calls=%async_computation.1 | async-start | bytes 2359296 | tf_op jit(solution)/shard_map/all_to_all | solution.py:88
  288.7 0.0 copy-done.5
  288.7 1.4 copy.52
  290.1 2.6 reshape.57
  292.7 28.8 %all-gather.5.cloned.1.call-done = bf16[16,512,512]{2,1,0:T(8,128)(2,1)} async-done(((bf16[1,512,512]{2,1,0:T(8,128)(2,1)}), bf16[16,512,512]{2,1,0:T(8,128)(2,1)}) %all-gather.5.cloned.1.call-update) | async-done | bytes 8388624 | tf_op jit(solution)/shard_map/all_gather | solution.py:61
  321.5 7.6 %gather_fusion.1 = bf16[12,512,512]{2,1,0:T(8,128)(2,1)} fusion(bf16[16,512,512]{2,1,0:T(8,128)(2,1)} %all-gather.5.cloned.1.call-done, s32[1024]{0:T(1024)S(1)} %pad_clamp_fusion), kind=kCustom, calls=%fused_computation.1 | custom fusion | bytes 12582960 | tf_op jit(solution)/shard_map/gather | solution.py:69
  329.1 4.5 %fusion.19 = bf16[96,12,512]{2,0,1:T(8,128)(2,1)S(1)} fusion(bf16[12,512,512]{2,1,0:T(8,128)(2,1)} %gather_fusion.1, bf16[96,12,512]{2,1,0:T(8,128)(2,1)S(1)} %reshape.57), kind=kOutput, calls=%fused_computation.36 | convolution fusion | flops 604569600 | bytes 8650752 | tf_op jit(solution)/shard_map/rab,abc->rac/dot_general | solution.py:81
  333.6 0.7 copy.54
  334.3 1.0 all_to_all.57
  335.3 0.3 copy.55
  335.5 0.0 all-to-all-done.1
  335.5 24.5 %all_to_all.64 = bf16[96,16,384]{2,0,1:T(8,128)(2,1)S(1)} all-to-all(bf16[96,16,384]{2,0,1:T(8,128)(2,1)S(1)} %copy.55), channel_id=1, replica_groups=mesh['dp'=16,'owner'=16] {'dp'}, dimensions={1} | all-to-all | bytes 2359296 | tf_op jit(solution)/shard_map/all_to_all | solution.py:88
  360.0 2.9 pad_maximum_fusion.2
  (7 shorter events, 0.0 us)
Async XLA Ops:
  6.5 182.6 %all-reduce.3.cloned.1.call-start = ((), (), s32[]{:S(2)}) async-start(), calls=%async_computation.6 | async-start | bytes 16777216 | tf_op jit(solution)/shard_map/psum | solution.py:56
  6.5 6.3 %copy-start.1 = (bf16[2,256,1536]{2,1,0:T(8,128)(2,1)S(1)}, bf16[2,256,1536]{2,1,0:T(8,128)(2,1)}, u32[]{:S(2)}) copy-start(bf16[2,256,1536]{2,1,0:T(8,128)(2,1)} %param.8) | copy-start | bytes 4718596
  33.6 231.4 %all-gather.3.cloned.1.call-start = ((), (), s32[]{:S(2)}) async-start(), calls=%async_computation.4 | async-start | bytes 8912896 | tf_op jit(solution)/shard_map/all_gather | solution.py:61
  34.0 175.4 %copy-start.3 = (f32[512,512]{1,0:T(8,128)}, f32[512,512]{1,0:T(8,128)S(1)}, u32[]{:S(2)}) copy-start(f32[512,512]{1,0:T(8,128)S(1)} %get-tuple-element.17) | copy-start | bytes 3145732
  209.1 112.4 %all-gather.5.cloned.1.call-start = ((), (), s32[]{:S(2)}) async-start(), calls=%async_computation.5 | async-start | bytes 8912896 | tf_op jit(solution)/shard_map/all_gather | solution.py:61
  215.6 9.4 %copy-start = (bf16[2,1536,384]{2,1,0:T(8,128)(2,1)S(1)}, bf16[2,1536,384]{2,1,0:T(8,128)(2,1)}, u32[]{:S(2)}) copy-start(bf16[2,1536,384]{2,1,0:T(8,128)(2,1)} %param.9) | copy-start | bytes 7077892
  225.0 2.0 copy-start.4
  227.0 6.2 %copy-start.2 = (bf16[1,1536,384]{2,1,0:T(8,128)(2,1)S(1)}, bf16[1,1536,384]{2,1,0:T(8,128)(2,1)}, u32[]{:S(2)}) copy-start(bf16[1,1536,384]{2,1,0:T(8,128)(2,1)} %get-tuple-element.12) | copy-start | bytes 3538948
  229.1 21.1 %all-to-all-start = ((bf16[16,96,384]{2,1,0:T(8,128)(2,1)}), bf16[16,96,384]{2,1,0:T(8,128)(2,1)S(1)}, u32[]{:S(2)}, u32[]{:S(2)}) async-start(bf16[16,96,384]{2,1,0:T(8,128)(2,1)} %bitcast.4), calls=%async_computation | async-start | bytes 2359296 | tf_op jit(solution)/shard_map/all_to_all | solution.py:79
  250.2 32.0 %all-to-all-start.2 = ((bf16[16,96,384]{2,1,0:T(8,128)(2,1)}), bf16[16,96,384]{2,1,0:T(8,128)(2,1)S(1)}, u32[]{:S(2)}, u32[]{:S(2)}) async-start(bf16[16,96,384]{2,1,0:T(8,128)(2,1)} %bitcast.47), calls=%async_computation.2 | async-start | bytes 2359296 | tf_op jit(solution)/shard_map/all_to_all | solution.py:79
  277.8 11.0 %copy-start.5 = (s32[12]{0:T(128)S(1)}, s32[12]{0:T(128)}, u32[]{:S(2)}) copy-start(s32[12]{0:T(128)} %constant.59) | copy-start | bytes 148
  282.1 53.4 %all-to-all-start.1 = ((bf16[96,16,384]{2,0,1:T(8,128)(2,1)}), bf16[96,16,384]{2,0,1:T(8,128)(2,1)}, u32[]{:S(2)}, u32[]{:S(2)}) async-start(bf16[96,16,384]{2,0,1:T(8,128)(2,1)} %copy.49), calls=%async_computation.1 | async-start | bytes 2359296 | tf_op jit(solution)/shard_map/all_to_all | solution.py:88
Sparse Core Ops, SparseCore 0:
  33.7 155.3 all-reduce.2
  209.2 55.7 all-gather.2
  267.0 54.4 all-gather.4
where the time goes:
time: 371 us; the launch traced here: 369 us
  waiting for transfers between devices  204 us (55%)
  matrix products  50.7 us (14%)
  local copies, waits for them, and re-layouts  46.7 us (13%)
  blocking collectives  24.5 us (7%)
  starting transfers between devices  15.5 us (4%)
  other arithmetic  14.9 us (4%)
  between operations  13.3 us (4%)
    psum x1, waiting for transfers between devices, body(): summed = lax.psum(partial_value, 'dp')  155 us
    all_gather x2, waiting for transfers between devices, body(): every_a = lax.all_gather(inverse_a, 'owner', axis=0, tiled=True)  35.2 us
    dot_general x4, matrix products, newton(): jnp.einsum('bij,bjk->bik', iterate, residue, preferred_element_type=jnp.f...  26.9 us
    all_to_all x1, blocking collectives, body(): lax.all_to_all(right, 'dp', split_axis=1, concat_axis=0, tiled=True)  24.5 us
    gather x2, local copies, waits for them, and re-layouts, body(): full_a = every_a[order]  15.2 us
    all_to_all x2, waiting for transfers between devices, body(): spread = lax.all_to_all(left, 'dp', split_axis=0, concat_axis=1, tiled=True)  13.5 us
    dot_general x2, matrix products, body(): jnp.einsum('rab,abc->rac', spread.reshape(count, blocks_a, BLK), full_a,...  8.93 us
    all_to_all x2, starting transfers between devices, body(): spread = lax.all_to_all(left, 'dp', split_axis=0, concat_axis=1, tiled=True)  8.64 us
  transfers between devices with their start and end apart: 6, of which 4 were waited for; matrix products, arithmetic and copies ran while one was open for 16% of the time, Pallas kernels for 0%

commit v1 on v0

v1 whole, which is shorter than its diff:
```python
import jax
import jax.numpy as jnp
from jax import lax
from jax.experimental import pallas as pl
from jax.experimental.pallas import tpu as pltpu
from jax.sharding import Mesh, PartitionSpec as P

BLK = 512
SUB = 128
damping = 0.1
TOKENS = 4096
F32 = jnp.float32
BF16 = jnp.bfloat16
VMEM = pltpu.VMEM

PAIRS = [(r, c) for r in range(4) for c in range(r, 4)]
LANES = 15 * SUB


def tn_dot(a, b):
    return lax.dot_general(a, b, (((0,), (0,)), ((), ())), preferred_element_type=F32)


def nn_dot(a, b):
    return lax.dot_general(a, b, (((1,), (0,)), ((), ())), preferred_element_type=F32)


def cov_kernel(pos, acts, grads, g0, g1, g2, g3, h0, h1, h2, h3, pack):
    x, y, part = pos[0], pos[1], pos[3]
    first = (g0, g1, g2, g3)
    second = (h0, h1, h2, h3)
    for layer in range(2):
        for b in range(3):
            rows = grads[layer, :, b * BLK:(b + 1) * BLK]
            top = tn_dot(rows[:, :256], rows).astype(BF16)
            low = tn_dot(rows[:, 256:], rows[:, 256:]).astype(BF16)
            for i, (r, c) in enumerate(PAIRS):
                s = 10 * b + i
                if r < 2:
                    piece = top[r * SUB:(r + 1) * SUB, c * SUB:(c + 1) * SUB]
                else:
                    piece = low[(r - 2) * SUB:(r - 1) * SUB, (c - 2) * SUB:(c - 1) * SUB]
                pack[layer, s // 15 * SUB:(s // 15 + 1) * SUB, s % 15 * SUB:(s % 15 + 1) * SUB] = piece
    for d in range(4):
        first[d][...] = pack[0, pl.ds(pl.multiple_of((x + d) % 4 * 64, 64), 64), :]
        second[d][0:64, :] = pack[1, pl.ds(pl.multiple_of((y + d) % 4 * 64, 64), 64), :]
    k = lax.broadcasted_iota(jnp.int32, (BLK, 64), 0)
    m = lax.broadcasted_iota(jnp.int32, (BLK, 64), 1)
    select = jnp.where(k == m // 16 * SUB + part * 16 + m % 16, 1.0, 0.0).astype(BF16)
    for d in range(4):
        start = (y + d) % 4 * (3 * BLK)
        for j in range(3):
            rows = acts[0, :, pl.ds(pl.multiple_of(start + j * BLK, BLK), BLK)]
            chosen = nn_dot(rows, select).astype(BF16)
            cov = tn_dot(chosen, rows).astype(BF16)
            for i, (r, c) in enumerate(PAIRS):
                s = 10 * j + i
                second[d][64 + s // 15 * 16:80 + s // 15 * 16, s % 15 * SUB:(s % 15 + 1) * SUB] = (
                    cov[r * 16:(r + 1) * 16, c * SUB:(c + 1) * SUB]
                )


def invert(packed_piece, full):
    for i, (r, c) in enumerate(PAIRS):
        piece = packed_piece(i).astype(F32)
        full[r * SUB:(r + 1) * SUB, c * SUB:(c + 1) * SUB] = piece
        if r != c:
            full[c * SUB:(c + 1) * SUB, r * SUB:(r + 1) * SUB] = piece.T
    ri = lax.broadcasted_iota(jnp.int32, (BLK, BLK), 0)
    ci = lax.broadcasted_iota(jnp.int32, (BLK, BLK), 1)
    diagonal = ri == ci
    matrix = full[...] + jnp.where(diagonal, damping, 0.0)
    two_eye = jnp.where(diagonal, 2.0, 0.0)
    sums = jnp.sum(jnp.abs(matrix), axis=0, keepdims=True)
    alpha = (1.0 / jnp.max(sums, axis=1, keepdims=True)).astype(BF16).astype(F32)
    low = matrix.astype(BF16)
    residue = (two_eye - low.astype(F32) * alpha).astype(BF16)
    iterate = (residue.astype(F32) * alpha).astype(BF16)
    image = nn_dot(low, iterate)
    residue = (two_eye - image).astype(BF16)
    return nn_dot(iterate, residue).astype(BF16)


def right_kernel(pos, mine, other, w_own, w_pair, w_mid, out, pack, full, diag):
    x, core = pos[0], pos[2]
    for z in range(8):
        layer, q = z // 4, z % 4
        at = pl.multiple_of(q * 32 + core * 16, 16)
        pack[layer, pl.ds(at, 16), :] = mine[z * 16:(z + 1) * 16, :]
        at = pl.multiple_of(q * 32 + (1 - core) * 16, 16)
        pack[layer, pl.ds(at, 16), :] = other[z * 16:(z + 1) * 16, :]
    base = x // 2 * BLK
    own = pl.multiple_of(x * 384 - base, SUB)
    pair = pl.multiple_of((x + 1 - 2 * (x % 2)) * 384 - base, SUB)
    mid = pl.multiple_of(jnp.where(x == 1, 768, 0), SUB)
    for layer in range(2):
        for b in range(2):
            at = b * BLK
            inverse = invert(
                lambda i: pack[layer, :, b * 1280 + i * SUB:b * 1280 + (i + 1) * SUB], full.at[layer, b]
            )
            diag[layer, at:at + BLK, at:at + BLK] = inverse
            diag[layer, at:at + BLK, BLK - at:2 * BLK - at] = jnp.zeros((BLK, BLK), BF16)
        columns = pl.ds(own, 384)
        total = nn_dot(w_own[layer], diag[layer, pl.ds(own, 384), columns])
        total += nn_dot(w_pair[layer], diag[layer, pl.ds(pair, 384), columns])
        total += nn_dot(w_mid[layer], diag[layer, pl.ds(mid, 256), columns])
        out[layer] = total.astype(BF16)


def left_kernel(pos, *refs):
    first, second, right, out, pack, full = refs[0:4], refs[4:8], refs[8], refs[9], refs[10], refs[11]
    x, y = pos[0], pos[1]
    for d in range(4):
        for e in range(4):
            at = (x + 4 - d) % 4 * 64 + (y + 4 - e) % 4 * 16
            pack[0, pl.ds(pl.multiple_of(at, 16), 16), :] = first[d][e * 16:(e + 1) * 16, :]
            at = (y + 4 - d) % 4 * 64 + (x + 4 - e) % 4 * 16
            pack[1, pl.ds(pl.multiple_of(at, 16), 16), :] = second[d][e * 16:(e + 1) * 16, :]
    for layer in range(2):
        for b in range(3):
            def piece(i):
                s = 10 * b + i
                return pack[layer, s // 15 * SUB:(s // 15 + 1) * SUB, s % 15 * SUB:(s % 15 + 1) * SUB]
            inverse = invert(piece, full.at[layer, b])
            at = b * BLK
            out[layer, at:at + BLK, :] = nn_dot(inverse, right[layer, at:at + BLK, :]).astype(BF16)


def call(kernel, pos, operands, in_specs, out_shape, scratch, flops):
    spec = pl.BlockSpec(memory_space=VMEM)
    return pl.pallas_call(
        kernel,
        grid_spec=pltpu.PrefetchScalarGridSpec(
            num_scalar_prefetch=1,
            grid=(1,),
            in_specs=in_specs,
            out_specs=[pl.BlockSpec(s.shape, lambda i, p, n=len(s.shape): (0,) * n) for s in out_shape],
            scratch_shapes=scratch,
        ),
        out_shape=out_shape,
        compiler_params=pltpu.CompilerParams(vmem_limit_bytes=48 * 1024 * 1024),
        cost_estimate=pl.CostEstimate(flops=flops, bytes_accessed=8_000_000, transcendentals=0),
    )(pos, *operands)


def whole(a):
    return pl.BlockSpec(a.shape, lambda i, p, n=a.ndim: (0,) * n)


def shift(a, axis, d):
    return lax.ppermute(a, axis, [(i, (i + d) % 4) for i in range(4)])


def add(parts):
    return sum(p.astype(F32) for p in parts)


def spread(parts, axis):
    return [parts[0]] + [shift(parts[d], axis, d) for d in (1, 2, 3)]


def gather(a, axis):
    return [a] + [shift(a, axis, d) for d in (1, 2, 3)]


def chunk(a, index, rows):
    return lax.dynamic_slice_in_dim(a, index % 4 * rows, rows, 0)


def body(acts, grads_out, weight_grad):
    y, x, z, c = (lax.axis_index(n) for n in ("y", "x", "z", "c"))
    part = z % 4 * 2 + c
    pos = jnp.stack([x, y, c, part, z // 4]).astype(jnp.int32)

    w_pair = lax.ppermute(weight_grad, "x", [(0, 1), (1, 0), (2, 3), (3, 2)])
    middle = lax.dynamic_slice_in_dim(weight_grad, jnp.where(x == 1, SUB, 0), 256, 2)
    w_mid = lax.ppermute(middle, "x", [(1, 2), (2, 1)])

    shapes = [jax.ShapeDtypeStruct((64, LANES), BF16)] * 4 + [jax.ShapeDtypeStruct((96, LANES), BF16)] * 4
    covs = call(
        cov_kernel, pos, (acts, grads_out),
        [pl.BlockSpec((1, 256, 6144), lambda i, p: (p[4], 0, 0)), whole(grads_out)],
        shapes, [VMEM((2, 256, LANES), BF16)], 3_000_000_000,
    )
    first = add(spread(covs[:4], "x")).astype(BF16)
    both = add(spread(covs[4:], "y")).astype(BF16)
    second, side = both[:64], both[64:]

    sends = [jnp.concatenate([chunk(second, x + d, 16), side], axis=0) for d in range(4)]
    both = add(spread(sends, "x")) * (1.0 / TOKENS)
    first = (add(spread([chunk(first, y + d, 16) for d in range(4)], "y")) * (1.0 / TOKENS)).astype(BF16)
    second = both[:16].astype(BF16)
    side = jnp.concatenate([both[16:32], both[32:48]], axis=1)
    side = lax.dynamic_slice_in_dim(side, x // 2 * 1280, 2560, 1).astype(BF16)

    sides = lax.all_to_all(jnp.tile(side, (8, 1)), "z", 0, 0, tiled=True)
    first = jnp.concatenate(gather(first, "y"), axis=0)
    second = jnp.concatenate(gather(second, "x"), axis=0)
    first = gather(first, "x")
    second = gather(second, "y")
    other = lax.ppermute(sides, "c", [(0, 1), (1, 0)])

    right = call(
        right_kernel, pos, (sides, other, weight_grad, w_pair, w_mid),
        [whole(a) for a in (sides, other, weight_grad, w_pair, w_mid)],
        [jax.ShapeDtypeStruct(weight_grad.shape, BF16)],
        [VMEM((2, 128, 2560), BF16), VMEM((2, 2, BLK, BLK), F32), VMEM((2, 1024, 1024), BF16)],
        5_000_000_000,
    )[0]
    operands = (*first, *second, right)
    return call(
        left_kernel, pos, operands, [whole(a) for a in operands],
        [jax.ShapeDtypeStruct(weight_grad.shape, BF16)],
        [VMEM((2, 256, LANES), BF16), VMEM((2, 3, BLK, BLK), F32)],
        5_000_000_000,
    )[0]


def solution(mesh):
    fine = Mesh(mesh.devices.reshape(4, 4, 8, 2), ("y", "x", "z", "c"))
    dp, owner = ("y", "x"), ("z", "c")
    in_specs = (P(None, dp, None), P(None, dp, owner), P(None, owner, dp))
    out_specs = P(None, owner, dp)
    return jax.shard_map(body, mesh=fine, in_specs=in_specs, out_specs=out_specs, check_vma=False)
```

time: 371 us -> 163 us (0.44)
  the two profiles are of different devices: /device:TPU:1 before, /device:TPU:198 now
where the time goes in v1:
time: 163 us
  waiting for transfers between devices  85.6 us (53%)
  starting transfers between devices  43.9 us (27%)
  Pallas kernels  24.9 us (15%)
  local copies, waits for them, and re-layouts  5.14 us (3%)
  other arithmetic  2.86 us (2%)
    ppermute x24, waiting for transfers between devices, shift(): return lax.ppermute(a, axis, [(i, (i + d) % 4) for i in range(4)])  85.6 us
    ppermute x24, starting transfers between devices, shift(): return lax.ppermute(a, axis, [(i, (i + d) % 4) for i in range(4)])  35.8 us
    pallas_call x3, Pallas kernels, call(): pl.pallas_call(kernel, grid_spec=pltpu.PrefetchScalarGridSpec(num_scalar_...  24.9 us
    all_to_all x1, starting transfers between devices, body(): sides = lax.all_to_all(jnp.tile(side, (8, 1)), 'z', 0, 0, tiled=True)  6.29 us
  transfers between devices with their start and end apart: 28, of which 17 were waited for; matrix products, arithmetic and copies ran while one was open for 3% of the time, Pallas kernels for 6%

profile of v1, /device:TPU:198, one launch (start us, length us, event | category | flops | bytes accessed | tf_op | source)
XLA Modules:
  0.0 162.6 jit_solution(16360478507804519789)
XLA Ops:
  0.0 0.1 stack.23.pos
  0.1 1.4 copy-done
  1.5 6.4 %shard_map.37 = (bf16[64,1920]{1,0:T(8,128)(2,1)S(1)}, bf16[64,1920]{1,0:T(8,128)(2,1)S(1)}, bf16[64,1920]{1,0:T(8,128)(2,1)S(1)}, bf16[64,1920]{1,0:T(8,128)(2,...) custom-call(s32[5]{0:T(128)S(1)} %stack.23.pos, ...), custom_call_target="tpu_custom_call" | custom-call | flops 3000000000 | bytes 8000000 | tf_op jit(solution)/shard_map/pallas_call | solution.py:132
  7.9 1.7 %collective-permute-start.12 = (bf16[96,1920]{1,0:T(8,128)(2,1)S(1)}, bf16[96,1920]{1,0:T(8,128)(2,1)S(1)}, u32[]{:S(2)}, u32[]{:S(2)}) collective-permute-start(bf16[96,1920]{1,0:T(8,128)(2,1)S(1)} %get-tuple-element.18), channel_id=1, source_target_pairs={{0,64},{64,128},{128,192},{192,0},{1,65},{65,129},{129,193},{193,1... | collective-permute-start | bytes 1105928 | tf_op jit(solution)/shard_map/ppermute | solution.py:152
  9.5 2.9 %collective-permute-start.13 = (bf16[96,1920]{1,0:T(8,128)(2,1)S(1)}, bf16[96,1920]{1,0:T(8,128)(2,1)}, u32[]{:S(2)}, u32[]{:S(2)}) collective-permute-start(bf16[96,1920]{1,0:T(8,128)(2,1)S(1)} %get-tuple-element.19), channel_id=1, source_target_pairs={{0,128},{64,192},{128,0},{192,64},{1,129},{65,193},{129,1},{193,65... | collective-permute-start | bytes 1105928 | tf_op jit(solution)/shard_map/ppermute | solution.py:152
  12.4 1.3 collective-permute-start.14
  13.8 5.8 %collective-permute-done.12 = bf16[96,1920]{1,0:T(8,128)(2,1)S(1)} collective-permute-done((bf16[96,1920]{1,0:T(8,128)(2,1)S(1)}, bf16[96,1920]{1,0:T(8,128)(2,1)S(1)}, u32[]{:S(2)}, u32[]{:S(2)}) %collective-permute-start.12) | collective-permute-done | bytes 368672 | tf_op jit(solution)/shard_map/ppermute | solution.py:152
  19.5 9.2 %collective-permute-done.13 = bf16[96,1920]{1,0:T(8,128)(2,1)} collective-permute-done((bf16[96,1920]{1,0:T(8,128)(2,1)S(1)}, bf16[96,1920]{1,0:T(8,128)(2,1)}, u32[]{:S(2)}, u32[]{:S(2)}) %collective-permute-start.13) | collective-permute-done | bytes 368672 | tf_op jit(solution)/shard_map/ppermute | solution.py:152
  28.7 0.0 collective-permute-done.14
  28.7 1.3 add_convert_fusion
  30.1 0.1 pad_maximum_fusion.4
  30.1 0.6 collective-permute-start.15
  30.7 2.4 %collective-permute-start.16 = (bf16[48,1920]{1,0:T(8,128)(2,1)S(1)}, bf16[48,1920]{1,0:T(8,128)(2,1)S(1)}, u32[]{:S(2)}, u32[]{:S(2)}) collective-permute-start(bf16[48,1920]{1,0:T(8,128)(2,1)S(1)} %get-tuple-element.32), channel_id=1, source_target_pairs={{0,32},{16,48},{32,0},{48,16},{1,33},{17,49},{33,1},{49,17},{2,34}... | collective-permute-start | bytes 552968 | tf_op jit(solution)/shard_map/ppermute | solution.py:152
  33.1 0.0 collective-permute-start.17
  33.1 1.1 collective-permute-start.25
  34.2 3.6 %collective-permute-done.15 = bf16[48,1920]{1,0:T(8,128)(2,1)S(1)} collective-permute-done((bf16[48,1920]{1,0:T(8,128)(2,1)S(1)}, bf16[48,1920]{1,0:T(8,128)(2,1)S(1)}, u32[]{:S(2)}, u32[]{:S(2)}) %collective-permute-start.15) | collective-permute-done | bytes 184352 | tf_op jit(solution)/shard_map/ppermute | solution.py:152
  37.8 2.0 %collective-permute-done.16 = bf16[48,1920]{1,0:T(8,128)(2,1)S(1)} collective-permute-done((bf16[48,1920]{1,0:T(8,128)(2,1)S(1)}, bf16[48,1920]{1,0:T(8,128)(2,1)S(1)}, u32[]{:S(2)}, u32[]{:S(2)}) %collective-permute-start.16) | collective-permute-done | bytes 184352 | tf_op jit(solution)/shard_map/ppermute | solution.py:152
  39.8 2.4 %collective-permute-done.17 = bf16[48,1920]{1,0:T(8,128)(2,1)S(1)} collective-permute-done((bf16[48,1920]{1,0:T(8,128)(2,1)S(1)}, bf16[48,1920]{1,0:T(8,128)(2,1)S(1)}, u32[]{:S(2)}, u32[]{:S(2)}) %collective-permute-start.17) | collective-permute-done | bytes 184352 | tf_op jit(solution)/shard_map/ppermute | solution.py:152
  42.2 0.1 add_multiply_fusion
  42.3 0.1 fusion.1
  42.4 0.9 tile.2
  43.3 6.3 %all-to-all-start = ((bf16[8,16,2560]{2,1,0:T(8,128)(2,1)}), bf16[8,16,2560]{2,1,0:T(8,128)(2,1)S(1)}, u32[]{:S(2)}, u32[]{:S(2)}) async-start(bf16[8,16,2560]{2,1,0:T(8,128)(2,1)} %tile.2), calls=%async_computation | async-start | bytes 1310720 | tf_op jit(solution)/shard_map/all_to_all | solution.py:197
  49.6 2.3 %collective-permute-start = (bf16[64,1920]{1,0:T(8,128)(2,1)S(1)}, bf16[64,1920]{1,0:T(8,128)(2,1)S(1)}, u32[]{:S(2)}, u32[]{:S(2)}) collective-permute-start(bf16[64,1920]{1,0:T(8,128)(2,1)S(1)} %get-tuple-element.14), channel_id=1, source_target_pairs={{0,16},{16,32},{32,48},{48,0},{1,17},{17,33},{33,49},{49,1},{2,18}... | collective-permute-start | bytes 737288 | tf_op jit(solution)/shard_map/ppermute | solution.py:152
  51.9 2.3 %collective-permute-start.1 = (bf16[64,1920]{1,0:T(8,128)(2,1)S(1)}, bf16[64,1920]{1,0:T(8,128)(2,1)}, u32[]{:S(2)}, u32[]{:S(2)}) collective-permute-start(bf16[64,1920]{1,0:T(8,128)(2,1)S(1)} %get-tuple-element.15), channel_id=1, source_target_pairs={{0,32},{16,48},{32,0},{48,16},{1,33},{17,49},{33,1},{49,17},{2,34}... | collective-permute-start | bytes 737288 | tf_op jit(solution)/shard_map/ppermute | solution.py:152
  54.2 0.0 collective-permute-start.2
  54.2 2.7 %constant_dynamic-slice_fusion = bf16[2,1536,256]{2,1,0:T(8,128)(2,1)} fusion(bf16[2,1536,384]{2,1,0:T(8,128)(2,1)} %w_own.1, s32[]{:T(128)S(6)} %select_n.98), kind=kLoop, calls=%fused_computation.15 | loop fusion | bytes 3145732 | tf_op jit(solution)/shard_map/dynamic_slice | solution.py:177
  56.8 0.7 collective-permute-start.26
  57.6 39.9 %collective-permute-done = bf16[64,1920]{1,0:T(8,128)(2,1)S(1)} collective-permute-done((bf16[64,1920]{1,0:T(8,128)(2,1)S(1)}, bf16[64,1920]{1,0:T(8,128)(2,1)S(1)}, u32[]{:S(2)}, u32[]{:S(2)}) %collective-permute-start) | collective-permute-done | bytes 245792 | tf_op jit(solution)/shard_map/ppermute | solution.py:152
  97.6 2.1 %collective-permute-done.1 = bf16[64,1920]{1,0:T(8,128)(2,1)} collective-permute-done((bf16[64,1920]{1,0:T(8,128)(2,1)S(1)}, bf16[64,1920]{1,0:T(8,128)(2,1)}, u32[]{:S(2)}, u32[]{:S(2)}) %collective-permute-start.1) | collective-permute-done | bytes 245792 | tf_op jit(solution)/shard_map/ppermute | solution.py:152
  99.7 1.3 collective-permute-done.2
  101.0 1.2 add_convert_fusion.1
  102.2 1.7 %collective-permute-start.3 = (bf16[16,1920]{1,0:T(8,128)(2,1)S(1)}, bf16[16,1920]{1,0:T(8,128)(2,1)S(1)}, u32[]{:S(2)}, u32[]{:S(2)}) collective-permute-start(bf16[16,1920]{1,0:T(8,128)(2,1)S(1)} %get-tuple-element.25), channel_id=1, source_target_pairs={{0,64},{64,128},{128,192},{192,0},{1,65},{65,129},{129,193},{193,1... | collective-permute-start | bytes 184328 | tf_op jit(solution)/shard_map/ppermute | solution.py:152
  103.9 3.1 %collective-permute-start.4 = (bf16[16,1920]{1,0:T(8,128)(2,1)S(1)}, bf16[16,1920]{1,0:T(8,128)(2,1)S(1)}, u32[]{:S(2)}, u32[]{:S(2)}) collective-permute-start(bf16[16,1920]{1,0:T(8,128)(2,1)S(1)} %get-tuple-element.27), channel_id=1, source_target_pairs={{0,128},{64,192},{128,0},{192,64},{1,129},{65,193},{129,1},{193,65... | collective-permute-start | bytes 184328 | tf_op jit(solution)/shard_map/ppermute | solution.py:152
  106.9 0.2 collective-permute-start.5
  107.2 1.2 collective-permute-done.3
  108.4 0.0 all-to-all-done
  108.4 0.0 collective-permute-start.24
  108.4 1.4 collective-permute-done.4
  109.8 1.4 collective-permute-done.5
  111.2 0.1 collective-permute-start.6
  111.3 2.9 %collective-permute-start.7 = (bf16[16,1920]{1,0:T(8,128)(2,1)S(1)}, bf16[16,1920]{1,0:T(8,128)(2,1)S(1)}, u32[]{:S(2)}, u32[]{:S(2)}) collective-permute-start(bf16[16,1920]{1,0:T(8,128)(2,1)S(1)} %multiply_convert_fusion), channel_id=1, source_target_pairs={{0,128},{64,192},{128,0},{192,64},{1,129},{65,193},{129,1},{193,65... | collective-permute-start | bytes 184328 | tf_op jit(solution)/shard_map/ppermute | solution.py:152
  114.2 3.2 %collective-permute-done.6 = bf16[16,1920]{1,0:T(8,128)(2,1)S(1)} collective-permute-done((bf16[16,1920]{1,0:T(8,128)(2,1)S(1)}, bf16[16,1920]{1,0:T(8,128)(2,1)S(1)}, u32[]{:S(2)}, u32[]{:S(2)}) %collective-permute-start.6) | collective-permute-done | bytes 61472 | tf_op jit(solution)/shard_map/ppermute | solution.py:152
  117.4 0.0 collective-permute-start.8
  117.4 0.0 collective-permute-done.7
  117.4 2.6 %collective-permute-start.18 = (bf16[16,1920]{1,0:T(8,128)(2,1)S(1)}, bf16[16,1920]{1,0:T(8,128)(2,1)S(1)}, u32[]{:S(2)}, u32[]{:S(2)}) collective-permute-start(bf16[16,1920]{1,0:T(8,128)(2,1)S(1)} %get-tuple-element.30), channel_id=1, source_target_pairs={{0,16},{16,32},{32,48},{48,0},{1,17},{17,33},{33,49},{49,1},{2,18}... | collective-permute-start | bytes 184328 | tf_op jit(solution)/shard_map/ppermute | solution.py:152
  120.0 1.6 collective-permute-done.8
  121.6 0.4 collective-permute-start.19
  122.0 0.4 collective-permute-done.18
  122.4 2.6 %collective-permute-start.20 = (bf16[16,1920]{1,0:T(8,128)(2,1)S(1)}, bf16[16,1920]{1,0:T(8,128)(2,1)S(1)}, u32[]{:S(2)}, u32[]{:S(2)}) collective-permute-start(bf16[16,1920]{1,0:T(8,128)(2,1)S(1)} %get-tuple-element.30), channel_id=1, source_target_pairs={{0,48},{16,0},{32,16},{48,32},{1,49},{17,1},{33,17},{49,33},{2,50}... | collective-permute-start | bytes 184328 | tf_op jit(solution)/shard_map/ppermute | solution.py:152
  125.1 2.9 %collective-permute-done.19 = bf16[16,1920]{1,0:T(8,128)(2,1)S(1)} collective-permute-done((bf16[16,1920]{1,0:T(8,128)(2,1)S(1)}, bf16[16,1920]{1,0:T(8,128)(2,1)S(1)}, u32[]{:S(2)}, u32[]{:S(2)}) %collective-permute-start.19) | collective-permute-done | bytes 61472 | tf_op jit(solution)/shard_map/ppermute | solution.py:152
  128.0 0.5 collective-permute-start.10
  128.4 2.8 %collective-permute-done.20 = bf16[16,1920]{1,0:T(8,128)(2,1)S(1)} collective-permute-done((bf16[16,1920]{1,0:T(8,128)(2,1)S(1)}, bf16[16,1920]{1,0:T(8,128)(2,1)S(1)}, u32[]{:S(2)}, u32[]{:S(2)}) %collective-permute-start.20) | collective-permute-done | bytes 61472 | tf_op jit(solution)/shard_map/ppermute | solution.py:152
  131.2 0.0 collective-permute-start.11
  131.3 4.6 %collective-permute-done.10.refs_2_ = bf16[64,1920]{1,0:T(8,128)(2,1)S(1)} collective-permute-done((bf16[64,1920]{1,0:T(8,128)(2,1)S(1)}, bf16[64,1920]{1,0:T(8,128)(2,1)S(1)}, u32[]{:S(2)}, u32[]{:S(2)}) %collective-permute-start.10) | collective-permute-done | bytes 245792 | tf_op jit(solution)/shard_map/ppermute | solution.py:152
  135.8 4.6 %collective-permute-start.9 = (bf16[64,1920]{1,0:T(8,128)(2,1)S(1)}, bf16[64,1920]{1,0:T(8,128)(2,1)S(1)}, u32[]{:S(2)}, u32[]{:S(2)}) collective-permute-start(bf16[64,1920]{1,0:T(8,128)(2,1)S(1)} %pad_maximum_fusion.refs_0_), channel_id=1, source_target_pairs={{0,16},{16,32},{32,48},{48,0},{1,17},{17,33},{33,49},{49,1},{2,18}... | collective-permute-start | bytes 737288 | tf_op jit(solution)/shard_map/ppermute | solution.py:152
  140.4 0.0 collective-permute-done.24.other
  140.4 2.9 %collective-permute-start.22 = (bf16[64,1920]{1,0:T(8,128)(2,1)S(1)}, bf16[64,1920]{1,0:T(8,128)(2,1)S(1)}, u32[]{:S(2)}, u32[]{:S(2)}) collective-permute-start(bf16[64,1920]{1,0:T(8,128)(2,1)S(1)} %pad_maximum_fusion.1.refs_4_), channel_id=1, source_target_pairs={{0,128},{64,192},{128,0},{192,64},{1,129},{65,193},{129,1},{193,65... | collective-permute-start | bytes 737288 | tf_op jit(solution)/shard_map/ppermute | solution.py:152
  143.4 0.0 collective-permute-done.25.w_pair
  143.4 0.6 collective-permute-start.23
  144.0 10.5 %shard_map.38.refs_8_ = bf16[2,1536,384]{2,1,0:T(8,128)(2,1)S(1)} custom-call(s32[5]{0:T(128)S(1)} %stack.23.pos, bf16[128,2560]{1,0:T(8,128)(2,1)S(1)} %bitcast.7, bf16[128,2560]{1,0:T(8,128)(2,1)S(1)} %collective-permute-done.24.other, bf16[2,1536,384]{2,1,0:T(8,128)(2,1)} %w_own.1, bf16[2,1536,384]{2,1,0:T(8,128)(2,1)} %collective-permute-done.25.w_pair, ...), custom_call_target="tpu_custom_call" | custom-call | flops 5000000000 | bytes 8000000 | tf_op jit(solution)/shard_map/pallas_call | solution.py:132
  154.5 0.0 collective-permute-done.9.refs_1_
  154.5 0.0 collective-permute-done.21.refs_5_
  154.6 0.0 collective-permute-done.23.refs_7_
  154.6 8.0 %shard_map.39 = bf16[2,1536,384]{2,1,0:T(8,128)(2,1)} custom-call(s32[5]{0:T(128)S(1)} %stack.23.pos, bf16[64,1920]{1,0:T(8,128)(2,1)S(1)} %pad_maximum_fusion.refs_0_, bf16[64,1920]{1,0:T(8,128)(2,1)S(1)} %collective-permute-done.9.refs_1_, bf16[64,1920]{1,0:T(8,128)(2,1)S(1)} %collective-permute-done.10.refs_2_, ...), custom_call_target="tpu_custom_call" | custom-call | flops 5000000000 | bytes 8000000 | tf_op jit(solution)/shard_map/pallas_call | solution.py:132
  (13 shorter events, 0.2 us)
Async XLA Ops:
  0.1 1.4 copy-start
  7.9 11.7 %collective-permute-start.12 = (bf16[96,1920]{1,0:T(8,128)(2,1)S(1)}, bf16[96,1920]{1,0:T(8,128)(2,1)S(1)}, u32[]{:S(2)}, u32[]{:S(2)}) collective-permute-start(bf16[96,1920]{1,0:T(8,128)(2,1)S(1)} %get-tuple-element.18), channel_id=1, source_target_pairs={{0,64},{64,128},{128,192},{192,0},{1,65},{65,129},{129,193},{193,1... | collective-permute-start | bytes 1105928 | tf_op jit(solution)/shard_map/ppermute | solution.py:152
  9.5 19.2 %collective-permute-start.13 = (bf16[96,1920]{1,0:T(8,128)(2,1)S(1)}, bf16[96,1920]{1,0:T(8,128)(2,1)}, u32[]{:S(2)}, u32[]{:S(2)}) collective-permute-start(bf16[96,1920]{1,0:T(8,128)(2,1)S(1)} %get-tuple-element.19), channel_id=1, source_target_pairs={{0,128},{64,192},{128,0},{192,64},{1,129},{65,193},{129,1},{193,65... | collective-permute-start | bytes 1105928 | tf_op jit(solution)/shard_map/ppermute | solution.py:152
  12.4 16.3 %collective-permute-start.14 = (bf16[96,1920]{1,0:T(8,128)(2,1)S(1)}, bf16[96,1920]{1,0:T(8,128)(2,1)}, u32[]{:S(2)}, u32[]{:S(2)}) collective-permute-start(bf16[96,1920]{1,0:T(8,128)(2,1)S(1)} %get-tuple-element.20), channel_id=1, source_target_pairs={{0,192},{64,0},{128,64},{192,128},{1,193},{65,1},{129,65},{193,129... | collective-permute-start | bytes 1105928 | tf_op jit(solution)/shard_map/ppermute | solution.py:152
  30.1 7.7 %collective-permute-start.15 = (bf16[48,1920]{1,0:T(8,128)(2,1)S(1)}, bf16[48,1920]{1,0:T(8,128)(2,1)S(1)}, u32[]{:S(2)}, u32[]{:S(2)}) collective-permute-start(bf16[48,1920]{1,0:T(8,128)(2,1)S(1)} %get-tuple-element.31), channel_id=1, source_target_pairs={{0,16},{16,32},{32,48},{48,0},{1,17},{17,33},{33,49},{49,1},{2,18}... | collective-permute-start | bytes 552968 | tf_op jit(solution)/shard_map/ppermute | solution.py:152
  30.7 9.1 %collective-permute-start.16 = (bf16[48,1920]{1,0:T(8,128)(2,1)S(1)}, bf16[48,1920]{1,0:T(8,128)(2,1)S(1)}, u32[]{:S(2)}, u32[]{:S(2)}) collective-permute-start(bf16[48,1920]{1,0:T(8,128)(2,1)S(1)} %get-tuple-element.32), channel_id=1, source_target_pairs={{0,32},{16,48},{32,0},{48,16},{1,33},{17,49},{33,1},{49,17},{2,34}... | collective-permute-start | bytes 552968 | tf_op jit(solution)/shard_map/ppermute | solution.py:152
  33.1 9.0 %collective-permute-start.17 = (bf16[48,1920]{1,0:T(8,128)(2,1)S(1)}, bf16[48,1920]{1,0:T(8,128)(2,1)S(1)}, u32[]{:S(2)}, u32[]{:S(2)}) collective-permute-start(bf16[48,1920]{1,0:T(8,128)(2,1)S(1)} %get-tuple-element.33), channel_id=1, source_target_pairs={{0,48},{16,0},{32,16},{48,32},{1,49},{17,1},{33,17},{49,33},{2,50}... | collective-permute-start | bytes 552968 | tf_op jit(solution)/shard_map/ppermute | solution.py:152
  33.1 110.2 %collective-permute-start.25 = (bf16[2,1536,384]{2,1,0:T(8,128)(2,1)}, bf16[2,1536,384]{2,1,0:T(8,128)(2,1)}, u32[]{:S(2)}, u32[]{:S(2)}) collective-permute-start(bf16[2,1536,384]{2,1,0:T(8,128)(2,1)} %w_own.1), channel_id=1, source_target_pairs={{0,16},{16,0},{32,48},{48,32},{1,17},{17,1},{33,49},{49,33},{2,18}... | collective-permute-start | bytes 7077896 | tf_op jit(solution)/shard_map/ppermute | solution.py:176
  43.3 65.0 %all-to-all-start = ((bf16[8,16,2560]{2,1,0:T(8,128)(2,1)}), bf16[8,16,2560]{2,1,0:T(8,128)(2,1)S(1)}, u32[]{:S(2)}, u32[]{:S(2)}) async-start(bf16[8,16,2560]{2,1,0:T(8,128)(2,1)} %tile.2), calls=%async_computation | async-start | bytes 1310720 | tf_op jit(solution)/shard_map/all_to_all | solution.py:197
  49.6 47.9 %collective-permute-start = (bf16[64,1920]{1,0:T(8,128)(2,1)S(1)}, bf16[64,1920]{1,0:T(8,128)(2,1)S(1)}, u32[]{:S(2)}, u32[]{:S(2)}) collective-permute-start(bf16[64,1920]{1,0:T(8,128)(2,1)S(1)} %get-tuple-element.14), channel_id=1, source_target_pairs={{0,16},{16,32},{32,48},{48,0},{1,17},{17,33},{33,49},{49,1},{2,18}... | collective-permute-start | bytes 737288 | tf_op jit(solution)/shard_map/ppermute | solution.py:152
  51.9 47.8 %collective-permute-start.1 = (bf16[64,1920]{1,0:T(8,128)(2,1)S(1)}, bf16[64,1920]{1,0:T(8,128)(2,1)}, u32[]{:S(2)}, u32[]{:S(2)}) collective-permute-start(bf16[64,1920]{1,0:T(8,128)(2,1)S(1)} %get-tuple-element.15), channel_id=1, source_target_pairs={{0,32},{16,48},{32,0},{48,16},{1,33},{17,49},{33,1},{49,17},{2,34}... | collective-permute-start | bytes 737288 | tf_op jit(solution)/shard_map/ppermute | solution.py:152
  54.2 46.8 %collective-permute-start.2 = (bf16[64,1920]{1,0:T(8,128)(2,1)S(1)}, bf16[64,1920]{1,0:T(8,128)(2,1)}, u32[]{:S(2)}, u32[]{:S(2)}) collective-permute-start(bf16[64,1920]{1,0:T(8,128)(2,1)S(1)} %get-tuple-element.16), channel_id=1, source_target_pairs={{0,48},{16,0},{32,16},{48,32},{1,49},{17,1},{33,17},{49,33},{2,50}... | collective-permute-start | bytes 737288 | tf_op jit(solution)/shard_map/ppermute | solution.py:152
  56.8 83.6 %collective-permute-start.26 = (bf16[2,1536,256]{2,1,0:T(8,128)(2,1)}, bf16[2,1536,256]{2,1,0:T(8,128)(2,1)S(1)}, u32[]{:S(2)}, u32[]{:S(2)}) collective-permute-start(bf16[2,1536,256]{2,1,0:T(8,128)(2,1)} %constant_dynamic-slice_fusion), channel_id=1, source_target_pairs={{16,32},{32,16},{17,33},{33,17},{18,34},{34,18},{19,35},{35,19},{2... | collective-permute-start | bytes 4718600 | tf_op jit(solution)/shard_map/ppermute | solution.py:178
  102.2 6.2 %collective-permute-start.3 = (bf16[16,1920]{1,0:T(8,128)(2,1)S(1)}, bf16[16,1920]{1,0:T(8,128)(2,1)S(1)}, u32[]{:S(2)}, u32[]{:S(2)}) collective-permute-start(bf16[16,1920]{1,0:T(8,128)(2,1)S(1)} %get-tuple-element.25), channel_id=1, source_target_pairs={{0,64},{64,128},{128,192},{192,0},{1,65},{65,129},{129,193},{193,1... | collective-permute-start | bytes 184328 | tf_op jit(solution)/shard_map/ppermute | solution.py:152
  103.9 5.9 %collective-permute-start.4 = (bf16[16,1920]{1,0:T(8,128)(2,1)S(1)}, bf16[16,1920]{1,0:T(8,128)(2,1)S(1)}, u32[]{:S(2)}, u32[]{:S(2)}) collective-permute-start(bf16[16,1920]{1,0:T(8,128)(2,1)S(1)} %get-tuple-element.27), channel_id=1, source_target_pairs={{0,128},{64,192},{128,0},{192,64},{1,129},{65,193},{129,1},{193,65... | collective-permute-start | bytes 184328 | tf_op jit(solution)/shard_map/ppermute | solution.py:152
  106.9 4.2 %collective-permute-start.5 = (bf16[16,1920]{1,0:T(8,128)(2,1)S(1)}, bf16[16,1920]{1,0:T(8,128)(2,1)S(1)}, u32[]{:S(2)}, u32[]{:S(2)}) collective-permute-start(bf16[16,1920]{1,0:T(8,128)(2,1)S(1)} %get-tuple-element.26), channel_id=1, source_target_pairs={{0,192},{64,0},{128,64},{192,128},{1,193},{65,1},{129,65},{193,129... | collective-permute-start | bytes 184328 | tf_op jit(solution)/shard_map/ppermute | solution.py:152
  108.4 32.1 %collective-permute-start.24 = (bf16[128,2560]{1,0:T(8,128)(2,1)S(1)}, bf16[128,2560]{1,0:T(8,128)(2,1)S(1)}, u32[]{:S(2)}, u32[]{:S(2)}) collective-permute-start(bf16[128,2560]{1,0:T(8,128)(2,1)S(1)} %bitcast.6), channel_id=1, source_target_pairs={{0,1},{1,0},{2,3},{3,2},{4,5},{5,4},{6,7},{7,6},{8,9},{9,8},{10,11... | collective-permute-start | bytes 1966088 | tf_op jit(solution)/shard_map/ppermute | solution.py:202
  111.2 6.2 %collective-permute-start.6 = (bf16[16,1920]{1,0:T(8,128)(2,1)S(1)}, bf16[16,1920]{1,0:T(8,128)(2,1)S(1)}, u32[]{:S(2)}, u32[]{:S(2)}) collective-permute-start(bf16[16,1920]{1,0:T(8,128)(2,1)S(1)} %multiply_convert_fusion), channel_id=1, source_target_pairs={{0,64},{64,128},{128,192},{192,0},{1,65},{65,129},{129,193},{193,1... | collective-permute-start | bytes 184328 | tf_op jit(solution)/shard_map/ppermute | solution.py:152
  111.3 6.1 %collective-permute-start.7 = (bf16[16,1920]{1,0:T(8,128)(2,1)S(1)}, bf16[16,1920]{1,0:T(8,128)(2,1)S(1)}, u32[]{:S(2)}, u32[]{:S(2)}) collective-permute-start(bf16[16,1920]{1,0:T(8,128)(2,1)S(1)} %multiply_convert_fusion), channel_id=1, source_target_pairs={{0,128},{64,192},{128,0},{192,64},{1,129},{65,193},{129,1},{193,65... | collective-permute-start | bytes 184328 | tf_op jit(solution)/shard_map/ppermute | solution.py:152
  117.4 4.2 %collective-permute-start.8 = (bf16[16,1920]{1,0:T(8,128)(2,1)S(1)}, bf16[16,1920]{1,0:T(8,128)(2,1)S(1)}, u32[]{:S(2)}, u32[]{:S(2)}) collective-permute-start(bf16[16,1920]{1,0:T(8,128)(2,1)S(1)} %multiply_convert_fusion), channel_id=1, source_target_pairs={{0,192},{64,0},{128,64},{192,128},{1,193},{65,1},{129,65},{193,129... | collective-permute-start | bytes 184328 | tf_op jit(solution)/shard_map/ppermute | solution.py:152
  117.4 5.0 %collective-permute-start.18 = (bf16[16,1920]{1,0:T(8,128)(2,1)S(1)}, bf16[16,1920]{1,0:T(8,128)(2,1)S(1)}, u32[]{:S(2)}, u32[]{:S(2)}) collective-permute-start(bf16[16,1920]{1,0:T(8,128)(2,1)S(1)} %get-tuple-element.30), channel_id=1, source_target_pairs={{0,16},{16,32},{32,48},{48,0},{1,17},{17,33},{33,49},{49,1},{2,18}... | collective-permute-start | bytes 184328 | tf_op jit(solution)/shard_map/ppermute | solution.py:152
  121.6 6.4 %collective-permute-start.19 = (bf16[16,1920]{1,0:T(8,128)(2,1)S(1)}, bf16[16,1920]{1,0:T(8,128)(2,1)S(1)}, u32[]{:S(2)}, u32[]{:S(2)}) collective-permute-start(bf16[16,1920]{1,0:T(8,128)(2,1)S(1)} %get-tuple-element.30), channel_id=1, source_target_pairs={{0,32},{16,48},{32,0},{48,16},{1,33},{17,49},{33,1},{49,17},{2,34}... | collective-permute-start | bytes 184328 | tf_op jit(solution)/shard_map/ppermute | solution.py:152
  122.4 8.8 %collective-permute-start.20 = (bf16[16,1920]{1,0:T(8,128)(2,1)S(1)}, bf16[16,1920]{1,0:T(8,128)(2,1)S(1)}, u32[]{:S(2)}, u32[]{:S(2)}) collective-permute-start(bf16[16,1920]{1,0:T(8,128)(2,1)S(1)} %get-tuple-element.30), channel_id=1, source_target_pairs={{0,48},{16,0},{32,16},{48,32},{1,49},{17,1},{33,17},{49,33},{2,50}... | collective-permute-start | bytes 184328 | tf_op jit(solution)/shard_map/ppermute | solution.py:152
  128.0 7.8 %collective-permute-start.10 = (bf16[64,1920]{1,0:T(8,128)(2,1)S(1)}, bf16[64,1920]{1,0:T(8,128)(2,1)S(1)}, u32[]{:S(2)}, u32[]{:S(2)}) collective-permute-start(bf16[64,1920]{1,0:T(8,128)(2,1)S(1)} %pad_maximum_fusion.refs_0_), channel_id=1, source_target_pairs={{0,32},{16,48},{32,0},{48,16},{1,33},{17,49},{33,1},{49,17},{2,34}... | collective-permute-start | bytes 737288 | tf_op jit(solution)/shard_map/ppermute | solution.py:152
  131.2 23.3 %collective-permute-start.11 = (bf16[64,1920]{1,0:T(8,128)(2,1)S(1)}, bf16[64,1920]{1,0:T(8,128)(2,1)S(1)}, u32[]{:S(2)}, u32[]{:S(2)}) collective-permute-start(bf16[64,1920]{1,0:T(8,128)(2,1)S(1)} %pad_maximum_fusion.refs_0_), channel_id=1, source_target_pairs={{0,48},{16,0},{32,16},{48,32},{1,49},{17,1},{33,17},{49,33},{2,50}... | collective-permute-start | bytes 737288 | tf_op jit(solution)/shard_map/ppermute | solution.py:152
  135.8 18.7 %collective-permute-start.9 = (bf16[64,1920]{1,0:T(8,128)(2,1)S(1)}, bf16[64,1920]{1,0:T(8,128)(2,1)S(1)}, u32[]{:S(2)}, u32[]{:S(2)}) collective-permute-start(bf16[64,1920]{1,0:T(8,128)(2,1)S(1)} %pad_maximum_fusion.refs_0_), channel_id=1, source_target_pairs={{0,16},{16,32},{32,48},{48,0},{1,17},{17,33},{33,49},{49,1},{2,18}... | collective-permute-start | bytes 737288 | tf_op jit(solution)/shard_map/ppermute | solution.py:152
  140.4 14.1 %collective-permute-start.21 = (bf16[64,1920]{1,0:T(8,128)(2,1)S(1)}, bf16[64,1920]{1,0:T(8,128)(2,1)S(1)}, u32[]{:S(2)}, u32[]{:S(2)}) collective-permute-start(bf16[64,1920]{1,0:T(8,128)(2,1)S(1)} %pad_maximum_fusion.1.refs_4_), channel_id=1, source_target_pairs={{0,64},{64,128},{128,192},{192,0},{1,65},{65,129},{129,193},{193,1... | collective-permute-start | bytes 737288 | tf_op jit(solution)/shard_map/ppermute | solution.py:152
  140.4 14.1 %collective-permute-start.22 = (bf16[64,1920]{1,0:T(8,128)(2,1)S(1)}, bf16[64,1920]{1,0:T(8,128)(2,1)S(1)}, u32[]{:S(2)}, u32[]{:S(2)}) collective-permute-start(bf16[64,1920]{1,0:T(8,128)(2,1)S(1)} %pad_maximum_fusion.1.refs_4_), channel_id=1, source_target_pairs={{0,128},{64,192},{128,0},{192,64},{1,129},{65,193},{129,1},{193,65... | collective-permute-start | bytes 737288 | tf_op jit(solution)/shard_map/ppermute | solution.py:152
  143.4 11.2 %collective-permute-start.23 = (bf16[64,1920]{1,0:T(8,128)(2,1)S(1)}, bf16[64,1920]{1,0:T(8,128)(2,1)S(1)}, u32[]{:S(2)}, u32[]{:S(2)}) collective-permute-start(bf16[64,1920]{1,0:T(8,128)(2,1)S(1)} %pad_maximum_fusion.1.refs_4_), channel_id=1, source_target_pairs={{0,192},{64,0},{128,64},{192,128},{1,193},{65,1},{129,65},{193,129... | collective-permute-start | bytes 737288 | tf_op jit(solution)/shard_map/ppermute | solution.py:152

commit v2 on v1

v2 whole, which is shorter than its diff:
```python
import jax
import jax.numpy as jnp
from jax import lax
from jax.experimental import pallas as pl
from jax.experimental.pallas import tpu as pltpu
from jax.sharding import Mesh, PartitionSpec as P

BLK = 512
SUB = 128
damping = 0.1
TOKENS = 4096
F32 = jnp.float32
BF16 = jnp.bfloat16
VMEM = pltpu.VMEM

PAIRS = [(r, c) for r in range(4) for c in range(r, 4)]
LANES = 15 * SUB


def tn_dot(a, b):
    return lax.dot_general(a, b, (((0,), (0,)), ((), ())), preferred_element_type=F32)


def nn_dot(a, b):
    return lax.dot_general(a, b, (((1,), (0,)), ((), ())), preferred_element_type=F32)


def cov_kernel(pos, acts, grads, h0, h1, h2, h3, pack):
    y, part = pos[1], pos[3]
    sends = (h0, h1, h2, h3)
    for layer in range(2):
        for b in range(3):
            rows = grads[layer, :, b * BLK:(b + 1) * BLK]
            top = tn_dot(rows[:, :256], rows).astype(BF16)
            low = tn_dot(rows[:, 256:], rows[:, 256:]).astype(BF16)
            for i, (r, c) in enumerate(PAIRS):
                s = 10 * b + i
                if r < 2:
                    piece = top[r * SUB:(r + 1) * SUB, c * SUB:(c + 1) * SUB]
                else:
                    piece = low[(r - 2) * SUB:(r - 1) * SUB, (c - 2) * SUB:(c - 1) * SUB]
                pack[layer, s // 15 * SUB:(s // 15 + 1) * SUB, s % 15 * SUB:(s % 15 + 1) * SUB] = piece
    for d in range(4):
        at = pl.multiple_of((y + d) % 4 * 64, 64)
        sends[d][0:64, :] = pack[0, pl.ds(at, 64), :]
        sends[d][64:128, :] = pack[1, pl.ds(at, 64), :]
    k = lax.broadcasted_iota(jnp.int32, (BLK, 64), 0)
    m = lax.broadcasted_iota(jnp.int32, (BLK, 64), 1)
    select = jnp.where(k == m // 16 * SUB + part * 16 + m % 16, 1.0, 0.0).astype(BF16)
    for d in range(4):
        start = (y + d) % 4 * (3 * BLK)
        for j in range(3):
            rows = acts[0, :, pl.ds(pl.multiple_of(start + j * BLK, BLK), BLK)]
            chosen = nn_dot(rows, select).astype(BF16)
            cov = tn_dot(chosen, rows).astype(BF16)
            for i, (r, c) in enumerate(PAIRS):
                s = 10 * j + i
                sends[d][128 + s // 15 * 16:144 + s // 15 * 16, s % 15 * SUB:(s % 15 + 1) * SUB] = (
                    cov[r * 16:(r + 1) * 16, c * SUB:(c + 1) * SUB]
                )


def invert(packed_piece, full):
    for i, (r, c) in enumerate(PAIRS):
        piece = packed_piece(i).astype(F32)
        full[r * SUB:(r + 1) * SUB, c * SUB:(c + 1) * SUB] = piece
        if r != c:
            full[c * SUB:(c + 1) * SUB, r * SUB:(r + 1) * SUB] = piece.T
    ri = lax.broadcasted_iota(jnp.int32, (BLK, BLK), 0)
    ci = lax.broadcasted_iota(jnp.int32, (BLK, BLK), 1)
    diagonal = ri == ci
    matrix = full[...] + jnp.where(diagonal, damping, 0.0)
    two_eye = jnp.where(diagonal, 2.0, 0.0)
    sums = jnp.sum(jnp.abs(matrix), axis=0, keepdims=True)
    alpha = (1.0 / jnp.max(sums, axis=1, keepdims=True)).astype(BF16).astype(F32)
    low = matrix.astype(BF16)
    residue = (two_eye - low.astype(F32) * alpha).astype(BF16)
    iterate = (residue.astype(F32) * alpha).astype(BF16)
    image = nn_dot(low, iterate)
    residue = (two_eye - image).astype(BF16)
    return nn_dot(iterate, residue).astype(BF16)


def right_kernel(pos, mine, other, w_own, w_pair, w_mid, out, pack, full, diag):
    x, core = pos[0], pos[2]
    for q in range(4):
        at = pl.multiple_of(q * 32 + core * 16, 16)
        pack[pl.ds(at, 16), :] = mine[q * 16:(q + 1) * 16, :]
        at = pl.multiple_of(q * 32 + (1 - core) * 16, 16)
        pack[pl.ds(at, 16), :] = other[q * 16:(q + 1) * 16, :]
    base = x // 2 * BLK
    own = pl.multiple_of(x * 384 - base, SUB)
    pair = pl.multiple_of((x + 1 - 2 * (x % 2)) * 384 - base, SUB)
    mid = pl.multiple_of(jnp.where(x == 1, 768, 0), SUB)
    for b in range(2):
        at = b * BLK
        inverse = invert(lambda i: pack[:, b * 1280 + i * SUB:b * 1280 + (i + 1) * SUB], full.at[b])
        diag[at:at + BLK, at:at + BLK] = inverse
        diag[at:at + BLK, BLK - at:2 * BLK - at] = jnp.zeros((BLK, BLK), BF16)
    columns = pl.ds(own, 384)
    total = nn_dot(w_own[0], diag[pl.ds(own, 384), columns])
    total += nn_dot(w_pair[...], diag[pl.ds(pair, 384), columns])
    total += nn_dot(w_mid[0], diag[pl.ds(mid, 256), columns])
    out[...] = total.astype(BF16)


def right(pos, sides, other, weight_grad, w_pair, w_mid, layer):
    rows = pl.BlockSpec((64, 2560), lambda i, p: (layer, 0))
    shape = jax.ShapeDtypeStruct(weight_grad.shape[1:], BF16)
    return call(
        right_kernel, pos, (sides, other, weight_grad, w_pair, w_mid),
        [rows, rows, of_layer(weight_grad, layer), whole(w_pair), of_layer(w_mid, layer)], [shape],
        [VMEM((128, 2560), BF16), VMEM((2, BLK, BLK), F32), VMEM((1024, 1024), BF16)], 2_500_000_000,
    )[0]


def left_kernel(pos, p0, p1, p2, p3, right, *refs):
    out, pack, full = refs[-3:]
    x, y = pos[0], pos[1]
    for d, part in enumerate((p0, p1, p2, p3)):
        for e in range(4):
            at = (y + 4 - d) % 4 * 64 + (x + 4 - e) % 4 * 16
            pack[pl.ds(pl.multiple_of(at, 16), 16), :] = part[e * 16:(e + 1) * 16, :]
    for b in range(3):
        def piece(i):
            s = 10 * b + i
            return pack[s // 15 * SUB:(s // 15 + 1) * SUB, s % 15 * SUB:(s % 15 + 1) * SUB]
        inverse = invert(piece, full.at[b])
        at = b * BLK
        out[0, at:at + BLK, :] = nn_dot(inverse, right[at:at + BLK, :]).astype(BF16)


def left(pos, parts, right, layer, before):
    operands = [*parts, right]
    in_specs = [whole(a) for a in operands]
    if before is not None:
        operands.append(before)
        in_specs.append(pl.BlockSpec(memory_space=pl.ANY))
    shape = jax.ShapeDtypeStruct((2,) + right.shape, BF16)
    return call(
        left_kernel, pos, operands, in_specs, [shape],
        [VMEM((256, LANES), BF16), VMEM((3, BLK, BLK), F32)], 2_500_000_000,
        out_specs=[of_layer(shape, layer)], aliases={} if before is None else {len(operands): 0},
    )[0]


def call(kernel, pos, operands, in_specs, out_shape, scratch, flops, out_specs=None, aliases={}):
    return pl.pallas_call(
        kernel,
        grid_spec=pltpu.PrefetchScalarGridSpec(
            num_scalar_prefetch=1,
            grid=(1,),
            in_specs=in_specs,
            out_specs=out_specs or [whole(s) for s in out_shape],
            scratch_shapes=scratch,
        ),
        out_shape=out_shape,
        input_output_aliases=aliases,
        compiler_params=pltpu.CompilerParams(vmem_limit_bytes=48 * 1024 * 1024),
        cost_estimate=pl.CostEstimate(flops=flops, bytes_accessed=8_000_000, transcendentals=0),
    )(pos, *operands)


def whole(a):
    return pl.BlockSpec(a.shape, lambda i, p, n=len(a.shape): (0,) * n)


def of_layer(a, layer):
    return pl.BlockSpec((1,) + a.shape[1:], lambda i, p: (layer, 0, 0))


def shift(a, axis, d):
    return lax.ppermute(a, axis, [(i, (i + d) % 4) for i in range(4)])


def add(parts):
    return sum(p.astype(F32) for p in parts)


def spread(parts, axis):
    return [parts[0]] + [shift(parts[d], axis, d) for d in (1, 2, 3)]


def gather(a, axis):
    return [a] + [shift(a, axis, d) for d in (1, 2, 3)]


def chunk(a, index, rows):
    return lax.dynamic_slice_in_dim(a, index % 4 * rows, rows, 0)


def body(acts, grads_out, weight_grad):
    y, x, z, c = (lax.axis_index(n) for n in ("y", "x", "z", "c"))
    part = z % 4 * 2 + c
    pos = jnp.stack([x, y, c, part, z // 4]).astype(jnp.int32)

    w_pair = [lax.ppermute(weight_grad[n], "x", [(0, 1), (1, 0), (2, 3), (3, 2)]) for n in range(2)]
    middle = lax.dynamic_slice_in_dim(weight_grad, jnp.where(x == 1, SUB, 0), 256, 2)
    w_mid = lax.ppermute(middle, "x", [(1, 2), (2, 1)])

    covs = call(
        cov_kernel, pos, (acts, grads_out),
        [pl.BlockSpec((1, 256, 6144), lambda i, p: (p[4], 0, 0)), whole(grads_out)],
        [jax.ShapeDtypeStruct((160, LANES), BF16)] * 4, [VMEM((2, 256, LANES), BF16)], 3_000_000_000,
    )
    rows = add(spread(covs, "y")).astype(BF16)
    rows, w_mid, w_pair[0] = lax.optimization_barrier((rows, w_mid, w_pair[0]))
    sends = [
        jnp.concatenate([chunk(rows[:64], x + d, 16), chunk(rows[64:128], x + d, 16), rows[128:]], axis=0)
        for d in range(4)
    ]
    rows = add(spread(sends, "x")) * (1.0 / TOKENS)
    side = jnp.concatenate([rows[32:48], rows[48:64]], axis=1)
    side = lax.dynamic_slice_in_dim(side, x // 2 * 1280, 2560, 1).astype(BF16)

    quarter = gather(rows[:32].astype(BF16), "x")
    first = gather(jnp.concatenate([q[:16] for q in quarter], axis=0), "y")
    second = gather(jnp.concatenate([q[16:] for q in quarter], axis=0), "y")
    sides = lax.all_to_all(jnp.tile(side, (8, 1)), "z", 0, 0, tiled=True)
    other = lax.ppermute(sides, "c", [(0, 1), (1, 0)])

    out = left(pos, first, right(pos, sides, other, weight_grad, w_pair[0], w_mid, 0), 0, None)
    return left(pos, second, right(pos, sides, other, weight_grad, w_pair[1], w_mid, 1), 1, out)


def solution(mesh):
    fine = Mesh(mesh.devices.reshape(4, 4, 8, 2), ("y", "x", "z", "c"))
    dp, owner = ("y", "x"), ("z", "c")
    in_specs = (P(None, dp, None), P(None, dp, owner), P(None, owner, dp))
    out_specs = P(None, owner, dp)
    return jax.shard_map(body, mesh=fine, in_specs=in_specs, out_specs=out_specs, check_vma=False)
```

time: 163 us -> 143 us (0.88)
  the two profiles are of different devices: /device:TPU:198 before, /device:TPU:1 now
where the time goes in v2:
time: 143 us; the launch traced here: 142 us
  waiting for transfers between devices  66.1 us (46%)
  starting transfers between devices  39.3 us (27%)
  Pallas kernels  28.7 us (20%)
  local copies, waits for them, and re-layouts  6.44 us (5%)
  other arithmetic  1.81 us (1%)
    ppermute x15, waiting for transfers between devices, shift(): return lax.ppermute(a, axis, [(i, (i + d) % 4) for i in range(4)])  66.1 us
    pallas_call x5, Pallas kernels, call(): pl.pallas_call(kernel, grid_spec=pltpu.PrefetchScalarGridSpec(num_scalar_...  28.7 us
    ppermute x15, starting transfers between devices, shift(): return lax.ppermute(a, axis, [(i, (i + d) % 4) for i in range(4)])  22 us
    all_to_all x1, starting transfers between devices, body(): sides = lax.all_to_all(jnp.tile(side, (8, 1)), 'z', 0, 0, tiled=True)  8.18 us
    ppermute x1, starting transfers between devices, body(): other = lax.ppermute(sides, 'c', [(0, 1), (1, 0)])  3.79 us
    ppermute x2, starting transfers between devices, body(): lax.ppermute(weight_grad[n], 'x', [(0, 1), (1, 0), (2, 3), (3, 2)])  3.32 us
  transfers between devices with their start and end apart: 20, of which 10 were waited for; matrix products, arithmetic and copies ran while one was open for 3% of the time, Pallas kernels for 17%

profile of v2, /device:TPU:1, one launch (start us, length us, event | category | flops | bytes accessed | tf_op | source)
XLA Modules:
  0.0 142.5 jit_solution(13731117740221222670)
XLA Ops:
  0.0 0.0 copy-start.1
  0.0 2.8 %constant_dynamic-slice_fusion.8 = bf16[2,1536,256]{2,1,0:T(8,128)(2,1)} fusion(bf16[2,1536,384]{2,1,0:T(8,128)(2,1)} %w_own.3, s32[]{:T(128)S(6)} %select_n.64), kind=kLoop, calls=%fused_computation.22 | loop fusion | bytes 3145732 | tf_op jit(solution)/shard_map/dynamic_slice | solution.py:198
  2.8 0.0 copy-start
  2.8 2.0 %collective-permute-start.3 = (bf16[2,1536,256]{2,1,0:T(8,128)(2,1)}, bf16[2,1536,256]{2,1,0:T(8,128)(2,1)}, u32[]{:S(2)}, u32[]{:S(2)}) collective-permute-start(bf16[2,1536,256]{2,1,0:T(8,128)(2,1)} %constant_dynamic-slice_fusion.8), channel_id=1, source_target_pairs={{16,32},{32,16},{17,33},{33,17},{18,34},{34,18},{19,35},{35,19},{2... | collective-permute-start | bytes 4718600 | tf_op jit(solution)/shard_map/ppermute | solution.py:199
  4.8 0.0 copy-done.1
  4.8 1.6 %slice_bitcast_fusion = (bf16[1536,384]{1,0:T(8,128)(2,1)}, bf16[1536,384]{1,0:T(8,128)(2,1)}) fusion(bf16[2,1536,384]{2,1,0:T(8,128)(2,1)S(1)} %copy-done.1), kind=kLoop, calls=%fused_computation.1 | loop fusion | bytes 4718592 | tf_op jit(solution)/shard_map/squeeze | solution.py:197
  6.4 3.3 %collective-permute-start.4 = (bf16[1536,384]{1,0:T(8,128)(2,1)}, bf16[1536,384]{1,0:T(8,128)(2,1)S(1)}, u32[]{:S(2)}, u32[]{:S(2)}) collective-permute-start(bf16[1536,384]{1,0:T(8,128)(2,1)} %get-tuple-element.20), channel_id=1, source_target_pairs={{0,16},{16,0},{32,48},{48,32},{1,17},{17,1},{33,49},{49,33},{2,18}... | collective-permute-start | bytes 3538952 | tf_op jit(solution)/shard_map/ppermute | solution.py:197
  9.7 0.1 stack.23.pos
  9.8 0.0 copy-done
  9.8 7.2 %shard_map.37 = (bf16[160,1920]{1,0:T(8,128)(2,1)S(1)}, bf16[160,1920]{1,0:T(8,128)(2,1)}, bf16[160,1920]{1,0:T(8,128)(2,1)}, bf16[160,1920]{1,0:T(8,128)(2,1)}) custom-call(s32[5]{0:T(128)S(1)} %stack.23.pos, bf16[2,256,6144]{2,1,0:T(8,128)(2,1)} %acts.1, bf16[2,256,1536]{2,1,0:T(8,128)(2,1)S(1)} %copy-done), custom_call_target="tpu_custom_call" | custom-call | flops 3000000000 | bytes 8000000 | tf_op jit(solution)/shard_map/pallas_call | solution.py:148
  17.0 1.3 collective-permute-start
  18.4 2.6 %collective-permute-start.1 = (bf16[160,1920]{1,0:T(8,128)(2,1)}, bf16[160,1920]{1,0:T(8,128)(2,1)S(1)}, u32[]{:S(2)}, u32[]{:S(2)}) collective-permute-start(bf16[160,1920]{1,0:T(8,128)(2,1)} %get-tuple-element.14), channel_id=1, source_target_pairs={{0,128},{64,192},{128,0},{192,64},{1,129},{65,193},{129,1},{193,65... | collective-permute-start | bytes 1843208 | tf_op jit(solution)/shard_map/ppermute | solution.py:173
  21.0 1.1 collective-permute-start.2
  22.0 10.7 %collective-permute-done = bf16[160,1920]{1,0:T(8,128)(2,1)S(1)} collective-permute-done((bf16[160,1920]{1,0:T(8,128)(2,1)}, bf16[160,1920]{1,0:T(8,128)(2,1)S(1)}, u32[]{:S(2)}, u32[]{:S(2)}) %collective-permute-start) | collective-permute-done | bytes 614432 | tf_op jit(solution)/shard_map/ppermute | solution.py:173
  32.7 14.3 %collective-permute-done.1 = bf16[160,1920]{1,0:T(8,128)(2,1)S(1)} collective-permute-done((bf16[160,1920]{1,0:T(8,128)(2,1)}, bf16[160,1920]{1,0:T(8,128)(2,1)S(1)}, u32[]{:S(2)}, u32[]{:S(2)}) %collective-permute-start.1) | collective-permute-done | bytes 614432 | tf_op jit(solution)/shard_map/ppermute | solution.py:173
  47.0 0.1 collective-permute-done.2
  47.1 1.4 add_convert_fusion
  48.6 0.0 collective-permute-done.4.w_pair
  48.6 0.0 collective-permute-done.3.w_mid
  48.7 0.1 constant_dynamic-slice_fusion.6
  48.7 0.1 pad_maximum_fusion.2
  48.8 0.2 collective-permute-start.5
  49.0 1.9 %collective-permute-start.6 = (bf16[64,1920]{1,0:T(8,128)(2,1)S(1)}, bf16[64,1920]{1,0:T(8,128)(2,1)S(1)}, u32[]{:S(2)}, u32[]{:S(2)}) collective-permute-start(bf16[64,1920]{1,0:T(8,128)(2,1)S(1)} %get-tuple-element.42), channel_id=1, source_target_pairs={{0,32},{16,48},{32,0},{48,16},{1,33},{17,49},{33,1},{49,17},{2,34}... | collective-permute-start | bytes 737288 | tf_op jit(solution)/shard_map/ppermute | solution.py:173
  50.9 1.4 collective-permute-start.7
  52.3 4.3 %collective-permute-done.5 = bf16[64,1920]{1,0:T(8,128)(2,1)S(1)} collective-permute-done((bf16[64,1920]{1,0:T(8,128)(2,1)S(1)}, bf16[64,1920]{1,0:T(8,128)(2,1)S(1)}, u32[]{:S(2)}, u32[]{:S(2)}) %collective-permute-start.5) | collective-permute-done | bytes 245792 | tf_op jit(solution)/shard_map/ppermute | solution.py:173
  56.5 3.6 %collective-permute-done.6 = bf16[64,1920]{1,0:T(8,128)(2,1)S(1)} collective-permute-done((bf16[64,1920]{1,0:T(8,128)(2,1)S(1)}, bf16[64,1920]{1,0:T(8,128)(2,1)S(1)}, u32[]{:S(2)}, u32[]{:S(2)}) %collective-permute-start.6) | collective-permute-done | bytes 245792 | tf_op jit(solution)/shard_map/ppermute | solution.py:173
  60.1 2.2 %collective-permute-done.7 = bf16[64,1920]{1,0:T(8,128)(2,1)S(1)} collective-permute-done((bf16[64,1920]{1,0:T(8,128)(2,1)S(1)}, bf16[64,1920]{1,0:T(8,128)(2,1)S(1)}, u32[]{:S(2)}, u32[]{:S(2)}) %collective-permute-start.7) | collective-permute-done | bytes 245792 | tf_op jit(solution)/shard_map/ppermute | solution.py:173
  62.4 0.1 add_multiply_fusion
  62.6 0.1 fusion.1
  62.7 0.9 tile.2
  63.6 8.2 %all-to-all-start = ((bf16[8,16,2560]{2,1,0:T(8,128)(2,1)}), bf16[8,16,2560]{2,1,0:T(8,128)(2,1)S(1)}, u32[]{:S(2)}, u32[]{:S(2)}) async-start(bf16[8,16,2560]{2,1,0:T(8,128)(2,1)} %tile.2), calls=%async_computation | async-start | bytes 1310720 | tf_op jit(solution)/shard_map/all_to_all | solution.py:219
  71.8 3.5 %collective-permute-start.10 = (bf16[32,1920]{1,0:T(8,128)(2,1)S(1)}, bf16[32,1920]{1,0:T(8,128)(2,1)S(1)}, u32[]{:S(2)}, u32[]{:S(2)}) collective-permute-start(bf16[32,1920]{1,0:T(8,128)(2,1)S(1)} %slice.77), channel_id=1, source_target_pairs={{0,48},{16,0},{32,16},{48,32},{1,49},{17,1},{33,17},{49,33},{2,50}... | collective-permute-start | bytes 368648 | tf_op jit(solution)/shard_map/ppermute | solution.py:173
  75.3 0.0 collective-permute-start.15
  75.3 1.3 collective-permute-start.9
  76.5 0.2 collective-permute-start.8
  76.7 0.4 collective-permute-done.10
  77.1 26.8 %collective-permute-done.9 = bf16[32,1920]{1,0:T(8,128)(2,1)S(1)} collective-permute-done((bf16[32,1920]{1,0:T(8,128)(2,1)S(1)}, bf16[32,1920]{1,0:T(8,128)(2,1)S(1)}, u32[]{:S(2)}, u32[]{:S(2)}) %collective-permute-start.9) | collective-permute-done | bytes 122912 | tf_op jit(solution)/shard_map/ppermute | solution.py:173
  103.9 0.0 all-to-all-done
  103.9 3.8 %collective-permute-start.14 = (bf16[128,2560]{1,0:T(8,128)(2,1)S(1)}, bf16[128,2560]{1,0:T(8,128)(2,1)S(1)}, u32[]{:S(2)}, u32[]{:S(2)}) collective-permute-start(bf16[128,2560]{1,0:T(8,128)(2,1)S(1)} %bitcast.10), channel_id=1, source_target_pairs={{0,1},{1,0},{2,3},{3,2},{4,5},{5,4},{6,7},{7,6},{8,9},{9,8},{10,11... | collective-permute-start | bytes 1966088 | tf_op jit(solution)/shard_map/ppermute | solution.py:220
  107.7 0.0 collective-permute-done.8
  107.7 0.9 fusion.4
  108.6 4.0 %collective-permute-start.18 = (bf16[64,1920]{1,0:T(8,128)(2,1)S(1)}, bf16[64,1920]{1,0:T(8,128)(2,1)S(1)}, u32[]{:S(2)}, u32[]{:S(2)}) collective-permute-start(bf16[64,1920]{1,0:T(8,128)(2,1)S(1)} %pad_maximum_fusion.5.p0), channel_id=1, source_target_pairs={{0,192},{64,0},{128,64},{192,128},{1,193},{65,1},{129,65},{193,129... | collective-permute-start | bytes 737288 | tf_op jit(solution)/shard_map/ppermute | solution.py:173
  112.6 0.0 collective-permute-start.17
  112.6 0.7 collective-permute-start.16
  113.3 0.0 collective-permute-done.14.other
  113.3 2.1 %collective-permute-start.13 = (bf16[64,1920]{1,0:T(8,128)(2,1)S(1)}, bf16[64,1920]{1,0:T(8,128)(2,1)S(1)}, u32[]{:S(2)}, u32[]{:S(2)}) collective-permute-start(bf16[64,1920]{1,0:T(8,128)(2,1)S(1)} %pad_maximum_fusion.4.p0), channel_id=1, source_target_pairs={{0,192},{64,0},{128,64},{192,128},{1,193},{65,1},{129,65},{193,129... | collective-permute-start | bytes 737288 | tf_op jit(solution)/shard_map/ppermute | solution.py:173
  115.4 5.9 %shard_map.39.right = bf16[1536,384]{1,0:T(8,128)(2,1)S(1)} custom-call(s32[5]{0:T(128)S(1)} %stack.23.pos, bf16[128,2560]{1,0:T(8,128)(2,1)S(1)} %bitcast.11, bf16[128,2560]{1,0:T(8,128)(2,1)S(1)} %collective-permute-done.14.other, bf16[2,1536,384]{2,1,0:T(8,128)(2,1)} %w_own.3, bf16[1536,384]{1,0:T(8,128)(2,1)S(1)} %collective-permute-done.4.w_pair, ...), custom_call_target="tpu_custom_call" | custom-call | flops 2500000000 | bytes 8000000 | tf_op jit(solution)/shard_map/pallas_call | solution.py:148
  121.3 0.0 collective-permute-done.15.w_pair
  121.3 1.8 %collective-permute-start.12 = (bf16[64,1920]{1,0:T(8,128)(2,1)S(1)}, bf16[64,1920]{1,0:T(8,128)(2,1)S(1)}, u32[]{:S(2)}, u32[]{:S(2)}) collective-permute-start(bf16[64,1920]{1,0:T(8,128)(2,1)S(1)} %pad_maximum_fusion.4.p0), channel_id=1, source_target_pairs={{0,128},{64,192},{128,0},{192,64},{1,129},{65,193},{129,1},{193,65... | collective-permute-start | bytes 737288 | tf_op jit(solution)/shard_map/ppermute | solution.py:173
  123.2 0.1 collective-permute-done.18.p3
  123.3 0.0 collective-permute-start.11
  123.3 5.9 %shard_map.38.right = bf16[1536,384]{1,0:T(8,128)(2,1)S(1)} custom-call(s32[5]{0:T(128)S(1)} %stack.23.pos, bf16[128,2560]{1,0:T(8,128)(2,1)S(1)} %bitcast.12, bf16[128,2560]{1,0:T(8,128)(2,1)S(1)} %collective-permute-done.14.other, bf16[2,1536,384]{2,1,0:T(8,128)(2,1)} %w_own.3, bf16[1536,384]{1,0:T(8,128)(2,1)S(1)} %collective-permute-done.15.w_pair, ...), custom_call_target="tpu_custom_call" | custom-call | flops 2500000000 | bytes 8000000 | tf_op jit(solution)/shard_map/pallas_call | solution.py:148
  129.2 0.0 collective-permute-done.17.p2
  129.2 0.0 collective-permute-done.16.p1
  129.2 4.8 %shard_map.40.refs_0_ = bf16[2,1536,384]{2,1,0:T(8,128)(2,1)} custom-call(s32[5]{0:T(128)S(1)} %stack.23.pos, bf16[64,1920]{1,0:T(8,128)(2,1)S(1)} %pad_maximum_fusion.5.p0, bf16[64,1920]{1,0:T(8,128)(2,1)S(1)} %collective-permute-done.16.p1, bf16[64,1920]{1,0:T(8,128)(2,1)S(1)} %collective-permute-done.17.p2, ...), custom_call_target="tpu_custom_call" | custom-call | flops 2500000000 | bytes 8000000 | tf_op jit(solution)/shard_map/pallas_call | solution.py:148
  134.0 0.0 collective-permute-done.13.p3
  134.0 0.0 collective-permute-done.12.p2
  134.0 3.6 %collective-permute-done.11.p1 = bf16[64,1920]{1,0:T(8,128)(2,1)S(1)} collective-permute-done((bf16[64,1920]{1,0:T(8,128)(2,1)S(1)}, bf16[64,1920]{1,0:T(8,128)(2,1)S(1)}, u32[]{:S(2)}, u32[]{:S(2)}) %collective-permute-start.11) | collective-permute-done | bytes 245792 | tf_op jit(solution)/shard_map/ppermute | solution.py:173
  137.6 4.9 %shard_map.41 = bf16[2,1536,384]{2,1,0:T(8,128)(2,1)} custom-call(s32[5]{0:T(128)S(1)} %stack.23.pos, bf16[64,1920]{1,0:T(8,128)(2,1)S(1)} %pad_maximum_fusion.4.p0, bf16[64,1920]{1,0:T(8,128)(2,1)S(1)} %collective-permute-done.11.p1, bf16[64,1920]{1,0:T(8,128)(2,1)S(1)} %collective-permute-done.12.p2, ...), custom_call_target="tpu_custom_call", output_to_operand_aliasing={{}: (6, {})} | custom-call | flops 2500000000 | bytes 8000000 | tf_op jit(solution)/shard_map/pallas_call | solution.py:148
  (8 shorter events, 0.1 us)
Async XLA Ops:
  0.0 4.8 %copy-start.1 = (bf16[2,1536,384]{2,1,0:T(8,128)(2,1)S(1)}, bf16[2,1536,384]{2,1,0:T(8,128)(2,1)}, u32[]{:S(2)}) copy-start(bf16[2,1536,384]{2,1,0:T(8,128)(2,1)} %w_own.3) | copy-start | bytes 7077892
  2.8 7.0 %copy-start = (bf16[2,256,1536]{2,1,0:T(8,128)(2,1)S(1)}, bf16[2,256,1536]{2,1,0:T(8,128)(2,1)}, u32[]{:S(2)}) copy-start(bf16[2,256,1536]{2,1,0:T(8,128)(2,1)} %grads.1) | copy-start | bytes 4718596
  2.8 45.8 %collective-permute-start.3 = (bf16[2,1536,256]{2,1,0:T(8,128)(2,1)}, bf16[2,1536,256]{2,1,0:T(8,128)(2,1)}, u32[]{:S(2)}, u32[]{:S(2)}) collective-permute-start(bf16[2,1536,256]{2,1,0:T(8,128)(2,1)} %constant_dynamic-slice_fusion.8), channel_id=1, source_target_pairs={{16,32},{32,16},{17,33},{33,17},{18,34},{34,18},{19,35},{35,19},{2... | collective-permute-start | bytes 4718600 | tf_op jit(solution)/shard_map/ppermute | solution.py:199
  6.4 42.1 %collective-permute-start.4 = (bf16[1536,384]{1,0:T(8,128)(2,1)}, bf16[1536,384]{1,0:T(8,128)(2,1)S(1)}, u32[]{:S(2)}, u32[]{:S(2)}) collective-permute-start(bf16[1536,384]{1,0:T(8,128)(2,1)} %get-tuple-element.20), channel_id=1, source_target_pairs={{0,16},{16,0},{32,48},{48,32},{1,17},{17,1},{33,49},{49,33},{2,18}... | collective-permute-start | bytes 3538952 | tf_op jit(solution)/shard_map/ppermute | solution.py:197
  17.0 15.7 %collective-permute-start = (bf16[160,1920]{1,0:T(8,128)(2,1)}, bf16[160,1920]{1,0:T(8,128)(2,1)S(1)}, u32[]{:S(2)}, u32[]{:S(2)}) collective-permute-start(bf16[160,1920]{1,0:T(8,128)(2,1)} %get-tuple-element.13), channel_id=1, source_target_pairs={{0,64},{64,128},{128,192},{192,0},{1,65},{65,129},{129,193},{193,1... | collective-permute-start | bytes 1843208 | tf_op jit(solution)/shard_map/ppermute | solution.py:173
  18.4 28.7 %collective-permute-start.1 = (bf16[160,1920]{1,0:T(8,128)(2,1)}, bf16[160,1920]{1,0:T(8,128)(2,1)S(1)}, u32[]{:S(2)}, u32[]{:S(2)}) collective-permute-start(bf16[160,1920]{1,0:T(8,128)(2,1)} %get-tuple-element.14), channel_id=1, source_target_pairs={{0,128},{64,192},{128,0},{192,64},{1,129},{65,193},{129,1},{193,65... | collective-permute-start | bytes 1843208 | tf_op jit(solution)/shard_map/ppermute | solution.py:173
  21.0 26.2 %collective-permute-start.2 = (bf16[160,1920]{1,0:T(8,128)(2,1)}, bf16[160,1920]{1,0:T(8,128)(2,1)}, u32[]{:S(2)}, u32[]{:S(2)}) collective-permute-start(bf16[160,1920]{1,0:T(8,128)(2,1)} %get-tuple-element.15), channel_id=1, source_target_pairs={{0,192},{64,0},{128,64},{192,128},{1,193},{65,1},{129,65},{193,129... | collective-permute-start | bytes 1843208 | tf_op jit(solution)/shard_map/ppermute | solution.py:173
  48.8 7.7 %collective-permute-start.5 = (bf16[64,1920]{1,0:T(8,128)(2,1)S(1)}, bf16[64,1920]{1,0:T(8,128)(2,1)S(1)}, u32[]{:S(2)}, u32[]{:S(2)}) collective-permute-start(bf16[64,1920]{1,0:T(8,128)(2,1)S(1)} %get-tuple-element.41), channel_id=1, source_target_pairs={{0,16},{16,32},{32,48},{48,0},{1,17},{17,33},{33,49},{49,1},{2,18}... | collective-permute-start | bytes 737288 | tf_op jit(solution)/shard_map/ppermute | solution.py:173
  49.0 11.1 %collective-permute-start.6 = (bf16[64,1920]{1,0:T(8,128)(2,1)S(1)}, bf16[64,1920]{1,0:T(8,128)(2,1)S(1)}, u32[]{:S(2)}, u32[]{:S(2)}) collective-permute-start(bf16[64,1920]{1,0:T(8,128)(2,1)S(1)} %get-tuple-element.42), channel_id=1, source_target_pairs={{0,32},{16,48},{32,0},{48,16},{1,33},{17,49},{33,1},{49,17},{2,34}... | collective-permute-start | bytes 737288 | tf_op jit(solution)/shard_map/ppermute | solution.py:173
  50.9 11.5 %collective-permute-start.7 = (bf16[64,1920]{1,0:T(8,128)(2,1)S(1)}, bf16[64,1920]{1,0:T(8,128)(2,1)S(1)}, u32[]{:S(2)}, u32[]{:S(2)}) collective-permute-start(bf16[64,1920]{1,0:T(8,128)(2,1)S(1)} %get-tuple-element.43), channel_id=1, source_target_pairs={{0,48},{16,0},{32,16},{48,32},{1,49},{17,1},{33,17},{49,33},{2,50}... | collective-permute-start | bytes 737288 | tf_op jit(solution)/shard_map/ppermute | solution.py:173
  63.6 40.4 %all-to-all-start = ((bf16[8,16,2560]{2,1,0:T(8,128)(2,1)}), bf16[8,16,2560]{2,1,0:T(8,128)(2,1)S(1)}, u32[]{:S(2)}, u32[]{:S(2)}) async-start(bf16[8,16,2560]{2,1,0:T(8,128)(2,1)} %tile.2), calls=%async_computation | async-start | bytes 1310720 | tf_op jit(solution)/shard_map/all_to_all | solution.py:219
  71.8 5.4 %collective-permute-start.10 = (bf16[32,1920]{1,0:T(8,128)(2,1)S(1)}, bf16[32,1920]{1,0:T(8,128)(2,1)S(1)}, u32[]{:S(2)}, u32[]{:S(2)}) collective-permute-start(bf16[32,1920]{1,0:T(8,128)(2,1)S(1)} %slice.77), channel_id=1, source_target_pairs={{0,48},{16,0},{32,16},{48,32},{1,49},{17,1},{33,17},{49,33},{2,50}... | collective-permute-start | bytes 368648 | tf_op jit(solution)/shard_map/ppermute | solution.py:173
  75.3 46.1 %collective-permute-start.15 = (bf16[1536,384]{1,0:T(8,128)(2,1)}, bf16[1536,384]{1,0:T(8,128)(2,1)S(1)}, u32[]{:S(2)}, u32[]{:S(2)}) collective-permute-start(bf16[1536,384]{1,0:T(8,128)(2,1)} %get-tuple-element.19), channel_id=1, source_target_pairs={{0,16},{16,0},{32,48},{48,32},{1,17},{17,1},{33,49},{49,33},{2,18}... | collective-permute-start | bytes 3538952 | tf_op jit(solution)/shard_map/ppermute | solution.py:197
  75.3 28.7 %collective-permute-start.9 = (bf16[32,1920]{1,0:T(8,128)(2,1)S(1)}, bf16[32,1920]{1,0:T(8,128)(2,1)S(1)}, u32[]{:S(2)}, u32[]{:S(2)}) collective-permute-start(bf16[32,1920]{1,0:T(8,128)(2,1)S(1)} %slice.77), channel_id=1, source_target_pairs={{0,32},{16,48},{32,0},{48,16},{1,33},{17,49},{33,1},{49,17},{2,34}... | collective-permute-start | bytes 368648 | tf_op jit(solution)/shard_map/ppermute | solution.py:173
  76.5 31.2 %collective-permute-start.8 = (bf16[32,1920]{1,0:T(8,128)(2,1)S(1)}, bf16[32,1920]{1,0:T(8,128)(2,1)}, u32[]{:S(2)}, u32[]{:S(2)}) collective-permute-start(bf16[32,1920]{1,0:T(8,128)(2,1)S(1)} %slice.77), channel_id=1, source_target_pairs={{0,16},{16,32},{32,48},{48,0},{1,17},{17,33},{33,49},{49,1},{2,18}... | collective-permute-start | bytes 368648 | tf_op jit(solution)/shard_map/ppermute | solution.py:173
  103.9 9.4 %collective-permute-start.14 = (bf16[128,2560]{1,0:T(8,128)(2,1)S(1)}, bf16[128,2560]{1,0:T(8,128)(2,1)S(1)}, u32[]{:S(2)}, u32[]{:S(2)}) collective-permute-start(bf16[128,2560]{1,0:T(8,128)(2,1)S(1)} %bitcast.10), channel_id=1, source_target_pairs={{0,1},{1,0},{2,3},{3,2},{4,5},{5,4},{6,7},{7,6},{8,9},{9,8},{10,11... | collective-permute-start | bytes 1966088 | tf_op jit(solution)/shard_map/ppermute | solution.py:220
  108.6 14.6 %collective-permute-start.18 = (bf16[64,1920]{1,0:T(8,128)(2,1)S(1)}, bf16[64,1920]{1,0:T(8,128)(2,1)S(1)}, u32[]{:S(2)}, u32[]{:S(2)}) collective-permute-start(bf16[64,1920]{1,0:T(8,128)(2,1)S(1)} %pad_maximum_fusion.5.p0), channel_id=1, source_target_pairs={{0,192},{64,0},{128,64},{192,128},{1,193},{65,1},{129,65},{193,129... | collective-permute-start | bytes 737288 | tf_op jit(solution)/shard_map/ppermute | solution.py:173
  112.6 16.5 %collective-permute-start.17 = (bf16[64,1920]{1,0:T(8,128)(2,1)S(1)}, bf16[64,1920]{1,0:T(8,128)(2,1)S(1)}, u32[]{:S(2)}, u32[]{:S(2)}) collective-permute-start(bf16[64,1920]{1,0:T(8,128)(2,1)S(1)} %pad_maximum_fusion.5.p0), channel_id=1, source_target_pairs={{0,128},{64,192},{128,0},{192,64},{1,129},{65,193},{129,1},{193,65... | collective-permute-start | bytes 737288 | tf_op jit(solution)/shard_map/ppermute | solution.py:173
  112.6 16.5 %collective-permute-start.16 = (bf16[64,1920]{1,0:T(8,128)(2,1)S(1)}, bf16[64,1920]{1,0:T(8,128)(2,1)S(1)}, u32[]{:S(2)}, u32[]{:S(2)}) collective-permute-start(bf16[64,1920]{1,0:T(8,128)(2,1)S(1)} %pad_maximum_fusion.5.p0), channel_id=1, source_target_pairs={{0,64},{64,128},{128,192},{192,0},{1,65},{65,129},{129,193},{193,1... | collective-permute-start | bytes 737288 | tf_op jit(solution)/shard_map/ppermute | solution.py:173
  113.3 20.7 %collective-permute-start.13 = (bf16[64,1920]{1,0:T(8,128)(2,1)S(1)}, bf16[64,1920]{1,0:T(8,128)(2,1)S(1)}, u32[]{:S(2)}, u32[]{:S(2)}) collective-permute-start(bf16[64,1920]{1,0:T(8,128)(2,1)S(1)} %pad_maximum_fusion.4.p0), channel_id=1, source_target_pairs={{0,192},{64,0},{128,64},{192,128},{1,193},{65,1},{129,65},{193,129... | collective-permute-start | bytes 737288 | tf_op jit(solution)/shard_map/ppermute | solution.py:173
  121.3 12.7 %collective-permute-start.12 = (bf16[64,1920]{1,0:T(8,128)(2,1)S(1)}, bf16[64,1920]{1,0:T(8,128)(2,1)S(1)}, u32[]{:S(2)}, u32[]{:S(2)}) collective-permute-start(bf16[64,1920]{1,0:T(8,128)(2,1)S(1)} %pad_maximum_fusion.4.p0), channel_id=1, source_target_pairs={{0,128},{64,192},{128,0},{192,64},{1,129},{65,193},{129,1},{193,65... | collective-permute-start | bytes 737288 | tf_op jit(solution)/shard_map/ppermute | solution.py:173
  123.3 14.4 %collective-permute-start.11 = (bf16[64,1920]{1,0:T(8,128)(2,1)S(1)}, bf16[64,1920]{1,0:T(8,128)(2,1)S(1)}, u32[]{:S(2)}, u32[]{:S(2)}) collective-permute-start(bf16[64,1920]{1,0:T(8,128)(2,1)S(1)} %pad_maximum_fusion.4.p0), channel_id=1, source_target_pairs={{0,64},{64,128},{128,192},{192,0},{1,65},{65,129},{129,193},{193,1... | collective-permute-start | bytes 737288 | tf_op jit(solution)/shard_map/ppermute | solution.py:173

commit v3 on v1

v3 whole, which is shorter than its diff:
```python
import jax
import jax.numpy as jnp
from jax import lax
from jax.experimental import pallas as pl
from jax.experimental.pallas import tpu as pltpu
from jax.sharding import Mesh, PartitionSpec as P

BLK = 512
SUB = 128
damping = 0.1
TOKENS = 4096
F32 = jnp.float32
BF16 = jnp.bfloat16
VMEM = pltpu.VMEM

PAIRS = [(r, c) for r in range(4) for c in range(r, 4)]
LANES = 15 * SUB


def tn_dot(a, b):
    return lax.dot_general(a, b, (((0,), (0,)), ((), ())), preferred_element_type=F32)


def nn_dot(a, b):
    return lax.dot_general(a, b, (((1,), (0,)), ((), ())), preferred_element_type=F32)


def side_kernel(pos, acts, s0, s1, s2, s3):
    y, part = pos[1], pos[3]
    k = lax.broadcasted_iota(jnp.int32, (BLK, 64), 0)
    m = lax.broadcasted_iota(jnp.int32, (BLK, 64), 1)
    select = jnp.where(k == m // 16 * SUB + part * 16 + m % 16, 1.0, 0.0).astype(BF16)
    for d, send in enumerate((s0, s1, s2, s3)):
        start = (y + d) % 4 * (3 * BLK)
        for j in range(3):
            rows = acts[0, :, pl.ds(pl.multiple_of(start + j * BLK, BLK), BLK)]
            chosen = nn_dot(rows, select).astype(BF16)
            cov = tn_dot(chosen, rows).astype(BF16)
            for i, (r, c) in enumerate(PAIRS):
                s = 10 * j + i
                send[s // 15 * 16:(s // 15 + 1) * 16, s % 15 * SUB:(s % 15 + 1) * SUB] = (
                    cov[r * 16:(r + 1) * 16, c * SUB:(c + 1) * SUB]
                )


def cov_kernel(pos, t0, t1, t2, t3, c0, c1, c2, c3, pack):
    x = pos[0]
    for b in range(3):
        top, low = 0.0, 0.0
        for tokens in (t0, t1, t2, t3):
            rows = tokens[:, b * BLK:(b + 1) * BLK]
            top += tn_dot(rows[:, :256], rows)
            low += tn_dot(rows[:, 256:], rows[:, 256:])
        top, low = top.astype(BF16), low.astype(BF16)
        for i, (r, c) in enumerate(PAIRS):
            if r < 2:
                piece = top[r * SUB:(r + 1) * SUB, c * SUB:(c + 1) * SUB]
            else:
                piece = low[(r - 2) * SUB:(r - 1) * SUB, (c - 2) * SUB:(c - 1) * SUB]
            pack[b, :, i * SUB:(i + 1) * SUB] = piece
    for d, send in enumerate((c0, c1, c2, c3)):
        send[...] = pack[jnp.minimum((x + d) % 4, 2)]


def unpack(piece, full):
    for i, (r, c) in enumerate(PAIRS):
        tile = piece(i)
        full[r * SUB:(r + 1) * SUB, c * SUB:(c + 1) * SUB] = tile.astype(full.dtype)
        if r != c:
            full[c * SUB:(c + 1) * SUB, r * SUB:(r + 1) * SUB] = tile.T.astype(full.dtype)


def invert(full):
    ri = lax.broadcasted_iota(jnp.int32, (BLK, BLK), 0)
    ci = lax.broadcasted_iota(jnp.int32, (BLK, BLK), 1)
    diagonal = ri == ci
    matrix = full[...] + jnp.where(diagonal, damping, 0.0)
    two_eye = jnp.where(diagonal, 2.0, 0.0)
    sums = jnp.sum(jnp.abs(matrix), axis=0, keepdims=True)
    alpha = (1.0 / jnp.max(sums, axis=1, keepdims=True)).astype(BF16).astype(F32)
    low = matrix.astype(BF16)
    residue = (two_eye - low.astype(F32) * alpha).astype(BF16)
    iterate = (residue.astype(F32) * alpha).astype(BF16)
    image = nn_dot(low, iterate)
    residue = (two_eye - image).astype(BF16)
    return nn_dot(iterate, residue).astype(BF16)


def newton_kernel(pos, c0, c1, c2, c3, out, full):
    def piece(i):
        at = slice(i * SUB, (i + 1) * SUB)
        return sum(c[:, at].astype(F32) for c in (c0, c1, c2, c3)) * (1.0 / TOKENS)

    unpack(piece, full)
    inverse = invert(full)
    for i, (r, c) in enumerate(PAIRS):
        out[:, i * SUB:(i + 1) * SUB] = inverse[r * SUB:(r + 1) * SUB, c * SUB:(c + 1) * SUB]


def factor_kernel(pos, mine, other, out, pack, full, diag):
    x, core = pos[0], pos[2]
    base = x // 2 * BLK
    own = pl.multiple_of(x * 384 - base, SUB)
    pair = pl.multiple_of((x + 1 - 2 * (x % 2)) * 384 - base, SUB)
    mid = pl.multiple_of(jnp.where(x == 1, 768, 0), SUB)
    columns = pl.ds(own, 384)
    for layer in range(2):
        for q in range(4):
            z = 4 * layer + q
            at = pl.multiple_of(q * 32 + core * 16, 16)
            pack[layer, pl.ds(at, 16), :] = mine[z * 16:(z + 1) * 16, :]
            at = pl.multiple_of(q * 32 + (1 - core) * 16, 16)
            pack[layer, pl.ds(at, 16), :] = other[z * 16:(z + 1) * 16, :]
        for b in range(2):
            at = b * BLK
            unpack(
                lambda i: pack[layer, :, b * 1280 + i * SUB:b * 1280 + (i + 1) * SUB].astype(F32),
                full.at[layer, b],
            )
            diag[layer, at:at + BLK, at:at + BLK] = invert(full.at[layer, b])
            diag[layer, at:at + BLK, BLK - at:2 * BLK - at] = jnp.zeros((BLK, BLK), BF16)
        out[layer, 0:384, :] = diag[layer, pl.ds(own, 384), columns]
        out[layer, 384:768, :] = diag[layer, pl.ds(pair, 384), columns]
        out[layer, 768:1024, :] = diag[layer, pl.ds(mid, 256), columns]


def right_kernel(pos, w_own, w_pair, w_mid, factor, out):
    total = nn_dot(w_own[0], factor[0, 0:384, :])
    total += nn_dot(w_pair[...], factor[0, 384:768, :])
    total += nn_dot(w_mid[...], factor[0, 768:1024, :])
    out[...] = total.astype(BF16)


def left_kernel(pos, p0, p1, p2, p3, r0, r1, out, pack, full):
    y, core = pos[1], pos[2]
    for layer, right in enumerate((r0, r1)):
        shift_of = (y + 4 - 2 * core - layer) % 4
        for d, part in enumerate((p0, p1, p2, p3)):
            @pl.when(shift_of == d)
            def _():
                pack[...] = part[...]
        for b in range(3):
            unpack(
                lambda i: pack[b * SUB:(b + 1) * SUB, i * SUB:(i + 1) * SUB].astype(F32),
                full.at[layer, b],
            )
            at = b * BLK
            out[layer, at:at + BLK, :] = nn_dot(full[layer, b], right[at:at + BLK, :]).astype(BF16)


def call(kernel, pos, operands, in_specs, out_shape, scratch, flops, out_specs=None, aliases={}):
    return pl.pallas_call(
        kernel,
        grid_spec=pltpu.PrefetchScalarGridSpec(
            num_scalar_prefetch=1,
            grid=(1,),
            in_specs=in_specs,
            out_specs=out_specs or [whole(s) for s in out_shape],
            scratch_shapes=scratch,
        ),
        out_shape=out_shape,
        input_output_aliases=aliases,
        compiler_params=pltpu.CompilerParams(vmem_limit_bytes=48 * 1024 * 1024),
        cost_estimate=pl.CostEstimate(flops=flops, bytes_accessed=8_000_000, transcendentals=0),
    )(pos, *operands)


def whole(a):
    return pl.BlockSpec(a.shape, lambda i, p, n=len(a.shape): (0,) * n)


def of_layer(a, layer):
    return pl.BlockSpec((1,) + a.shape[1:], lambda i, p: (layer, 0, 0))


def add(parts):
    return sum(p.astype(F32) for p in parts)


def send(a, axes, links):
    return lax.ppermute(a, axes, links)


def ring(d):
    return [(i, (i + d) % 4) for i in range(4)]


def to_handler(d):
    return [(y * 2 + c, (y + d) % 4 * 2 + c) for y in range(4) for c in range(2) if (y + d) % 4 // 2 == c]


def from_handler(d):
    return [(y * 2 + c, (y + d) % 4 * 2 + c) for y in range(4) for c in range(2) if y // 2 == c]


def along_x(d, source, target):
    return [
        ((y * 4 + x) * 2 + y // 2, (y * 4 + (x + d) % 4) * 2 + y // 2)
        for y in range(4) for x in range(4) if x < source and (x + d) % 4 < target
    ]


def body(acts, grads_out, weight_grad):
    y, x, z, c = (lax.axis_index(n) for n in ("y", "x", "z", "c"))
    pos = jnp.stack([x, y, c, z % 4 * 2 + c, z // 4]).astype(jnp.int32)
    shifts = (1, 2, 3)

    odd = lax.dynamic_index_in_dim(grads_out, (y + 1) % 2, 0, False)
    even = lax.dynamic_index_in_dim(grads_out, y % 2, 0, False)
    tokens = [even] + [send(even if d == 2 else odd, ("y", "c"), to_handler(d)) for d in shifts]

    def exchange(w):
        middle = lax.dynamic_slice_in_dim(w, jnp.where(x == 1, SUB, 0), 256, 1)
        return [send(w, "x", [(0, 1), (1, 0), (2, 3), (3, 2)]), send(middle, "x", [(1, 2), (2, 1)])]

    w_first = exchange(weight_grad[0])

    sides = call(
        side_kernel, pos, (acts,), [pl.BlockSpec((1, 256, 6144), lambda i, p: (p[4], 0, 0))],
        [jax.ShapeDtypeStruct((32, LANES), BF16)] * 4, [], 1_000_000_000,
    )
    side = add([sides[0]] + [send(sides[d], "y", ring(d)) for d in shifts]).astype(BF16)

    covs = call(
        cov_kernel, pos, tokens, [whole(t) for t in tokens],
        [jax.ShapeDtypeStruct((SUB, 1280), BF16)] * 4, [VMEM((3, SUB, 1280), BF16)], 1_500_000_000,
    )
    side, covs, w_first = lax.optimization_barrier((side, covs, w_first))
    covs = [covs[0]] + [send(covs[d], ("y", "x", "c"), along_x(d, 4, 3)) for d in shifts]
    side = add([side] + [send(side, "x", ring(d)) for d in shifts]) * (1.0 / TOKENS)
    side = jnp.concatenate([side[:16], side[16:]], axis=1)
    side = lax.dynamic_slice_in_dim(side, x // 2 * 1280, 2560, 1).astype(BF16)

    inverse = call(
        newton_kernel, pos, covs, [whole(t) for t in covs],
        [jax.ShapeDtypeStruct((SUB, 1280), BF16)], [VMEM((BLK, BLK), F32)], 600_000_000,
    )[0]
    row = jnp.stack([inverse] + [send(inverse, ("y", "x", "c"), along_x(d, 3, 4)) for d in shifts])
    row = jnp.concatenate([lax.dynamic_index_in_dim(row, (x + 4 - b) % 4, 0, False) for b in range(3)], axis=0)

    row, w_second = lax.optimization_barrier((row, weight_grad[1]))
    parts = [row] + [send(row, ("y", "c"), from_handler(d)) for d in shifts]
    w_second = exchange(w_second)

    mine = lax.all_to_all(jnp.tile(side, (8, 1)), "z", 0, 0, tiled=True)
    other = lax.ppermute(mine, "c", [(0, 1), (1, 0)])
    factor = call(
        factor_kernel, pos, (mine, other), [whole(mine), whole(other)],
        [jax.ShapeDtypeStruct((2, 1024, 384), BF16)],
        [VMEM((2, SUB, 2560), BF16), VMEM((2, 2, BLK, BLK), F32), VMEM((2, 1024, 1024), BF16)], 2_500_000_000,
    )[0]
    rights = [
        call(
            right_kernel, pos, (weight_grad, *w, factor),
            [of_layer(weight_grad, layer), whole(w[0]), whole(w[1]), of_layer(factor, layer)],
            [jax.ShapeDtypeStruct(weight_grad.shape[1:], BF16)], [], 1_200_000_000,
        )[0]
        for layer, w in enumerate((w_first, w_second))
    ]
    operands = (*parts, *rights)
    return call(
        left_kernel, pos, operands, [whole(a) for a in operands],
        [jax.ShapeDtypeStruct(weight_grad.shape, BF16)],
        [VMEM((3 * SUB, 1280), BF16), VMEM((2, 3, BLK, BLK), BF16)], 1_500_000_000,
    )[0]


def solution(mesh):
    fine = Mesh(mesh.devices.reshape(4, 4, 8, 2), ("y", "x", "z", "c"))
    dp, owner = ("y", "x"), ("z", "c")
    in_specs = (P(None, dp, None), P(None, dp, owner), P(None, owner, dp))
    out_specs = P(None, owner, dp)
    return jax.shard_map(body, mesh=fine, in_specs=in_specs, out_specs=out_specs, check_vma=False)
```

time: 163 us -> 154 us (0.945)
  the two profiles are of different devices: /device:TPU:198 before, /device:TPU:1 now
where the time goes in v3:
time: 154 us; the launch traced here: 153 us
  starting transfers between devices  69.4 us (45%)
  waiting for transfers between devices  38.1 us (25%)
  Pallas kernels  29.2 us (19%)
  local copies, waits for them, and re-layouts  13.3 us (9%)
  other arithmetic  2.54 us (2%)
    ppermute x22, starting transfers between devices, send(): return lax.ppermute(a, axes, links)  44.9 us
    ppermute x22, waiting for transfers between devices, send(): return lax.ppermute(a, axes, links)  34.6 us
    pallas_call x7, Pallas kernels, call(): pl.pallas_call(kernel, grid_spec=pltpu.PrefetchScalarGridSpec(num_scalar_...  29.2 us
    ppermute x1, starting transfers between devices, body(): other = lax.ppermute(mine, 'c', [(0, 1), (1, 0)])  16.2 us
    all_to_all x1, starting transfers between devices, body(): mine = lax.all_to_all(jnp.tile(side, (8, 1)), 'z', 0, 0, tiled=True)  8.36 us
    unnamed x18, local copies, waits for them, and re-layouts  5.89 us
    all_to_all x1, waiting for transfers between devices, body(): mine = lax.all_to_all(jnp.tile(side, (8, 1)), 'z', 0, 0, tiled=True)  3.44 us
  transfers between devices with their start and end apart: 24, of which 3 were waited for; matrix products, arithmetic and copies ran while one was open for 6% of the time, Pallas kernels for 12%

profile of v3, /device:TPU:1, one launch (start us, length us, event | category | flops | bytes accessed | tf_op | source)
XLA Modules:
  0.0 152.9 jit_solution(14126460266070419951)
XLA Ops:
  0.0 0.1 stack.38.pos
  0.1 5.8 %shard_map.37 = (bf16[32,1920]{1,0:T(8,128)(2,1)S(1)}, bf16[32,1920]{1,0:T(8,128)(2,1)S(1)}, bf16[32,1920]{1,0:T(8,128)(2,1)S(1)}, bf16[32,1920]{1,0:T(8,128)(2,1)S(1)}) custom-call(s32[5]{0:T(128)S(1)} %stack.38.pos, bf16[2,256,6144]{2,1,0:T(8,128)(2,1)} %acts.1), custom_call_target="tpu_custom_call" | custom-call | flops 1000000000 | bytes 8000000 | tf_op jit(solution)/shard_map/pallas_call | solution.py:152
  5.9 2.2 %collective-permute-start = (bf16[32,1920]{1,0:T(8,128)(2,1)S(1)}, bf16[32,1920]{1,0:T(8,128)(2,1)S(1)}, u32[]{:S(2)}, u32[]{:S(2)}) collective-permute-start(bf16[32,1920]{1,0:T(8,128)(2,1)S(1)} %get-tuple-element.23), channel_id=1, source_target_pairs={{0,64},{64,128},{128,192},{192,0},{1,65},{65,129},{129,193},{193,1... | collective-permute-start | bytes 368648 | tf_op jit(solution)/shard_map/ppermute | solution.py:181
  8.1 2.6 %collective-permute-start.1 = (bf16[32,1920]{1,0:T(8,128)(2,1)S(1)}, bf16[32,1920]{1,0:T(8,128)(2,1)S(1)}, u32[]{:S(2)}, u32[]{:S(2)}) collective-permute-start(bf16[32,1920]{1,0:T(8,128)(2,1)S(1)} %get-tuple-element.24), channel_id=1, source_target_pairs={{0,128},{64,192},{128,0},{192,64},{1,129},{65,193},{129,1},{193,65... | collective-permute-start | bytes 368648 | tf_op jit(solution)/shard_map/ppermute | solution.py:181
  10.8 2.0 %slice_bitcast_fusion = (bf16[1536,384]{1,0:T(8,128)(2,1)}, bf16[1536,384]{1,0:T(8,128)(2,1)}, bf16[1,1536,384]{2,1,0:T(8,128)(2,1)}) fusion(bf16[2,1536,384]{2,1,0:T(8,128)(2,1)S(1)} %copy-done.7), kind=kLoop, calls=%fused_computation.1 | loop fusion | bytes 5898240 | tf_op jit(solution)/shard_map/squeeze | solution.py:241
  12.8 1.2 collective-permute-start.6
  14.0 2.4 %dynamic-slice_bitcast_fusion.1 = (bf16[256,1536]{1,0:T(8,128)(2,1)}, bf16[256,1536]{1,0:T(8,128)(2,1)S(1)}) fusion(bf16[2,256,1536]{2,1,0:T(8,128)(2,1)} %param.4, s32[]{:T(128)S(6)} %select_n.66, s32[]{:T(128)S(6)} %select_n.64), kind=kLoop, calls=%fused_computation.4 | loop fusion | bytes 3145736 | tf_op jit(solution)/shard_map/jit(dynamic_index_in_dim)/squeeze | solution.py:208
  16.3 1.5 %collective-permute-start.3 = (bf16[256,1536]{1,0:T(8,128)(2,1)}, bf16[256,1536]{1,0:T(8,128)(2,1)}, u32[]{:S(2)}, u32[]{:S(2)}) collective-permute-start(bf16[256,1536]{1,0:T(8,128)(2,1)} %get-tuple-element.42), channel_id=1, source_target_pairs={{0,64},{65,129},{129,193},{192,0},{2,66},{67,131},{131,195},{194,2... | collective-permute-start | bytes 2359304 | tf_op jit(solution)/shard_map/ppermute | solution.py:181
  17.9 3.6 %collective-permute-start.5 = (bf16[256,1536]{1,0:T(8,128)(2,1)}, bf16[256,1536]{1,0:T(8,128)(2,1)}, u32[]{:S(2)}, u32[]{:S(2)}) collective-permute-start(bf16[256,1536]{1,0:T(8,128)(2,1)} %get-tuple-element.42), channel_id=1, source_target_pairs={{1,193},{64,0},{128,64},{193,129},{3,195},{66,2},{130,66},{195,131... | collective-permute-start | bytes 2359304 | tf_op jit(solution)/shard_map/ppermute | solution.py:181
  21.5 0.0 collective-permute-done
  21.5 2.3 %collective-permute-start.4 = (bf16[256,1536]{1,0:T(8,128)(2,1)S(1)}, bf16[256,1536]{1,0:T(8,128)(2,1)S(1)}, u32[]{:S(2)}, u32[]{:S(2)}) collective-permute-start(bf16[256,1536]{1,0:T(8,128)(2,1)S(1)} %get-tuple-element.43.t0), channel_id=1, source_target_pairs={{1,129},{65,193},{128,0},{192,64},{3,131},{67,195},{130,2},{194,66... | collective-permute-start | bytes 2359304 | tf_op jit(solution)/shard_map/ppermute | solution.py:181
  23.8 0.0 collective-permute-done.1
  23.8 0.3 collective-permute-start.2
  24.1 1.2 dynamic-slice_bitcast_fusion
  25.3 18.9 %collective-permute-done.2 = bf16[32,1920]{1,0:T(8,128)(2,1)S(1)} collective-permute-done((bf16[32,1920]{1,0:T(8,128)(2,1)S(1)}, bf16[32,1920]{1,0:T(8,128)(2,1)S(1)}, u32[]{:S(2)}, u32[]{:S(2)}) %collective-permute-start.2) | collective-permute-done | bytes 122912 | tf_op jit(solution)/shard_map/ppermute | solution.py:181
  44.2 0.7 collective-permute-start.7
  44.9 0.1 add_convert_fusion
  45.0 0.0 collective-permute-done.3.t1
  45.0 0.0 collective-permute-done.4.t2
  45.0 3.5 %shard_map.38 = (bf16[128,1280]{1,0:T(8,128)(2,1)S(1)}, bf16[128,1280]{1,0:T(8,128)(2,1)S(1)}, bf16[128,1280]{1,0:T(8,128)(2,1)S(1)}, bf16[128,1280]{1,0:T(8,128)(2,1)S(1)}) custom-call(s32[5]{0:T(128)S(1)} %stack.38.pos, bf16[256,1536]{1,0:T(8,128)(2,1)S(1)} %get-tuple-element.43.t0, bf16[256,1536]{1,0:T(8,128)(2,1)} %collective-permute-done.3.t1, ...), custom_call_target="tpu_custom_call" | custom-call | flops 1500000000 | bytes 8000000 | tf_op jit(solution)/shard_map/pallas_call | solution.py:152
  48.6 0.7 copy-done.1
  49.3 0.7 copy-done.2
  50.0 0.7 copy-done.5
  50.7 16.0 %collective-permute-start.17 = (bf16[32,1920]{1,0:T(8,128)(2,1)S(1)}, bf16[32,1920]{1,0:T(8,128)(2,1)S(1)}, u32[]{:S(2)}, u32[]{:S(2)}) collective-permute-start(bf16[32,1920]{1,0:T(8,128)(2,1)S(1)} %add_convert_fusion), channel_id=1, source_target_pairs={{0,16},{16,32},{32,48},{48,0},{1,17},{17,33},{33,49},{49,1},{2,18}... | collective-permute-start | bytes 368648 | tf_op jit(solution)/shard_map/ppermute | solution.py:181
  66.7 1.1 collective-permute-start.18
  67.8 2.1 %collective-permute-start.19 = (bf16[32,1920]{1,0:T(8,128)(2,1)S(1)}, bf16[32,1920]{1,0:T(8,128)(2,1)S(1)}, u32[]{:S(2)}, u32[]{:S(2)}) collective-permute-start(bf16[32,1920]{1,0:T(8,128)(2,1)S(1)} %add_convert_fusion), channel_id=1, source_target_pairs={{0,48},{16,0},{32,16},{48,32},{1,49},{17,1},{33,17},{49,33},{2,50}... | collective-permute-start | bytes 368648 | tf_op jit(solution)/shard_map/ppermute | solution.py:181
  69.9 0.7 collective-permute-start.10
  70.6 1.4 collective-permute-start.8
  72.0 0.0 collective-permute-done.17
  72.0 1.4 collective-permute-start.9
  73.4 0.1 add_multiply_fusion
  73.5 0.1 fusion.1
  73.6 0.9 tile.2
  74.5 8.4 %all-to-all-start = ((bf16[8,16,2560]{2,1,0:T(8,128)(2,1)}), bf16[8,16,2560]{2,1,0:T(8,128)(2,1)S(1)}, u32[]{:S(2)}, u32[]{:S(2)}) async-start(bf16[8,16,2560]{2,1,0:T(8,128)(2,1)} %tile.2), calls=%async_computation | async-start | bytes 1310720 | tf_op jit(solution)/shard_map/all_to_all | solution.py:245
  82.9 0.7 copy-done.3
  83.6 0.0 collective-permute-done.8.c1
  83.6 0.0 collective-permute-done.9.c2
  83.6 1.0 copy-done.4
  84.6 1.0 copy-done.6
  85.6 2.9 %shard_map.39 = bf16[128,1280]{1,0:T(8,128)(2,1)S(1)} custom-call(s32[5]{0:T(128)S(1)} %stack.38.pos, bf16[128,1280]{1,0:T(8,128)(2,1)S(1)} %copy-done.6, bf16[128,1280]{1,0:T(8,128)(2,1)} %collective-permute-done.8.c1, bf16[128,1280]{1,0:T(8,128)(2,1)} %collective-permute-done.9.c2, bf16[128,1280]{1,0:T(8,128)(2,1)S(1)} %copy-done.4), custom_call_target="tpu_custom_call" | custom-call | flops 600000000 | bytes 8000000 | tf_op jit(solution)/shard_map/pallas_call | solution.py:152
  88.5 0.7 collective-permute-start.11
  89.2 1.4 collective-permute-start.12
  90.6 1.4 collective-permute-start.13
  92.0 0.0 collective-permute-done.11
  92.0 0.0 collective-permute-done.12
  92.0 1.2 pad_maximum_fusion
  93.2 0.8 dynamic-slice_bitcast_fusion.5
  94.0 3.4 %all-to-all-done = bf16[8,16,2560]{2,1,0:T(8,128)(2,1)S(1)} async-done(((bf16[8,16,2560]{2,1,0:T(8,128)(2,1)}), bf16[8,16,2560]{2,1,0:T(8,128)(2,1)S(1)}, u32[]{:S(2)}, u32[]{:S(2)}) %all-to-all-start) | async-done | bytes 655392 | tf_op jit(solution)/shard_map/all_to_all | solution.py:245
  97.5 16.2 %collective-permute-start.20 = (bf16[128,2560]{1,0:T(8,128)(2,1)S(1)}, bf16[128,2560]{1,0:T(8,128)(2,1)S(1)}, u32[]{:S(2)}, u32[]{:S(2)}) collective-permute-start(bf16[128,2560]{1,0:T(8,128)(2,1)S(1)} %bitcast.26), channel_id=1, source_target_pairs={{0,1},{1,0},{2,3},{3,2},{4,5},{5,4},{6,7},{7,6},{8,9},{9,8},{10,11... | collective-permute-start | bytes 1966088 | tf_op jit(solution)/shard_map/ppermute | solution.py:246
  113.7 1.0 pad_maximum_fusion.1.p0
  114.7 0.3 collective-permute-start.21
  115.0 1.3 collective-permute-start.14
  116.3 1.3 collective-permute-start.15
  117.6 0.7 collective-permute-start.16
  118.4 0.1 constant_dynamic-slice_fusion
  118.4 0.0 collective-permute-done.20.other
  118.4 0.7 collective-permute-start.22
  119.2 3.9 %shard_map.40.factor = bf16[2,1024,384]{2,1,0:T(8,128)(2,1)S(1)} custom-call(s32[5]{0:T(128)S(1)} %stack.38.pos, bf16[128,2560]{1,0:T(8,128)(2,1)S(1)} %bitcast.27, bf16[128,2560]{1,0:T(8,128)(2,1)S(1)} %collective-permute-done.20.other), custom_call_target="tpu_custom_call" | custom-call | flops 2500000000 | bytes 8000000 | tf_op jit(solution)/shard_map/pallas_call | solution.py:152
  123.1 3.8 %shard_map.41.r0 = bf16[1536,384]{1,0:T(8,128)(2,1)S(1)} custom-call(s32[5]{0:T(128)S(1)} %stack.38.pos, bf16[2,1536,384]{2,1,0:T(8,128)(2,1)} %w_own.3, bf16[1536,384]{1,0:T(8,128)(2,1)S(1)} %collective-permute-done.6.w_pair, bf16[1536,256]{1,0:T(8,128)(2,1)S(1)} %collective-permute-done.7.w_mid, bf16[2,1024,384]{2,1,0:T(8,128)(2,1)S(1)} %shard_map.40.factor), custom_call_target="tpu_custom_call" | custom-call | flops 1200000000 | bytes 8000000 | tf_op jit(solution)/shard_map/pallas_call | solution.py:152
  126.9 15.6 %collective-permute-done.21.w_pair = bf16[1536,384]{1,0:T(8,128)(2,1)S(1)} collective-permute-done((bf16[1536,384]{1,0:T(8,128)(2,1)S(1)}, bf16[1536,384]{1,0:T(8,128)(2,1)S(1)}, u32[]{:S(2)}, u32[]{:S(2)}) %collective-permute-start.21) | collective-permute-done | bytes 1179680 | tf_op jit(solution)/shard_map/ppermute | solution.py:181
  142.5 3.8 %shard_map.42.r1 = bf16[1536,384]{1,0:T(8,128)(2,1)S(1)} custom-call(s32[5]{0:T(128)S(1)} %stack.38.pos, bf16[2,1536,384]{2,1,0:T(8,128)(2,1)} %w_own.3, bf16[1536,384]{1,0:T(8,128)(2,1)S(1)} %collective-permute-done.21.w_pair, bf16[1536,256]{1,0:T(8,128)(2,1)S(1)} %collective-permute-done.22.w_mid, bf16[2,1024,384]{2,1,0:T(8,128)(2,1)S(1)} %shard_map.40.factor), custom_call_target="tpu_custom_call" | custom-call | flops 1200000000 | bytes 8000000 | tf_op jit(solution)/shard_map/pallas_call | solution.py:152
  146.4 1.0 copy-done
  147.4 0.0 collective-permute-done.14.p1
  147.4 5.4 %shard_map.43 = bf16[2,1536,384]{2,1,0:T(8,128)(2,1)} custom-call(s32[5]{0:T(128)S(1)} %stack.38.pos, bf16[384,1280]{1,0:T(8,128)(2,1)S(1)} %pad_maximum_fusion.1.p0, bf16[384,1280]{1,0:T(8,128)(2,1)S(1)} %collective-permute-done.14.p1, bf16[384,1280]{1,0:T(8,128)(2,1)S(1)} %collective-permute-done.15.p2, bf16[384,1280]{1,0:T(8,128)(2,1)S(1)} %collective-permute-done.16.p3, ...), custom_call_target="tpu_custom_call" | custom-call | flops 1500000000 | bytes 8000000 | tf_op jit(solution)/shard_map/pallas_call | solution.py:152
  (22 shorter events, 0.1 us)
Async XLA Ops:
  0.1 10.7 %copy-start.7 = (bf16[2,1536,384]{2,1,0:T(8,128)(2,1)S(1)}, bf16[2,1536,384]{2,1,0:T(8,128)(2,1)}, u32[]{:S(2)}) copy-start(bf16[2,1536,384]{2,1,0:T(8,128)(2,1)} %w_own.3) | copy-start | bytes 7077892
  5.9 15.5 %collective-permute-start = (bf16[32,1920]{1,0:T(8,128)(2,1)S(1)}, bf16[32,1920]{1,0:T(8,128)(2,1)S(1)}, u32[]{:S(2)}, u32[]{:S(2)}) collective-permute-start(bf16[32,1920]{1,0:T(8,128)(2,1)S(1)} %get-tuple-element.23), channel_id=1, source_target_pairs={{0,64},{64,128},{128,192},{192,0},{1,65},{65,129},{129,193},{193,1... | collective-permute-start | bytes 368648 | tf_op jit(solution)/shard_map/ppermute | solution.py:181
  8.1 15.6 %collective-permute-start.1 = (bf16[32,1920]{1,0:T(8,128)(2,1)S(1)}, bf16[32,1920]{1,0:T(8,128)(2,1)S(1)}, u32[]{:S(2)}, u32[]{:S(2)}) collective-permute-start(bf16[32,1920]{1,0:T(8,128)(2,1)S(1)} %get-tuple-element.24), channel_id=1, source_target_pairs={{0,128},{64,192},{128,0},{192,64},{1,129},{65,193},{129,1},{193,65... | collective-permute-start | bytes 368648 | tf_op jit(solution)/shard_map/ppermute | solution.py:181
  12.8 38.0 %collective-permute-start.6 = (bf16[1536,384]{1,0:T(8,128)(2,1)}, bf16[1536,384]{1,0:T(8,128)(2,1)S(1)}, u32[]{:S(2)}, u32[]{:S(2)}) collective-permute-start(bf16[1536,384]{1,0:T(8,128)(2,1)} %get-tuple-element.40), channel_id=1, source_target_pairs={{0,16},{16,0},{32,48},{48,32},{1,17},{17,1},{33,49},{49,33},{2,18}... | collective-permute-start | bytes 3538952 | tf_op jit(solution)/shard_map/ppermute | solution.py:181
  16.3 28.7 %collective-permute-start.3 = (bf16[256,1536]{1,0:T(8,128)(2,1)}, bf16[256,1536]{1,0:T(8,128)(2,1)}, u32[]{:S(2)}, u32[]{:S(2)}) collective-permute-start(bf16[256,1536]{1,0:T(8,128)(2,1)} %get-tuple-element.42), channel_id=1, source_target_pairs={{0,64},{65,129},{129,193},{192,0},{2,66},{67,131},{131,195},{194,2... | collective-permute-start | bytes 2359304 | tf_op jit(solution)/shard_map/ppermute | solution.py:181
  17.9 27.2 %collective-permute-start.5 = (bf16[256,1536]{1,0:T(8,128)(2,1)}, bf16[256,1536]{1,0:T(8,128)(2,1)}, u32[]{:S(2)}, u32[]{:S(2)}) collective-permute-start(bf16[256,1536]{1,0:T(8,128)(2,1)} %get-tuple-element.42), channel_id=1, source_target_pairs={{1,193},{64,0},{128,64},{193,129},{3,195},{66,2},{130,66},{195,131... | collective-permute-start | bytes 2359304 | tf_op jit(solution)/shard_map/ppermute | solution.py:181
  21.5 23.5 %collective-permute-start.4 = (bf16[256,1536]{1,0:T(8,128)(2,1)S(1)}, bf16[256,1536]{1,0:T(8,128)(2,1)S(1)}, u32[]{:S(2)}, u32[]{:S(2)}) collective-permute-start(bf16[256,1536]{1,0:T(8,128)(2,1)S(1)} %get-tuple-element.43.t0), channel_id=1, source_target_pairs={{1,129},{65,193},{128,0},{192,64},{3,131},{67,195},{130,2},{194,66... | collective-permute-start | bytes 2359304 | tf_op jit(solution)/shard_map/ppermute | solution.py:181
  23.8 20.5 %collective-permute-start.2 = (bf16[32,1920]{1,0:T(8,128)(2,1)S(1)}, bf16[32,1920]{1,0:T(8,128)(2,1)S(1)}, u32[]{:S(2)}, u32[]{:S(2)}) collective-permute-start(bf16[32,1920]{1,0:T(8,128)(2,1)S(1)} %get-tuple-element.25), channel_id=1, source_target_pairs={{0,192},{64,0},{128,64},{192,128},{1,193},{65,1},{129,65},{193,129... | collective-permute-start | bytes 368648 | tf_op jit(solution)/shard_map/ppermute | solution.py:181
  44.2 6.5 %collective-permute-start.7 = (bf16[1536,256]{1,0:T(8,128)(2,1)S(1)}, bf16[1536,256]{1,0:T(8,128)(2,1)S(1)}, u32[]{:S(2)}, u32[]{:S(2)}) collective-permute-start(bf16[1536,256]{1,0:T(8,128)(2,1)S(1)} %dynamic-slice_bitcast_fusion), channel_id=1, source_target_pairs={{16,32},{32,16},{17,33},{33,17},{18,34},{34,18},{19,35},{35,19},{2... | collective-permute-start | bytes 2359304 | tf_op jit(solution)/shard_map/ppermute | solution.py:181
  48.5 0.7 copy-start.1
  49.3 0.7 copy-start.2
  50.0 0.7 copy-start.5
  50.7 21.3 %collective-permute-start.17 = (bf16[32,1920]{1,0:T(8,128)(2,1)S(1)}, bf16[32,1920]{1,0:T(8,128)(2,1)S(1)}, u32[]{:S(2)}, u32[]{:S(2)}) collective-permute-start(bf16[32,1920]{1,0:T(8,128)(2,1)S(1)} %add_convert_fusion), channel_id=1, source_target_pairs={{0,16},{16,32},{32,48},{48,0},{1,17},{17,33},{33,49},{49,1},{2,18}... | collective-permute-start | bytes 368648 | tf_op jit(solution)/shard_map/ppermute | solution.py:181
  66.7 6.7 %collective-permute-start.18 = (bf16[32,1920]{1,0:T(8,128)(2,1)S(1)}, bf16[32,1920]{1,0:T(8,128)(2,1)S(1)}, u32[]{:S(2)}, u32[]{:S(2)}) collective-permute-start(bf16[32,1920]{1,0:T(8,128)(2,1)S(1)} %add_convert_fusion), channel_id=1, source_target_pairs={{0,32},{16,48},{32,0},{48,16},{1,33},{17,49},{33,1},{49,17},{2,34}... | collective-permute-start | bytes 368648 | tf_op jit(solution)/shard_map/ppermute | solution.py:181
  67.8 5.6 %collective-permute-start.19 = (bf16[32,1920]{1,0:T(8,128)(2,1)S(1)}, bf16[32,1920]{1,0:T(8,128)(2,1)S(1)}, u32[]{:S(2)}, u32[]{:S(2)}) collective-permute-start(bf16[32,1920]{1,0:T(8,128)(2,1)S(1)} %add_convert_fusion), channel_id=1, source_target_pairs={{0,48},{16,0},{32,16},{48,32},{1,49},{17,1},{33,17},{49,33},{2,50}... | collective-permute-start | bytes 368648 | tf_op jit(solution)/shard_map/ppermute | solution.py:181
  69.9 13.0 %collective-permute-start.10 = (bf16[128,1280]{1,0:T(8,128)(2,1)}, bf16[128,1280]{1,0:T(8,128)(2,1)S(1)}, u32[]{:S(2)}, u32[]{:S(2)}) collective-permute-start(bf16[128,1280]{1,0:T(8,128)(2,1)} %copy-done.2), channel_id=1, source_target_pairs={{16,0},{32,16},{48,32},{80,64},{96,80},{112,96},{145,129},{161,145... | collective-permute-start | bytes 983048 | tf_op jit(solution)/shard_map/ppermute | solution.py:181
  70.6 13.0 %collective-permute-start.8 = (bf16[128,1280]{1,0:T(8,128)(2,1)}, bf16[128,1280]{1,0:T(8,128)(2,1)}, u32[]{:S(2)}, u32[]{:S(2)}) collective-permute-start(bf16[128,1280]{1,0:T(8,128)(2,1)} %copy-done.1), channel_id=1, source_target_pairs={{0,16},{16,32},{48,0},{64,80},{80,96},{112,64},{129,145},{145,161}... | collective-permute-start | bytes 983048 | tf_op jit(solution)/shard_map/ppermute | solution.py:181
  72.0 11.6 %collective-permute-start.9 = (bf16[128,1280]{1,0:T(8,128)(2,1)S(1)}, bf16[128,1280]{1,0:T(8,128)(2,1)}, u32[]{:S(2)}, u32[]{:S(2)}) collective-permute-start(bf16[128,1280]{1,0:T(8,128)(2,1)S(1)} %get-tuple-element.32), channel_id=1, source_target_pairs={{0,32},{32,0},{48,16},{64,96},{96,64},{112,80},{129,161},{161,129}... | collective-permute-start | bytes 983048 | tf_op jit(solution)/shard_map/ppermute | solution.py:181
  74.5 23.0 %all-to-all-start = ((bf16[8,16,2560]{2,1,0:T(8,128)(2,1)}), bf16[8,16,2560]{2,1,0:T(8,128)(2,1)S(1)}, u32[]{:S(2)}, u32[]{:S(2)}) async-start(bf16[8,16,2560]{2,1,0:T(8,128)(2,1)} %tile.2), calls=%async_computation | async-start | bytes 1310720 | tf_op jit(solution)/shard_map/all_to_all | solution.py:245
  82.9 0.7 copy-start.3
  83.6 1.0 copy-start.4
  84.6 1.0 copy-start.6
  88.5 3.5 %collective-permute-start.11 = (bf16[128,1280]{1,0:T(8,128)(2,1)S(1)}, bf16[128,1280]{1,0:T(8,128)(2,1)S(1)}, u32[]{:S(2)}, u32[]{:S(2)}) collective-permute-start(bf16[128,1280]{1,0:T(8,128)(2,1)S(1)} %shard_map.39), channel_id=1, source_target_pairs={{0,16},{16,32},{32,48},{64,80},{80,96},{96,112},{129,145},{145,161... | collective-permute-start | bytes 983048 | tf_op jit(solution)/shard_map/ppermute | solution.py:181
  89.2 2.8 %collective-permute-start.12 = (bf16[128,1280]{1,0:T(8,128)(2,1)S(1)}, bf16[128,1280]{1,0:T(8,128)(2,1)}, u32[]{:S(2)}, u32[]{:S(2)}) collective-permute-start(bf16[128,1280]{1,0:T(8,128)(2,1)S(1)} %shard_map.39), channel_id=1, source_target_pairs={{0,32},{16,48},{32,0},{64,96},{80,112},{96,64},{129,161},{145,177}... | collective-permute-start | bytes 983048 | tf_op jit(solution)/shard_map/ppermute | solution.py:181
  90.6 1.4 collective-permute-start.13
  97.5 17.3 %copy-start.8 = (bf16[1536,384]{1,0:T(8,128)(2,1)S(1)}, bf16[1536,384]{1,0:T(8,128)(2,1)}, u32[]{:S(2)}) copy-start(bf16[1536,384]{1,0:T(8,128)(2,1)} %get-tuple-element.38) | copy-start | bytes 3538948
  97.5 21.0 %collective-permute-start.20 = (bf16[128,2560]{1,0:T(8,128)(2,1)S(1)}, bf16[128,2560]{1,0:T(8,128)(2,1)S(1)}, u32[]{:S(2)}, u32[]{:S(2)}) collective-permute-start(bf16[128,2560]{1,0:T(8,128)(2,1)S(1)} %bitcast.26), channel_id=1, source_target_pairs={{0,1},{1,0},{2,3},{3,2},{4,5},{5,4},{6,7},{7,6},{8,9},{9,8},{10,11... | collective-permute-start | bytes 1966088 | tf_op jit(solution)/shard_map/ppermute | solution.py:246
  114.7 27.8 %collective-permute-start.21 = (bf16[1536,384]{1,0:T(8,128)(2,1)S(1)}, bf16[1536,384]{1,0:T(8,128)(2,1)S(1)}, u32[]{:S(2)}, u32[]{:S(2)}) collective-permute-start(bf16[1536,384]{1,0:T(8,128)(2,1)S(1)} %copy-done.8), channel_id=1, source_target_pairs={{0,16},{16,0},{32,48},{48,32},{1,17},{17,1},{33,49},{49,33},{2,18}... | collective-permute-start | bytes 3538952 | tf_op jit(solution)/shard_map/ppermute | solution.py:181
  115.0 32.4 %collective-permute-start.14 = (bf16[384,1280]{1,0:T(8,128)(2,1)S(1)}, bf16[384,1280]{1,0:T(8,128)(2,1)S(1)}, u32[]{:S(2)}, u32[]{:S(2)}) collective-permute-start(bf16[384,1280]{1,0:T(8,128)(2,1)S(1)} %pad_maximum_fusion.1.p0), channel_id=1, source_target_pairs={{0,64},{64,128},{129,193},{193,1},{2,66},{66,130},{131,195},{195,3... | collective-permute-start | bytes 2949128 | tf_op jit(solution)/shard_map/ppermute | solution.py:181
  116.3 31.1 %collective-permute-start.15 = (bf16[384,1280]{1,0:T(8,128)(2,1)S(1)}, bf16[384,1280]{1,0:T(8,128)(2,1)S(1)}, u32[]{:S(2)}, u32[]{:S(2)}) collective-permute-start(bf16[384,1280]{1,0:T(8,128)(2,1)S(1)} %pad_maximum_fusion.1.p0), channel_id=1, source_target_pairs={{0,128},{64,192},{129,1},{193,65},{2,130},{66,194},{131,3},{195,67... | collective-permute-start | bytes 2949128 | tf_op jit(solution)/shard_map/ppermute | solution.py:181
  117.6 29.8 %collective-permute-start.16 = (bf16[384,1280]{1,0:T(8,128)(2,1)S(1)}, bf16[384,1280]{1,0:T(8,128)(2,1)S(1)}, u32[]{:S(2)}, u32[]{:S(2)}) collective-permute-start(bf16[384,1280]{1,0:T(8,128)(2,1)S(1)} %pad_maximum_fusion.1.p0), channel_id=1, source_target_pairs={{0,192},{64,0},{129,65},{193,129},{2,194},{66,2},{131,67},{195,131... | collective-permute-start | bytes 2949128 | tf_op jit(solution)/shard_map/ppermute | solution.py:181
  118.4 8.5 %collective-permute-start.22 = (bf16[1536,256]{1,0:T(8,128)(2,1)S(1)}, bf16[1536,256]{1,0:T(8,128)(2,1)S(1)}, u32[]{:S(2)}, u32[]{:S(2)}) collective-permute-start(bf16[1536,256]{1,0:T(8,128)(2,1)S(1)} %constant_dynamic-slice_fusion), channel_id=1, source_target_pairs={{16,32},{32,16},{17,33},{33,17},{18,34},{34,18},{19,35},{35,19},{2... | collective-permute-start | bytes 2359304 | tf_op jit(solution)/shard_map/ppermute | solution.py:181
  146.4 1.0 copy-start

commit v4 on v3

--- a/solution.py
+++ b/solution.py
@@ -25,22 +25,45 @@
     return lax.dot_general(a, b, (((1,), (0,)), ((), ())), preferred_element_type=F32)
 
 
-def side_kernel(pos, acts, s0, s1, s2, s3):
-    y, part = pos[1], pos[3]
+def token_kernel(pos, grads, odd, even, sems):
+    y = pos[1]
+    copies = [
+        pltpu.make_async_copy(grads.at[(y + 1) % 2], odd, sems.at[0]),
+        pltpu.make_async_copy(grads.at[y % 2], even, sems.at[1]),
+    ]
+    for copy in copies:
+        copy.start()
+    for copy in copies:
+        copy.wait()
+
+
+def columns_kernel(pos, w, whole0, mid0, whole1, mid1, sems):
+    columns = pl.ds(pl.multiple_of(jnp.where(pos[0] == 1, SUB, 0), SUB), 256)
+    copies = [
+        pltpu.make_async_copy(w.at[0], whole0, sems.at[0]),
+        pltpu.make_async_copy(w.at[0, :, columns], mid0, sems.at[1]),
+        pltpu.make_async_copy(w.at[1], whole1, sems.at[2]),
+        pltpu.make_async_copy(w.at[1, :, columns], mid1, sems.at[3]),
+    ]
+    for copy in copies:
+        copy.start()
+    for copy in copies:
+        copy.wait()
+
+
+def side_kernel(pos, acts, out):
+    part = pos[3]
     k = lax.broadcasted_iota(jnp.int32, (BLK, 64), 0)
     m = lax.broadcasted_iota(jnp.int32, (BLK, 64), 1)
     select = jnp.where(k == m // 16 * SUB + part * 16 + m % 16, 1.0, 0.0).astype(BF16)
-    for d, send in enumerate((s0, s1, s2, s3)):
-        start = (y + d) % 4 * (3 * BLK)
-        for j in range(3):
-            rows = acts[0, :, pl.ds(pl.multiple_of(start + j * BLK, BLK), BLK)]
-            chosen = nn_dot(rows, select).astype(BF16)
-            cov = tn_dot(chosen, rows).astype(BF16)
-            for i, (r, c) in enumerate(PAIRS):
-                s = 10 * j + i
-                send[s // 15 * 16:(s // 15 + 1) * 16, s % 15 * SUB:(s % 15 + 1) * SUB] = (
-                    cov[r * 16:(r + 1) * 16, c * SUB:(c + 1) * SUB]
-                )
+    for b in range(12):
+        rows = acts[0, :, b * BLK:(b + 1) * BLK]
+        chosen = nn_dot(rows, select).astype(BF16)
+        cov = tn_dot(chosen, rows).astype(BF16)
+        for i, (r, c) in enumerate(PAIRS):
+            s = 10 * (b % 3) + i
+            at = b // 3 * 32 + s // 15 * 16
+            out[at:at + 16, s % 15 * SUB:(s % 15 + 1) * SUB] = cov[r * 16:(r + 1) * 16, c * SUB:(c + 1) * SUB]
 
 
 def cov_kernel(pos, t0, t1, t2, t3, c0, c1, c2, c3, pack):
@@ -95,6 +118,15 @@
     inverse = invert(full)
     for i, (r, c) in enumerate(PAIRS):
         out[:, i * SUB:(i + 1) * SUB] = inverse[r * SUB:(r + 1) * SUB, c * SUB:(c + 1) * SUB]
+
+
+def row_kernel(pos, p0, p1, p2, p3, out):
+    x = pos[0]
+    for b in range(3):
+        for d, part in enumerate((p0, p1, p2, p3)):
+            @pl.when((x + 4 - b) % 4 == d)
+            def _():
+                out[b * SUB:(b + 1) * SUB, :] = part[...]
 
 
 def factor_kernel(pos, mine, other, out, pack, full, diag):
@@ -124,28 +156,36 @@
         out[layer, 768:1024, :] = diag[layer, pl.ds(mid, 256), columns]
 
 
-def right_kernel(pos, w_own, w_pair, w_mid, factor, out):
+def right_product(w_own, w_pair, w_mid, factor):
     total = nn_dot(w_own[0], factor[0, 0:384, :])
     total += nn_dot(w_pair[...], factor[0, 384:768, :])
     total += nn_dot(w_mid[...], factor[0, 768:1024, :])
-    out[...] = total.astype(BF16)
-
-
-def left_kernel(pos, p0, p1, p2, p3, r0, r1, out, pack, full):
+    return total.astype(BF16)
+
+
+def right_kernel(pos, w_own, w_pair, w_mid, factor, out):
+    out[...] = right_product(w_own, w_pair, w_mid, factor)
+
+
+def left_product(pos, layer, parts, right, out, pack, full):
     y, core = pos[1], pos[2]
-    for layer, right in enumerate((r0, r1)):
-        shift_of = (y + 4 - 2 * core - layer) % 4
-        for d, part in enumerate((p0, p1, p2, p3)):
-            @pl.when(shift_of == d)
-            def _():
-                pack[...] = part[...]
-        for b in range(3):
-            unpack(
-                lambda i: pack[b * SUB:(b + 1) * SUB, i * SUB:(i + 1) * SUB].astype(F32),
-                full.at[layer, b],
-            )
-            at = b * BLK
-            out[layer, at:at + BLK, :] = nn_dot(full[layer, b], right[at:at + BLK, :]).astype(BF16)
+    for d, part in enumerate(parts):
+        @pl.when((y + 4 - 2 * core - layer) % 4 == d)
+        def _():
+            pack[...] = part[...]
+    for b in range(3):
+        unpack(lambda i: pack[b * SUB:(b + 1) * SUB, i * SUB:(i + 1) * SUB].astype(F32), full.at[b])
+        at = b * BLK
+        out[0, at:at + BLK, :] = nn_dot(full[b], right[at:at + BLK, :]).astype(BF16)
+
+
+def left_kernel(pos, p0, p1, p2, p3, right, out, pack, full):
+    left_product(pos, 0, (p0, p1, p2, p3), right, out, pack, full)
+
+
+def last_kernel(pos, p0, p1, p2, p3, w_own, w_pair, w_mid, factor, before, out, pack, full, right):
+    right[...] = right_product(w_own, w_pair, w_mid, factor)
+    left_product(pos, 1, (p0, p1, p2, p3), right, out, pack, full)
 
 
 def call(kernel, pos, operands, in_specs, out_shape, scratch, flops, out_specs=None, aliases={}):
@@ -160,17 +200,25 @@
         ),
         out_shape=out_shape,
         input_output_aliases=aliases,
-        compiler_params=pltpu.CompilerParams(vmem_limit_bytes=48 * 1024 * 1024),
-        cost_estimate=pl.CostEstimate(flops=flops, bytes_accessed=8_000_000, transcendentals=0),
+        compiler_params=pltpu.CompilerParams(vmem_limit_bytes=24 * 1024 * 1024),
+        cost_estimate=pl.CostEstimate(flops=flops, bytes_accessed=4_000_000, transcendentals=0),
     )(pos, *operands)
 
 
+ANYWHERE = pl.BlockSpec(memory_space=pl.ANY)
+ONCE = pl.Buffered(1)
+
+
 def whole(a):
-    return pl.BlockSpec(a.shape, lambda i, p, n=len(a.shape): (0,) * n)
+    return pl.BlockSpec(a.shape, lambda i, p, n=len(a.shape): (0,) * n, pipeline_mode=ONCE)
 
 
 def of_layer(a, layer):
-    return pl.BlockSpec((1,) + a.shape[1:], lambda i, p: (layer, 0, 0))
+    return pl.BlockSpec((1,) + a.shape[1:], lambda i, p: (layer, 0, 0), pipeline_mode=ONCE)
+
+
+def shape(*dims):
+    return jax.ShapeDtypeStruct(dims, BF16)
 
 
 def add(parts):
@@ -179,10 +227,6 @@
 
 def send(a, axes, links):
     return lax.ppermute(a, axes, links)
-
-
-def ring(d):
-    return [(i, (i + d) % 4) for i in range(4)]
 
 
 def to_handler(d):
@@ -204,64 +248,85 @@
     y, x, z, c = (lax.axis_index(n) for n in ("y", "x", "z", "c"))
     pos = jnp.stack([x, y, c, z % 4 * 2 + c, z // 4]).astype(jnp.int32)
     shifts = (1, 2, 3)
-
-    odd = lax.dynamic_index_in_dim(grads_out, (y + 1) % 2, 0, False)
-    even = lax.dynamic_index_in_dim(grads_out, y % 2, 0, False)
+    tokens, hidden = grads_out.shape[1:]
+    rows, width = weight_grad.shape[1:]
+    barrier = lax.optimization_barrier
+
+    odd, even = call(
+        token_kernel, pos, (grads_out,), [ANYWHERE], [shape(tokens, hidden)] * 2,
+        [pltpu.SemaphoreType.DMA((2,))], 0, out_specs=[ANYWHERE] * 2,
+    )
     tokens = [even] + [send(even if d == 2 else odd, ("y", "c"), to_handler(d)) for d in shifts]
 
-    def exchange(w):
-        middle = lax.dynamic_slice_in_dim(w, jnp.where(x == 1, SUB, 0), 256, 1)
+    w_ready, _ = barrier((weight_grad, odd))
+    whole0, mid0, whole1, mid1 = call(
+        columns_kernel, pos, (w_ready,), [ANYWHERE], [shape(rows, width), shape(rows, 256)] * 2,
+        [pltpu.SemaphoreType.DMA((4,))], 0, out_specs=[ANYWHERE] * 4,
+    )
+
+    def exchange(w, middle):
         return [send(w, "x", [(0, 1), (1, 0), (2, 3), (3, 2)]), send(middle, "x", [(1, 2), (2, 1)])]
 
-    w_first = exchange(weight_grad[0])
-
-    sides = call(
-        side_kernel, pos, (acts,), [pl.BlockSpec((1, 256, 6144), lambda i, p: (p[4], 0, 0))],
-        [jax.ShapeDtypeStruct((32, LANES), BF16)] * 4, [], 1_000_000_000,
-    )
-    side = add([sides[0]] + [send(sides[d], "y", ring(d)) for d in shifts]).astype(BF16)
+    w_first = exchange(whole0, mid0)
+
+    acts, tokens[1] = barrier((acts, tokens[1]))
+    side = call(
+        side_kernel, pos, (acts,),
+        [pl.BlockSpec((1,) + acts.shape[1:], lambda i, p: (p[4], 0, 0), pipeline_mode=ONCE)],
+        [shape(128, LANES)], [], 1_000_000_000,
+    )[0]
+    side = lax.all_to_all(side, "y", 0, 0, tiled=True)
+    side = add([side[32 * d:32 * (d + 1)] for d in range(4)]).astype(BF16)
+    side, tokens[2], tokens[3] = barrier((side, tokens[2], tokens[3]))
 
     covs = call(
         cov_kernel, pos, tokens, [whole(t) for t in tokens],
-        [jax.ShapeDtypeStruct((SUB, 1280), BF16)] * 4, [VMEM((3, SUB, 1280), BF16)], 1_500_000_000,
+        [shape(SUB, 1280)] * 4, [VMEM((3, SUB, 1280), BF16)], 1_500_000_000,
     )
-    side, covs, w_first = lax.optimization_barrier((side, covs, w_first))
     covs = [covs[0]] + [send(covs[d], ("y", "x", "c"), along_x(d, 4, 3)) for d in shifts]
-    side = add([side] + [send(side, "x", ring(d)) for d in shifts]) * (1.0 / TOKENS)
+    side, covs[1] = barrier((side, covs[1]))
+    side = lax.all_to_all(jnp.tile(side, (4, 1)), "x", 0, 0, tiled=True)
+    side = add([side[32 * d:32 * (d + 1)] for d in range(4)]) * (1.0 / TOKENS)
     side = jnp.concatenate([side[:16], side[16:]], axis=1)
     side = lax.dynamic_slice_in_dim(side, x // 2 * 1280, 2560, 1).astype(BF16)
+    covs, w_first = barrier((covs, w_first))
 
     inverse = call(
         newton_kernel, pos, covs, [whole(t) for t in covs],
-        [jax.ShapeDtypeStruct((SUB, 1280), BF16)], [VMEM((BLK, BLK), F32)], 600_000_000,
-    )[0]
-    row = jnp.stack([inverse] + [send(inverse, ("y", "x", "c"), along_x(d, 3, 4)) for d in shifts])
-    row = jnp.concatenate([lax.dynamic_index_in_dim(row, (x + 4 - b) % 4, 0, False) for b in range(3)], axis=0)
-
-    row, w_second = lax.optimization_barrier((row, weight_grad[1]))
+        [shape(SUB, 1280)], [VMEM((BLK, BLK), F32)], 600_000_000,
+    )[0]
+    parts = [inverse] + [send(inverse, ("y", "x", "c"), along_x(d, 3, 4)) for d in shifts]
+    side, parts[1] = barrier((side, parts[1]))
+    row = call(row_kernel, pos, parts, [whole(t) for t in parts], [shape(3 * SUB, 1280)], [], 0)[0]
+
+    row, whole1, mid1 = barrier((row, whole1, mid1))
     parts = [row] + [send(row, ("y", "c"), from_handler(d)) for d in shifts]
-    w_second = exchange(w_second)
+    w_second = exchange(whole1, mid1)
 
     mine = lax.all_to_all(jnp.tile(side, (8, 1)), "z", 0, 0, tiled=True)
     other = lax.ppermute(mine, "c", [(0, 1), (1, 0)])
     factor = call(
-        factor_kernel, pos, (mine, other), [whole(mine), whole(other)],
-        [jax.ShapeDtypeStruct((2, 1024, 384), BF16)],
+        factor_kernel, pos, (mine, other), [whole(mine), whole(other)], [shape(2, 1024, 384)],
         [VMEM((2, SUB, 2560), BF16), VMEM((2, 2, BLK, BLK), F32), VMEM((2, 1024, 1024), BF16)], 2_500_000_000,
     )[0]
-    rights = [
-        call(
-            right_kernel, pos, (weight_grad, *w, factor),
-            [of_layer(weight_grad, layer), whole(w[0]), whole(w[1]), of_layer(factor, layer)],
-            [jax.ShapeDtypeStruct(weight_grad.shape[1:], BF16)], [], 1_200_000_000,
-        )[0]
-        for layer, w in enumerate((w_first, w_second))
-    ]
-    operands = (*parts, *rights)
+
+    def products(layer, w):
+        specs = [of_layer(weight_grad, layer), whole(w[0]), whole(w[1]), of_layer(factor, layer)]
+        return (weight_grad, *w, factor), specs
+
+    out = shape(*weight_grad.shape)
+    scratch = [VMEM((3 * SUB, 1280), BF16), VMEM((3, BLK, BLK), BF16)]
+    operands, specs = products(0, w_first)
+    right = call(right_kernel, pos, operands, specs, [shape(rows, width)], [], 1_200_000_000)[0]
+    operands = (*parts, right)
+    before = call(
+        left_kernel, pos, operands, [whole(a) for a in operands], [out], scratch, 600_000_000,
+        out_specs=[of_layer(out, 0)],
+    )[0]
+    operands, specs = products(1, w_second)
     return call(
-        left_kernel, pos, operands, [whole(a) for a in operands],
-        [jax.ShapeDtypeStruct(weight_grad.shape, BF16)],
-        [VMEM((3 * SUB, 1280), BF16), VMEM((2, 3, BLK, BLK), BF16)], 1_500_000_000,
+        last_kernel, pos, (*parts, *operands, before), [whole(a) for a in parts] + specs + [ANYWHERE], [out],
+        scratch + [VMEM((rows, width), BF16)], 1_800_000_000, out_specs=[of_layer(out, 1)], aliases={9: 0},
     )[0]
 
 

time: 154 us -> 166 us (1.078)
  Pallas kernels: 29.2 us -> 35.1 us
  starting transfers between devices: 69.4 us -> 74.4 us
  waiting for transfers between devices: 38.1 us -> 40 us
    all_to_all x0 -> x2, starting transfers between devices: none -> 21.4 us  [the longest x1 17.2 us: body(): side = lax.all_to_all(side, 'y', 0, 0, tiled=True)]
    ppermute x22 -> x16, starting transfers between devices: 44.9 us -> 27.2 us  [send(): return lax.ppermute(a, axes, links)]
    all_to_all x1, waiting for transfers between devices: 3.44 us -> 10.9 us  [body(): mine = lax.all_to_all(jnp.tile(side, (8, 1)), 'z', 0, 0, tiled=True)]
    pallas_call x7 -> x10, Pallas kernels: 29.2 us -> 35.1 us  [call(): pl.pallas_call(kernel, grid_spec=pltpu.PrefetchScalarGridSpec(num_scalar_...]
    unnamed x18 -> x26, local copies, waits for them, and re-layouts: 5.89 us -> 11.5 us
    ppermute x22 -> x16, waiting for transfers between devices: 34.6 us -> 29 us  [send(): return lax.ppermute(a, axes, links)]
    squeeze x3 -> x0, local copies, waits for them, and re-layouts: 5.17 us -> none  [the longest x1 2.36 us: body(): odd = lax.dynamic_index_in_dim(grads_out, (y + 1) % 2, 0, False)]
  transfers between devices with their start and end apart: 24 -> 20, of which waited for: 3 -> 5; matrix products, arithmetic and copies ran while one was open for 6% -> 2% of each run, Pallas kernels for 12% -> 14%
where the time goes in v4:
time: 166 us; the launch traced here: 165 us
  starting transfers between devices  74.4 us (45%)
  waiting for transfers between devices  40 us (24%)
  Pallas kernels  35.1 us (21%)
  local copies, waits for them, and re-layouts  13.3 us (8%)
  other arithmetic  2.42 us (1%)
    pallas_call x10, Pallas kernels, call(): pl.pallas_call(kernel, grid_spec=pltpu.PrefetchScalarGridSpec(num_scalar_...  35.1 us
    ppermute x16, waiting for transfers between devices, send(): return lax.ppermute(a, axes, links)  29 us
    ppermute x16, starting transfers between devices, send(): return lax.ppermute(a, axes, links)  27.2 us
    ppermute x1, starting transfers between devices, body(): other = lax.ppermute(mine, 'c', [(0, 1), (1, 0)])  17.7 us
    all_to_all x1, starting transfers between devices, body(): side = lax.all_to_all(side, 'y', 0, 0, tiled=True)  17.2 us
    unnamed x26, local copies, waits for them, and re-layouts  11.5 us
    all_to_all x1, waiting for transfers between devices, body(): mine = lax.all_to_all(jnp.tile(side, (8, 1)), 'z', 0, 0, tiled=True)  10.9 us
    all_to_all x1, starting transfers between devices, body(): mine = lax.all_to_all(jnp.tile(side, (8, 1)), 'z', 0, 0, tiled=True)  8.18 us
  transfers between devices with their start and end apart: 20, of which 5 were waited for; matrix products, arithmetic and copies ran while one was open for 2% of the time, Pallas kernels for 14%

profile of v4, /device:TPU:1, one launch (start us, length us, event | category | flops | bytes accessed | tf_op | source)
XLA Modules:
  0.0 165.4 jit_solution(15518991104853017867)
XLA Ops:
  0.0 0.1 stack.23.pos
  0.1 1.4 copy-done.2
  1.5 1.7 %shard_map.37 = (bf16[256,1536]{1,0:T(8,128)(2,1)}, bf16[256,1536]{1,0:T(8,128)(2,1)}) custom-call(s32[5]{0:T(128)S(1)} %stack.23.pos, bf16[2,256,1536]{2,1,0:T(8,128)(2,1)S(1)} %copy-done.2), custom_call_target="tpu_custom_call" | custom-call | bytes 4000000 | tf_op jit(solution)/shard_map/pallas_call | solution.py:192
  3.2 0.7 collective-permute-start
  3.9 0.0 collective-permute-done.t1
  4.0 0.9 copy-done.7
  4.8 2.8 %copy-done.1 = bf16[2,256,6144]{2,1,0:T(8,128)(2,1)S(1)} copy-done((bf16[2,256,6144]{2,1,0:T(8,128)(2,1)S(1)}, bf16[2,256,6144]{2,1,0:T(8,128)(2,1)}, u32[]{:S(2)}) %copy-start.1) | copy-done | bytes 6291480
  7.6 4.6 %shard_map.38 = bf16[128,1920]{1,0:T(8,128)(2,1)} custom-call(s32[5]{0:T(128)S(1)} %stack.23.pos, bf16[2,256,6144]{2,1,0:T(8,128)(2,1)S(1)} %copy-done.1), custom_call_target="tpu_custom_call" | custom-call | flops 1000000000 | bytes 4000000 | tf_op jit(solution)/shard_map/pallas_call | solution.py:192
  12.2 17.2 %all-to-all-start = ((bf16[4,32,1920]{2,1,0:T(8,128)(2,1)}), bf16[4,32,1920]{2,1,0:T(8,128)(2,1)}, u32[]{:S(2)}, u32[]{:S(2)}) async-start(bf16[4,32,1920]{2,1,0:T(8,128)(2,1)} %bitcast.5), calls=%async_computation | async-start | bytes 983040 | tf_op jit(solution)/shard_map/all_to_all | solution.py:278
  29.4 5.8 %collective-permute-start.1 = (bf16[256,1536]{1,0:T(8,128)(2,1)}, bf16[256,1536]{1,0:T(8,128)(2,1)}, u32[]{:S(2)}, u32[]{:S(2)}) collective-permute-start(bf16[256,1536]{1,0:T(8,128)(2,1)} %get-tuple-element.34.t0), channel_id=1, source_target_pairs={{1,129},{65,193},{128,0},{192,64},{3,131},{67,195},{130,2},{194,66... | collective-permute-start | bytes 2359304 | tf_op jit(solution)/shard_map/ppermute | solution.py:229
  35.2 2.2 %collective-permute-start.2 = (bf16[256,1536]{1,0:T(8,128)(2,1)}, bf16[256,1536]{1,0:T(8,128)(2,1)}, u32[]{:S(2)}, u32[]{:S(2)}) collective-permute-start(bf16[256,1536]{1,0:T(8,128)(2,1)} %get-tuple-element.35), channel_id=1, source_target_pairs={{1,193},{64,0},{128,64},{193,129},{3,195},{66,2},{130,66},{195,131... | collective-permute-start | bytes 2359304 | tf_op jit(solution)/shard_map/ppermute | solution.py:229
  37.4 1.9 %shard_map.40 = (bf16[1536,384]{1,0:T(8,128)(2,1)}, bf16[1536,256]{1,0:T(8,128)(2,1)}, bf16[1536,384]{1,0:T(8,128)(2,1)S(1)}, bf16[1536,256]{1,0:T(8,128)(2,1)S(1)}) custom-call(s32[5]{0:T(128)S(1)} %stack.23.pos, bf16[2,1536,384]{2,1,0:T(8,128)(2,1)S(1)} %copy-done), custom_call_target="tpu_custom_call" | custom-call | bytes 4000000 | tf_op jit(solution)/shard_map/pallas_call | solution.py:192
  39.3 1.0 copy-done.3
  40.3 0.9 copy-done.5
  41.2 1.5 collective-permute-start.7
  42.8 2.9 %collective-permute-start.6 = (bf16[1536,384]{1,0:T(8,128)(2,1)}, bf16[1536,384]{1,0:T(8,128)(2,1)S(1)}, u32[]{:S(2)}, u32[]{:S(2)}) collective-permute-start(bf16[1536,384]{1,0:T(8,128)(2,1)} %get-tuple-element.47), channel_id=1, source_target_pairs={{0,16},{16,0},{32,48},{48,32},{1,17},{17,1},{33,49},{49,33},{2,18}... | collective-permute-start | bytes 3538952 | tf_op jit(solution)/shard_map/ppermute | solution.py:229
  45.6 0.0 all-to-all-done
  45.6 1.1 fusion.2
  46.8 0.0 collective-permute-done.1.t2
  46.8 7.8 %collective-permute-done.2.t3 = bf16[256,1536]{1,0:T(8,128)(2,1)} collective-permute-done((bf16[256,1536]{1,0:T(8,128)(2,1)}, bf16[256,1536]{1,0:T(8,128)(2,1)}, u32[]{:S(2)}, u32[]{:S(2)}) %collective-permute-start.2) | collective-permute-done | bytes 786464 | tf_op jit(solution)/shard_map/ppermute | solution.py:229
  54.6 1.1 copy-done.8
  55.8 4.6 %shard_map.39 = (bf16[128,1280]{1,0:T(8,128)(2,1)S(1)}, bf16[128,1280]{1,0:T(8,128)(2,1)S(1)}, bf16[128,1280]{1,0:T(8,128)(2,1)}, bf16[128,1280]{1,0:T(8,128)(2,1)}) custom-call(s32[5]{0:T(128)S(1)} %stack.23.pos, bf16[256,1536]{1,0:T(8,128)(2,1)} %get-tuple-element.34.t0, bf16[256,1536]{1,0:T(8,128)(2,1)S(1)} %copy-done.8, ...), custom_call_target="tpu_custom_call" | custom-call | flops 1500000000 | bytes 4000000 | tf_op jit(solution)/shard_map/pallas_call | solution.py:192
  60.3 0.7 copy-done.11
  61.1 0.7 collective-permute-start.3
  61.7 1.4 collective-permute-start.4
  63.2 1.4 collective-permute-start.5
  64.5 0.0 collective-permute-done.3.c1
  64.5 0.7 copy-done.9
  65.3 0.8 tile.4
  66.1 4.1 %all-to-all-start.1 = ((bf16[4,32,1920]{2,1,0:T(8,128)(2,1)}), bf16[4,32,1920]{2,1,0:T(8,128)(2,1)}, u32[]{:S(2)}, u32[]{:S(2)}) async-start(bf16[4,32,1920]{2,1,0:T(8,128)(2,1)} %tile.4), calls=%async_computation.1 | async-start | bytes 983040 | tf_op jit(solution)/shard_map/all_to_all | solution.py:288
  70.3 0.0 collective-permute-done.7.w_mid
  70.3 1.5 collective-permute-done.6.w_pair
  71.8 0.0 collective-permute-done.4.c2
  71.8 0.0 collective-permute-done.5.c3
  71.8 1.0 copy-done.10
  72.8 1.0 copy-done.12
  73.8 3.7 %shard_map.41.p0 = bf16[128,1280]{1,0:T(8,128)(2,1)} custom-call(s32[5]{0:T(128)S(1)} %stack.23.pos, bf16[128,1280]{1,0:T(8,128)(2,1)S(1)} %copy-done.12, bf16[128,1280]{1,0:T(8,128)(2,1)S(1)} %copy-done.10, bf16[128,1280]{1,0:T(8,128)(2,1)} %collective-permute-done.4.c2, bf16[128,1280]{1,0:T(8,128)(2,1)} %collective-permute-done.5.c3), custom_call_target="tpu_custom_call" | custom-call | flops 600000000 | bytes 4000000 | tf_op jit(solution)/shard_map/pallas_call | solution.py:192
  77.4 1.4 collective-permute-start.8
  78.8 0.0 all-to-all-done.1
  78.8 1.2 add_multiply_fusion
  80.0 0.1 fusion.1
  80.1 0.0 collective-permute-done.8.p1
  80.1 0.9 tile.5
  81.0 8.2 %all-to-all-start.2 = ((bf16[8,16,2560]{2,1,0:T(8,128)(2,1)}), bf16[8,16,2560]{2,1,0:T(8,128)(2,1)}, u32[]{:S(2)}, u32[]{:S(2)}) async-start(bf16[8,16,2560]{2,1,0:T(8,128)(2,1)} %tile.5), calls=%async_computation.2 | async-start | bytes 1310720 | tf_op jit(solution)/shard_map/all_to_all | solution.py:306
  89.2 1.4 collective-permute-start.10
  90.6 1.4 collective-permute-start.9
  92.0 10.9 %all-to-all-done.2 = bf16[8,16,2560]{2,1,0:T(8,128)(2,1)} async-done(((bf16[8,16,2560]{2,1,0:T(8,128)(2,1)}), bf16[8,16,2560]{2,1,0:T(8,128)(2,1)}, u32[]{:S(2)}, u32[]{:S(2)}) %all-to-all-start.2) | async-done | bytes 655392 | tf_op jit(solution)/shard_map/all_to_all | solution.py:306
  102.9 17.7 %collective-permute-start.16 = (bf16[128,2560]{1,0:T(8,128)(2,1)}, bf16[128,2560]{1,0:T(8,128)(2,1)S(1)}, u32[]{:S(2)}, u32[]{:S(2)}) collective-permute-start(bf16[128,2560]{1,0:T(8,128)(2,1)} %bitcast.9.mine), channel_id=1, source_target_pairs={{0,1},{1,0},{2,3},{3,2},{4,5},{5,4},{6,7},{7,6},{8,9},{9,8},{10,11... | collective-permute-start | bytes 1966088 | tf_op jit(solution)/shard_map/ppermute | solution.py:307
  120.6 0.0 collective-permute-done.10.p3
  120.6 0.0 collective-permute-done.9.p2
  120.6 1.9 %shard_map.42.p0 = bf16[384,1280]{1,0:T(8,128)(2,1)S(1)} custom-call(s32[5]{0:T(128)S(1)} %stack.23.pos, bf16[128,1280]{1,0:T(8,128)(2,1)} %shard_map.41.p0, bf16[128,1280]{1,0:T(8,128)(2,1)} %collective-permute-done.8.p1, bf16[128,1280]{1,0:T(8,128)(2,1)} %collective-permute-done.9.p2, bf16[128,1280]{1,0:T(8,128)(2,1)} %collective-permute-done.10.p3), custom_call_target="tpu_custom_call" | custom-call | bytes 4000000 | tf_op jit(solution)/shard_map/pallas_call | solution.py:192
  122.5 2.3 %collective-permute-start.14 = (bf16[1536,384]{1,0:T(8,128)(2,1)S(1)}, bf16[1536,384]{1,0:T(8,128)(2,1)S(1)}, u32[]{:S(2)}, u32[]{:S(2)}) collective-permute-start(bf16[1536,384]{1,0:T(8,128)(2,1)S(1)} %copy-done.4), channel_id=1, source_target_pairs={{0,16},{16,0},{32,48},{48,32},{1,17},{17,1},{33,49},{49,33},{2,18}... | collective-permute-start | bytes 3538952 | tf_op jit(solution)/shard_map/ppermute | solution.py:229
  124.8 0.7 collective-permute-start.13
  125.5 1.3 collective-permute-start.12
  126.8 1.3 collective-permute-start.11
  128.1 0.0 collective-permute-done.16.other
  128.2 0.9 collective-permute-start.15
  129.1 5.0 %shard_map.43.factor = bf16[2,1024,384]{2,1,0:T(8,128)(2,1)S(1)} custom-call(s32[5]{0:T(128)S(1)} %stack.23.pos, bf16[128,2560]{1,0:T(8,128)(2,1)} %bitcast.9.mine, bf16[128,2560]{1,0:T(8,128)(2,1)S(1)} %collective-permute-done.16.other), custom_call_target="tpu_custom_call" | custom-call | flops 2500000000 | bytes 4000000 | tf_op jit(solution)/shard_map/pallas_call | solution.py:192
  134.1 3.7 %shard_map.44.right = bf16[1536,384]{1,0:T(8,128)(2,1)S(1)} custom-call(s32[5]{0:T(128)S(1)} %stack.23.pos, bf16[2,1536,384]{2,1,0:T(8,128)(2,1)S(1)} %copy-done, bf16[1536,384]{1,0:T(8,128)(2,1)S(1)} %collective-permute-done.6.w_pair, bf16[1536,256]{1,0:T(8,128)(2,1)} %collective-permute-done.7.w_mid, bf16[2,1024,384]{2,1,0:T(8,128)(2,1)S(1)} %shard_map.43.factor), custom_call_target="tpu_custom_call" | custom-call | flops 1200000000 | bytes 4000000 | tf_op jit(solution)/shard_map/pallas_call | solution.py:192
  137.8 0.0 collective-permute-done.13.p3
  137.8 9.2 %collective-permute-done.12.p2 = bf16[384,1280]{1,0:T(8,128)(2,1)S(1)} collective-permute-done((bf16[384,1280]{1,0:T(8,128)(2,1)S(1)}, bf16[384,1280]{1,0:T(8,128)(2,1)S(1)}, u32[]{:S(2)}, u32[]{:S(2)}) %collective-permute-start.12) | collective-permute-done | bytes 983072 | tf_op jit(solution)/shard_map/ppermute | solution.py:229
  147.0 10.4 %collective-permute-done.11.p1 = bf16[384,1280]{1,0:T(8,128)(2,1)S(1)} collective-permute-done((bf16[384,1280]{1,0:T(8,128)(2,1)S(1)}, bf16[384,1280]{1,0:T(8,128)(2,1)S(1)}, u32[]{:S(2)}, u32[]{:S(2)}) %collective-permute-start.11) | collective-permute-done | bytes 983072 | tf_op jit(solution)/shard_map/ppermute | solution.py:229
  157.4 2.7 %shard_map.45.before = bf16[2,1536,384]{2,1,0:T(8,128)(2,1)} custom-call(s32[5]{0:T(128)S(1)} %stack.23.pos, bf16[384,1280]{1,0:T(8,128)(2,1)S(1)} %shard_map.42.p0, bf16[384,1280]{1,0:T(8,128)(2,1)S(1)} %collective-permute-done.11.p1, bf16[384,1280]{1,0:T(8,128)(2,1)S(1)} %collective-permute-done.12.p2, bf16[384,1280]{1,0:T(8,128)(2,1)S(1)} %collective-permute-done.13.p3, ...), custom_call_target="tpu_custom_call" | custom-call | flops 600000000 | bytes 4000000 | tf_op jit(solution)/shard_map/pallas_call | solution.py:192
  160.1 5.3 %shard_map.46 = bf16[2,1536,384]{2,1,0:T(8,128)(2,1)} custom-call(s32[5]{0:T(128)S(1)} %stack.23.pos, bf16[384,1280]{1,0:T(8,128)(2,1)S(1)} %shard_map.42.p0, bf16[384,1280]{1,0:T(8,128)(2,1)S(1)} %collective-permute-done.11.p1, bf16[384,1280]{1,0:T(8,128)(2,1)S(1)} %collective-permute-done.12.p2, ...), custom_call_target="tpu_custom_call", output_to_operand_aliasing={{}: (9, {})} | custom-call | flops 1800000000 | bytes 4000000 | tf_op jit(solution)/shard_map/pallas_call | solution.py:192
  (19 shorter events, 0.0 us)
Async XLA Ops:
  0.1 1.4 copy-start.2
  3.2 0.7 collective-permute-start
  3.9 0.9 copy-start.7
  4.8 2.8 %copy-start.1 = (bf16[2,256,6144]{2,1,0:T(8,128)(2,1)S(1)}, bf16[2,256,6144]{2,1,0:T(8,128)(2,1)}, u32[]{:S(2)}) copy-start(bf16[2,256,6144]{2,1,0:T(8,128)(2,1)} %acts) | copy-start | bytes 18874372
  7.6 29.8 %copy-start = (bf16[2,1536,384]{2,1,0:T(8,128)(2,1)S(1)}, bf16[2,1536,384]{2,1,0:T(8,128)(2,1)}, u32[]{:S(2)}) copy-start(bf16[2,1536,384]{2,1,0:T(8,128)(2,1)} %w_own.3) | copy-start | bytes 7077892
  12.2 33.4 %all-to-all-start = ((bf16[4,32,1920]{2,1,0:T(8,128)(2,1)}), bf16[4,32,1920]{2,1,0:T(8,128)(2,1)}, u32[]{:S(2)}, u32[]{:S(2)}) async-start(bf16[4,32,1920]{2,1,0:T(8,128)(2,1)} %bitcast.5), calls=%async_computation | async-start | bytes 983040 | tf_op jit(solution)/shard_map/all_to_all | solution.py:278
  29.4 17.3 %collective-permute-start.1 = (bf16[256,1536]{1,0:T(8,128)(2,1)}, bf16[256,1536]{1,0:T(8,128)(2,1)}, u32[]{:S(2)}, u32[]{:S(2)}) collective-permute-start(bf16[256,1536]{1,0:T(8,128)(2,1)} %get-tuple-element.34.t0), channel_id=1, source_target_pairs={{1,129},{65,193},{128,0},{192,64},{3,131},{67,195},{130,2},{194,66... | collective-permute-start | bytes 2359304 | tf_op jit(solution)/shard_map/ppermute | solution.py:229
  35.2 19.4 %collective-permute-start.2 = (bf16[256,1536]{1,0:T(8,128)(2,1)}, bf16[256,1536]{1,0:T(8,128)(2,1)}, u32[]{:S(2)}, u32[]{:S(2)}) collective-permute-start(bf16[256,1536]{1,0:T(8,128)(2,1)} %get-tuple-element.35), channel_id=1, source_target_pairs={{1,193},{64,0},{128,64},{193,129},{3,195},{66,2},{130,66},{195,131... | collective-permute-start | bytes 2359304 | tf_op jit(solution)/shard_map/ppermute | solution.py:229
  39.3 1.0 copy-start.3
  40.3 0.9 copy-start.5
  41.2 29.0 %collective-permute-start.7 = (bf16[1536,256]{1,0:T(8,128)(2,1)}, bf16[1536,256]{1,0:T(8,128)(2,1)}, u32[]{:S(2)}, u32[]{:S(2)}) collective-permute-start(bf16[1536,256]{1,0:T(8,128)(2,1)} %get-tuple-element.48), channel_id=1, source_target_pairs={{16,32},{32,16},{17,33},{33,17},{18,34},{34,18},{19,35},{35,19},{2... | collective-permute-start | bytes 2359304 | tf_op jit(solution)/shard_map/ppermute | solution.py:229
  42.8 29.0 %collective-permute-start.6 = (bf16[1536,384]{1,0:T(8,128)(2,1)}, bf16[1536,384]{1,0:T(8,128)(2,1)S(1)}, u32[]{:S(2)}, u32[]{:S(2)}) collective-permute-start(bf16[1536,384]{1,0:T(8,128)(2,1)} %get-tuple-element.47), channel_id=1, source_target_pairs={{0,16},{16,0},{32,48},{48,32},{1,17},{17,1},{33,49},{49,33},{2,18}... | collective-permute-start | bytes 3538952 | tf_op jit(solution)/shard_map/ppermute | solution.py:229
  54.6 1.1 copy-start.8
  60.3 0.7 copy-start.11
  61.1 3.5 %collective-permute-start.3 = (bf16[128,1280]{1,0:T(8,128)(2,1)S(1)}, bf16[128,1280]{1,0:T(8,128)(2,1)S(1)}, u32[]{:S(2)}, u32[]{:S(2)}) collective-permute-start(bf16[128,1280]{1,0:T(8,128)(2,1)S(1)} %get-tuple-element.42), channel_id=1, source_target_pairs={{0,16},{16,32},{48,0},{64,80},{80,96},{112,64},{129,145},{145,161}... | collective-permute-start | bytes 983048 | tf_op jit(solution)/shard_map/ppermute | solution.py:229
  61.7 10.1 %collective-permute-start.4 = (bf16[128,1280]{1,0:T(8,128)(2,1)}, bf16[128,1280]{1,0:T(8,128)(2,1)}, u32[]{:S(2)}, u32[]{:S(2)}) collective-permute-start(bf16[128,1280]{1,0:T(8,128)(2,1)} %get-tuple-element.44), channel_id=1, source_target_pairs={{0,32},{32,0},{48,16},{64,96},{96,64},{112,80},{129,161},{161,129}... | collective-permute-start | bytes 983048 | tf_op jit(solution)/shard_map/ppermute | solution.py:229
  63.2 8.6 %collective-permute-start.5 = (bf16[128,1280]{1,0:T(8,128)(2,1)}, bf16[128,1280]{1,0:T(8,128)(2,1)}, u32[]{:S(2)}, u32[]{:S(2)}) collective-permute-start(bf16[128,1280]{1,0:T(8,128)(2,1)} %get-tuple-element.45), channel_id=1, source_target_pairs={{16,0},{32,16},{48,32},{80,64},{96,80},{112,96},{145,129},{161,145... | collective-permute-start | bytes 983048 | tf_op jit(solution)/shard_map/ppermute | solution.py:229
  64.5 0.7 copy-start.9
  66.1 12.7 %all-to-all-start.1 = ((bf16[4,32,1920]{2,1,0:T(8,128)(2,1)}), bf16[4,32,1920]{2,1,0:T(8,128)(2,1)}, u32[]{:S(2)}, u32[]{:S(2)}) async-start(bf16[4,32,1920]{2,1,0:T(8,128)(2,1)} %tile.4), calls=%async_computation.1 | async-start | bytes 983040 | tf_op jit(solution)/shard_map/all_to_all | solution.py:288
  71.8 1.0 copy-start.10
  72.8 1.0 copy-start.12
  77.4 2.7 %collective-permute-start.8 = (bf16[128,1280]{1,0:T(8,128)(2,1)}, bf16[128,1280]{1,0:T(8,128)(2,1)}, u32[]{:S(2)}, u32[]{:S(2)}) collective-permute-start(bf16[128,1280]{1,0:T(8,128)(2,1)} %shard_map.41.p0), channel_id=1, source_target_pairs={{0,16},{16,32},{32,48},{64,80},{80,96},{96,112},{129,145},{145,161... | collective-permute-start | bytes 983048 | tf_op jit(solution)/shard_map/ppermute | solution.py:229
  81.0 21.9 %all-to-all-start.2 = ((bf16[8,16,2560]{2,1,0:T(8,128)(2,1)}), bf16[8,16,2560]{2,1,0:T(8,128)(2,1)}, u32[]{:S(2)}, u32[]{:S(2)}) async-start(bf16[8,16,2560]{2,1,0:T(8,128)(2,1)} %tile.5), calls=%async_computation.2 | async-start | bytes 1310720 | tf_op jit(solution)/shard_map/all_to_all | solution.py:306
  89.2 31.4 %collective-permute-start.10 = (bf16[128,1280]{1,0:T(8,128)(2,1)}, bf16[128,1280]{1,0:T(8,128)(2,1)}, u32[]{:S(2)}, u32[]{:S(2)}) collective-permute-start(bf16[128,1280]{1,0:T(8,128)(2,1)} %shard_map.41.p0), channel_id=1, source_target_pairs={{0,48},{16,0},{32,16},{64,112},{80,64},{96,80},{129,177},{145,129}... | collective-permute-start | bytes 983048 | tf_op jit(solution)/shard_map/ppermute | solution.py:229
  90.6 30.0 %collective-permute-start.9 = (bf16[128,1280]{1,0:T(8,128)(2,1)}, bf16[128,1280]{1,0:T(8,128)(2,1)}, u32[]{:S(2)}, u32[]{:S(2)}) collective-permute-start(bf16[128,1280]{1,0:T(8,128)(2,1)} %shard_map.41.p0), channel_id=1, source_target_pairs={{0,32},{16,48},{32,0},{64,96},{80,112},{96,64},{129,161},{145,177}... | collective-permute-start | bytes 983048 | tf_op jit(solution)/shard_map/ppermute | solution.py:229
  102.9 19.6 %copy-start.4 = (bf16[1536,384]{1,0:T(8,128)(2,1)S(1)}, bf16[1536,384]{1,0:T(8,128)(2,1)}, u32[]{:S(2)}) copy-start(bf16[1536,384]{1,0:T(8,128)(2,1)} %copy-done.3) | copy-start | bytes 3538948
  102.9 25.2 %copy-start.6 = (bf16[1536,256]{1,0:T(8,128)(2,1)S(1)}, bf16[1536,256]{1,0:T(8,128)(2,1)}, u32[]{:S(2)}) copy-start(bf16[1536,256]{1,0:T(8,128)(2,1)} %copy-done.5) | copy-start | bytes 2359300
  102.9 25.2 %collective-permute-start.16 = (bf16[128,2560]{1,0:T(8,128)(2,1)}, bf16[128,2560]{1,0:T(8,128)(2,1)S(1)}, u32[]{:S(2)}, u32[]{:S(2)}) collective-permute-start(bf16[128,2560]{1,0:T(8,128)(2,1)} %bitcast.9.mine), channel_id=1, source_target_pairs={{0,1},{1,0},{2,3},{3,2},{4,5},{5,4},{6,7},{7,6},{8,9},{9,8},{10,11... | collective-permute-start | bytes 1966088 | tf_op jit(solution)/shard_map/ppermute | solution.py:307
  122.5 37.6 %collective-permute-start.14 = (bf16[1536,384]{1,0:T(8,128)(2,1)S(1)}, bf16[1536,384]{1,0:T(8,128)(2,1)S(1)}, u32[]{:S(2)}, u32[]{:S(2)}) collective-permute-start(bf16[1536,384]{1,0:T(8,128)(2,1)S(1)} %copy-done.4), channel_id=1, source_target_pairs={{0,16},{16,0},{32,48},{48,32},{1,17},{17,1},{33,49},{49,33},{2,18}... | collective-permute-start | bytes 3538952 | tf_op jit(solution)/shard_map/ppermute | solution.py:229
  124.8 12.9 %collective-permute-start.13 = (bf16[384,1280]{1,0:T(8,128)(2,1)S(1)}, bf16[384,1280]{1,0:T(8,128)(2,1)S(1)}, u32[]{:S(2)}, u32[]{:S(2)}) collective-permute-start(bf16[384,1280]{1,0:T(8,128)(2,1)S(1)} %shard_map.42.p0), channel_id=1, source_target_pairs={{0,192},{64,0},{129,65},{193,129},{2,194},{66,2},{131,67},{195,131... | collective-permute-start | bytes 2949128 | tf_op jit(solution)/shard_map/ppermute | solution.py:229
  125.5 21.4 %collective-permute-start.12 = (bf16[384,1280]{1,0:T(8,128)(2,1)S(1)}, bf16[384,1280]{1,0:T(8,128)(2,1)S(1)}, u32[]{:S(2)}, u32[]{:S(2)}) collective-permute-start(bf16[384,1280]{1,0:T(8,128)(2,1)S(1)} %shard_map.42.p0), channel_id=1, source_target_pairs={{0,128},{64,192},{129,1},{193,65},{2,130},{66,194},{131,3},{195,67... | collective-permute-start | bytes 2949128 | tf_op jit(solution)/shard_map/ppermute | solution.py:229
  126.8 30.6 %collective-permute-start.11 = (bf16[384,1280]{1,0:T(8,128)(2,1)S(1)}, bf16[384,1280]{1,0:T(8,128)(2,1)S(1)}, u32[]{:S(2)}, u32[]{:S(2)}) collective-permute-start(bf16[384,1280]{1,0:T(8,128)(2,1)S(1)} %shard_map.42.p0), channel_id=1, source_target_pairs={{0,64},{64,128},{129,193},{193,1},{2,66},{66,130},{131,195},{195,3... | collective-permute-start | bytes 2949128 | tf_op jit(solution)/shard_map/ppermute | solution.py:229
  128.2 31.9 %collective-permute-start.15 = (bf16[1536,256]{1,0:T(8,128)(2,1)S(1)}, bf16[1536,256]{1,0:T(8,128)(2,1)S(1)}, u32[]{:S(2)}, u32[]{:S(2)}) collective-permute-start(bf16[1536,256]{1,0:T(8,128)(2,1)S(1)} %copy-done.6), channel_id=1, source_target_pairs={{16,32},{32,16},{17,33},{33,17},{18,34},{34,18},{19,35},{35,19},{2... | collective-permute-start | bytes 2359304 | tf_op jit(solution)/shard_map/ppermute | solution.py:229

commit v5 on v4

v5 whole, which is shorter than its diff:
```python
import jax
import jax.numpy as jnp
from jax import lax
from jax.experimental import pallas as pl
from jax.experimental.pallas import tpu as pltpu
from jax.sharding import Mesh, PartitionSpec as P

BLK = 512
SUB = 128
damping = 0.1
TOKENS = 4096
F32 = jnp.float32
BF16 = jnp.bfloat16
VMEM = pltpu.VMEM

PAIRS = [(r, c) for r in range(4) for c in range(r, 4)]
LANES = 15 * SUB


def tn_dot(a, b):
    return lax.dot_general(a, b, (((0,), (0,)), ((), ())), preferred_element_type=F32)


def nn_dot(a, b):
    return lax.dot_general(a, b, (((1,), (0,)), ((), ())), preferred_element_type=F32)


def columns_kernel(pos, w, whole0, mid0, whole1, mid1, sems):
    columns = pl.ds(pl.multiple_of(jnp.where(pos[0] == 1, SUB, 0), SUB), 256)
    copies = [
        pltpu.make_async_copy(w.at[0], whole0, sems.at[0]),
        pltpu.make_async_copy(w.at[0, :, columns], mid0, sems.at[1]),
        pltpu.make_async_copy(w.at[1], whole1, sems.at[2]),
        pltpu.make_async_copy(w.at[1, :, columns], mid1, sems.at[3]),
    ]
    for copy in copies:
        copy.start()
    for copy in copies:
        copy.wait()


def side_kernel(pos, acts, out):
    part = pos[3]
    k = lax.broadcasted_iota(jnp.int32, (BLK, 64), 0)
    m = lax.broadcasted_iota(jnp.int32, (BLK, 64), 1)
    select = jnp.where(k == m // 16 * SUB + part * 16 + m % 16, 1.0, 0.0).astype(BF16)
    for b in range(12):
        rows = acts[0, :, b * BLK:(b + 1) * BLK]
        chosen = nn_dot(rows, select).astype(BF16)
        cov = tn_dot(chosen, rows).astype(BF16)
        for i, (r, c) in enumerate(PAIRS):
            s = 10 * (b % 3) + i
            at = b // 3 * 32 + s // 15 * 16
            out[at:at + 16, s % 15 * SUB:(s % 15 + 1) * SUB] = cov[r * 16:(r + 1) * 16, c * SUB:(c + 1) * SUB]


def cov_kernel(pos, grads, h0, h1, h2, h3, pack):
    y = pos[1]
    for layer in range(2):
        for b in range(3):
            rows = grads[layer, :, b * BLK:(b + 1) * BLK]
            top = tn_dot(rows[:, :256], rows).astype(BF16)
            low = tn_dot(rows[:, 256:], rows[:, 256:]).astype(BF16)
            for i, (r, c) in enumerate(PAIRS):
                s = 10 * b + i
                if r < 2:
                    piece = top[r * SUB:(r + 1) * SUB, c * SUB:(c + 1) * SUB]
                else:
                    piece = low[(r - 2) * SUB:(r - 1) * SUB, (c - 2) * SUB:(c - 1) * SUB]
                pack[layer, s // 15 * SUB:(s // 15 + 1) * SUB, s % 15 * SUB:(s % 15 + 1) * SUB] = piece
    for d, out in enumerate((h0, h1, h2, h3)):
        at = pl.multiple_of((y + d) % 4 * 64, 64)
        out[0:64, :] = pack[0, pl.ds(at, 64), :]
        out[64:128, :] = pack[1, pl.ds(at, 64), :]


def unpack(piece, full):
    for i, (r, c) in enumerate(PAIRS):
        tile = piece(i)
        full[r * SUB:(r + 1) * SUB, c * SUB:(c + 1) * SUB] = tile.astype(full.dtype)
        if r != c:
            full[c * SUB:(c + 1) * SUB, r * SUB:(r + 1) * SUB] = tile.T.astype(full.dtype)


def invert(full):
    ri = lax.broadcasted_iota(jnp.int32, (BLK, BLK), 0)
    ci = lax.broadcasted_iota(jnp.int32, (BLK, BLK), 1)
    diagonal = ri == ci
    matrix = full[...] + jnp.where(diagonal, damping, 0.0)
    two_eye = jnp.where(diagonal, 2.0, 0.0)
    sums = jnp.sum(jnp.abs(matrix), axis=0, keepdims=True)
    alpha = (1.0 / jnp.max(sums, axis=1, keepdims=True)).astype(BF16).astype(F32)
    low = matrix.astype(BF16)
    residue = (two_eye - low.astype(F32) * alpha).astype(BF16)
    iterate = (residue.astype(F32) * alpha).astype(BF16)
    image = nn_dot(low, iterate)
    residue = (two_eye - image).astype(BF16)
    return nn_dot(iterate, residue).astype(BF16)


def factor_kernel(pos, mine, other, out, pack, full, diag):
    x, core = pos[0], pos[2]
    base = x // 2 * BLK
    own = pl.multiple_of(x * 384 - base, SUB)
    pair = pl.multiple_of((x + 1 - 2 * (x % 2)) * 384 - base, SUB)
    mid = pl.multiple_of(jnp.where(x == 1, 768, 0), SUB)
    columns = pl.ds(own, 384)
    for layer in range(2):
        for q in range(4):
            z = 4 * layer + q
            at = pl.multiple_of(q * 32 + core * 16, 16)
            pack[layer, pl.ds(at, 16), :] = mine[z * 16:(z + 1) * 16, :]
            at = pl.multiple_of(q * 32 + (1 - core) * 16, 16)
            pack[layer, pl.ds(at, 16), :] = other[z * 16:(z + 1) * 16, :]
        for b in range(2):
            at = b * BLK
            unpack(
                lambda i: pack[layer, :, b * 1280 + i * SUB:b * 1280 + (i + 1) * SUB].astype(F32),
                full.at[layer, b],
            )
            diag[layer, at:at + BLK, at:at + BLK] = invert(full.at[layer, b])
            diag[layer, at:at + BLK, BLK - at:2 * BLK - at] = jnp.zeros((BLK, BLK), BF16)
        out[layer, 0:384, :] = diag[layer, pl.ds(own, 384), columns]
        out[layer, 384:768, :] = diag[layer, pl.ds(pair, 384), columns]
        out[layer, 768:1024, :] = diag[layer, pl.ds(mid, 256), columns]


def right_product(w_own, w_pair, w_mid, factor):
    total = nn_dot(w_own[0], factor[0, 0:384, :])
    total += nn_dot(w_pair[...], factor[0, 384:768, :])
    total += nn_dot(w_mid[...], factor[0, 768:1024, :])
    return total.astype(BF16)


def right_kernel(pos, w_own, w_pair, w_mid, factor, out):
    out[...] = right_product(w_own, w_pair, w_mid, factor)


def left_product(pos, layer, parts, right, out, pack, full):
    x, y = pos[0], pos[1]
    for d, part in enumerate(parts):
        for e in range(4):
            at = (y + 4 - d) % 4 * 64 + (x + 4 - e) % 4 * 16
            rows = 32 * e + 16 * layer
            pack[pl.ds(pl.multiple_of(at, 16), 16), :] = part[rows:rows + 16, :]
    for b in range(3):
        def piece(i):
            s = 10 * b + i
            return pack[s // 15 * SUB:(s // 15 + 1) * SUB, s % 15 * SUB:(s % 15 + 1) * SUB].astype(F32)

        unpack(piece, full.at[b])
        at = b * BLK
        out[0, at:at + BLK, :] = nn_dot(invert(full.at[b]), right[at:at + BLK, :]).astype(BF16)


def left_kernel(pos, p0, p1, p2, p3, right, out, pack, full):
    left_product(pos, 0, (p0, p1, p2, p3), right, out, pack, full)


def last_kernel(pos, p0, p1, p2, p3, w_own, w_pair, w_mid, factor, before, out, pack, full, right):
    right[...] = right_product(w_own, w_pair, w_mid, factor)
    left_product(pos, 1, (p0, p1, p2, p3), right, out, pack, full)


def call(kernel, pos, operands, in_specs, out_shape, scratch, out_specs=None, aliases={}):
    return pl.pallas_call(
        kernel,
        grid_spec=pltpu.PrefetchScalarGridSpec(
            num_scalar_prefetch=1,
            grid=(1,),
            in_specs=in_specs,
            out_specs=out_specs or [whole(s) for s in out_shape],
            scratch_shapes=scratch,
        ),
        out_shape=out_shape,
        input_output_aliases=aliases,
        compiler_params=pltpu.CompilerParams(vmem_limit_bytes=24 * 1024 * 1024),
        cost_estimate=pl.CostEstimate(flops=0, bytes_accessed=0, transcendentals=0),
    )(pos, *operands)


ANYWHERE = pl.BlockSpec(memory_space=pl.ANY)
ONCE = pl.Buffered(1)


def whole(a):
    return pl.BlockSpec(a.shape, lambda i, p, n=len(a.shape): (0,) * n, pipeline_mode=ONCE)


def of_layer(a, layer):
    return pl.BlockSpec((1,) + a.shape[1:], lambda i, p: (layer, 0, 0), pipeline_mode=ONCE)


def shape(*dims):
    return jax.ShapeDtypeStruct(dims, BF16)


def add(parts):
    return sum(p.astype(F32) for p in parts)


def spread(parts, axis):
    return [parts[0]] + [lax.ppermute(parts[d], axis, [(i, (i + d) % 4) for i in range(4)]) for d in (1, 2, 3)]


def chunk(a, index, rows):
    return lax.dynamic_slice_in_dim(a, index % 4 * rows, rows, 0)


def exchange(w, middle):
    pair = lax.ppermute(w, "x", [(0, 1), (1, 0), (2, 3), (3, 2)])
    return [pair, lax.ppermute(middle, "x", [(1, 2), (2, 1)])]


def body(acts, grads_out, weight_grad):
    y, x, z, c = (lax.axis_index(n) for n in ("y", "x", "z", "c"))
    pos = jnp.stack([x, y, c, z % 4 * 2 + c, z // 4]).astype(jnp.int32)
    rows, width = weight_grad.shape[1:]
    barrier = lax.optimization_barrier

    whole0, mid0, whole1, mid1 = call(
        columns_kernel, pos, (weight_grad,), [ANYWHERE], [shape(rows, width), shape(rows, 256)] * 2,
        [pltpu.SemaphoreType.DMA((4,))], out_specs=[ANYWHERE] * 4,
    )
    w_first = exchange(whole0, mid0)

    side = call(
        side_kernel, pos, (acts,),
        [pl.BlockSpec((1,) + acts.shape[1:], lambda i, p: (p[4], 0, 0), pipeline_mode=ONCE)],
        [shape(128, LANES)], [],
    )[0]
    side, grads_out = barrier((side, grads_out))
    side = lax.all_to_all(side, "y", 0, 0, tiled=True)
    side = add([side[32 * d:32 * (d + 1)] for d in range(4)]).astype(BF16)
    side = lax.all_to_all(jnp.tile(side, (4, 1)), "x", 0, 0, tiled=True)
    side = add([side[32 * d:32 * (d + 1)] for d in range(4)]) * (1.0 / TOKENS)
    side = jnp.concatenate([side[:16], side[16:]], axis=1)
    side = lax.dynamic_slice_in_dim(side, x // 2 * 1280, 2560, 1).astype(BF16)
    mine = lax.all_to_all(jnp.tile(side, (8, 1)), "z", 0, 0, tiled=True)

    covs = call(
        cov_kernel, pos, (grads_out,), [whole(grads_out)],
        [shape(128, LANES)] * 4, [VMEM((2, 256, LANES), BF16)],
    )
    quarter = add(spread(covs, "y")).astype(BF16)
    quarter, mine, w_first = barrier((quarter, mine, w_first))
    quarter = [
        jnp.concatenate([chunk(quarter[:64], x + d, 16), chunk(quarter[64:], x + d, 16)], axis=0) for d in range(4)
    ]
    own = (add(spread(quarter, "x")) * (1.0 / TOKENS)).astype(BF16)
    quarter = jnp.concatenate(spread([own] * 4, "x"), axis=0)
    quarter, whole1, mid1 = barrier((quarter, whole1, mid1))
    w_second = exchange(whole1, mid1)
    parts = spread([quarter] * 4, "y")

    other = lax.ppermute(mine, "c", [(0, 1), (1, 0)])
    factor = call(
        factor_kernel, pos, (mine, other), [whole(mine), whole(other)], [shape(2, 1024, 384)],
        [VMEM((2, SUB, 2560), BF16), VMEM((2, 2, BLK, BLK), F32), VMEM((2, 1024, 1024), BF16)],
    )[0]

    def products(layer, w):
        specs = [of_layer(weight_grad, layer), whole(w[0]), whole(w[1]), of_layer(factor, layer)]
        return (weight_grad, *w, factor), specs

    out = shape(*weight_grad.shape)
    scratch = [VMEM((256, LANES), BF16), VMEM((3, BLK, BLK), F32)]
    operands, specs = products(0, w_first)
    right = call(right_kernel, pos, operands, specs, [shape(rows, width)], [])[0]
    operands = (*parts, right)
    before = call(
        left_kernel, pos, operands, [whole(a) for a in operands], [out], scratch, out_specs=[of_layer(out, 0)]
    )[0]
    operands, specs = products(1, w_second)
    return call(
        last_kernel, pos, (*parts, *operands, before), [whole(a) for a in parts] + specs + [ANYWHERE], [out],
        scratch + [VMEM((rows, width), BF16)], out_specs=[of_layer(out, 1)], aliases={9: 0},
    )[0]


def solution(mesh):
    fine = Mesh(mesh.devices.reshape(4, 4, 8, 2), ("y", "x", "z", "c"))
    dp, owner = ("y", "x"), ("z", "c")
    in_specs = (P(None, dp, None), P(None, dp, owner), P(None, owner, dp))
    out_specs = P(None, owner, dp)
    return jax.shard_map(body, mesh=fine, in_specs=in_specs, out_specs=out_specs, check_vma=False)
```

time: 166 us -> 137 us (0.83)
  starting transfers between devices: 74.4 us -> 34.5 us
  blocking collectives: 0 us -> 13.2 us
  Pallas kernels: 35.1 us -> 27.4 us
  waiting for transfers between devices: 40 us -> 47.7 us
  local copies, waits for them, and re-layouts: 13.3 us -> 8.19 us
    all_to_all x1 -> x0, starting transfers between devices: 17.2 us -> none  [body(): side = lax.all_to_all(side, 'y', 0, 0, tiled=True)]
    ppermute x16, waiting for transfers between devices: 29 us -> 45.1 us  [the longest x12 45.1 us: spread(): lax.ppermute(parts[d], axis, [(i, (i + d) % 4) for i in range(4)])]
    all_to_all x0 -> x1, blocking collectives: none -> 13.2 us  [body(): side = lax.all_to_all(side, 'y', 0, 0, tiled=True)]
    ppermute x16, starting transfers between devices: 27.2 us -> 14.9 us  [the longest x12 11.2 us: spread(): lax.ppermute(parts[d], axis, [(i, (i + d) % 4) for i in range(4)])]
    all_to_all x1, waiting for transfers between devices: 10.9 us -> 0.01 us  [body(): mine = lax.all_to_all(jnp.tile(side, (8, 1)), 'z', 0, 0, tiled=True)]
    ppermute x1, starting transfers between devices: 17.7 us -> 7.31 us  [body(): other = lax.ppermute(mine, 'c', [(0, 1), (1, 0)])]
    pallas_call x10 -> x7, Pallas kernels: 35.1 us -> 27.4 us  [call(): pl.pallas_call(kernel, grid_spec=pltpu.PrefetchScalarGridSpec(num_scalar_...]
    unnamed x26 -> x14, local copies, waits for them, and re-layouts: 11.5 us -> 5.22 us
  transfers between devices with their start and end apart: 20 -> 19, of which waited for: 5 -> 12; matrix products, arithmetic and copies ran while one was open for 2% -> 3% of each run, Pallas kernels for 14% -> 13%
where the time goes in v5:
time: 137 us; the launch traced here: 135 us
  waiting for transfers between devices  47.7 us (35%)
  starting transfers between devices  34.5 us (25%)
  Pallas kernels  27.4 us (20%)
  blocking collectives  13.2 us (10%)
  local copies, waits for them, and re-layouts  8.19 us (6%)
  other arithmetic  3.84 us (3%)
    ppermute x12, waiting for transfers between devices, spread(): lax.ppermute(parts[d], axis, [(i, (i + d) % 4) for i in range(4)])  45.1 us
    pallas_call x7, Pallas kernels, call(): pl.pallas_call(kernel, grid_spec=pltpu.PrefetchScalarGridSpec(num_scalar_...  27.4 us
    all_to_all x1, blocking collectives, body(): side = lax.all_to_all(side, 'y', 0, 0, tiled=True)  13.2 us
    ppermute x12, starting transfers between devices, spread(): lax.ppermute(parts[d], axis, [(i, (i + d) % 4) for i in range(4)])  11.2 us
    all_to_all x1, starting transfers between devices, body(): mine = lax.all_to_all(jnp.tile(side, (8, 1)), 'z', 0, 0, tiled=True)  8.18 us
    ppermute x1, starting transfers between devices, body(): other = lax.ppermute(mine, 'c', [(0, 1), (1, 0)])  7.31 us
    unnamed x14, local copies, waits for them, and re-layouts  5.22 us
    all_to_all x1, starting transfers between devices, body(): side = lax.all_to_all(jnp.tile(side, (4, 1)), 'x', 0, 0, tiled=True)  4.13 us
  transfers between devices with their start and end apart: 19, of which 12 were waited for; matrix products, arithmetic and copies ran while one was open for 3% of the time, Pallas kernels for 13%

profile of v5, /device:TPU:1, one launch (start us, length us, event | category | flops | bytes accessed | tf_op | source)
XLA Modules:
  0.0 135.0 jit_solution(832681448490769527)
XLA Ops:
  0.0 0.1 stack.23.pos
  0.1 2.8 %copy-done.1 = bf16[2,256,6144]{2,1,0:T(8,128)(2,1)S(1)} copy-done((bf16[2,256,6144]{2,1,0:T(8,128)(2,1)S(1)}, bf16[2,256,6144]{2,1,0:T(8,128)(2,1)}, u32[]{:S(2)}) %copy-start.1) | copy-done | bytes 6291480
  2.9 3.8 %shard_map.37 = bf16[128,1920]{1,0:T(8,128)(2,1)S(1)} custom-call(s32[5]{0:T(128)S(1)} %stack.23.pos, bf16[2,256,6144]{2,1,0:T(8,128)(2,1)S(1)} %copy-done.1), custom_call_target="tpu_custom_call" | custom-call | tf_op jit(solution)/shard_map/pallas_call | solution.py:166
  6.7 0.0 copy-start
  6.7 13.2 %all_to_all.24 = bf16[4,32,1920]{2,1,0:T(8,128)(2,1)S(1)} all-to-all(bf16[4,32,1920]{2,1,0:T(8,128)(2,1)S(1)} %bitcast.15), channel_id=1, replica_groups=mesh['y'=4,'x'=4,'z'=8,'c'=2] {'y'}, dimensions={0} | all-to-all | bytes 983040 | tf_op jit(solution)/shard_map/all_to_all | solution.py:233
  19.8 0.1 fusion.2
  19.9 0.8 tile.4
  20.7 4.1 %all-to-all-start.1 = ((bf16[4,32,1920]{2,1,0:T(8,128)(2,1)}), bf16[4,32,1920]{2,1,0:T(8,128)(2,1)}, u32[]{:S(2)}, u32[]{:S(2)}) async-start(bf16[4,32,1920]{2,1,0:T(8,128)(2,1)} %tile.4), calls=%async_computation.1 | async-start | bytes 983040 | tf_op jit(solution)/shard_map/all_to_all | solution.py:235
  24.9 0.0 copy-done
  24.9 1.9 %shard_map.39 = (bf16[1536,384]{1,0:T(8,128)(2,1)}, bf16[1536,256]{1,0:T(8,128)(2,1)}, bf16[1536,384]{1,0:T(8,128)(2,1)S(1)}, bf16[1536,256]{1,0:T(8,128)(2,1)S(1)}) custom-call(s32[5]{0:T(128)S(1)} %stack.23.pos, bf16[2,1536,384]{2,1,0:T(8,128)(2,1)S(1)} %copy-done), custom_call_target="tpu_custom_call" | custom-call | tf_op jit(solution)/shard_map/pallas_call | solution.py:166
  26.7 0.0 copy-start.3
  26.8 1.0 copy-done.3
  27.8 1.4 %collective-permute-start.3 = (bf16[1536,384]{1,0:T(8,128)(2,1)}, bf16[1536,384]{1,0:T(8,128)(2,1)}, u32[]{:S(2)}, u32[]{:S(2)}) collective-permute-start(bf16[1536,384]{1,0:T(8,128)(2,1)} %get-tuple-element.28), channel_id=1, source_target_pairs={{0,16},{16,0},{32,48},{48,32},{1,17},{17,1},{33,49},{49,33},{2,18}... | collective-permute-start | bytes 3538952 | tf_op jit(solution)/shard_map/ppermute | solution.py:211
  29.2 2.6 %all-to-all-done.1 = bf16[4,32,1920]{2,1,0:T(8,128)(2,1)} async-done(((bf16[4,32,1920]{2,1,0:T(8,128)(2,1)}), bf16[4,32,1920]{2,1,0:T(8,128)(2,1)}, u32[]{:S(2)}, u32[]{:S(2)}) %all-to-all-start.1) | async-done | bytes 491552 | tf_op jit(solution)/shard_map/all_to_all | solution.py:235
  31.7 1.2 add_multiply_fusion
  32.9 0.1 fusion.1
  33.0 0.9 tile.5
  33.9 0.0 copy-done.5
  33.9 8.2 %all-to-all-start.2 = ((bf16[8,16,2560]{2,1,0:T(8,128)(2,1)}), bf16[8,16,2560]{2,1,0:T(8,128)(2,1)S(1)}, u32[]{:S(2)}, u32[]{:S(2)}) async-start(bf16[8,16,2560]{2,1,0:T(8,128)(2,1)} %tile.5), calls=%async_computation.2 | async-start | bytes 1310720 | tf_op jit(solution)/shard_map/all_to_all | solution.py:239
  42.1 1.4 %copy-done.2 = bf16[2,256,1536]{2,1,0:T(8,128)(2,1)S(1)} copy-done((bf16[2,256,1536]{2,1,0:T(8,128)(2,1)S(1)}, bf16[2,256,1536]{2,1,0:T(8,128)(2,1)}, u32[]{:S(2)}) %copy-start.2) | copy-done | bytes 1572888
  43.5 2.6 %shard_map.38 = (bf16[128,1920]{1,0:T(8,128)(2,1)S(1)}, bf16[128,1920]{1,0:T(8,128)(2,1)}, bf16[128,1920]{1,0:T(8,128)(2,1)}, bf16[128,1920]{1,0:T(8,128)(2,1)}) custom-call(s32[5]{0:T(128)S(1)} %stack.23.pos, bf16[2,256,1536]{2,1,0:T(8,128)(2,1)S(1)} %copy-done.2), custom_call_target="tpu_custom_call" | custom-call | tf_op jit(solution)/shard_map/pallas_call | solution.py:166
  46.1 0.3 collective-permute-start
  46.4 1.8 %collective-permute-start.1 = (bf16[128,1920]{1,0:T(8,128)(2,1)}, bf16[128,1920]{1,0:T(8,128)(2,1)}, u32[]{:S(2)}, u32[]{:S(2)}) collective-permute-start(bf16[128,1920]{1,0:T(8,128)(2,1)} %get-tuple-element.25), channel_id=1, source_target_pairs={{0,128},{64,192},{128,0},{192,64},{1,129},{65,193},{129,1},{193,65... | collective-permute-start | bytes 1474568 | tf_op jit(solution)/shard_map/ppermute | solution.py:203
  48.2 0.6 collective-permute-start.2
  48.8 1.5 %collective-permute-start.4 = (bf16[1536,256]{1,0:T(8,128)(2,1)}, bf16[1536,256]{1,0:T(8,128)(2,1)}, u32[]{:S(2)}, u32[]{:S(2)}) collective-permute-start(bf16[1536,256]{1,0:T(8,128)(2,1)} %get-tuple-element.29), channel_id=1, source_target_pairs={{16,32},{32,16},{17,33},{33,17},{18,34},{34,18},{19,35},{35,19},{2... | collective-permute-start | bytes 2359304 | tf_op jit(solution)/shard_map/ppermute | solution.py:212
  50.4 6.7 %collective-permute-done = bf16[128,1920]{1,0:T(8,128)(2,1)} collective-permute-done((bf16[128,1920]{1,0:T(8,128)(2,1)}, bf16[128,1920]{1,0:T(8,128)(2,1)}, u32[]{:S(2)}, u32[]{:S(2)}) %collective-permute-start) | collective-permute-done | bytes 491552 | tf_op jit(solution)/shard_map/ppermute | solution.py:203
  57.1 7.9 %collective-permute-done.1 = bf16[128,1920]{1,0:T(8,128)(2,1)} collective-permute-done((bf16[128,1920]{1,0:T(8,128)(2,1)}, bf16[128,1920]{1,0:T(8,128)(2,1)}, u32[]{:S(2)}, u32[]{:S(2)}) %collective-permute-start.1) | collective-permute-done | bytes 491552 | tf_op jit(solution)/shard_map/ppermute | solution.py:203
  65.0 4.8 %collective-permute-done.2 = bf16[128,1920]{1,0:T(8,128)(2,1)} collective-permute-done((bf16[128,1920]{1,0:T(8,128)(2,1)}, bf16[128,1920]{1,0:T(8,128)(2,1)}, u32[]{:S(2)}, u32[]{:S(2)}) %collective-permute-start.2) | collective-permute-done | bytes 491552 | tf_op jit(solution)/shard_map/ppermute | solution.py:203
  69.8 2.3 %add_convert_fusion = bf16[128,1920]{1,0:T(8,128)(2,1)} fusion(bf16[128,1920]{1,0:T(8,128)(2,1)} %collective-permute-done.2, bf16[128,1920]{1,0:T(8,128)(2,1)} %collective-permute-done.1, bf16[128,1920]{1,0:T(8,128)(2,1)} %collective-permute-done, bf16[128,1920]{1,0:T(8,128)(2,1)S(1)} %get-tuple-element.23), kind=kLoop, calls=%fused_computation | loop fusion | flops 1966080 | bytes 2457600 | tf_op jit(solution)/shard_map/convert_element_type | solution.py:245
  72.1 0.0 collective-permute-done.4.w_mid
  72.1 0.0 collective-permute-done.3.w_pair
  72.1 0.0 all-to-all-done.2
  72.1 1.1 fusion.3
  73.3 0.1 constant_dynamic-slice_fusion.6
  73.3 0.1 collective-permute-start.5
  73.4 1.5 %collective-permute-start.6 = (bf16[32,1920]{1,0:T(8,128)(2,1)S(1)}, bf16[32,1920]{1,0:T(8,128)(2,1)S(1)}, u32[]{:S(2)}, u32[]{:S(2)}) collective-permute-start(bf16[32,1920]{1,0:T(8,128)(2,1)S(1)} %pad_maximum_fusion.2), channel_id=1, source_target_pairs={{0,32},{16,48},{32,0},{48,16},{1,33},{17,49},{33,1},{49,17},{2,34}... | collective-permute-start | bytes 368648 | tf_op jit(solution)/shard_map/ppermute | solution.py:203
  74.9 1.6 %collective-permute-start.7 = (bf16[32,1920]{1,0:T(8,128)(2,1)S(1)}, bf16[32,1920]{1,0:T(8,128)(2,1)S(1)}, u32[]{:S(2)}, u32[]{:S(2)}) collective-permute-start(bf16[32,1920]{1,0:T(8,128)(2,1)S(1)} %pad_maximum_fusion.3), channel_id=1, source_target_pairs={{0,48},{16,0},{32,16},{48,32},{1,49},{17,1},{33,17},{49,33},{2,50}... | collective-permute-start | bytes 368648 | tf_op jit(solution)/shard_map/ppermute | solution.py:203
  76.5 3.2 %collective-permute-done.5 = bf16[32,1920]{1,0:T(8,128)(2,1)S(1)} collective-permute-done((bf16[32,1920]{1,0:T(8,128)(2,1)S(1)}, bf16[32,1920]{1,0:T(8,128)(2,1)S(1)}, u32[]{:S(2)}, u32[]{:S(2)}) %collective-permute-start.5) | collective-permute-done | bytes 122912 | tf_op jit(solution)/shard_map/ppermute | solution.py:203
  79.7 0.0 collective-permute-done.6
  79.7 1.0 collective-permute-done.7
  80.6 0.1 multiply_convert_fusion
  80.7 2.2 %collective-permute-start.10 = (bf16[32,1920]{1,0:T(8,128)(2,1)S(1)}, bf16[32,1920]{1,0:T(8,128)(2,1)S(1)}, u32[]{:S(2)}, u32[]{:S(2)}) collective-permute-start(bf16[32,1920]{1,0:T(8,128)(2,1)S(1)} %multiply_convert_fusion), channel_id=1, source_target_pairs={{0,48},{16,0},{32,16},{48,32},{1,49},{17,1},{33,17},{49,33},{2,50}... | collective-permute-start | bytes 368648 | tf_op jit(solution)/shard_map/ppermute | solution.py:203
  82.9 0.0 collective-permute-start.9
  82.9 0.7 collective-permute-start.8
  83.6 2.5 %collective-permute-done.10 = bf16[32,1920]{1,0:T(8,128)(2,1)S(1)} collective-permute-done((bf16[32,1920]{1,0:T(8,128)(2,1)S(1)}, bf16[32,1920]{1,0:T(8,128)(2,1)S(1)}, u32[]{:S(2)}, u32[]{:S(2)}) %collective-permute-start.10) | collective-permute-done | bytes 122912 | tf_op jit(solution)/shard_map/ppermute | solution.py:203
  86.0 2.2 %collective-permute-done.9 = bf16[32,1920]{1,0:T(8,128)(2,1)S(1)} collective-permute-done((bf16[32,1920]{1,0:T(8,128)(2,1)S(1)}, bf16[32,1920]{1,0:T(8,128)(2,1)S(1)}, u32[]{:S(2)}, u32[]{:S(2)}) %collective-permute-start.9) | collective-permute-done | bytes 122912 | tf_op jit(solution)/shard_map/ppermute | solution.py:203
  88.2 0.9 collective-permute-done.8
  89.2 0.0 copy-done.4
  89.2 0.1 collective-permute-start.14
  89.3 7.3 %collective-permute-start.16 = (bf16[128,2560]{1,0:T(8,128)(2,1)S(1)}, bf16[128,2560]{1,0:T(8,128)(2,1)S(1)}, u32[]{:S(2)}, u32[]{:S(2)}) collective-permute-start(bf16[128,2560]{1,0:T(8,128)(2,1)S(1)} %bitcast.13), channel_id=1, source_target_pairs={{0,1},{1,0},{2,3},{3,2},{4,5},{5,4},{6,7},{7,6},{8,9},{9,8},{10,11... | collective-permute-start | bytes 1966088 | tf_op jit(solution)/shard_map/ppermute | solution.py:256
  96.6 0.7 collective-permute-start.15
  97.3 1.8 %collective-permute-start.13 = (bf16[128,1920]{1,0:T(8,128)(2,1)S(1)}, bf16[128,1920]{1,0:T(8,128)(2,1)S(1)}, u32[]{:S(2)}, u32[]{:S(2)}) collective-permute-start(bf16[128,1920]{1,0:T(8,128)(2,1)S(1)} %pad_maximum_fusion.p0), channel_id=1, source_target_pairs={{0,192},{64,0},{128,64},{192,128},{1,193},{65,1},{129,65},{193,129... | collective-permute-start | bytes 1474568 | tf_op jit(solution)/shard_map/ppermute | solution.py:203
  99.2 0.0 collective-permute-start.12
  99.2 0.0 collective-permute-done.16.other
  99.2 0.7 collective-permute-start.11
  99.9 3.9 %shard_map.40.factor = bf16[2,1024,384]{2,1,0:T(8,128)(2,1)S(1)} custom-call(s32[5]{0:T(128)S(1)} %stack.23.pos, bf16[128,2560]{1,0:T(8,128)(2,1)S(1)} %bitcast.14, bf16[128,2560]{1,0:T(8,128)(2,1)S(1)} %collective-permute-done.16.other), custom_call_target="tpu_custom_call" | custom-call | tf_op jit(solution)/shard_map/pallas_call | solution.py:166
  103.8 4.0 %shard_map.41.right = bf16[1536,384]{1,0:T(8,128)(2,1)S(1)} custom-call(s32[5]{0:T(128)S(1)} %stack.23.pos, bf16[2,1536,384]{2,1,0:T(8,128)(2,1)S(1)} %copy-done, bf16[1536,384]{1,0:T(8,128)(2,1)} %collective-permute-done.3.w_pair, bf16[1536,256]{1,0:T(8,128)(2,1)} %collective-permute-done.4.w_mid, bf16[2,1024,384]{2,1,0:T(8,128)(2,1)S(1)} %shard_map.40.factor), custom_call_target="tpu_custom_call" | custom-call | tf_op jit(solution)/shard_map/pallas_call | solution.py:166
  107.8 2.4 %collective-permute-done.13.p3 = bf16[128,1920]{1,0:T(8,128)(2,1)S(1)} collective-permute-done((bf16[128,1920]{1,0:T(8,128)(2,1)S(1)}, bf16[128,1920]{1,0:T(8,128)(2,1)S(1)}, u32[]{:S(2)}, u32[]{:S(2)}) %collective-permute-start.13) | collective-permute-done | bytes 491552 | tf_op jit(solution)/shard_map/ppermute | solution.py:203
  110.3 2.8 %collective-permute-done.12.p2 = bf16[128,1920]{1,0:T(8,128)(2,1)S(1)} collective-permute-done((bf16[128,1920]{1,0:T(8,128)(2,1)S(1)}, bf16[128,1920]{1,0:T(8,128)(2,1)S(1)}, u32[]{:S(2)}, u32[]{:S(2)}) %collective-permute-start.12) | collective-permute-done | bytes 491552 | tf_op jit(solution)/shard_map/ppermute | solution.py:203
  113.0 10.8 %collective-permute-done.11.p1 = bf16[128,1920]{1,0:T(8,128)(2,1)S(1)} collective-permute-done((bf16[128,1920]{1,0:T(8,128)(2,1)S(1)}, bf16[128,1920]{1,0:T(8,128)(2,1)S(1)}, u32[]{:S(2)}, u32[]{:S(2)}) %collective-permute-start.11) | collective-permute-done | bytes 491552 | tf_op jit(solution)/shard_map/ppermute | solution.py:203
  123.8 4.9 %shard_map.42.before = bf16[2,1536,384]{2,1,0:T(8,128)(2,1)} custom-call(s32[5]{0:T(128)S(1)} %stack.23.pos, bf16[128,1920]{1,0:T(8,128)(2,1)S(1)} %pad_maximum_fusion.p0, bf16[128,1920]{1,0:T(8,128)(2,1)S(1)} %collective-permute-done.11.p1, bf16[128,1920]{1,0:T(8,128)(2,1)S(1)} %collective-permute-done.12.p2, ...), custom_call_target="tpu_custom_call" | custom-call | tf_op jit(solution)/shard_map/pallas_call | solution.py:166
  128.7 0.0 collective-permute-done.15.w_mid
  128.7 0.0 collective-permute-done.14.w_pair
  128.7 6.3 %shard_map.43 = bf16[2,1536,384]{2,1,0:T(8,128)(2,1)} custom-call(s32[5]{0:T(128)S(1)} %stack.23.pos, bf16[128,1920]{1,0:T(8,128)(2,1)S(1)} %pad_maximum_fusion.p0, bf16[128,1920]{1,0:T(8,128)(2,1)S(1)} %collective-permute-done.11.p1, bf16[128,1920]{1,0:T(8,128)(2,1)S(1)} %collective-permute-done.12.p2, ...), custom_call_target="tpu_custom_call", output_to_operand_aliasing={{}: (9, {})} | custom-call | tf_op jit(solution)/shard_map/pallas_call | solution.py:166
  (11 shorter events, 0.1 us)
Async XLA Ops:
  0.1 2.8 %copy-start.1 = (bf16[2,256,6144]{2,1,0:T(8,128)(2,1)S(1)}, bf16[2,256,6144]{2,1,0:T(8,128)(2,1)}, u32[]{:S(2)}) copy-start(bf16[2,256,6144]{2,1,0:T(8,128)(2,1)} %acts.1) | copy-start | bytes 18874372
  6.7 18.2 %copy-start = (bf16[2,1536,384]{2,1,0:T(8,128)(2,1)S(1)}, bf16[2,1536,384]{2,1,0:T(8,128)(2,1)}, u32[]{:S(2)}) copy-start(bf16[2,1536,384]{2,1,0:T(8,128)(2,1)} %w_own.3) | copy-start | bytes 7077892
  20.7 11.0 %all-to-all-start.1 = ((bf16[4,32,1920]{2,1,0:T(8,128)(2,1)}), bf16[4,32,1920]{2,1,0:T(8,128)(2,1)}, u32[]{:S(2)}, u32[]{:S(2)}) async-start(bf16[4,32,1920]{2,1,0:T(8,128)(2,1)} %tile.4), calls=%async_computation.1 | async-start | bytes 983040 | tf_op jit(solution)/shard_map/all_to_all | solution.py:235
  26.7 1.0 copy-start.3
  27.8 6.2 %copy-start.5 = (bf16[1536,256]{1,0:T(8,128)(2,1)}, bf16[1536,256]{1,0:T(8,128)(2,1)S(1)}, u32[]{:S(2)}) copy-start(bf16[1536,256]{1,0:T(8,128)(2,1)S(1)} %get-tuple-element.35) | copy-start | bytes 2359300
  27.8 44.4 %collective-permute-start.3 = (bf16[1536,384]{1,0:T(8,128)(2,1)}, bf16[1536,384]{1,0:T(8,128)(2,1)}, u32[]{:S(2)}, u32[]{:S(2)}) collective-permute-start(bf16[1536,384]{1,0:T(8,128)(2,1)} %get-tuple-element.28), channel_id=1, source_target_pairs={{0,16},{16,0},{32,48},{48,32},{1,17},{17,1},{33,49},{49,33},{2,18}... | collective-permute-start | bytes 3538952 | tf_op jit(solution)/shard_map/ppermute | solution.py:211
  33.9 38.2 %all-to-all-start.2 = ((bf16[8,16,2560]{2,1,0:T(8,128)(2,1)}), bf16[8,16,2560]{2,1,0:T(8,128)(2,1)S(1)}, u32[]{:S(2)}, u32[]{:S(2)}) async-start(bf16[8,16,2560]{2,1,0:T(8,128)(2,1)} %tile.5), calls=%async_computation.2 | async-start | bytes 1310720 | tf_op jit(solution)/shard_map/all_to_all | solution.py:239
  42.1 1.4 %copy-start.2 = (bf16[2,256,1536]{2,1,0:T(8,128)(2,1)S(1)}, bf16[2,256,1536]{2,1,0:T(8,128)(2,1)}, u32[]{:S(2)}) copy-start(bf16[2,256,1536]{2,1,0:T(8,128)(2,1)} %grads) | copy-start | bytes 4718596
  46.1 10.9 %collective-permute-start = (bf16[128,1920]{1,0:T(8,128)(2,1)}, bf16[128,1920]{1,0:T(8,128)(2,1)}, u32[]{:S(2)}, u32[]{:S(2)}) collective-permute-start(bf16[128,1920]{1,0:T(8,128)(2,1)} %get-tuple-element.24), channel_id=1, source_target_pairs={{0,64},{64,128},{128,192},{192,0},{1,65},{65,129},{129,193},{193,1... | collective-permute-start | bytes 1474568 | tf_op jit(solution)/shard_map/ppermute | solution.py:203
  46.4 18.6 %collective-permute-start.1 = (bf16[128,1920]{1,0:T(8,128)(2,1)}, bf16[128,1920]{1,0:T(8,128)(2,1)}, u32[]{:S(2)}, u32[]{:S(2)}) collective-permute-start(bf16[128,1920]{1,0:T(8,128)(2,1)} %get-tuple-element.25), channel_id=1, source_target_pairs={{0,128},{64,192},{128,0},{192,64},{1,129},{65,193},{129,1},{193,65... | collective-permute-start | bytes 1474568 | tf_op jit(solution)/shard_map/ppermute | solution.py:203
  48.2 21.6 %collective-permute-start.2 = (bf16[128,1920]{1,0:T(8,128)(2,1)}, bf16[128,1920]{1,0:T(8,128)(2,1)}, u32[]{:S(2)}, u32[]{:S(2)}) collective-permute-start(bf16[128,1920]{1,0:T(8,128)(2,1)} %get-tuple-element.26), channel_id=1, source_target_pairs={{0,192},{64,0},{128,64},{192,128},{1,193},{65,1},{129,65},{193,129... | collective-permute-start | bytes 1474568 | tf_op jit(solution)/shard_map/ppermute | solution.py:203
  48.8 23.3 %collective-permute-start.4 = (bf16[1536,256]{1,0:T(8,128)(2,1)}, bf16[1536,256]{1,0:T(8,128)(2,1)}, u32[]{:S(2)}, u32[]{:S(2)}) collective-permute-start(bf16[1536,256]{1,0:T(8,128)(2,1)} %get-tuple-element.29), channel_id=1, source_target_pairs={{16,32},{32,16},{17,33},{33,17},{18,34},{34,18},{19,35},{35,19},{2... | collective-permute-start | bytes 2359304 | tf_op jit(solution)/shard_map/ppermute | solution.py:212
  73.2 16.0 %copy-start.4 = (bf16[1536,384]{1,0:T(8,128)(2,1)S(1)}, bf16[1536,384]{1,0:T(8,128)(2,1)}, u32[]{:S(2)}) copy-start(bf16[1536,384]{1,0:T(8,128)(2,1)} %copy-done.3) | copy-start | bytes 3538948
  73.2 23.4 %copy-start.6 = (bf16[1536,256]{1,0:T(8,128)(2,1)S(1)}, bf16[1536,256]{1,0:T(8,128)(2,1)}, u32[]{:S(2)}) copy-start(bf16[1536,256]{1,0:T(8,128)(2,1)} %copy-done.5) | copy-start | bytes 2359300
  73.3 6.3 %collective-permute-start.5 = (bf16[32,1920]{1,0:T(8,128)(2,1)S(1)}, bf16[32,1920]{1,0:T(8,128)(2,1)S(1)}, u32[]{:S(2)}, u32[]{:S(2)}) collective-permute-start(bf16[32,1920]{1,0:T(8,128)(2,1)S(1)} %pad_maximum_fusion.1), channel_id=1, source_target_pairs={{0,16},{16,32},{32,48},{48,0},{1,17},{17,33},{33,49},{49,1},{2,18}... | collective-permute-start | bytes 368648 | tf_op jit(solution)/shard_map/ppermute | solution.py:203
  73.4 6.2 %collective-permute-start.6 = (bf16[32,1920]{1,0:T(8,128)(2,1)S(1)}, bf16[32,1920]{1,0:T(8,128)(2,1)S(1)}, u32[]{:S(2)}, u32[]{:S(2)}) collective-permute-start(bf16[32,1920]{1,0:T(8,128)(2,1)S(1)} %pad_maximum_fusion.2), channel_id=1, source_target_pairs={{0,32},{16,48},{32,0},{48,16},{1,33},{17,49},{33,1},{49,17},{2,34}... | collective-permute-start | bytes 368648 | tf_op jit(solution)/shard_map/ppermute | solution.py:203
  74.9 5.7 %collective-permute-start.7 = (bf16[32,1920]{1,0:T(8,128)(2,1)S(1)}, bf16[32,1920]{1,0:T(8,128)(2,1)S(1)}, u32[]{:S(2)}, u32[]{:S(2)}) collective-permute-start(bf16[32,1920]{1,0:T(8,128)(2,1)S(1)} %pad_maximum_fusion.3), channel_id=1, source_target_pairs={{0,48},{16,0},{32,16},{48,32},{1,49},{17,1},{33,17},{49,33},{2,50}... | collective-permute-start | bytes 368648 | tf_op jit(solution)/shard_map/ppermute | solution.py:203
  80.7 5.3 %collective-permute-start.10 = (bf16[32,1920]{1,0:T(8,128)(2,1)S(1)}, bf16[32,1920]{1,0:T(8,128)(2,1)S(1)}, u32[]{:S(2)}, u32[]{:S(2)}) collective-permute-start(bf16[32,1920]{1,0:T(8,128)(2,1)S(1)} %multiply_convert_fusion), channel_id=1, source_target_pairs={{0,48},{16,0},{32,16},{48,32},{1,49},{17,1},{33,17},{49,33},{2,50}... | collective-permute-start | bytes 368648 | tf_op jit(solution)/shard_map/ppermute | solution.py:203
  82.9 5.3 %collective-permute-start.9 = (bf16[32,1920]{1,0:T(8,128)(2,1)S(1)}, bf16[32,1920]{1,0:T(8,128)(2,1)S(1)}, u32[]{:S(2)}, u32[]{:S(2)}) collective-permute-start(bf16[32,1920]{1,0:T(8,128)(2,1)S(1)} %multiply_convert_fusion), channel_id=1, source_target_pairs={{0,32},{16,48},{32,0},{48,16},{1,33},{17,49},{33,1},{49,17},{2,34}... | collective-permute-start | bytes 368648 | tf_op jit(solution)/shard_map/ppermute | solution.py:203
  82.9 6.3 %collective-permute-start.8 = (bf16[32,1920]{1,0:T(8,128)(2,1)S(1)}, bf16[32,1920]{1,0:T(8,128)(2,1)S(1)}, u32[]{:S(2)}, u32[]{:S(2)}) collective-permute-start(bf16[32,1920]{1,0:T(8,128)(2,1)S(1)} %multiply_convert_fusion), channel_id=1, source_target_pairs={{0,16},{16,32},{32,48},{48,0},{1,17},{17,33},{33,49},{49,1},{2,18}... | collective-permute-start | bytes 368648 | tf_op jit(solution)/shard_map/ppermute | solution.py:203
  89.2 39.4 %collective-permute-start.14 = (bf16[1536,384]{1,0:T(8,128)(2,1)S(1)}, bf16[1536,384]{1,0:T(8,128)(2,1)S(1)}, u32[]{:S(2)}, u32[]{:S(2)}) collective-permute-start(bf16[1536,384]{1,0:T(8,128)(2,1)S(1)} %copy-done.4), channel_id=1, source_target_pairs={{0,16},{16,0},{32,48},{48,32},{1,17},{17,1},{33,49},{49,33},{2,18}... | collective-permute-start | bytes 3538952 | tf_op jit(solution)/shard_map/ppermute | solution.py:211
  89.3 9.9 %collective-permute-start.16 = (bf16[128,2560]{1,0:T(8,128)(2,1)S(1)}, bf16[128,2560]{1,0:T(8,128)(2,1)S(1)}, u32[]{:S(2)}, u32[]{:S(2)}) collective-permute-start(bf16[128,2560]{1,0:T(8,128)(2,1)S(1)} %bitcast.13), channel_id=1, source_target_pairs={{0,1},{1,0},{2,3},{3,2},{4,5},{5,4},{6,7},{7,6},{8,9},{9,8},{10,11... | collective-permute-start | bytes 1966088 | tf_op jit(solution)/shard_map/ppermute | solution.py:256
  96.6 32.0 %collective-permute-start.15 = (bf16[1536,256]{1,0:T(8,128)(2,1)S(1)}, bf16[1536,256]{1,0:T(8,128)(2,1)S(1)}, u32[]{:S(2)}, u32[]{:S(2)}) collective-permute-start(bf16[1536,256]{1,0:T(8,128)(2,1)S(1)} %copy-done.6), channel_id=1, source_target_pairs={{16,32},{32,16},{17,33},{33,17},{18,34},{34,18},{19,35},{35,19},{2... | collective-permute-start | bytes 2359304 | tf_op jit(solution)/shard_map/ppermute | solution.py:212
  97.3 12.9 %collective-permute-start.13 = (bf16[128,1920]{1,0:T(8,128)(2,1)S(1)}, bf16[128,1920]{1,0:T(8,128)(2,1)S(1)}, u32[]{:S(2)}, u32[]{:S(2)}) collective-permute-start(bf16[128,1920]{1,0:T(8,128)(2,1)S(1)} %pad_maximum_fusion.p0), channel_id=1, source_target_pairs={{0,192},{64,0},{128,64},{192,128},{1,193},{65,1},{129,65},{193,129... | collective-permute-start | bytes 1474568 | tf_op jit(solution)/shard_map/ppermute | solution.py:203
  99.2 13.8 %collective-permute-start.12 = (bf16[128,1920]{1,0:T(8,128)(2,1)S(1)}, bf16[128,1920]{1,0:T(8,128)(2,1)S(1)}, u32[]{:S(2)}, u32[]{:S(2)}) collective-permute-start(bf16[128,1920]{1,0:T(8,128)(2,1)S(1)} %pad_maximum_fusion.p0), channel_id=1, source_target_pairs={{0,128},{64,192},{128,0},{192,64},{1,129},{65,193},{129,1},{193,65... | collective-permute-start | bytes 1474568 | tf_op jit(solution)/shard_map/ppermute | solution.py:203
  99.2 24.6 %collective-permute-start.11 = (bf16[128,1920]{1,0:T(8,128)(2,1)S(1)}, bf16[128,1920]{1,0:T(8,128)(2,1)S(1)}, u32[]{:S(2)}, u32[]{:S(2)}) collective-permute-start(bf16[128,1920]{1,0:T(8,128)(2,1)S(1)} %pad_maximum_fusion.p0), channel_id=1, source_target_pairs={{0,64},{64,128},{128,192},{192,0},{1,65},{65,129},{129,193},{193,1... | collective-permute-start | bytes 1474568 | tf_op jit(solution)/shard_map/ppermute | solution.py:203

commit v6 on v5

--- a/solution.py
+++ b/solution.py
@@ -25,13 +25,12 @@
     return lax.dot_general(a, b, (((1,), (0,)), ((), ())), preferred_element_type=F32)
 
 
-def columns_kernel(pos, w, whole0, mid0, whole1, mid1, sems):
+def columns_kernel(pos, w, whole0, whole1, mid, sems):
     columns = pl.ds(pl.multiple_of(jnp.where(pos[0] == 1, SUB, 0), SUB), 256)
     copies = [
         pltpu.make_async_copy(w.at[0], whole0, sems.at[0]),
-        pltpu.make_async_copy(w.at[0, :, columns], mid0, sems.at[1]),
-        pltpu.make_async_copy(w.at[1], whole1, sems.at[2]),
-        pltpu.make_async_copy(w.at[1, :, columns], mid1, sems.at[3]),
+        pltpu.make_async_copy(w.at[1], whole1, sems.at[1]),
+        pltpu.make_async_copy(w.at[:, :, columns], mid, sems.at[2]),
     ]
     for copy in copies:
         copy.start()
@@ -99,7 +98,7 @@
 
 
 def factor_kernel(pos, mine, other, out, pack, full, diag):
-    x, core = pos[0], pos[2]
+    x, core, zl = pos[0], pos[2], pos[5]
     base = x // 2 * BLK
     own = pl.multiple_of(x * 384 - base, SUB)
     pair = pl.multiple_of((x + 1 - 2 * (x % 2)) * 384 - base, SUB)
@@ -107,11 +106,12 @@
     columns = pl.ds(own, 384)
     for layer in range(2):
         for q in range(4):
-            z = 4 * layer + q
-            at = pl.multiple_of(q * 32 + core * 16, 16)
-            pack[layer, pl.ds(at, 16), :] = mine[z * 16:(z + 1) * 16, :]
-            at = pl.multiple_of(q * 32 + (1 - core) * 16, 16)
-            pack[layer, pl.ds(at, 16), :] = other[z * 16:(z + 1) * 16, :]
+            parity = zl if q % 2 == 0 else 1 - zl
+            rows = slice(64 * layer + 16 * q, 64 * layer + 16 * q + 16)
+            at = pl.multiple_of(q // 2 * 64 + parity * 32 + core * 16, 16)
+            pack[layer, pl.ds(at, 16), :] = mine[rows, :]
+            at = pl.multiple_of(q // 2 * 64 + parity * 32 + (1 - core) * 16, 16)
+            pack[layer, pl.ds(at, 16), :] = other[rows, :]
         for b in range(2):
             at = b * BLK
             unpack(
@@ -128,7 +128,7 @@
 def right_product(w_own, w_pair, w_mid, factor):
     total = nn_dot(w_own[0], factor[0, 0:384, :])
     total += nn_dot(w_pair[...], factor[0, 384:768, :])
-    total += nn_dot(w_mid[...], factor[0, 768:1024, :])
+    total += nn_dot(w_mid[0], factor[0, 768:1024, :])
     return total.astype(BF16)
 
 
@@ -136,13 +136,12 @@
     out[...] = right_product(w_own, w_pair, w_mid, factor)
 
 
-def left_product(pos, layer, parts, right, out, pack, full):
+def left_product(pos, parts, right, out, pack, full):
     x, y = pos[0], pos[1]
     for d, part in enumerate(parts):
         for e in range(4):
             at = (y + 4 - d) % 4 * 64 + (x + 4 - e) % 4 * 16
-            rows = 32 * e + 16 * layer
-            pack[pl.ds(pl.multiple_of(at, 16), 16), :] = part[rows:rows + 16, :]
+            pack[pl.ds(pl.multiple_of(at, 16), 16), :] = part[16 * e:16 * e + 16, :]
     for b in range(3):
         def piece(i):
             s = 10 * b + i
@@ -154,12 +153,12 @@
 
 
 def left_kernel(pos, p0, p1, p2, p3, right, out, pack, full):
-    left_product(pos, 0, (p0, p1, p2, p3), right, out, pack, full)
+    left_product(pos, (p0, p1, p2, p3), right, out, pack, full)
 
 
 def last_kernel(pos, p0, p1, p2, p3, w_own, w_pair, w_mid, factor, before, out, pack, full, right):
     right[...] = right_product(w_own, w_pair, w_mid, factor)
-    left_product(pos, 1, (p0, p1, p2, p3), right, out, pack, full)
+    left_product(pos, (p0, p1, p2, p3), right, out, pack, full)
 
 
 def call(kernel, pos, operands, in_specs, out_shape, scratch, out_specs=None, aliases={}):
@@ -207,80 +206,84 @@
     return lax.dynamic_slice_in_dim(a, index % 4 * rows, rows, 0)
 
 
-def exchange(w, middle):
-    pair = lax.ppermute(w, "x", [(0, 1), (1, 0), (2, 3), (3, 2)])
-    return [pair, lax.ppermute(middle, "x", [(1, 2), (2, 1)])]
+def paired(w):
+    return lax.ppermute(w, "x", [(0, 1), (1, 0), (2, 3), (3, 2)])
 
 
 def body(acts, grads_out, weight_grad):
-    y, x, z, c = (lax.axis_index(n) for n in ("y", "x", "z", "c"))
-    pos = jnp.stack([x, y, c, z % 4 * 2 + c, z // 4]).astype(jnp.int32)
+    y, x, zh, zl, c = (lax.axis_index(n) for n in ("y", "x", "zh", "zl", "c"))
+    pos = jnp.stack([x, y, c, zh % 2 * 4 + zl * 2 + c, zh // 2, zl]).astype(jnp.int32)
     rows, width = weight_grad.shape[1:]
     barrier = lax.optimization_barrier
 
-    whole0, mid0, whole1, mid1 = call(
-        columns_kernel, pos, (weight_grad,), [ANYWHERE], [shape(rows, width), shape(rows, 256)] * 2,
-        [pltpu.SemaphoreType.DMA((4,))], out_specs=[ANYWHERE] * 4,
+    covs = call(
+        cov_kernel, pos, (grads_out,), [whole(grads_out)],
+        [shape(128, LANES)] * 4, [VMEM((2, 256, LANES), BF16)],
     )
-    w_first = exchange(whole0, mid0)
+    covs = list(covs)
+    covs[0], acts, w_ready = barrier((covs[0], acts, weight_grad))
+    quarter = add(spread(covs, "y")).astype(BF16)
+
+    whole0, whole1, mid = call(
+        columns_kernel, pos, (w_ready,), [ANYWHERE], [shape(rows, width), shape(rows, width), shape(2, rows, 256)],
+        [pltpu.SemaphoreType.DMA((3,))], out_specs=[ANYWHERE] * 3,
+    )
+    pair0, mid = paired(whole0), lax.ppermute(mid, "x", [(1, 2), (2, 1)])
 
     side = call(
         side_kernel, pos, (acts,),
         [pl.BlockSpec((1,) + acts.shape[1:], lambda i, p: (p[4], 0, 0), pipeline_mode=ONCE)],
         [shape(128, LANES)], [],
     )[0]
-    side, grads_out = barrier((side, grads_out))
     side = lax.all_to_all(side, "y", 0, 0, tiled=True)
     side = add([side[32 * d:32 * (d + 1)] for d in range(4)]).astype(BF16)
-    side = lax.all_to_all(jnp.tile(side, (4, 1)), "x", 0, 0, tiled=True)
-    side = add([side[32 * d:32 * (d + 1)] for d in range(4)]) * (1.0 / TOKENS)
-    side = jnp.concatenate([side[:16], side[16:]], axis=1)
+
+    quarter, side, pair0, mid = barrier((quarter, side, pair0, mid))
+    sends = [
+        jnp.concatenate([chunk(quarter[:64], x + d, 16), chunk(quarter[64:], x + d, 16), side], axis=0)
+        for d in range(4)
+    ]
+    both = add(spread(sends, "x")) * (1.0 / TOKENS)
+    side = jnp.concatenate([both[32:48], both[48:64]], axis=1)
     side = lax.dynamic_slice_in_dim(side, x // 2 * 1280, 2560, 1).astype(BF16)
-    mine = lax.all_to_all(jnp.tile(side, (8, 1)), "z", 0, 0, tiled=True)
-
-    covs = call(
-        cov_kernel, pos, (grads_out,), [whole(grads_out)],
-        [shape(128, LANES)] * 4, [VMEM((2, 256, LANES), BF16)],
-    )
-    quarter = add(spread(covs, "y")).astype(BF16)
-    quarter, mine, w_first = barrier((quarter, mine, w_first))
-    quarter = [
-        jnp.concatenate([chunk(quarter[:64], x + d, 16), chunk(quarter[64:], x + d, 16)], axis=0) for d in range(4)
-    ]
-    own = (add(spread(quarter, "x")) * (1.0 / TOKENS)).astype(BF16)
-    quarter = jnp.concatenate(spread([own] * 4, "x"), axis=0)
-    quarter, whole1, mid1 = barrier((quarter, whole1, mid1))
-    w_second = exchange(whole1, mid1)
-    parts = spread([quarter] * 4, "y")
-
+
+    quarter = spread([both[:32].astype(BF16)] * 4, "x")
+    first, second = (jnp.concatenate([q[16 * n:16 * n + 16] for q in quarter], axis=0) for n in range(2))
+    side = jnp.concatenate([side, lax.ppermute(side, "zl", [(0, 1), (1, 0)])], axis=0)
+    first, second, side, whole1 = barrier((first, second, side, whole1))
+    pair1 = paired(whole1)
+    first = spread([first] * 4, "y")
+    mine = lax.all_to_all(jnp.tile(side, (4, 1)), "zh", 0, 0, tiled=True)
+    first, second, mine = barrier((first, second, mine))
+    second = spread([second] * 4, "y")
     other = lax.ppermute(mine, "c", [(0, 1), (1, 0)])
     factor = call(
         factor_kernel, pos, (mine, other), [whole(mine), whole(other)], [shape(2, 1024, 384)],
         [VMEM((2, SUB, 2560), BF16), VMEM((2, 2, BLK, BLK), F32), VMEM((2, 1024, 1024), BF16)],
     )[0]
 
-    def products(layer, w):
-        specs = [of_layer(weight_grad, layer), whole(w[0]), whole(w[1]), of_layer(factor, layer)]
-        return (weight_grad, *w, factor), specs
+    def products(layer, w_pair):
+        specs = [of_layer(weight_grad, layer), whole(w_pair), of_layer(mid, layer), of_layer(factor, layer)]
+        return (weight_grad, w_pair, mid, factor), specs
 
     out = shape(*weight_grad.shape)
     scratch = [VMEM((256, LANES), BF16), VMEM((3, BLK, BLK), F32)]
-    operands, specs = products(0, w_first)
+    operands, specs = products(0, pair0)
     right = call(right_kernel, pos, operands, specs, [shape(rows, width)], [])[0]
-    operands = (*parts, right)
+    operands = (*first, right)
     before = call(
         left_kernel, pos, operands, [whole(a) for a in operands], [out], scratch, out_specs=[of_layer(out, 0)]
     )[0]
-    operands, specs = products(1, w_second)
+    operands, specs = products(1, pair1)
     return call(
-        last_kernel, pos, (*parts, *operands, before), [whole(a) for a in parts] + specs + [ANYWHERE], [out],
+        last_kernel, pos, (*second, *operands, before), [whole(a) for a in second] + specs + [ANYWHERE], [out],
         scratch + [VMEM((rows, width), BF16)], out_specs=[of_layer(out, 1)], aliases={9: 0},
     )[0]
 
 
 def solution(mesh):
-    fine = Mesh(mesh.devices.reshape(4, 4, 8, 2), ("y", "x", "z", "c"))
-    dp, owner = ("y", "x"), ("z", "c")
+    fine = Mesh(mesh.devices.reshape(4, 4, 4, 2, 2), ("y", "x", "zh", "zl", "c"))
+    dp, owner = ("y", "x"), ("zh", "zl", "c")
     in_specs = (P(None, dp, None), P(None, dp, owner), P(None, owner, dp))
     out_specs = P(None, owner, dp)
     return jax.shard_map(body, mesh=fine, in_specs=in_specs, out_specs=out_specs, check_vma=False)

time: 137 us -> 139 us (1.015)
  blocking collectives: 13.2 us -> 0 us
  starting transfers between devices: 34.5 us -> 43.3 us
  local copies, waits for them, and re-layouts: 8.19 us -> 16.7 us
  waiting for transfers between devices: 47.7 us -> 45.7 us
    all_to_all x1 -> x0, blocking collectives: 13.2 us -> none  [body(): side = lax.all_to_all(side, 'y', 0, 0, tiled=True)]
    ppermute x12 -> x15, starting transfers between devices: 11.2 us -> 24.1 us  [spread(): lax.ppermute(parts[d], axis, [(i, (i + d) % 4) for i in range(4)])]
    unnamed x14 -> x40, local copies, waits for them, and re-layouts: 5.22 us -> 15.6 us
    ppermute x1, starting transfers between devices: 7.31 us -> 0.85 us  [body(): other = lax.ppermute(mine, 'c', [(0, 1), (1, 0)])]
    all_to_all x2, waiting for transfers between devices: 2.56 us -> 0.01 us  [the longest x1 0.01 us: body(): side = lax.all_to_all(side, 'y', 0, 0, tiled=True)]
    ppermute x4, starting transfers between devices: 3.75 us -> 6.09 us  [the longest x2 3.61 us: paired(): return lax.ppermute(w, 'x', [(0, 1), (1, 0), (2, 3), (3, 2)])]
    ppermute x12 -> x15, waiting for transfers between devices: 45.1 us -> 45.7 us  [spread(): lax.ppermute(parts[d], axis, [(i, (i + d) % 4) for i in range(4)])]
  transfers between devices with their start and end apart: 19 -> 22, of which waited for: 12 -> 9; matrix products, arithmetic and copies ran while one was open for 3% -> 2% of each run, Pallas kernels for 13% -> 12%
where the time goes in v6:
time: 139 us; the launch traced here: 137 us
  waiting for transfers between devices  45.7 us (33%)
  starting transfers between devices  43.3 us (31%)
  Pallas kernels  27.2 us (20%)
  local copies, waits for them, and re-layouts  16.7 us (12%)
  other arithmetic  4.14 us (3%)
    ppermute x15, waiting for transfers between devices, spread(): lax.ppermute(parts[d], axis, [(i, (i + d) % 4) for i in range(4)])  45.7 us
    pallas_call x7, Pallas kernels, call(): pl.pallas_call(kernel, grid_spec=pltpu.PrefetchScalarGridSpec(num_scalar_...  27.2 us
    ppermute x15, starting transfers between devices, spread(): lax.ppermute(parts[d], axis, [(i, (i + d) % 4) for i in range(4)])  24.1 us
    unnamed x40, local copies, waits for them, and re-layouts  15.6 us
    all_to_all x1, starting transfers between devices, body(): mine = lax.all_to_all(jnp.tile(side, (4, 1)), 'zh', 0, 0, tiled=True)  7.28 us
    all_to_all x1, starting transfers between devices, body(): side = lax.all_to_all(side, 'y', 0, 0, tiled=True)  5.01 us
    ppermute x2, starting transfers between devices, paired(): return lax.ppermute(w, 'x', [(0, 1), (1, 0), (2, 3), (3, 2)])  3.61 us
  transfers between devices with their start and end apart: 22, of which 9 were waited for; matrix products, arithmetic and copies ran while one was open for 2% of the time, Pallas kernels for 12%

profile of v6, /device:TPU:1, one launch (start us, length us, event | category | flops | bytes accessed | tf_op | source)
XLA Modules:
  0.0 137.3 jit_solution(7650535895997678075)
XLA Ops:
  0.0 0.1 stack.27.pos
  0.1 1.4 %copy-done.6 = bf16[2,256,1536]{2,1,0:T(8,128)(2,1)S(1)} copy-done((bf16[2,256,1536]{2,1,0:T(8,128)(2,1)S(1)}, bf16[2,256,1536]{2,1,0:T(8,128)(2,1)}, u32[]{:S(2)}) %copy-start.6) | copy-done | bytes 1572888
  1.5 1.5 %shard_map.37 = (bf16[128,1920]{1,0:T(8,128)(2,1)S(1)}, bf16[128,1920]{1,0:T(8,128)(2,1)S(1)}, bf16[128,1920]{1,0:T(8,128)(2,1)S(1)}, bf16[128,1920]{1,0:T(8,128)(2,1)S(1)}) custom-call(s32[6]{0:T(128)S(1)} %stack.27.pos, bf16[2,256,1536]{2,1,0:T(8,128)(2,1)S(1)} %copy-done.6), custom_call_target="tpu_custom_call" | custom-call | tf_op jit(solution)/shard_map/pallas_call | solution.py:165
  3.0 0.8 copy-done.17
  3.8 0.8 copy-done.18
  4.6 0.8 copy-done.19
  5.3 1.7 %copy-done = bf16[2,1536,384]{2,1,0:T(8,128)(2,1)S(1)} copy-done((bf16[2,1536,384]{2,1,0:T(8,128)(2,1)S(1)}, bf16[2,1536,384]{2,1,0:T(8,128)(2,1)}, u32[]{:S(2)}) %copy-start) | copy-done | bytes 2359320
  7.0 2.2 %shard_map.39 = (bf16[1536,384]{1,0:T(8,128)(2,1)S(1)}, bf16[1536,384]{1,0:T(8,128)(2,1)S(1)}, bf16[2,1536,256]{2,1,0:T(8,128)(2,1)}) custom-call(s32[6]{0:T(128)S(1)} %stack.27.pos, bf16[2,1536,384]{2,1,0:T(8,128)(2,1)S(1)} %copy-done), custom_call_target="tpu_custom_call" | custom-call | tf_op jit(solution)/shard_map/pallas_call | solution.py:165
  9.2 1.0 copy-done.15
  10.3 1.0 copy-done.16
  11.3 0.7 collective-permute-start.4
  12.0 0.0 copy-start.2
  12.1 2.8 %copy-done.2 = bf16[2,256,6144]{2,1,0:T(8,128)(2,1)S(1)} copy-done((bf16[2,256,6144]{2,1,0:T(8,128)(2,1)S(1)}, bf16[2,256,6144]{2,1,0:T(8,128)(2,1)}, u32[]{:S(2)}) %copy-start.2) | copy-done | bytes 6291480
  14.8 4.6 %shard_map.38 = bf16[128,1920]{1,0:T(8,128)(2,1)} custom-call(s32[6]{0:T(128)S(1)} %stack.27.pos, bf16[2,256,6144]{2,1,0:T(8,128)(2,1)S(1)} %copy-done.2), custom_call_target="tpu_custom_call" | custom-call | tf_op jit(solution)/shard_map/pallas_call | solution.py:165
  19.4 5.0 %all-to-all-start = ((bf16[4,32,1920]{2,1,0:T(8,128)(2,1)}), bf16[4,32,1920]{2,1,0:T(8,128)(2,1)}, u32[]{:S(2)}, u32[]{:S(2)}) async-start(bf16[4,32,1920]{2,1,0:T(8,128)(2,1)} %bitcast.6), calls=%async_computation | async-start | bytes 983040 | tf_op jit(solution)/shard_map/all_to_all | solution.py:238
  24.4 3.6 %collective-permute-start.3 = (bf16[1536,384]{1,0:T(8,128)(2,1)}, bf16[1536,384]{1,0:T(8,128)(2,1)S(1)}, u32[]{:S(2)}, u32[]{:S(2)}) collective-permute-start(bf16[1536,384]{1,0:T(8,128)(2,1)} %copy-done.16), channel_id=1, source_target_pairs={{0,16},{16,0},{32,48},{48,32},{1,17},{17,1},{33,49},{49,33},{2,18}... | collective-permute-start | bytes 3538952 | tf_op jit(solution)/shard_map/ppermute | solution.py:210
  28.0 1.4 %collective-permute-start = (bf16[128,1920]{1,0:T(8,128)(2,1)}, bf16[128,1920]{1,0:T(8,128)(2,1)}, u32[]{:S(2)}, u32[]{:S(2)}) collective-permute-start(bf16[128,1920]{1,0:T(8,128)(2,1)} %copy-done.19), channel_id=1, source_target_pairs={{0,64},{64,128},{128,192},{192,0},{1,65},{65,129},{129,193},{193,1... | collective-permute-start | bytes 1474568 | tf_op jit(solution)/shard_map/ppermute | solution.py:202
  29.4 2.5 %collective-permute-start.1 = (bf16[128,1920]{1,0:T(8,128)(2,1)}, bf16[128,1920]{1,0:T(8,128)(2,1)}, u32[]{:S(2)}, u32[]{:S(2)}) collective-permute-start(bf16[128,1920]{1,0:T(8,128)(2,1)} %copy-done.18), channel_id=1, source_target_pairs={{0,128},{64,192},{128,0},{192,64},{1,129},{65,193},{129,1},{193,65... | collective-permute-start | bytes 1474568 | tf_op jit(solution)/shard_map/ppermute | solution.py:202
  31.9 1.1 collective-permute-start.2
  33.0 1.1 fusion.2
  34.2 10.6 %collective-permute-done = bf16[128,1920]{1,0:T(8,128)(2,1)} collective-permute-done((bf16[128,1920]{1,0:T(8,128)(2,1)}, bf16[128,1920]{1,0:T(8,128)(2,1)}, u32[]{:S(2)}, u32[]{:S(2)}) %collective-permute-start) | collective-permute-done | bytes 491552 | tf_op jit(solution)/shard_map/ppermute | solution.py:202
  44.8 9.2 %collective-permute-done.1 = bf16[128,1920]{1,0:T(8,128)(2,1)} collective-permute-done((bf16[128,1920]{1,0:T(8,128)(2,1)}, bf16[128,1920]{1,0:T(8,128)(2,1)}, u32[]{:S(2)}, u32[]{:S(2)}) %collective-permute-start.1) | collective-permute-done | bytes 491552 | tf_op jit(solution)/shard_map/ppermute | solution.py:202
  54.0 0.0 collective-permute-done.2
  54.0 1.6 %add_convert_fusion = bf16[128,1920]{1,0:T(8,128)(2,1)S(1)} fusion(bf16[128,1920]{1,0:T(8,128)(2,1)} %collective-permute-done.2, bf16[128,1920]{1,0:T(8,128)(2,1)} %collective-permute-done.1, bf16[128,1920]{1,0:T(8,128)(2,1)} %collective-permute-done, bf16[128,1920]{1,0:T(8,128)(2,1)S(1)} %get-tuple-element.30), kind=kLoop, calls=%fused_computation | loop fusion | flops 1966080 | bytes 2457600 | tf_op jit(solution)/shard_map/convert_element_type | solution.py:225
  55.7 0.0 collective-permute-done.4.w_mid
  55.7 0.1 constant_dynamic-slice_fusion.6
  55.8 1.1 pad_maximum_fusion.2
  56.9 0.0 copy-done.7
  56.9 0.5 copy-done.3
  57.4 3.0 %collective-permute-start.5 = (bf16[64,1920]{1,0:T(8,128)(2,1)}, bf16[64,1920]{1,0:T(8,128)(2,1)S(1)}, u32[]{:S(2)}, u32[]{:S(2)}) collective-permute-start(bf16[64,1920]{1,0:T(8,128)(2,1)} %get-tuple-element.73), channel_id=1, source_target_pairs={{0,16},{16,32},{32,48},{48,0},{1,17},{17,33},{33,49},{49,1},{2,18}... | collective-permute-start | bytes 737288 | tf_op jit(solution)/shard_map/ppermute | solution.py:202
  60.4 0.6 collective-permute-start.6
  61.0 2.1 %collective-permute-start.7 = (bf16[64,1920]{1,0:T(8,128)(2,1)S(1)}, bf16[64,1920]{1,0:T(8,128)(2,1)S(1)}, u32[]{:S(2)}, u32[]{:S(2)}) collective-permute-start(bf16[64,1920]{1,0:T(8,128)(2,1)S(1)} %get-tuple-element.75), channel_id=1, source_target_pairs={{0,48},{16,0},{32,16},{48,32},{1,49},{17,1},{33,17},{49,33},{2,50}... | collective-permute-start | bytes 737288 | tf_op jit(solution)/shard_map/ppermute | solution.py:202
  63.1 1.4 %collective-permute-done.5 = bf16[64,1920]{1,0:T(8,128)(2,1)S(1)} collective-permute-done((bf16[64,1920]{1,0:T(8,128)(2,1)}, bf16[64,1920]{1,0:T(8,128)(2,1)S(1)}, u32[]{:S(2)}, u32[]{:S(2)}) %collective-permute-start.5) | collective-permute-done | bytes 245792 | tf_op jit(solution)/shard_map/ppermute | solution.py:202
  64.5 6.1 %collective-permute-done.6 = bf16[64,1920]{1,0:T(8,128)(2,1)S(1)} collective-permute-done((bf16[64,1920]{1,0:T(8,128)(2,1)}, bf16[64,1920]{1,0:T(8,128)(2,1)S(1)}, u32[]{:S(2)}, u32[]{:S(2)}) %collective-permute-start.6) | collective-permute-done | bytes 245792 | tf_op jit(solution)/shard_map/ppermute | solution.py:202
  70.6 0.1 add_multiply_fusion
  70.8 0.1 fusion.1
  70.9 1.7 %collective-permute-start.11 = (bf16[16,2560]{1,0:T(8,128)(2,1)S(1)}, bf16[16,2560]{1,0:T(8,128)(2,1)S(1)}, u32[]{:S(2)}, u32[]{:S(2)}) collective-permute-start(bf16[16,2560]{1,0:T(8,128)(2,1)S(1)} %fusion.1), channel_id=1, source_target_pairs={{0,2},{2,0},{1,3},{3,1},{4,6},{6,4},{5,7},{7,5},{8,10},{10,8},{9,1... | collective-permute-start | bytes 245768 | tf_op jit(solution)/shard_map/ppermute | solution.py:252
  72.6 3.0 %collective-permute-start.10 = (bf16[32,1920]{1,0:T(8,128)(2,1)S(1)}, bf16[32,1920]{1,0:T(8,128)(2,1)S(1)}, u32[]{:S(2)}, u32[]{:S(2)}) collective-permute-start(bf16[32,1920]{1,0:T(8,128)(2,1)S(1)} %slice.86), channel_id=1, source_target_pairs={{0,48},{16,0},{32,16},{48,32},{1,49},{17,1},{33,17},{49,33},{2,50}... | collective-permute-start | bytes 368648 | tf_op jit(solution)/shard_map/ppermute | solution.py:202
  75.6 2.2 %collective-permute-start.9 = (bf16[32,1920]{1,0:T(8,128)(2,1)S(1)}, bf16[32,1920]{1,0:T(8,128)(2,1)S(1)}, u32[]{:S(2)}, u32[]{:S(2)}) collective-permute-start(bf16[32,1920]{1,0:T(8,128)(2,1)S(1)} %slice.86), channel_id=1, source_target_pairs={{0,32},{16,48},{32,0},{48,16},{1,33},{17,49},{33,1},{49,17},{2,34}... | collective-permute-start | bytes 368648 | tf_op jit(solution)/shard_map/ppermute | solution.py:202
  77.8 0.5 collective-permute-done.10
  78.3 2.6 %collective-permute-done.9 = bf16[32,1920]{1,0:T(8,128)(2,1)S(1)} collective-permute-done((bf16[32,1920]{1,0:T(8,128)(2,1)S(1)}, bf16[32,1920]{1,0:T(8,128)(2,1)S(1)}, u32[]{:S(2)}, u32[]{:S(2)}) %collective-permute-start.9) | collective-permute-done | bytes 122912 | tf_op jit(solution)/shard_map/ppermute | solution.py:202
  80.9 3.3 %collective-permute-done.8 = bf16[32,1920]{1,0:T(8,128)(2,1)S(1)} collective-permute-done((bf16[32,1920]{1,0:T(8,128)(2,1)S(1)}, bf16[32,1920]{1,0:T(8,128)(2,1)S(1)}, u32[]{:S(2)}, u32[]{:S(2)}) %collective-permute-start.8) | collective-permute-done | bytes 122912 | tf_op jit(solution)/shard_map/ppermute | solution.py:202
  84.3 0.9 tile.2
  85.1 7.3 %all-to-all-start.1 = ((bf16[4,32,2560]{2,1,0:T(8,128)(2,1)}), bf16[4,32,2560]{2,1,0:T(8,128)(2,1)S(1)}, u32[]{:S(2)}, u32[]{:S(2)}) async-start(bf16[4,32,2560]{2,1,0:T(8,128)(2,1)} %tile.2), calls=%async_computation.1 | async-start | bytes 1310720 | tf_op jit(solution)/shard_map/all_to_all | solution.py:256
  92.4 3.8 %collective-permute-start.14 = (bf16[64,1920]{1,0:T(8,128)(2,1)S(1)}, bf16[64,1920]{1,0:T(8,128)(2,1)S(1)}, u32[]{:S(2)}, u32[]{:S(2)}) collective-permute-start(bf16[64,1920]{1,0:T(8,128)(2,1)S(1)} %pad_maximum_fusion.4.p0), channel_id=1, source_target_pairs={{0,192},{64,0},{128,64},{192,128},{1,193},{65,1},{129,65},{193,129... | collective-permute-start | bytes 737288 | tf_op jit(solution)/shard_map/ppermute | solution.py:202
  96.2 0.0 collective-permute-start.13
  96.2 0.7 collective-permute-start.12
  96.9 8.9 %collective-permute-done.14.p3 = bf16[64,1920]{1,0:T(8,128)(2,1)S(1)} collective-permute-done((bf16[64,1920]{1,0:T(8,128)(2,1)S(1)}, bf16[64,1920]{1,0:T(8,128)(2,1)S(1)}, u32[]{:S(2)}, u32[]{:S(2)}) %collective-permute-start.14) | collective-permute-done | bytes 245792 | tf_op jit(solution)/shard_map/ppermute | solution.py:202
  105.8 0.7 copy-done.9
  106.5 0.7 copy-done.11
  107.2 3.0 %collective-permute-done.12.p1 = bf16[64,1920]{1,0:T(8,128)(2,1)S(1)} collective-permute-done((bf16[64,1920]{1,0:T(8,128)(2,1)S(1)}, bf16[64,1920]{1,0:T(8,128)(2,1)S(1)}, u32[]{:S(2)}, u32[]{:S(2)}) %collective-permute-start.12) | collective-permute-done | bytes 245792 | tf_op jit(solution)/shard_map/ppermute | solution.py:202
  110.2 0.7 copy-done.13
  110.9 0.9 collective-permute-start.19
  111.8 3.2 %collective-permute-start.17 = (bf16[64,1920]{1,0:T(8,128)(2,1)S(1)}, bf16[64,1920]{1,0:T(8,128)(2,1)S(1)}, u32[]{:S(2)}, u32[]{:S(2)}) collective-permute-start(bf16[64,1920]{1,0:T(8,128)(2,1)S(1)} %pad_maximum_fusion.5.p0), channel_id=1, source_target_pairs={{0,192},{64,0},{128,64},{192,128},{1,193},{65,1},{129,65},{193,129... | collective-permute-start | bytes 737288 | tf_op jit(solution)/shard_map/ppermute | solution.py:202
  114.9 0.0 collective-permute-start.16
  115.0 0.6 collective-permute-start.15
  115.5 0.0 collective-permute-done.19.other
  115.5 3.9 %shard_map.40.factor = bf16[2,1024,384]{2,1,0:T(8,128)(2,1)S(1)} custom-call(s32[6]{0:T(128)S(1)} %stack.27.pos, bf16[128,2560]{1,0:T(8,128)(2,1)S(1)} %bitcast.11, bf16[128,2560]{1,0:T(8,128)(2,1)S(1)} %collective-permute-done.19.other), custom_call_target="tpu_custom_call" | custom-call | tf_op jit(solution)/shard_map/pallas_call | solution.py:165
  119.5 1.4 %copy-done.4 = bf16[2,1536,256]{2,1,0:T(8,128)(2,1)S(1)} copy-done((bf16[2,1536,256]{2,1,0:T(8,128)(2,1)S(1)}, bf16[2,1536,256]{2,1,0:T(8,128)(2,1)}, u32[]{:S(2)}) %copy-start.4) | copy-done | bytes 1572888
  120.9 1.3 copy-done.8
  122.2 2.6 %shard_map.41.right = bf16[1536,384]{1,0:T(8,128)(2,1)S(1)} custom-call(s32[6]{0:T(128)S(1)} %stack.27.pos, bf16[2,1536,384]{2,1,0:T(8,128)(2,1)S(1)} %copy-done.1, bf16[1536,384]{1,0:T(8,128)(2,1)S(1)} %copy-done.8, bf16[2,1536,256]{2,1,0:T(8,128)(2,1)S(1)} %copy-done.4, bf16[2,1024,384]{2,1,0:T(8,128)(2,1)S(1)} %shard_map.40.factor), custom_call_target="tpu_custom_call" | custom-call | tf_op jit(solution)/shard_map/pallas_call | solution.py:165
  124.8 4.9 %shard_map.42.before = bf16[2,1536,384]{2,1,0:T(8,128)(2,1)} custom-call(s32[6]{0:T(128)S(1)} %stack.27.pos, bf16[64,1920]{1,0:T(8,128)(2,1)S(1)} %pad_maximum_fusion.4.p0, bf16[64,1920]{1,0:T(8,128)(2,1)S(1)} %copy-done.14, bf16[64,1920]{1,0:T(8,128)(2,1)S(1)} %copy-done.12, bf16[64,1920]{1,0:T(8,128)(2,1)S(1)} %copy-done.10, ...), custom_call_target="tpu_custom_call" | custom-call | tf_op jit(solution)/shard_map/pallas_call | solution.py:165
  129.6 0.0 collective-permute-done.17.p3
  129.7 7.6 %shard_map.43 = bf16[2,1536,384]{2,1,0:T(8,128)(2,1)} custom-call(s32[6]{0:T(128)S(1)} %stack.27.pos, bf16[64,1920]{1,0:T(8,128)(2,1)S(1)} %pad_maximum_fusion.5.p0, bf16[64,1920]{1,0:T(8,128)(2,1)S(1)} %collective-permute-done.15.p1, bf16[64,1920]{1,0:T(8,128)(2,1)S(1)} %collective-permute-done.16.p2, ...), custom_call_target="tpu_custom_call", output_to_operand_aliasing={{}: (9, {})} | custom-call | tf_op jit(solution)/shard_map/pallas_call | solution.py:165
  (44 shorter events, 0.2 us)
Async XLA Ops:
  0.1 1.4 %copy-start.6 = (bf16[2,256,1536]{2,1,0:T(8,128)(2,1)S(1)}, bf16[2,256,1536]{2,1,0:T(8,128)(2,1)}, u32[]{:S(2)}) copy-start(bf16[2,256,1536]{2,1,0:T(8,128)(2,1)} %grads.1) | copy-start | bytes 4718596
  3.0 0.8 copy-start.17
  3.8 0.8 copy-start.18
  4.5 0.8 copy-start.19
  5.3 1.7 %copy-start = (bf16[2,1536,384]{2,1,0:T(8,128)(2,1)S(1)}, bf16[2,1536,384]{2,1,0:T(8,128)(2,1)}, u32[]{:S(2)}) copy-start(bf16[2,1536,384]{2,1,0:T(8,128)(2,1)} %w_own.3) | copy-start | bytes 7077892
  9.2 1.1 copy-start.15
  10.3 1.0 copy-start.16
  11.3 44.4 %collective-permute-start.4 = (bf16[2,1536,256]{2,1,0:T(8,128)(2,1)}, bf16[2,1536,256]{2,1,0:T(8,128)(2,1)S(1)}, u32[]{:S(2)}, u32[]{:S(2)}) collective-permute-start(bf16[2,1536,256]{2,1,0:T(8,128)(2,1)} %get-tuple-element.37), channel_id=1, source_target_pairs={{16,32},{32,16},{17,33},{33,17},{18,34},{34,18},{19,35},{35,19},{2... | collective-permute-start | bytes 4718600 | tf_op jit(solution)/shard_map/ppermute | solution.py:231
  12.0 2.8 %copy-start.2 = (bf16[2,256,6144]{2,1,0:T(8,128)(2,1)S(1)}, bf16[2,256,6144]{2,1,0:T(8,128)(2,1)}, u32[]{:S(2)}) copy-start(bf16[2,256,6144]{2,1,0:T(8,128)(2,1)} %acts) | copy-start | bytes 18874372
  19.4 13.6 %all-to-all-start = ((bf16[4,32,1920]{2,1,0:T(8,128)(2,1)}), bf16[4,32,1920]{2,1,0:T(8,128)(2,1)}, u32[]{:S(2)}, u32[]{:S(2)}) async-start(bf16[4,32,1920]{2,1,0:T(8,128)(2,1)} %bitcast.6), calls=%async_computation | async-start | bytes 983040 | tf_op jit(solution)/shard_map/all_to_all | solution.py:238
  24.4 31.2 %collective-permute-start.3 = (bf16[1536,384]{1,0:T(8,128)(2,1)}, bf16[1536,384]{1,0:T(8,128)(2,1)S(1)}, u32[]{:S(2)}, u32[]{:S(2)}) collective-permute-start(bf16[1536,384]{1,0:T(8,128)(2,1)} %copy-done.16), channel_id=1, source_target_pairs={{0,16},{16,0},{32,48},{48,32},{1,17},{17,1},{33,49},{49,33},{2,18}... | collective-permute-start | bytes 3538952 | tf_op jit(solution)/shard_map/ppermute | solution.py:210
  28.0 16.8 %collective-permute-start = (bf16[128,1920]{1,0:T(8,128)(2,1)}, bf16[128,1920]{1,0:T(8,128)(2,1)}, u32[]{:S(2)}, u32[]{:S(2)}) collective-permute-start(bf16[128,1920]{1,0:T(8,128)(2,1)} %copy-done.19), channel_id=1, source_target_pairs={{0,64},{64,128},{128,192},{192,0},{1,65},{65,129},{129,193},{193,1... | collective-permute-start | bytes 1474568 | tf_op jit(solution)/shard_map/ppermute | solution.py:202
  29.4 24.6 %collective-permute-start.1 = (bf16[128,1920]{1,0:T(8,128)(2,1)}, bf16[128,1920]{1,0:T(8,128)(2,1)}, u32[]{:S(2)}, u32[]{:S(2)}) collective-permute-start(bf16[128,1920]{1,0:T(8,128)(2,1)} %copy-done.18), channel_id=1, source_target_pairs={{0,128},{64,192},{128,0},{192,64},{1,129},{65,193},{129,1},{193,65... | collective-permute-start | bytes 1474568 | tf_op jit(solution)/shard_map/ppermute | solution.py:202
  31.9 22.1 %collective-permute-start.2 = (bf16[128,1920]{1,0:T(8,128)(2,1)}, bf16[128,1920]{1,0:T(8,128)(2,1)}, u32[]{:S(2)}, u32[]{:S(2)}) collective-permute-start(bf16[128,1920]{1,0:T(8,128)(2,1)} %copy-done.17), channel_id=1, source_target_pairs={{0,192},{64,0},{128,64},{192,128},{1,193},{65,1},{129,65},{193,129... | collective-permute-start | bytes 1474568 | tf_op jit(solution)/shard_map/ppermute | solution.py:202
  55.7 1.2 copy-start.7
  55.7 1.7 %copy-start.3 = (bf16[2,1536,256]{2,1,0:T(8,128)(2,1)}, bf16[2,1536,256]{2,1,0:T(8,128)(2,1)S(1)}, u32[]{:S(2)}) copy-start(bf16[2,1536,256]{2,1,0:T(8,128)(2,1)S(1)} %collective-permute-done.4.w_mid) | copy-start | bytes 4718596
  57.4 7.1 %collective-permute-start.5 = (bf16[64,1920]{1,0:T(8,128)(2,1)}, bf16[64,1920]{1,0:T(8,128)(2,1)S(1)}, u32[]{:S(2)}, u32[]{:S(2)}) collective-permute-start(bf16[64,1920]{1,0:T(8,128)(2,1)} %get-tuple-element.73), channel_id=1, source_target_pairs={{0,16},{16,32},{32,48},{48,0},{1,17},{17,33},{33,49},{49,1},{2,18}... | collective-permute-start | bytes 737288 | tf_op jit(solution)/shard_map/ppermute | solution.py:202
  60.4 10.2 %collective-permute-start.6 = (bf16[64,1920]{1,0:T(8,128)(2,1)}, bf16[64,1920]{1,0:T(8,128)(2,1)S(1)}, u32[]{:S(2)}, u32[]{:S(2)}) collective-permute-start(bf16[64,1920]{1,0:T(8,128)(2,1)} %get-tuple-element.74), channel_id=1, source_target_pairs={{0,32},{16,48},{32,0},{48,16},{1,33},{17,49},{33,1},{49,17},{2,34}... | collective-permute-start | bytes 737288 | tf_op jit(solution)/shard_map/ppermute | solution.py:202
  61.0 9.6 %collective-permute-start.7 = (bf16[64,1920]{1,0:T(8,128)(2,1)S(1)}, bf16[64,1920]{1,0:T(8,128)(2,1)S(1)}, u32[]{:S(2)}, u32[]{:S(2)}) collective-permute-start(bf16[64,1920]{1,0:T(8,128)(2,1)S(1)} %get-tuple-element.75), channel_id=1, source_target_pairs={{0,48},{16,0},{32,16},{48,32},{1,49},{17,1},{33,17},{49,33},{2,50}... | collective-permute-start | bytes 737288 | tf_op jit(solution)/shard_map/ppermute | solution.py:202
  70.9 6.9 %collective-permute-start.11 = (bf16[16,2560]{1,0:T(8,128)(2,1)S(1)}, bf16[16,2560]{1,0:T(8,128)(2,1)S(1)}, u32[]{:S(2)}, u32[]{:S(2)}) collective-permute-start(bf16[16,2560]{1,0:T(8,128)(2,1)S(1)} %fusion.1), channel_id=1, source_target_pairs={{0,2},{2,0},{1,3},{3,1},{4,6},{6,4},{5,7},{7,5},{8,10},{10,8},{9,1... | collective-permute-start | bytes 245768 | tf_op jit(solution)/shard_map/ppermute | solution.py:252
  72.6 5.6 %collective-permute-start.10 = (bf16[32,1920]{1,0:T(8,128)(2,1)S(1)}, bf16[32,1920]{1,0:T(8,128)(2,1)S(1)}, u32[]{:S(2)}, u32[]{:S(2)}) collective-permute-start(bf16[32,1920]{1,0:T(8,128)(2,1)S(1)} %slice.86), channel_id=1, source_target_pairs={{0,48},{16,0},{32,16},{48,32},{1,49},{17,1},{33,17},{49,33},{2,50}... | collective-permute-start | bytes 368648 | tf_op jit(solution)/shard_map/ppermute | solution.py:202
  75.6 5.2 %collective-permute-start.9 = (bf16[32,1920]{1,0:T(8,128)(2,1)S(1)}, bf16[32,1920]{1,0:T(8,128)(2,1)S(1)}, u32[]{:S(2)}, u32[]{:S(2)}) collective-permute-start(bf16[32,1920]{1,0:T(8,128)(2,1)S(1)} %slice.86), channel_id=1, source_target_pairs={{0,32},{16,48},{32,0},{48,16},{1,33},{17,49},{33,1},{49,17},{2,34}... | collective-permute-start | bytes 368648 | tf_op jit(solution)/shard_map/ppermute | solution.py:202
  77.8 6.4 %collective-permute-start.8 = (bf16[32,1920]{1,0:T(8,128)(2,1)S(1)}, bf16[32,1920]{1,0:T(8,128)(2,1)S(1)}, u32[]{:S(2)}, u32[]{:S(2)}) collective-permute-start(bf16[32,1920]{1,0:T(8,128)(2,1)S(1)} %slice.86), channel_id=1, source_target_pairs={{0,16},{16,32},{32,48},{48,0},{1,17},{17,33},{33,49},{49,1},{2,18}... | collective-permute-start | bytes 368648 | tf_op jit(solution)/shard_map/ppermute | solution.py:202
  85.1 25.8 %all-to-all-start.1 = ((bf16[4,32,2560]{2,1,0:T(8,128)(2,1)}), bf16[4,32,2560]{2,1,0:T(8,128)(2,1)S(1)}, u32[]{:S(2)}, u32[]{:S(2)}) async-start(bf16[4,32,2560]{2,1,0:T(8,128)(2,1)} %tile.2), calls=%async_computation.1 | async-start | bytes 1310720 | tf_op jit(solution)/shard_map/all_to_all | solution.py:256
  92.4 27.1 %copy-start.1 = (bf16[2,1536,384]{2,1,0:T(8,128)(2,1)S(1)}, bf16[2,1536,384]{2,1,0:T(8,128)(2,1)}, u32[]{:S(2)}) copy-start(bf16[2,1536,384]{2,1,0:T(8,128)(2,1)} %w_own.3) | copy-start | bytes 7077892
  92.4 37.2 %collective-permute-start.18 = (bf16[1536,384]{1,0:T(8,128)(2,1)}, bf16[1536,384]{1,0:T(8,128)(2,1)}, u32[]{:S(2)}, u32[]{:S(2)}) collective-permute-start(bf16[1536,384]{1,0:T(8,128)(2,1)} %copy-done.15), channel_id=1, source_target_pairs={{0,16},{16,0},{32,48},{48,32},{1,17},{17,1},{33,49},{49,33},{2,18}... | collective-permute-start | bytes 3538952 | tf_op jit(solution)/shard_map/ppermute | solution.py:210
  92.4 13.4 %collective-permute-start.14 = (bf16[64,1920]{1,0:T(8,128)(2,1)S(1)}, bf16[64,1920]{1,0:T(8,128)(2,1)S(1)}, u32[]{:S(2)}, u32[]{:S(2)}) collective-permute-start(bf16[64,1920]{1,0:T(8,128)(2,1)S(1)} %pad_maximum_fusion.4.p0), channel_id=1, source_target_pairs={{0,192},{64,0},{128,64},{192,128},{1,193},{65,1},{129,65},{193,129... | collective-permute-start | bytes 737288 | tf_op jit(solution)/shard_map/ppermute | solution.py:202
  96.2 10.3 %collective-permute-start.13 = (bf16[64,1920]{1,0:T(8,128)(2,1)S(1)}, bf16[64,1920]{1,0:T(8,128)(2,1)S(1)}, u32[]{:S(2)}, u32[]{:S(2)}) collective-permute-start(bf16[64,1920]{1,0:T(8,128)(2,1)S(1)} %pad_maximum_fusion.4.p0), channel_id=1, source_target_pairs={{0,128},{64,192},{128,0},{192,64},{1,129},{65,193},{129,1},{193,65... | collective-permute-start | bytes 737288 | tf_op jit(solution)/shard_map/ppermute | solution.py:202
  96.2 14.0 %collective-permute-start.12 = (bf16[64,1920]{1,0:T(8,128)(2,1)S(1)}, bf16[64,1920]{1,0:T(8,128)(2,1)S(1)}, u32[]{:S(2)}, u32[]{:S(2)}) collective-permute-start(bf16[64,1920]{1,0:T(8,128)(2,1)S(1)} %pad_maximum_fusion.4.p0), channel_id=1, source_target_pairs={{0,64},{64,128},{128,192},{192,0},{1,65},{65,129},{129,193},{193,1... | collective-permute-start | bytes 737288 | tf_op jit(solution)/shard_map/ppermute | solution.py:202
  105.8 0.7 copy-start.9
  106.5 0.7 copy-start.11
  110.2 0.7 copy-start.13
  110.9 4.6 %collective-permute-start.19 = (bf16[128,2560]{1,0:T(8,128)(2,1)S(1)}, bf16[128,2560]{1,0:T(8,128)(2,1)S(1)}, u32[]{:S(2)}, u32[]{:S(2)}) collective-permute-start(bf16[128,2560]{1,0:T(8,128)(2,1)S(1)} %bitcast.10), channel_id=1, source_target_pairs={{0,1},{1,0},{2,3},{3,2},{4,5},{5,4},{6,7},{7,6},{8,9},{9,8},{10,11... | collective-permute-start | bytes 1966088 | tf_op jit(solution)/shard_map/ppermute | solution.py:259
  111.8 17.9 %collective-permute-start.17 = (bf16[64,1920]{1,0:T(8,128)(2,1)S(1)}, bf16[64,1920]{1,0:T(8,128)(2,1)S(1)}, u32[]{:S(2)}, u32[]{:S(2)}) collective-permute-start(bf16[64,1920]{1,0:T(8,128)(2,1)S(1)} %pad_maximum_fusion.5.p0), channel_id=1, source_target_pairs={{0,192},{64,0},{128,64},{192,128},{1,193},{65,1},{129,65},{193,129... | collective-permute-start | bytes 737288 | tf_op jit(solution)/shard_map/ppermute | solution.py:202
  114.9 14.7 %collective-permute-start.16 = (bf16[64,1920]{1,0:T(8,128)(2,1)S(1)}, bf16[64,1920]{1,0:T(8,128)(2,1)S(1)}, u32[]{:S(2)}, u32[]{:S(2)}) collective-permute-start(bf16[64,1920]{1,0:T(8,128)(2,1)S(1)} %pad_maximum_fusion.5.p0), channel_id=1, source_target_pairs={{0,128},{64,192},{128,0},{192,64},{1,129},{65,193},{129,1},{193,65... | collective-permute-start | bytes 737288 | tf_op jit(solution)/shard_map/ppermute | solution.py:202
  115.0 14.7 %collective-permute-start.15 = (bf16[64,1920]{1,0:T(8,128)(2,1)S(1)}, bf16[64,1920]{1,0:T(8,128)(2,1)S(1)}, u32[]{:S(2)}, u32[]{:S(2)}) collective-permute-start(bf16[64,1920]{1,0:T(8,128)(2,1)S(1)} %pad_maximum_fusion.5.p0), channel_id=1, source_target_pairs={{0,64},{64,128},{128,192},{192,0},{1,65},{65,129},{129,193},{193,1... | collective-permute-start | bytes 737288 | tf_op jit(solution)/shard_map/ppermute | solution.py:202
  119.5 1.4 %copy-start.4 = (bf16[2,1536,256]{2,1,0:T(8,128)(2,1)S(1)}, bf16[2,1536,256]{2,1,0:T(8,128)(2,1)}, u32[]{:S(2)}) copy-start(bf16[2,1536,256]{2,1,0:T(8,128)(2,1)} %copy-done.3) | copy-start | bytes 4718596
  120.9 1.3 copy-start.8
  122.2 2.6 %copy-start.10 = (bf16[64,1920]{1,0:T(8,128)(2,1)S(1)}, bf16[64,1920]{1,0:T(8,128)(2,1)}, u32[]{:S(2)}) copy-start(bf16[64,1920]{1,0:T(8,128)(2,1)} %copy-done.9) | copy-start | bytes 737284
  122.2 2.6 %copy-start.12 = (bf16[64,1920]{1,0:T(8,128)(2,1)S(1)}, bf16[64,1920]{1,0:T(8,128)(2,1)}, u32[]{:S(2)}) copy-start(bf16[64,1920]{1,0:T(8,128)(2,1)} %copy-done.11) | copy-start | bytes 737284
  122.2 2.6 %copy-start.14 = (bf16[64,1920]{1,0:T(8,128)(2,1)S(1)}, bf16[64,1920]{1,0:T(8,128)(2,1)}, u32[]{:S(2)}) copy-start(bf16[64,1920]{1,0:T(8,128)(2,1)} %copy-done.13) | copy-start | bytes 737284
  124.8 4.9 %copy-start.5 = (bf16[2,1536,256]{2,1,0:T(8,128)(2,1)S(1)}, bf16[2,1536,256]{2,1,0:T(8,128)(2,1)}, u32[]{:S(2)}) copy-start(bf16[2,1536,256]{2,1,0:T(8,128)(2,1)} %copy-done.3) | copy-start | bytes 4718596

commit v7 on v6

v7 whole, which is shorter than its diff:
```python
import jax
import jax.numpy as jnp
from jax import lax
from jax.experimental import pallas as pl
from jax.experimental.pallas import tpu as pltpu
from jax.sharding import Mesh, PartitionSpec as P

BLK = 512
SUB = 128
damping = 0.1
TOKENS = 4096
F32 = jnp.float32
BF16 = jnp.bfloat16
VMEM = pltpu.VMEM

PAIRS = [(r, c) for r in range(4) for c in range(r, 4)]
LANES = 15 * SUB


def tn_dot(a, b):
    return lax.dot_general(a, b, (((0,), (0,)), ((), ())), preferred_element_type=F32)


def nn_dot(a, b):
    return lax.dot_general(a, b, (((1,), (0,)), ((), ())), preferred_element_type=F32)


def cov_kernel(pos, acts, grads, w, h0, h1, h2, h3, early, late, mid, pack, sems):
    x, y, part = pos[0], pos[1], pos[3]
    columns = pl.ds(pl.multiple_of(jnp.where(x == 1, SUB, 0), SUB), 256)
    full = w.shape[1]
    copies = [
        pltpu.make_async_copy(w.at[:, :, columns], mid, sems.at[0]),
        pltpu.make_async_copy(w.at[0], early.at[pl.ds(0, full)], sems.at[1]),
        pltpu.make_async_copy(w.at[1, pl.ds(0, BLK)], early.at[pl.ds(full, BLK)], sems.at[2]),
        pltpu.make_async_copy(w.at[1, pl.ds(BLK, full - BLK)], late, sems.at[3]),
    ]
    for copy in copies:
        copy.start()
    sends = (h0, h1, h2, h3)
    for layer in range(2):
        for b in range(3):
            rows = grads[layer, :, b * BLK:(b + 1) * BLK]
            top = tn_dot(rows[:, :256], rows).astype(BF16)
            low = tn_dot(rows[:, 256:], rows[:, 256:]).astype(BF16)
            for i, (r, c) in enumerate(PAIRS):
                s = 10 * b + i
                if r < 2:
                    piece = top[r * SUB:(r + 1) * SUB, c * SUB:(c + 1) * SUB]
                else:
                    piece = low[(r - 2) * SUB:(r - 1) * SUB, (c - 2) * SUB:(c - 1) * SUB]
                pack[layer, s // 15 * SUB:(s // 15 + 1) * SUB, s % 15 * SUB:(s % 15 + 1) * SUB] = piece
    for d, send in enumerate(sends):
        at = pl.multiple_of((y + d) % 4 * 64, 64)
        send[0:64, :] = pack[0, pl.ds(at, 64), :]
        send[64:128, :] = pack[1, pl.ds(at, 64), :]
    k = lax.broadcasted_iota(jnp.int32, (BLK, 64), 0)
    m = lax.broadcasted_iota(jnp.int32, (BLK, 64), 1)
    select = jnp.where(k == m // 16 * SUB + part * 16 + m % 16, 1.0, 0.0).astype(BF16)
    for d, send in enumerate(sends):
        start = (y + d) % 4 * (3 * BLK)
        for b in range(3):
            rows = acts[0, :, pl.ds(pl.multiple_of(start + b * BLK, BLK), BLK)]
            chosen = nn_dot(rows, select).astype(BF16)
            cov = tn_dot(chosen, rows).astype(BF16)
            for i, (r, c) in enumerate(PAIRS):
                s = 10 * b + i
                at = 128 + s // 15 * 16
                send[at:at + 16, s % 15 * SUB:(s % 15 + 1) * SUB] = cov[r * 16:(r + 1) * 16, c * SUB:(c + 1) * SUB]
    for copy in copies:
        copy.wait()


def unpack(piece, full):
    for i, (r, c) in enumerate(PAIRS):
        tile = piece(i)
        full[r * SUB:(r + 1) * SUB, c * SUB:(c + 1) * SUB] = tile.astype(full.dtype)
        if r != c:
            full[c * SUB:(c + 1) * SUB, r * SUB:(r + 1) * SUB] = tile.T.astype(full.dtype)


def invert(full):
    ri = lax.broadcasted_iota(jnp.int32, (BLK, BLK), 0)
    ci = lax.broadcasted_iota(jnp.int32, (BLK, BLK), 1)
    diagonal = ri == ci
    matrix = full[...] + jnp.where(diagonal, damping, 0.0)
    two_eye = jnp.where(diagonal, 2.0, 0.0)
    sums = jnp.sum(jnp.abs(matrix), axis=0, keepdims=True)
    alpha = (1.0 / jnp.max(sums, axis=1, keepdims=True)).astype(BF16).astype(F32)
    low = matrix.astype(BF16)
    residue = (two_eye - low.astype(F32) * alpha).astype(BF16)
    iterate = (residue.astype(F32) * alpha).astype(BF16)
    image = nn_dot(low, iterate)
    residue = (two_eye - image).astype(BF16)
    return nn_dot(iterate, residue).astype(BF16)


OFFSETS = (0, -1, 1, -2, 2, -3, 3, -4)


def factor_kernel(pos, mine, other, out, pack, full, diag):
    x, core, z = pos[0], pos[2], pos[5]
    for n, offset in enumerate(OFFSETS):
        rows = slice(16 * n, 16 * n + 16)
        at = (z + 8 + offset) % 8 * 32
        pack[pl.ds(pl.multiple_of(at + core * 16, 16), 16), :] = mine[rows, :]
        pack[pl.ds(pl.multiple_of(at + 16 - core * 16, 16), 16), :] = other[rows, :]
    base = x // 2 * BLK
    own = pl.multiple_of(x * 384 - base, SUB)
    pair = pl.multiple_of((x + 1 - 2 * (x % 2)) * 384 - base, SUB)
    mid = pl.multiple_of(jnp.where(x == 1, 768, 0), SUB)
    columns = pl.ds(own, 384)
    for layer in range(2):
        for b in range(2):
            at = b * BLK
            unpack(
                lambda i: pack[layer * SUB:(layer + 1) * SUB, b * 1280 + i * SUB:b * 1280 + (i + 1) * SUB].astype(F32),
                full.at[layer, b],
            )
            diag[layer, at:at + BLK, at:at + BLK] = invert(full.at[layer, b])
            diag[layer, at:at + BLK, BLK - at:2 * BLK - at] = jnp.zeros((BLK, BLK), BF16)
        out[layer, 0:384, :] = diag[layer, pl.ds(own, 384), columns]
        out[layer, 384:768, :] = diag[layer, pl.ds(pair, 384), columns]
        out[layer, 768:1024, :] = diag[layer, pl.ds(mid, 256), columns]


def right_kernel(pos, w_own, w_mid, factor, *refs):
    out, at = refs[-1], 0
    for pair in refs[:-1]:
        rows = slice(at, at + pair.shape[0])
        total = nn_dot(w_own[0, rows, :], factor[0, 0:384, :])
        total += nn_dot(pair[...], factor[0, 384:768, :])
        total += nn_dot(w_mid[0, rows, :], factor[0, 768:1024, :])
        out[rows, :] = total.astype(BF16)
        at += pair.shape[0]


def left_kernel(pos, gathered, r0, r1, out, pack, full, ready, sems):
    copies = []
    for layer, right in enumerate((r0, r1)):
        for k in range(16):
            rows = 32 * k + 16 * layer
            pack[layer, 16 * k:16 * k + 16, :] = gathered[rows:rows + 16, :]
        for b in range(3):
            def piece(i):
                s = 10 * b + i
                return pack[layer, s // 15 * SUB:(s // 15 + 1) * SUB, s % 15 * SUB:(s % 15 + 1) * SUB].astype(F32)

            unpack(piece, full.at[layer, b])
            at = b * BLK
            n = 3 * layer + b
            ready[n] = nn_dot(invert(full.at[layer, b]), right[at:at + BLK, :]).astype(BF16)
            copies.append(pltpu.make_async_copy(ready.at[n], out.at[layer, pl.ds(at, BLK)], sems.at[n]))
            copies[-1].start()
    for copy in copies:
        copy.wait()


def call(kernel, pos, operands, in_specs, out_shape, scratch, out_specs=None, aliases={}):
    return pl.pallas_call(
        kernel,
        grid_spec=pltpu.PrefetchScalarGridSpec(
            num_scalar_prefetch=1,
            grid=(1,),
            in_specs=in_specs,
            out_specs=out_specs or [whole(s) for s in out_shape],
            scratch_shapes=scratch,
        ),
        out_shape=out_shape,
        input_output_aliases=aliases,
        compiler_params=pltpu.CompilerParams(vmem_limit_bytes=56 * 1024 * 1024),
        cost_estimate=pl.CostEstimate(flops=0, bytes_accessed=0, transcendentals=0),
    )(pos, *operands)


ANYWHERE = pl.BlockSpec(memory_space=pl.ANY)
ONCE = pl.Buffered(1)


def whole(a):
    return pl.BlockSpec(a.shape, lambda i, p, n=len(a.shape): (0,) * n, pipeline_mode=ONCE)


def of_layer(a, layer):
    return pl.BlockSpec((1,) + a.shape[1:], lambda i, p: (layer, 0, 0), pipeline_mode=ONCE)


def shape(*dims):
    return jax.ShapeDtypeStruct(dims, BF16)


def add(parts):
    return sum(p.astype(F32) for p in parts)


def spread(parts, axis):
    return [parts[0]] + [lax.ppermute(parts[d], axis, [(i, (i + d) % 4) for i in range(4)]) for d in (1, 2, 3)]


def chunk(a, index, rows):
    return lax.dynamic_slice_in_dim(a, index % 4 * rows, rows, 0)


def paired(w):
    return lax.ppermute(w, "x", [(0, 1), (1, 0), (2, 3), (3, 2)])


def body(acts, grads_out, weight_grad):
    y, x, z, c = (lax.axis_index(n) for n in ("y", "x", "z", "c"))
    pos = jnp.stack([x, y, c, z % 4 * 2 + c, z // 4, z]).astype(jnp.int32)
    rows, width = weight_grad.shape[1:]
    barrier = lax.optimization_barrier

    covs = call(
        cov_kernel, pos, (acts, grads_out, weight_grad),
        [
            pl.BlockSpec((1,) + acts.shape[1:], lambda i, p: (p[4], 0, 0), pipeline_mode=ONCE),
            whole(grads_out), ANYWHERE,
        ],
        [shape(160, LANES)] * 4 + [shape(rows + BLK, width), shape(rows - BLK, width), shape(2, rows, 256)],
        [VMEM((2, 256, LANES), BF16), pltpu.SemaphoreType.DMA((4,))],
        out_specs=[whole(shape(160, LANES))] * 4 + [ANYWHERE] * 3,
    )
    early, late, mid = covs[4:]
    early, mid = paired(early), lax.ppermute(mid, "x", [(1, 2), (2, 1)])

    quarter = add(spread(covs[:4], "y")).astype(BF16)
    quarter, early, mid = barrier((quarter, early, mid))
    sends = [
        jnp.concatenate([chunk(quarter[:64], x + d, 16), chunk(quarter[64:128], x + d, 16), quarter[128:]], axis=0)
        for d in range(4)
    ]
    both = add(spread(sends, "x")) * (1.0 / TOKENS)
    side = jnp.concatenate([both[32:48], both[48:64]], axis=1)
    side = lax.dynamic_slice_in_dim(side, x // 2 * 1280, 2560, 1).astype(BF16)
    own, side, late = barrier((both[:32].astype(BF16), side, late))

    gathered = lax.all_to_all(jnp.tile(own, (16, 1)), ("y", "x"), 0, 0, tiled=True)
    late = paired(late)
    up = down = side
    mine = [side]
    for step in range(1, 5):
        up = lax.ppermute(up, "z", [(i, (i + 1) % 8) for i in range(8)])
        mine.append(up)
        if step < 4:
            down = lax.ppermute(down, "z", [(i, (i + 7) % 8) for i in range(8)])
            mine.append(down)
    mine = jnp.concatenate(mine, axis=0)
    other = lax.ppermute(mine, "c", [(0, 1), (1, 0)])
    factor = call(
        factor_kernel, pos, (mine, other), [whole(mine), whole(other)], [shape(2, 1024, 384)],
        [VMEM((256, 2560), BF16), VMEM((2, 2, BLK, BLK), F32), VMEM((2, 1024, 1024), BF16)],
    )[0]
    rights = []
    for layer in range(2):
        if layer == 0:
            pairs = [(early, pl.BlockSpec((rows, width), lambda i, p: (0, 0), pipeline_mode=ONCE))]
        else:
            block = rows // BLK
            pairs = [
                (early, pl.BlockSpec((BLK, width), lambda i, p: (block, 0), pipeline_mode=ONCE)),
                (late, whole(late)),
            ]
        rights.append(call(
            right_kernel, pos, (weight_grad, mid, factor, *(p[0] for p in pairs)),
            [of_layer(weight_grad, layer), of_layer(mid, layer), of_layer(factor, layer), *(p[1] for p in pairs)],
            [shape(rows, width)], [],
        )[0])
    return call(
        left_kernel, pos, (gathered, *rights), [whole(gathered), whole(rights[0]), whole(rights[1])],
        [shape(*weight_grad.shape)],
        [
            VMEM((2, 256, LANES), BF16), VMEM((2, 3, BLK, BLK), F32), VMEM((6, BLK, width), BF16),
            pltpu.SemaphoreType.DMA((6,)),
        ],
        out_specs=[ANYWHERE],
    )[0]


def solution(mesh):
    fine = Mesh(mesh.devices.reshape(4, 4, 8, 2), ("y", "x", "z", "c"))
    dp, owner = ("y", "x"), ("z", "c")
    in_specs = (P(None, dp, None), P(None, dp, owner), P(None, owner, dp))
    out_specs = P(None, owner, dp)
    return jax.shard_map(body, mesh=fine, in_specs=in_specs, out_specs=out_specs, check_vma=False)
```

time: 139 us -> 253 us (1.82)
  Pallas kernels: 27.2 us -> 152 us
  local copies, waits for them, and re-layouts: 16.7 us -> 7.9 us
    pallas_call x7 -> x5, Pallas kernels: 27.2 us -> 152 us  [call(): pl.pallas_call(kernel, grid_spec=pltpu.PrefetchScalarGridSpec(num_scalar_...]
    ppermute x15 -> x6, waiting for transfers between devices: 45.7 us -> 33.2 us  [spread(): lax.ppermute(parts[d], axis, [(i, (i + d) % 4) for i in range(4)])]
    unnamed x40 -> x19, local copies, waits for them, and re-layouts: 15.6 us -> 4.88 us
    ppermute x15 -> x6, starting transfers between devices: 24.1 us -> 13.4 us  [spread(): lax.ppermute(parts[d], axis, [(i, (i + d) % 4) for i in range(4)])]
    ppermute x2 -> x8, waiting for transfers between devices: 0.01 us -> 10.7 us  [the longest x4 10.6 us: body(): up = lax.ppermute(up, 'z', [(i, (i + 1) % 8) for i in range(8)])]
    ppermute x2 -> x8, starting transfers between devices: 2.48 us -> 12 us  [the longest x3 11.2 us: body(): down = lax.ppermute(down, 'z', [(i, (i + 7) % 8) for i in range(8)])]
    ppermute x1, starting transfers between devices: 0.85 us -> 6.29 us  [body(): other = lax.ppermute(mine, 'c', [(0, 1), (1, 0)])]
    all_to_all x2 -> x1, starting transfers between devices: 12.3 us -> 7.72 us  [body(): lax.all_to_all(jnp.tile(own, (16, 1)), ('y', 'x'), 0, 0, tiled=True)]
  transfers between devices with their start and end apart: 22 -> 18, of which waited for: 9 -> 7; matrix products, arithmetic and copies ran while one was open for 2% -> 2% of each run, Pallas kernels for 12% -> 7%
where the time goes in v7:
time: 253 us; the launch traced here: 252 us
  Pallas kernels  152 us (60%)
  waiting for transfers between devices  45.5 us (18%)
  starting transfers between devices  41.9 us (17%)
  local copies, waits for them, and re-layouts  7.9 us (3%)
  other arithmetic  3.95 us (2%)
    pallas_call x5, Pallas kernels, call(): pl.pallas_call(kernel, grid_spec=pltpu.PrefetchScalarGridSpec(num_scalar_...  152 us
    ppermute x6, waiting for transfers between devices, spread(): lax.ppermute(parts[d], axis, [(i, (i + d) % 4) for i in range(4)])  33.2 us
    ppermute x6, starting transfers between devices, spread(): lax.ppermute(parts[d], axis, [(i, (i + d) % 4) for i in range(4)])  13.4 us
    ppermute x3, starting transfers between devices, body(): down = lax.ppermute(down, 'z', [(i, (i + 7) % 8) for i in range(8)])  11.2 us
    ppermute x4, waiting for transfers between devices, body(): up = lax.ppermute(up, 'z', [(i, (i + 1) % 8) for i in range(8)])  10.6 us
    all_to_all x1, starting transfers between devices, body(): lax.all_to_all(jnp.tile(own, (16, 1)), ('y', 'x'), 0, 0, tiled=True)  7.72 us
    ppermute x1, starting transfers between devices, body(): other = lax.ppermute(mine, 'c', [(0, 1), (1, 0)])  6.29 us
  transfers between devices with their start and end apart: 18, of which 7 were waited for; matrix products, arithmetic and copies ran while one was open for 2% of the time, Pallas kernels for 7%

profile of v7, /device:TPU:1, one launch (start us, length us, event | category | flops | bytes accessed | tf_op | source)
XLA Modules:
  0.0 252.1 jit_solution(2640080914434511665)
XLA Ops:
  0.0 0.7 stack.27.pos
  0.7 124.8 %shard_map.37 = (bf16[160,1920]{1,0:T(8,128)(2,1)}, bf16[160,1920]{1,0:T(8,128)(2,1)}, bf16[160,1920]{1,0:T(8,128)(2,1)}, bf16[160,1920]{1,0:T(8,128)(2,1)}, bf1...) custom-call(s32[6]{0:T(128)} %stack.27.pos, bf16[2,256,6144]{2,1,0:T(8,128)(2,1)} %acts.1, ...), custom_call_target="tpu_custom_call" | custom-call | tf_op jit(solution)/shard_map/pallas_call | solution.py:160
  125.4 2.1 collective-permute-start.3
  127.6 0.7 collective-permute-start.4
  128.3 1.4 collective-permute-start
  129.7 2.6 %collective-permute-start.1 = (bf16[160,1920]{1,0:T(8,128)(2,1)}, bf16[160,1920]{1,0:T(8,128)(2,1)}, u32[]{:S(2)}, u32[]{:S(2)}) collective-permute-start(bf16[160,1920]{1,0:T(8,128)(2,1)} %get-tuple-element.20), channel_id=1, source_target_pairs={{0,128},{64,192},{128,0},{192,64},{1,129},{65,193},{129,1},{193,65... | collective-permute-start | bytes 1843208 | tf_op jit(solution)/shard_map/ppermute | solution.py:197
  132.3 1.1 collective-permute-start.2
  133.4 10.8 %collective-permute-done = bf16[160,1920]{1,0:T(8,128)(2,1)} collective-permute-done((bf16[160,1920]{1,0:T(8,128)(2,1)}, bf16[160,1920]{1,0:T(8,128)(2,1)}, u32[]{:S(2)}, u32[]{:S(2)}) %collective-permute-start) | collective-permute-done | bytes 614432 | tf_op jit(solution)/shard_map/ppermute | solution.py:197
  144.2 14.6 %collective-permute-done.1 = bf16[160,1920]{1,0:T(8,128)(2,1)} collective-permute-done((bf16[160,1920]{1,0:T(8,128)(2,1)}, bf16[160,1920]{1,0:T(8,128)(2,1)}, u32[]{:S(2)}, u32[]{:S(2)}) %collective-permute-start.1) | collective-permute-done | bytes 614432 | tf_op jit(solution)/shard_map/ppermute | solution.py:197
  158.7 0.0 collective-permute-done.2
  158.7 1.9 add_convert_fusion
  160.7 0.0 collective-permute-done.3.refs_0_
  160.7 0.0 copy-start.1
  160.7 0.0 collective-permute-done.4.w_mid
  160.7 0.0 copy-start.2
  160.8 0.9 constant_dynamic-slice_fusion.6
  161.6 0.9 pad_maximum_fusion.2
  162.5 0.0 copy-done.1
  162.5 0.0 copy-done.2
  162.5 3.9 %collective-permute-start.5 = (bf16[64,1920]{1,0:T(8,128)(2,1)}, bf16[64,1920]{1,0:T(8,128)(2,1)S(1)}, u32[]{:S(2)}, u32[]{:S(2)}) collective-permute-start(bf16[64,1920]{1,0:T(8,128)(2,1)} %get-tuple-element.43), channel_id=1, source_target_pairs={{0,16},{16,32},{32,48},{48,0},{1,17},{17,33},{33,49},{49,1},{2,18}... | collective-permute-start | bytes 737288 | tf_op jit(solution)/shard_map/ppermute | solution.py:197
  166.4 2.5 collective-permute-start.6
  168.9 2.0 collective-permute-start.7
  170.9 0.0 collective-permute-done.5
  170.9 7.8 %collective-permute-done.6 = bf16[64,1920]{1,0:T(8,128)(2,1)S(1)} collective-permute-done((bf16[64,1920]{1,0:T(8,128)(2,1)}, bf16[64,1920]{1,0:T(8,128)(2,1)S(1)}, u32[]{:S(2)}, u32[]{:S(2)}) %collective-permute-start.6) | collective-permute-done | bytes 245792 | tf_op jit(solution)/shard_map/ppermute | solution.py:197
  178.7 0.0 collective-permute-done.7
  178.7 1.0 add_multiply_fusion
  179.8 0.1 fusion.1
  179.9 5.7 %collective-permute-start.9 = (bf16[16,2560]{1,0:T(8,128)(2,1)S(1)}, bf16[16,2560]{1,0:T(8,128)(2,1)}, u32[]{:S(2)}, u32[]{:S(2)}) collective-permute-start(bf16[16,2560]{1,0:T(8,128)(2,1)S(1)} %fusion.1), channel_id=1, source_target_pairs={{0,14},{2,0},{4,2},{6,4},{8,6},{10,8},{12,10},{14,12},{1,15},{3,1}... | collective-permute-start | bytes 245768 | tf_op jit(solution)/shard_map/ppermute | solution.py:246
  185.5 0.0 collective-permute-start.8
  185.5 0.4 collective-permute-start.16
  186.0 1.4 tile.2
  187.4 7.7 %all-to-all-start = ((bf16[16,32,1920]{2,1,0:T(8,128)(2,1)}), bf16[16,32,1920]{2,1,0:T(8,128)(2,1)S(1)}, u32[]{:S(2)}, u32[]{:S(2)}) async-start(bf16[16,32,1920]{2,1,0:T(8,128)(2,1)} %tile.2), calls=%async_computation | async-start | bytes 3932160 | tf_op jit(solution)/shard_map/all_to_all | solution.py:238
  195.1 0.0 collective-permute-done.9
  195.1 2.7 %collective-permute-start.11 = (bf16[16,2560]{1,0:T(8,128)(2,1)}, bf16[16,2560]{1,0:T(8,128)(2,1)S(1)}, u32[]{:S(2)}, u32[]{:S(2)}) collective-permute-start(bf16[16,2560]{1,0:T(8,128)(2,1)} %collective-permute-done.9), channel_id=1, source_target_pairs={{0,14},{2,0},{4,2},{6,4},{8,6},{10,8},{12,10},{14,12},{1,15},{3,1}... | collective-permute-start | bytes 245768 | tf_op jit(solution)/shard_map/ppermute | solution.py:246
  197.8 0.0 collective-permute-done.8
  197.8 0.0 collective-permute-start.10
  197.8 0.9 constant_dynamic-update-slice_fusion.6
  198.7 0.9 constant_dynamic-update-slice_fusion.5
  199.6 0.0 collective-permute-done.11
  199.6 2.9 %collective-permute-start.13 = (bf16[16,2560]{1,0:T(8,128)(2,1)S(1)}, bf16[16,2560]{1,0:T(8,128)(2,1)S(1)}, u32[]{:S(2)}, u32[]{:S(2)}) collective-permute-start(bf16[16,2560]{1,0:T(8,128)(2,1)S(1)} %collective-permute-done.11), channel_id=1, source_target_pairs={{0,14},{2,0},{4,2},{6,4},{8,6},{10,8},{12,10},{14,12},{1,15},{3,1}... | collective-permute-start | bytes 245768 | tf_op jit(solution)/shard_map/ppermute | solution.py:246
  202.5 0.3 collective-permute-done.10
  202.8 0.0 collective-permute-start.12
  202.8 4.8 %collective-permute-done.12 = bf16[16,2560]{1,0:T(8,128)(2,1)S(1)} collective-permute-done((bf16[16,2560]{1,0:T(8,128)(2,1)S(1)}, bf16[16,2560]{1,0:T(8,128)(2,1)S(1)}, u32[]{:S(2)}, u32[]{:S(2)}) %collective-permute-start.12) | collective-permute-done | bytes 81952 | tf_op jit(solution)/shard_map/ppermute | solution.py:243
  207.6 0.0 collective-permute-start.14
  207.6 0.0 collective-permute-done.13
  207.6 5.6 %collective-permute-done.14 = bf16[16,2560]{1,0:T(8,128)(2,1)S(1)} collective-permute-done((bf16[16,2560]{1,0:T(8,128)(2,1)S(1)}, bf16[16,2560]{1,0:T(8,128)(2,1)S(1)}, u32[]{:S(2)}, u32[]{:S(2)}) %collective-permute-start.14) | collective-permute-done | bytes 81952 | tf_op jit(solution)/shard_map/ppermute | solution.py:243
  213.2 0.0 copy-start.3
  213.2 6.3 %collective-permute-start.15 = (bf16[128,2560]{1,0:T(8,128)(2,1)S(1)}, bf16[128,2560]{1,0:T(8,128)(2,1)S(1)}, u32[]{:S(2)}, u32[]{:S(2)}) collective-permute-start(bf16[128,2560]{1,0:T(8,128)(2,1)S(1)} %constant_dynamic-update-slice_fusion.mine), channel_id=1, source_target_pairs={{0,1},{1,0},{2,3},{3,2},{4,5},{5,4},{6,7},{7,6},{8,9},{9,8},{10,11... | collective-permute-start | bytes 1966088 | tf_op jit(solution)/shard_map/ppermute | solution.py:249
  219.5 1.7 collective-permute-done.15.other
  221.2 0.0 copy-done.3
  221.2 0.0 copy-start.5
  221.2 0.8 copy-done.5
  222.1 6.5 %shard_map.38.factor = bf16[2,1024,384]{2,1,0:T(8,128)(2,1)} custom-call(s32[6]{0:T(128)} %stack.27.pos, bf16[128,2560]{1,0:T(8,128)(2,1)} %copy-done.3, bf16[128,2560]{1,0:T(8,128)(2,1)} %copy-done.5), custom_call_target="tpu_custom_call" | custom-call | tf_op jit(solution)/shard_map/pallas_call | solution.py:160
  228.6 5.8 %shard_map.39.r0 = bf16[1536,384]{1,0:T(8,128)(2,1)} custom-call(s32[6]{0:T(128)} %stack.27.pos, bf16[2,1536,384]{2,1,0:T(8,128)(2,1)} %w_own.3, bf16[2,1536,256]{2,1,0:T(8,128)(2,1)} %copy-done.2, bf16[2,1024,384]{2,1,0:T(8,128)(2,1)} %shard_map.38.factor, bf16[2048,384]{1,0:T(8,128)(2,1)} %copy-done.1), custom_call_target="tpu_custom_call" | custom-call | tf_op jit(solution)/shard_map/pallas_call | solution.py:160
  234.4 0.0 collective-permute-done.16.refs_1_
  234.4 0.0 copy-start.4
  234.4 0.9 copy-done.4
  235.3 5.8 %shard_map.40.r1 = bf16[1536,384]{1,0:T(8,128)(2,1)} custom-call(s32[6]{0:T(128)} %stack.27.pos, bf16[2,1536,384]{2,1,0:T(8,128)(2,1)} %w_own.3, bf16[2,1536,256]{2,1,0:T(8,128)(2,1)} %copy-done.2, bf16[2,1024,384]{2,1,0:T(8,128)(2,1)} %shard_map.38.factor, bf16[2048,384]{1,0:T(8,128)(2,1)} %copy-done.1, bf16[1024,384]{1,0:T(8,128)(2,1)} %copy-done.4), custom_call_target="tpu_custom_call" | custom-call | tf_op jit(solution)/shard_map/pallas_call | solution.py:160
  241.0 0.0 all-to-all-done
  241.1 0.0 copy-start
  241.1 1.3 copy-done
  242.3 9.6 %shard_map.41 = bf16[2,1536,384]{2,1,0:T(8,128)(2,1)} custom-call(s32[6]{0:T(128)} %stack.27.pos, bf16[512,1920]{1,0:T(8,128)(2,1)} %bitcast.7, bf16[1536,384]{1,0:T(8,128)(2,1)} %shard_map.39.r0, bf16[1536,384]{1,0:T(8,128)(2,1)} %shard_map.40.r1), custom_call_target="tpu_custom_call" | custom-call | tf_op jit(solution)/shard_map/pallas_call | solution.py:160
  (10 shorter events, 0.1 us)
Async XLA Ops:
  125.4 35.2 %collective-permute-start.3 = (bf16[2048,384]{1,0:T(8,128)(2,1)}, bf16[2048,384]{1,0:T(8,128)(2,1)S(1)}, u32[]{:S(2)}, u32[]{:S(2)}) collective-permute-start(bf16[2048,384]{1,0:T(8,128)(2,1)} %get-tuple-element.22), channel_id=1, source_target_pairs={{0,16},{16,0},{32,48},{48,32},{1,17},{17,1},{33,49},{49,33},{2,18}... | collective-permute-start | bytes 4718600 | tf_op jit(solution)/shard_map/ppermute | solution.py:205
  127.6 33.1 %collective-permute-start.4 = (bf16[2,1536,256]{2,1,0:T(8,128)(2,1)}, bf16[2,1536,256]{2,1,0:T(8,128)(2,1)S(1)}, u32[]{:S(2)}, u32[]{:S(2)}) collective-permute-start(bf16[2,1536,256]{2,1,0:T(8,128)(2,1)} %get-tuple-element.23), channel_id=1, source_target_pairs={{16,32},{32,16},{17,33},{33,17},{18,34},{34,18},{19,35},{35,19},{2... | collective-permute-start | bytes 4718600 | tf_op jit(solution)/shard_map/ppermute | solution.py:225
  128.3 15.9 %collective-permute-start = (bf16[160,1920]{1,0:T(8,128)(2,1)}, bf16[160,1920]{1,0:T(8,128)(2,1)}, u32[]{:S(2)}, u32[]{:S(2)}) collective-permute-start(bf16[160,1920]{1,0:T(8,128)(2,1)} %get-tuple-element.19), channel_id=1, source_target_pairs={{0,64},{64,128},{128,192},{192,0},{1,65},{65,129},{129,193},{193,1... | collective-permute-start | bytes 1843208 | tf_op jit(solution)/shard_map/ppermute | solution.py:197
  129.7 29.0 %collective-permute-start.1 = (bf16[160,1920]{1,0:T(8,128)(2,1)}, bf16[160,1920]{1,0:T(8,128)(2,1)}, u32[]{:S(2)}, u32[]{:S(2)}) collective-permute-start(bf16[160,1920]{1,0:T(8,128)(2,1)} %get-tuple-element.20), channel_id=1, source_target_pairs={{0,128},{64,192},{128,0},{192,64},{1,129},{65,193},{129,1},{193,65... | collective-permute-start | bytes 1843208 | tf_op jit(solution)/shard_map/ppermute | solution.py:197
  132.3 26.4 %collective-permute-start.2 = (bf16[160,1920]{1,0:T(8,128)(2,1)}, bf16[160,1920]{1,0:T(8,128)(2,1)}, u32[]{:S(2)}, u32[]{:S(2)}) collective-permute-start(bf16[160,1920]{1,0:T(8,128)(2,1)} %get-tuple-element.21), channel_id=1, source_target_pairs={{0,192},{64,0},{128,64},{192,128},{1,193},{65,1},{129,65},{193,129... | collective-permute-start | bytes 1843208 | tf_op jit(solution)/shard_map/ppermute | solution.py:197
  160.7 1.9 copy-start.1
  160.7 1.8 copy-start.2
  162.5 8.4 %collective-permute-start.5 = (bf16[64,1920]{1,0:T(8,128)(2,1)}, bf16[64,1920]{1,0:T(8,128)(2,1)S(1)}, u32[]{:S(2)}, u32[]{:S(2)}) collective-permute-start(bf16[64,1920]{1,0:T(8,128)(2,1)} %get-tuple-element.43), channel_id=1, source_target_pairs={{0,16},{16,32},{32,48},{48,0},{1,17},{17,33},{33,49},{49,1},{2,18}... | collective-permute-start | bytes 737288 | tf_op jit(solution)/shard_map/ppermute | solution.py:197
  166.4 12.3 %collective-permute-start.6 = (bf16[64,1920]{1,0:T(8,128)(2,1)}, bf16[64,1920]{1,0:T(8,128)(2,1)S(1)}, u32[]{:S(2)}, u32[]{:S(2)}) collective-permute-start(bf16[64,1920]{1,0:T(8,128)(2,1)} %get-tuple-element.44), channel_id=1, source_target_pairs={{0,32},{16,48},{32,0},{48,16},{1,33},{17,49},{33,1},{49,17},{2,34}... | collective-permute-start | bytes 737288 | tf_op jit(solution)/shard_map/ppermute | solution.py:197
  168.9 9.8 %collective-permute-start.7 = (bf16[64,1920]{1,0:T(8,128)(2,1)S(1)}, bf16[64,1920]{1,0:T(8,128)(2,1)S(1)}, u32[]{:S(2)}, u32[]{:S(2)}) collective-permute-start(bf16[64,1920]{1,0:T(8,128)(2,1)S(1)} %get-tuple-element.45), channel_id=1, source_target_pairs={{0,48},{16,0},{32,16},{48,32},{1,49},{17,1},{33,17},{49,33},{2,50}... | collective-permute-start | bytes 737288 | tf_op jit(solution)/shard_map/ppermute | solution.py:197
  179.9 15.2 %collective-permute-start.9 = (bf16[16,2560]{1,0:T(8,128)(2,1)S(1)}, bf16[16,2560]{1,0:T(8,128)(2,1)}, u32[]{:S(2)}, u32[]{:S(2)}) collective-permute-start(bf16[16,2560]{1,0:T(8,128)(2,1)S(1)} %fusion.1), channel_id=1, source_target_pairs={{0,14},{2,0},{4,2},{6,4},{8,6},{10,8},{12,10},{14,12},{1,15},{3,1}... | collective-permute-start | bytes 245768 | tf_op jit(solution)/shard_map/ppermute | solution.py:246
  185.5 12.3 %collective-permute-start.8 = (bf16[16,2560]{1,0:T(8,128)(2,1)S(1)}, bf16[16,2560]{1,0:T(8,128)(2,1)}, u32[]{:S(2)}, u32[]{:S(2)}) collective-permute-start(bf16[16,2560]{1,0:T(8,128)(2,1)S(1)} %fusion.1), channel_id=1, source_target_pairs={{0,2},{2,4},{4,6},{6,8},{8,10},{10,12},{12,14},{14,0},{1,3},{3,5},... | collective-permute-start | bytes 245768 | tf_op jit(solution)/shard_map/ppermute | solution.py:243
  185.5 48.8 %collective-permute-start.16 = (bf16[1024,384]{1,0:T(8,128)(2,1)}, bf16[1024,384]{1,0:T(8,128)(2,1)S(1)}, u32[]{:S(2)}, u32[]{:S(2)}) collective-permute-start(bf16[1024,384]{1,0:T(8,128)(2,1)} %get-tuple-element.30), channel_id=1, source_target_pairs={{0,16},{16,0},{32,48},{48,32},{1,17},{17,1},{33,49},{49,33},{2,18}... | collective-permute-start | bytes 2359304 | tf_op jit(solution)/shard_map/ppermute | solution.py:205
  187.4 53.7 %all-to-all-start = ((bf16[16,32,1920]{2,1,0:T(8,128)(2,1)}), bf16[16,32,1920]{2,1,0:T(8,128)(2,1)S(1)}, u32[]{:S(2)}, u32[]{:S(2)}) async-start(bf16[16,32,1920]{2,1,0:T(8,128)(2,1)} %tile.2), calls=%async_computation | async-start | bytes 3932160 | tf_op jit(solution)/shard_map/all_to_all | solution.py:238
  195.1 4.5 %collective-permute-start.11 = (bf16[16,2560]{1,0:T(8,128)(2,1)}, bf16[16,2560]{1,0:T(8,128)(2,1)S(1)}, u32[]{:S(2)}, u32[]{:S(2)}) collective-permute-start(bf16[16,2560]{1,0:T(8,128)(2,1)} %collective-permute-done.9), channel_id=1, source_target_pairs={{0,14},{2,0},{4,2},{6,4},{8,6},{10,8},{12,10},{14,12},{1,15},{3,1}... | collective-permute-start | bytes 245768 | tf_op jit(solution)/shard_map/ppermute | solution.py:246
  197.8 5.0 %collective-permute-start.10 = (bf16[16,2560]{1,0:T(8,128)(2,1)}, bf16[16,2560]{1,0:T(8,128)(2,1)S(1)}, u32[]{:S(2)}, u32[]{:S(2)}) collective-permute-start(bf16[16,2560]{1,0:T(8,128)(2,1)} %collective-permute-done.8), channel_id=1, source_target_pairs={{0,2},{2,4},{4,6},{6,8},{8,10},{10,12},{12,14},{14,0},{1,3},{3,5},... | collective-permute-start | bytes 245768 | tf_op jit(solution)/shard_map/ppermute | solution.py:243
  199.6 8.0 %collective-permute-start.13 = (bf16[16,2560]{1,0:T(8,128)(2,1)S(1)}, bf16[16,2560]{1,0:T(8,128)(2,1)S(1)}, u32[]{:S(2)}, u32[]{:S(2)}) collective-permute-start(bf16[16,2560]{1,0:T(8,128)(2,1)S(1)} %collective-permute-done.11), channel_id=1, source_target_pairs={{0,14},{2,0},{4,2},{6,4},{8,6},{10,8},{12,10},{14,12},{1,15},{3,1}... | collective-permute-start | bytes 245768 | tf_op jit(solution)/shard_map/ppermute | solution.py:246
  202.8 4.8 %collective-permute-start.12 = (bf16[16,2560]{1,0:T(8,128)(2,1)S(1)}, bf16[16,2560]{1,0:T(8,128)(2,1)S(1)}, u32[]{:S(2)}, u32[]{:S(2)}) collective-permute-start(bf16[16,2560]{1,0:T(8,128)(2,1)S(1)} %collective-permute-done.10), channel_id=1, source_target_pairs={{0,2},{2,4},{4,6},{6,8},{8,10},{10,12},{12,14},{14,0},{1,3},{3,5},... | collective-permute-start | bytes 245768 | tf_op jit(solution)/shard_map/ppermute | solution.py:243
  207.6 5.6 %collective-permute-start.14 = (bf16[16,2560]{1,0:T(8,128)(2,1)S(1)}, bf16[16,2560]{1,0:T(8,128)(2,1)S(1)}, u32[]{:S(2)}, u32[]{:S(2)}) collective-permute-start(bf16[16,2560]{1,0:T(8,128)(2,1)S(1)} %collective-permute-done.12), channel_id=1, source_target_pairs={{0,2},{2,4},{4,6},{6,8},{8,10},{10,12},{12,14},{14,0},{1,3},{3,5},... | collective-permute-start | bytes 245768 | tf_op jit(solution)/shard_map/ppermute | solution.py:243
  213.2 8.0 %copy-start.3 = (bf16[128,2560]{1,0:T(8,128)(2,1)}, bf16[128,2560]{1,0:T(8,128)(2,1)S(1)}, u32[]{:S(2)}) copy-start(bf16[128,2560]{1,0:T(8,128)(2,1)S(1)} %constant_dynamic-update-slice_fusion.mine) | copy-start | bytes 1966084
  213.2 8.0 %collective-permute-start.15 = (bf16[128,2560]{1,0:T(8,128)(2,1)S(1)}, bf16[128,2560]{1,0:T(8,128)(2,1)S(1)}, u32[]{:S(2)}, u32[]{:S(2)}) collective-permute-start(bf16[128,2560]{1,0:T(8,128)(2,1)S(1)} %constant_dynamic-update-slice_fusion.mine), channel_id=1, source_target_pairs={{0,1},{1,0},{2,3},{3,2},{4,5},{5,4},{6,7},{7,6},{8,9},{9,8},{10,11... | collective-permute-start | bytes 1966088 | tf_op jit(solution)/shard_map/ppermute | solution.py:249
  221.2 0.8 copy-start.5
  234.4 0.9 copy-start.4
  241.1 1.3 copy-start

commit v8 on v7

v8 whole, which is shorter than its diff:
```python
import jax
import jax.numpy as jnp
from jax import lax
from jax.experimental import pallas as pl
from jax.experimental.pallas import tpu as pltpu
from jax.sharding import Mesh, PartitionSpec as P

BLK = 512
SUB = 128
damping = 0.1
TOKENS = 4096
F32 = jnp.float32
BF16 = jnp.bfloat16
VMEM = pltpu.VMEM

PAIRS = [(r, c) for r in range(4) for c in range(r, 4)]
LANES = 15 * SUB


def tn_dot(a, b):
    return lax.dot_general(a, b, (((0,), (0,)), ((), ())), preferred_element_type=F32)


def nn_dot(a, b):
    return lax.dot_general(a, b, (((1,), (0,)), ((), ())), preferred_element_type=F32)


def relay(copies, sems):
    loads = [pltpu.make_async_copy(a, b, sems.at[0, n]) for n, (a, b, _) in enumerate(copies)]
    stores = [pltpu.make_async_copy(b, c, sems.at[1, n]) for n, (_, b, c) in enumerate(copies)]
    for load in loads:
        load.start()
    for load, store in zip(loads, stores):
        load.wait()
        store.start()
    for store in stores:
        store.wait()


def middle(pos):
    return pl.ds(pl.multiple_of(jnp.where(pos[0] == 1, SUB, 0), SUB), 256)


def early_kernel(pos, w, whole0, mid0, held, held_mid, sems):
    full, rest = w.shape[1], w.shape[1] - BLK
    relay([
        (w.at[0], held, whole0),
        (w.at[0, :, middle(pos)], held_mid.at[pl.ds(0, full)], mid0.at[pl.ds(0, full)]),
        (w.at[1, pl.ds(0, rest), middle(pos)], held_mid.at[pl.ds(full, rest)], mid0.at[pl.ds(full, rest)]),
    ], sems)


def late_kernel(pos, w, whole1, mid1, held, held_mid, sems):
    rest = w.shape[1] - BLK
    relay([(w.at[1], held, whole1), (w.at[1, pl.ds(rest, BLK), middle(pos)], held_mid, mid1)], sems)


def cov_kernel(pos, grads, h0, h1, h2, h3, pack):
    y = pos[1]
    for layer in range(2):
        for b in range(3):
            rows = grads[layer, :, b * BLK:(b + 1) * BLK]
            top = tn_dot(rows[:, :256], rows).astype(BF16)
            low = tn_dot(rows[:, 256:], rows[:, 256:]).astype(BF16)
            for i, (r, c) in enumerate(PAIRS):
                s = 10 * b + i
                if r < 2:
                    piece = top[r * SUB:(r + 1) * SUB, c * SUB:(c + 1) * SUB]
                else:
                    piece = low[(r - 2) * SUB:(r - 1) * SUB, (c - 2) * SUB:(c - 1) * SUB]
                pack[layer, s // 15 * SUB:(s // 15 + 1) * SUB, s % 15 * SUB:(s % 15 + 1) * SUB] = piece
    for d, send in enumerate((h0, h1, h2, h3)):
        at = pl.multiple_of((y + d) % 4 * 64, 64)
        send[0:64, :] = pack[0, pl.ds(at, 64), :]
        send[64:128, :] = pack[1, pl.ds(at, 64), :]


def side_kernel(pos, acts, out):
    part = pos[3]
    k = lax.broadcasted_iota(jnp.int32, (BLK, 64), 0)
    m = lax.broadcasted_iota(jnp.int32, (BLK, 64), 1)
    select = jnp.where(k == m // 16 * SUB + part * 16 + m % 16, 1.0, 0.0).astype(BF16)
    for b in range(3):
        rows = acts[0, :, b * BLK:(b + 1) * BLK]
        chosen = nn_dot(rows, select).astype(BF16)
        cov = tn_dot(chosen, rows).astype(BF16)
        for i, (r, c) in enumerate(PAIRS):
            s = 10 * b + i
            at = s // 15 * 16
            out[at:at + 16, s % 15 * SUB:(s % 15 + 1) * SUB] = cov[r * 16:(r + 1) * 16, c * SUB:(c + 1) * SUB]


def total_kernel(pos, parts, out):
    total = (parts[0:32, :].astype(F32) + parts[32:64, :].astype(F32)) + (
        parts[64:96, :].astype(F32) + parts[96:128, :].astype(F32)
    )
    for n in range(4):
        out[32 * n:32 * n + 32, :] = total.astype(BF16)


def chosen_kernel(pos, parts, out):
    x = pos[0]
    total = ((parts[0:32, :].astype(F32) + parts[32:64, :].astype(F32)) + (
        parts[64:96, :].astype(F32) + parts[96:128, :].astype(F32)
    )) * (1.0 / TOKENS)
    upper, lower = total[0:16, :].astype(BF16), total[16:32, :].astype(BF16)

    @pl.when(x < 2)
    def _():
        for n in range(8):
            out[16 * n:16 * n + 16, 0:LANES] = upper
            out[16 * n:16 * n + 16, LANES:2560] = lower[:, 0:640]

    @pl.when(x >= 2)
    def _():
        for n in range(8):
            out[16 * n:16 * n + 16, 0:640] = upper[:, 1280:LANES]
            out[16 * n:16 * n + 16, 640:2560] = lower


def unpack(piece, full):
    for i, (r, c) in enumerate(PAIRS):
        tile = piece(i)
        full[r * SUB:(r + 1) * SUB, c * SUB:(c + 1) * SUB] = tile.astype(full.dtype)
        if r != c:
            full[c * SUB:(c + 1) * SUB, r * SUB:(r + 1) * SUB] = tile.T.astype(full.dtype)


def invert(full):
    ri = lax.broadcasted_iota(jnp.int32, (BLK, BLK), 0)
    ci = lax.broadcasted_iota(jnp.int32, (BLK, BLK), 1)
    diagonal = ri == ci
    matrix = full[...] + jnp.where(diagonal, damping, 0.0)
    two_eye = jnp.where(diagonal, 2.0, 0.0)
    sums = jnp.sum(jnp.abs(matrix), axis=0, keepdims=True)
    alpha = (1.0 / jnp.max(sums, axis=1, keepdims=True)).astype(BF16).astype(F32)
    low = matrix.astype(BF16)
    residue = (two_eye - low.astype(F32) * alpha).astype(BF16)
    iterate = (residue.astype(F32) * alpha).astype(BF16)
    image = nn_dot(low, iterate)
    residue = (two_eye - image).astype(BF16)
    return nn_dot(iterate, residue).astype(BF16)


def twice_kernel(pos, a, out):
    out[0:128, :] = a[...]
    out[128:256, :] = a[...]


def factor_kernel(pos, both, out, pack, full, diag):
    x = pos[0]
    for z in range(8):
        for core in range(2):
            rows = 128 * core + 16 * z
            pack[32 * z + 16 * core:32 * z + 16 * core + 16, :] = both[rows:rows + 16, :]
    base = x // 2 * BLK
    own = pl.multiple_of(x * 384 - base, SUB)
    pair = pl.multiple_of((x + 1 - 2 * (x % 2)) * 384 - base, SUB)
    mid = pl.multiple_of(jnp.where(x == 1, 768, 0), SUB)
    columns = pl.ds(own, 384)
    for layer in range(2):
        for b in range(2):
            at = b * BLK
            unpack(
                lambda i: pack[layer * SUB:(layer + 1) * SUB, b * 1280 + i * SUB:b * 1280 + (i + 1) * SUB].astype(F32),
                full.at[layer, b],
            )
            diag[layer, at:at + BLK, at:at + BLK] = invert(full.at[layer, b])
            diag[layer, at:at + BLK, BLK - at:2 * BLK - at] = jnp.zeros((BLK, BLK), BF16)
        out[layer, 0:384, :] = diag[layer, pl.ds(own, 384), columns]
        out[layer, 384:768, :] = diag[layer, pl.ds(pair, 384), columns]
        out[layer, 768:1024, :] = diag[layer, pl.ds(mid, 256), columns]


def right_kernel(pos, w_own, w_pair, factor, *refs):
    out, at = refs[-1], 0
    for mid in refs[:-1]:
        rows = slice(at, at + mid.shape[0])
        total = nn_dot(w_own[0, rows, :], factor[0, 0:384, :])
        total += nn_dot(w_pair[rows, :], factor[0, 384:768, :])
        total += nn_dot(mid[...], factor[0, 768:1024, :])
        out[rows, :] = total.astype(BF16)
        at += mid.shape[0]


def left_kernel(pos, p0, p1, p2, p3, r0, r1, out, pack, full, ready, sems):
    x, y = pos[0], pos[1]
    copies = []
    for layer, right in enumerate((r0, r1)):
        for d, part in enumerate((p0, p1, p2, p3)):
            for e in range(4):
                at = (y + 4 - d) % 4 * 64 + (x + 4 - e) % 4 * 16
                rows = 32 * e + 16 * layer
                pack[layer, pl.ds(pl.multiple_of(at, 16), 16), :] = part[rows:rows + 16, :]
        for b in range(3):
            def piece(i):
                s = 10 * b + i
                return pack[layer, s // 15 * SUB:(s // 15 + 1) * SUB, s % 15 * SUB:(s % 15 + 1) * SUB].astype(F32)

            unpack(piece, full.at[layer, b])
            at = b * BLK
            n = 3 * layer + b
            ready[n] = nn_dot(invert(full.at[layer, b]), right[at:at + BLK, :]).astype(BF16)
            copies.append(pltpu.make_async_copy(ready.at[n], out.at[layer, pl.ds(at, BLK)], sems.at[n]))
            copies[-1].start()
    for copy in copies:
        copy.wait()


def call(kernel, pos, operands, in_specs, out_shape, scratch, out_specs=None, vmem=40, flops=0, grid=1):
    return pl.pallas_call(
        kernel,
        grid_spec=pltpu.PrefetchScalarGridSpec(
            num_scalar_prefetch=1,
            grid=(grid,),
            in_specs=in_specs,
            out_specs=out_specs or [whole(s) for s in out_shape],
            scratch_shapes=scratch,
        ),
        out_shape=out_shape,
        compiler_params=pltpu.CompilerParams(vmem_limit_bytes=vmem * 1024 * 1024),
        cost_estimate=pl.CostEstimate(flops=flops, bytes_accessed=0, transcendentals=0),
    )(pos, *operands)


ANYWHERE = pl.BlockSpec(memory_space=pl.ANY)
ONCE = pl.Buffered(1)


def whole(a):
    return pl.BlockSpec(a.shape, lambda i, p, n=len(a.shape): (0,) * n, pipeline_mode=ONCE)


def of_layer(a, layer):
    return pl.BlockSpec((1,) + a.shape[1:], lambda i, p: (layer, 0, 0), pipeline_mode=ONCE)


def part(rows, n):
    return pl.BlockSpec((rows, 256), lambda i, p: (n, 0), pipeline_mode=ONCE)


def shape(*dims):
    return jax.ShapeDtypeStruct(dims, BF16)


def add(parts):
    return sum(p.astype(F32) for p in parts)


def spread(parts, axis):
    return [parts[0]] + [lax.ppermute(parts[d], axis, [(i, (i + d) % 4) for i in range(4)]) for d in (1, 2, 3)]


def chunk(a, index, rows):
    return lax.dynamic_slice_in_dim(a, index % 4 * rows, rows, 0)


def exchange(w, middle):
    pair = lax.ppermute(w, "x", [(0, 1), (1, 0), (2, 3), (3, 2)])
    return [pair, lax.ppermute(middle, "x", [(1, 2), (2, 1)])]


def body(acts, grads_out, weight_grad):
    y, x, z, c = (lax.axis_index(n) for n in ("y", "x", "z", "c"))
    pos = jnp.stack([x, y, c, z % 4 * 2 + c, z // 4, z]).astype(jnp.int32)
    rows, width = weight_grad.shape[1:]
    barrier = lax.optimization_barrier

    def relayed(kernel, w, *shapes, **options):
        return call(
            kernel, pos, (w,), [ANYWHERE], list(shapes),
            [VMEM(a.shape, BF16) for a in shapes] + [pltpu.SemaphoreType.DMA((2, 3))],
            out_specs=[ANYWHERE] * 2, vmem=60, **options,
        )

    w_early = exchange(*relayed(early_kernel, weight_grad, shape(rows, width), shape(2 * rows - BLK, 256)))

    def blocks(operands):
        pos, acts, grads_out, weight_grad = operands
        side = call(
            side_kernel, pos, (acts,),
            [pl.BlockSpec((1, acts.shape[1], 3 * BLK), lambda i, p: (p[4], 0, i))],
            [shape(128, LANES)], [], out_specs=[pl.BlockSpec((32, LANES), lambda i, p: (i, 0))], vmem=60, grid=4,
        )[0]
        covs = call(
            cov_kernel, pos, (grads_out,), [whole(grads_out)], [shape(128, LANES)] * 4,
            [VMEM((2, 256, LANES), BF16)], vmem=60, flops=10_000_000_000,
        )
        w_late = relayed(late_kernel, weight_grad, shape(rows, width), shape(BLK, 256), flops=5_000_000_000)
        return lax.all_to_all(side, "y", 0, 0, tiled=True), *w_late, *covs

    always = x + y + z + c < 64
    late = (rows, width), (BLK, 256)
    side, *covs = lax.cond(
        always, blocks, lambda operands: tuple(jnp.zeros(n, BF16) for n in ((128, LANES), *late, *((128, LANES),) * 4)),
        (pos, acts, grads_out, weight_grad),
    )
    w_late, covs = covs[:2], covs[2:]
    covs = spread(covs, "y")

    def sum_side(operands):
        pos, side, _ = operands
        side = call(total_kernel, pos, (side,), [whole(side)], [shape(128, LANES)], [])[0]
        side = lax.all_to_all(side, "x", 0, 0, tiled=True)
        return call(chosen_kernel, pos, (side,), [whole(side)], [shape(128, 2560)], [])[0]

    side = lax.cond(always, sum_side, lambda operands: jnp.zeros((128, 2560), BF16), (pos, side, covs[0]))
    mine = lax.all_to_all(side, "z", 0, 0, tiled=True)
    *covs, _ = barrier((*covs, side))
    quarter = add(covs).astype(BF16)
    quarter, w_early = barrier((quarter, w_early))

    sends = [
        jnp.concatenate([chunk(quarter[:64], x + d, 16), chunk(quarter[64:], x + d, 16)], axis=0) for d in range(4)
    ]
    own = (add(spread(sends, "x")) * (1.0 / TOKENS)).astype(BF16)
    quarter = jnp.concatenate(spread([own] * 4, "x"), axis=0)
    quarter, w_late = barrier((quarter, w_late))
    w_late = exchange(*w_late)
    parts = spread([quarter] * 4, "y")

    twice = call(twice_kernel, pos, (mine,), [whole(mine)], [shape(256, 2560)], [], flops=60_000_000_000)[0]

    def invert_side(operands):
        pos, twice, _ = operands
        both = lax.all_to_all(twice, "c", 0, 0, tiled=True)
        return call(
            factor_kernel, pos, (both,), [whole(both)], [shape(2, 1024, 384)],
            [VMEM((256, 2560), BF16), VMEM((2, 2, BLK, BLK), F32), VMEM((2, 1024, 1024), BF16)],
        )[0]

    factor = lax.cond(
        always, invert_side, lambda operands: jnp.zeros((2, 1024, 384), BF16), (pos, twice, parts[0])
    )
    block = rows // BLK
    rights = []
    for layer, pair in enumerate((w_early[0], w_late[0])):
        mids = [(w_early[1], part(rows, 0))] if layer == 0 else [
            (w_early[1], part(BLK, n)) for n in range(block, 2 * block - 1)
        ] + [(w_late[1], whole(w_late[1]))]
        rights.append(call(
            right_kernel, pos, (weight_grad, pair, factor, *(m[0] for m in mids)),
            [of_layer(weight_grad, layer), whole(pair), of_layer(factor, layer), *(m[1] for m in mids)],
            [shape(rows, width)], [],
        )[0])
    return call(
        left_kernel, pos, (*parts, *rights), [whole(a) for a in (*parts, *rights)],
        [shape(*weight_grad.shape)],
        [
            VMEM((2, 256, LANES), BF16), VMEM((2, 3, BLK, BLK), F32), VMEM((6, BLK, width), BF16),
            pltpu.SemaphoreType.DMA((6,)),
        ],
        out_specs=[ANYWHERE],
    )[0]


def solution(mesh):
    fine = Mesh(mesh.devices.reshape(4, 4, 8, 2), ("y", "x", "z", "c"))
    dp, owner = ("y", "x"), ("z", "c")
    in_specs = (P(None, dp, None), P(None, dp, owner), P(None, owner, dp))
    out_specs = P(None, owner, dp)
    return jax.shard_map(body, mesh=fine, in_specs=in_specs, out_specs=out_specs, check_vma=False)
```

time: 253 us -> 119 us (0.47)
  the two profiles are of different devices: /device:TPU:1 before, /device:TPU:200 now
where the time goes in v8:
time: 119 us; the launch traced here: 118 us
  Pallas kernels  43.9 us (37%)
  starting transfers between devices  36.2 us (30%)
  waiting for transfers between devices  18.4 us (15%)
  blocking collectives  16.2 us (14%)
  other arithmetic  1.57 us (1%)
  local copies, waits for them, and re-layouts  1.46 us (1%)
    pallas_call x11, Pallas kernels, call(): pl.pallas_call(kernel, grid_spec=pltpu.PrefetchScalarGridSpec(num_scalar_...  43.9 us
    ppermute x12, starting transfers between devices, spread(): lax.ppermute(parts[d], axis, [(i, (i + d) % 4) for i in range(4)])  18.6 us
    ppermute x12, waiting for transfers between devices, spread(): lax.ppermute(parts[d], axis, [(i, (i + d) % 4) for i in range(4)])  12.2 us
    all_to_all x1, blocking collectives, sum_side(): side = lax.all_to_all(side, 'x', 0, 0, tiled=True)  10.3 us
    all_to_all x1, starting transfers between devices, body(): mine = lax.all_to_all(side, 'z', 0, 0, tiled=True)  6.3 us
    ppermute x2, waiting for transfers between devices, exchange(): pair = lax.ppermute(w, 'x', [(0, 1), (1, 0), (2, 3), (3, 2)])  5.96 us
    all_to_all x1, blocking collectives, invert_side(): both = lax.all_to_all(twice, 'c', 0, 0, tiled=True)  5.92 us
    all_to_all x1, starting transfers between devices, blocks(): return (lax.all_to_all(side, 'y', 0, 0, tiled=True), *w_late, *covs)  4.91 us
  transfers between devices with their start and end apart: 18, of which 7 were waited for; matrix products, arithmetic and copies ran while one was open for 1% of the time, Pallas kernels for 27%

profile of v8, /device:TPU:200, one launch (start us, length us, event | category | flops | bytes accessed | tf_op | source)
XLA Modules:
  0.0 118.0 jit_solution(981932524394013480)
XLA Ops:
  0.0 0.1 stack.27.pos
  0.1 3.3 %shard_map.39 = (bf16[1536,384]{1,0:T(8,128)(2,1)}, bf16[2560,256]{1,0:T(8,128)(2,1)}) custom-call(s32[6]{0:T(128)S(1)} %stack.27.pos, bf16[2,1536,384]{2,1,0:T(8,128)(2,1)} %w_own.3), custom_call_target="tpu_custom_call" | custom-call | tf_op jit(solution)/shard_map/pallas_call | solution.py:211
  3.4 0.7 collective-permute-start.4
  4.1 4.2 %collective-permute-start.3 = (bf16[1536,384]{1,0:T(8,128)(2,1)}, bf16[1536,384]{1,0:T(8,128)(2,1)S(1)}, u32[]{:S(2)}, u32[]{:S(2)}) collective-permute-start(bf16[1536,384]{1,0:T(8,128)(2,1)} %get-tuple-element.69), channel_id=1, source_target_pairs={{0,16},{16,0},{32,48},{48,32},{1,17},{17,1},{33,49},{49,33},{2,18}... | collective-permute-start | bytes 3538952 | tf_op jit(solution)/shard_map/ppermute | solution.py:259
  8.4 18.5 %conditional.3 = (bf16[128,1920]{1,0:T(8,128)(2,1)}, bf16[1536,384]{1,0:T(8,128)(2,1)}, bf16[512,256]{1,0:T(8,128)(2,1)}, bf16[128,1920]{1,0:T(8,128)(2,1)S(1)},...) conditional(s32[]{:T(128)} %convert_element_type.35, () %tuple.28, ...), branch_computations={%region_0.1_spmd, %region_1.2_spmd} | conditional | flops 15000000512 | bytes 3899462 | solution.py:294
  8.4 6.4 %branch_1_fun.6 = bf16[128,1920]{1,0:T(8,128)(2,1)} custom-call(s32[6]{0:T(128)S(1)} %get-tuple-element.26.pos, bf16[2,256,6144]{2,1,0:T(8,128)(2,1)} %get-tuple-element.81.acts), custom_call_target="tpu_custom_call" | custom-call | tf_op jit(solution)/shard_map/cond/branch_1_fun/pallas_call | solution.py:211
  14.7 4.9 %all-to-all-start = ((bf16[4,32,1920]{2,1,0:T(8,128)(2,1)}), bf16[4,32,1920]{2,1,0:T(8,128)(2,1)}, u32[]{:S(2)}, u32[]{:S(2)}) async-start(bf16[4,32,1920]{2,1,0:T(8,128)(2,1)} %bitcast.17), calls=%async_computation | async-start | bytes 983040 | tf_op jit(solution)/shard_map/cond/branch_1_fun/all_to_all | solution.py:290
  19.7 4.0 %branch_1_fun.8 = (bf16[128,1920]{1,0:T(8,128)(2,1)S(1)}, bf16[128,1920]{1,0:T(8,128)(2,1)}, bf16[128,1920]{1,0:T(8,128)(2,1)}, bf16[128,1920]{1,0:T(8,128)(2,1)}) custom-call(s32[6]{0:T(128)S(1)} %get-tuple-element.26.pos, bf16[2,256,1536]{2,1,0:T(8,128)(2,1)} %get-tuple-element.82.grads), custom_call_target="tpu_custom_call" | custom-call | flops 10000000000 | tf_op jit(solution)/shard_map/cond/branch_1_fun/pallas_call | solution.py:211
  23.6 3.0 %branch_1_fun.7 = (bf16[1536,384]{1,0:T(8,128)(2,1)}, bf16[512,256]{1,0:T(8,128)(2,1)}) custom-call(s32[6]{0:T(128)S(1)} %get-tuple-element.26.pos, bf16[2,1536,384]{2,1,0:T(8,128)(2,1)} %get-tuple-element.29.w), custom_call_target="tpu_custom_call" | custom-call | flops 5000000000 | tf_op jit(solution)/shard_map/cond/branch_1_fun/pallas_call | solution.py:211
  26.7 0.2 all-to-all-done
  26.9 1.3 %collective-permute-start = (bf16[128,1920]{1,0:T(8,128)(2,1)}, bf16[128,1920]{1,0:T(8,128)(2,1)S(1)}, u32[]{:S(2)}, u32[]{:S(2)}) collective-permute-start(bf16[128,1920]{1,0:T(8,128)(2,1)} %get-tuple-element.61), channel_id=1, source_target_pairs={{0,64},{64,128},{128,192},{192,0},{1,65},{65,129},{129,193},{193,1... | collective-permute-start | bytes 1474568 | tf_op jit(solution)/shard_map/ppermute | solution.py:251
  28.2 2.2 %collective-permute-start.1 = (bf16[128,1920]{1,0:T(8,128)(2,1)}, bf16[128,1920]{1,0:T(8,128)(2,1)}, u32[]{:S(2)}, u32[]{:S(2)}) collective-permute-start(bf16[128,1920]{1,0:T(8,128)(2,1)} %get-tuple-element.62), channel_id=1, source_target_pairs={{0,128},{64,192},{128,0},{192,64},{1,129},{65,193},{129,1},{193,65... | collective-permute-start | bytes 1474568 | tf_op jit(solution)/shard_map/ppermute | solution.py:251
  30.4 1.0 collective-permute-start.2
  31.4 13.5 %conditional.4 = (bf16[128,2560]{1,0:T(8,128)(2,1)}) conditional(s32[]{:T(128)} %convert_element_type.35, () %tuple.30, (s32[6]{0:T(128)S(1)}, bf16[128,1920]{1,0:T(8,128)(2,1)}) %tuple.31), branch_computations={%region_2.3_spmd, %region_3.4_spmd} | conditional | bytes 983048 | solution.py:307
  31.4 1.6 %branch_1_fun.9 = bf16[128,1920]{1,0:T(8,128)(2,1)S(1)} custom-call(s32[6]{0:T(128)S(1)} %get-tuple-element.37.pos, bf16[128,1920]{1,0:T(8,128)(2,1)} %get-tuple-element.38.parts), custom_call_target="tpu_custom_call" | custom-call | tf_op jit(solution)/shard_map/cond/branch_1_fun/pallas_call | solution.py:211
  33.1 10.3 %all_to_all.36 = bf16[4,32,1920]{2,1,0:T(8,128)(2,1)S(1)} all-to-all(bf16[4,32,1920]{2,1,0:T(8,128)(2,1)S(1)} %bitcast.15), channel_id=1, replica_groups=mesh['y'=4,'x'=4,'z'=8,'c'=2] {'x'}, dimensions={0} | all-to-all | bytes 983040 | tf_op jit(solution)/shard_map/cond/branch_1_fun/all_to_all | solution.py:304
  43.4 1.5 %branch_1_fun.10 = bf16[128,2560]{1,0:T(8,128)(2,1)} custom-call(s32[6]{0:T(128)S(1)} %get-tuple-element.37.pos, bf16[128,1920]{1,0:T(8,128)(2,1)S(1)} %bitcast.16), custom_call_target="tpu_custom_call" | custom-call | tf_op jit(solution)/shard_map/cond/branch_1_fun/pallas_call | solution.py:211
  44.9 6.3 %all-to-all-start.3 = ((bf16[8,16,2560]{2,1,0:T(8,128)(2,1)}), bf16[8,16,2560]{2,1,0:T(8,128)(2,1)}, u32[]{:S(2)}, u32[]{:S(2)}) async-start(bf16[8,16,2560]{2,1,0:T(8,128)(2,1)} %bitcast.12), calls=%async_computation.3 | async-start | bytes 1310720 | tf_op jit(solution)/shard_map/all_to_all | solution.py:308
  51.2 0.0 collective-permute-done
  51.2 0.0 collective-permute-done.1
  51.2 0.4 collective-permute-done.2
  51.6 1.4 %add_convert_fusion = bf16[128,1920]{1,0:T(8,128)(2,1)S(1)} fusion(bf16[128,1920]{1,0:T(8,128)(2,1)} %collective-permute-done.2, bf16[128,1920]{1,0:T(8,128)(2,1)} %collective-permute-done.1, bf16[128,1920]{1,0:T(8,128)(2,1)S(1)} %collective-permute-done, bf16[128,1920]{1,0:T(8,128)(2,1)S(1)} %get-tuple-element.65), kind=kLoop, calls=%fused_computation | loop fusion | flops 1966080 | bytes 2457600 | tf_op jit(solution)/shard_map/convert_element_type | solution.py:310
  53.0 0.0 collective-permute-done.3.w_pair
  53.0 0.0 copy-start
  53.1 0.0 collective-permute-done.4.refs_0_.refs_1_
  53.1 0.1 constant_dynamic-slice_fusion.6
  53.2 0.7 collective-permute-start.5
  53.9 2.1 %collective-permute-start.6 = (bf16[32,1920]{1,0:T(8,128)(2,1)S(1)}, bf16[32,1920]{1,0:T(8,128)(2,1)S(1)}, u32[]{:S(2)}, u32[]{:S(2)}) collective-permute-start(bf16[32,1920]{1,0:T(8,128)(2,1)S(1)} %pad_maximum_fusion.2), channel_id=1, source_target_pairs={{0,32},{16,48},{32,0},{48,16},{1,33},{17,49},{33,1},{49,17},{2,34}... | collective-permute-start | bytes 368648 | tf_op jit(solution)/shard_map/ppermute | solution.py:251
  56.0 0.0 copy-done
  56.0 1.3 %collective-permute-start.7 = (bf16[32,1920]{1,0:T(8,128)(2,1)S(1)}, bf16[32,1920]{1,0:T(8,128)(2,1)S(1)}, u32[]{:S(2)}, u32[]{:S(2)}) collective-permute-start(bf16[32,1920]{1,0:T(8,128)(2,1)S(1)} %pad_maximum_fusion.3), channel_id=1, source_target_pairs={{0,48},{16,0},{32,16},{48,32},{1,49},{17,1},{33,17},{49,33},{2,50}... | collective-permute-start | bytes 368648 | tf_op jit(solution)/shard_map/ppermute | solution.py:251
  57.2 4.5 %collective-permute-done.5 = bf16[32,1920]{1,0:T(8,128)(2,1)S(1)} collective-permute-done((bf16[32,1920]{1,0:T(8,128)(2,1)S(1)}, bf16[32,1920]{1,0:T(8,128)(2,1)S(1)}, u32[]{:S(2)}, u32[]{:S(2)}) %collective-permute-start.5) | collective-permute-done | bytes 122912 | tf_op jit(solution)/shard_map/ppermute | solution.py:251
  61.8 0.0 collective-permute-done.6
  61.8 0.7 collective-permute-done.7
  62.4 0.1 multiply_convert_fusion
  62.5 2.8 %collective-permute-start.10 = (bf16[32,1920]{1,0:T(8,128)(2,1)S(1)}, bf16[32,1920]{1,0:T(8,128)(2,1)S(1)}, u32[]{:S(2)}, u32[]{:S(2)}) collective-permute-start(bf16[32,1920]{1,0:T(8,128)(2,1)S(1)} %multiply_convert_fusion), channel_id=1, source_target_pairs={{0,48},{16,0},{32,16},{48,32},{1,49},{17,1},{33,17},{49,33},{2,50}... | collective-permute-start | bytes 368648 | tf_op jit(solution)/shard_map/ppermute | solution.py:251
  65.3 0.0 collective-permute-start.8
  65.3 1.6 %collective-permute-start.9 = (bf16[32,1920]{1,0:T(8,128)(2,1)S(1)}, bf16[32,1920]{1,0:T(8,128)(2,1)S(1)}, u32[]{:S(2)}, u32[]{:S(2)}) collective-permute-start(bf16[32,1920]{1,0:T(8,128)(2,1)S(1)} %multiply_convert_fusion), channel_id=1, source_target_pairs={{0,32},{16,48},{32,0},{48,16},{1,33},{17,49},{33,1},{49,17},{2,34}... | collective-permute-start | bytes 368648 | tf_op jit(solution)/shard_map/ppermute | solution.py:251
  66.8 0.9 collective-permute-done.10
  67.7 5.7 %collective-permute-done.8 = bf16[32,1920]{1,0:T(8,128)(2,1)S(1)} collective-permute-done((bf16[32,1920]{1,0:T(8,128)(2,1)S(1)}, bf16[32,1920]{1,0:T(8,128)(2,1)S(1)}, u32[]{:S(2)}, u32[]{:S(2)}) %collective-permute-start.8) | collective-permute-done | bytes 122912 | tf_op jit(solution)/shard_map/ppermute | solution.py:251
  73.4 0.0 collective-permute-done.9
  73.4 0.1 collective-permute-start.11
  73.5 3.1 %collective-permute-start.12 = (bf16[128,1920]{1,0:T(8,128)(2,1)S(1)}, bf16[128,1920]{1,0:T(8,128)(2,1)}, u32[]{:S(2)}, u32[]{:S(2)}) collective-permute-start(bf16[128,1920]{1,0:T(8,128)(2,1)S(1)} %pad_maximum_fusion.p0), channel_id=1, source_target_pairs={{0,128},{64,192},{128,0},{192,64},{1,129},{65,193},{129,1},{193,65... | collective-permute-start | bytes 1474568 | tf_op jit(solution)/shard_map/ppermute | solution.py:251
  76.7 2.5 %collective-permute-start.13 = (bf16[128,1920]{1,0:T(8,128)(2,1)S(1)}, bf16[128,1920]{1,0:T(8,128)(2,1)}, u32[]{:S(2)}, u32[]{:S(2)}) collective-permute-start(bf16[128,1920]{1,0:T(8,128)(2,1)S(1)} %pad_maximum_fusion.p0), channel_id=1, source_target_pairs={{0,192},{64,0},{128,64},{192,128},{1,193},{65,1},{129,65},{193,129... | collective-permute-start | bytes 1474568 | tf_op jit(solution)/shard_map/ppermute | solution.py:251
  79.2 0.0 collective-permute-start.14
  79.2 1.4 %collective-permute-start.15 = (bf16[512,256]{1,0:T(8,128)(2,1)}, bf16[512,256]{1,0:T(8,128)(2,1)}, u32[]{:S(2)}, u32[]{:S(2)}) collective-permute-start(bf16[512,256]{1,0:T(8,128)(2,1)} %get-tuple-element.78), channel_id=1, source_target_pairs={{16,32},{32,16},{17,33},{33,17},{18,34},{34,18},{19,35},{35,19},{2... | collective-permute-start | bytes 786440 | tf_op jit(solution)/shard_map/ppermute | solution.py:260
  80.6 0.0 all-to-all-done.3
  80.6 2.8 %shard_map.40 = bf16[256,2560]{1,0:T(8,128)(2,1)} custom-call(s32[6]{0:T(128)S(1)} %stack.27.pos, bf16[128,2560]{1,0:T(8,128)(2,1)} %bitcast.13.a), custom_call_target="tpu_custom_call" | custom-call | flops 60000002048 | tf_op jit(solution)/shard_map/pallas_call | solution.py:211
  83.3 10.9 %conditional.5 = (bf16[2,1024,384]{2,1,0:T(8,128)(2,1)}) conditional(s32[]{:T(128)} %convert_element_type.35, () %tuple.35, (bf16[256,2560]{1,0:T(8,128)(2,1)}, s32[6]{0:T(128)S(1)}) %tuple.36), branch_computations={%region_4.5_spmd, %region_5.6_spmd} | conditional | bytes 2621448 | solution.py:332
  83.3 5.9 %all_to_all.37 = bf16[2,128,2560]{2,1,0:T(8,128)(2,1)S(1)} all-to-all(bf16[2,128,2560]{2,1,0:T(8,128)(2,1)} %bitcast.18), channel_id=1, replica_groups=mesh['y'=4,'x'=4,'z'=8,'c'=2] {'c'}, dimensions={0} | all-to-all | bytes 2621440 | tf_op jit(solution)/shard_map/cond/branch_1_fun/all_to_all | solution.py:326
  89.3 5.0 %branch_1_fun.11 = bf16[2,1024,384]{2,1,0:T(8,128)(2,1)} custom-call(s32[6]{0:T(128)S(1)} %get-tuple-element.39.pos, bf16[256,2560]{1,0:T(8,128)(2,1)S(1)} %bitcast.14), custom_call_target="tpu_custom_call" | custom-call | tf_op jit(solution)/shard_map/cond/branch_1_fun/pallas_call | solution.py:211
  94.2 0.0 copy-start.1
  94.2 1.3 %copy-done.1 = bf16[1536,384]{1,0:T(8,128)(2,1)S(1)} copy-done((bf16[1536,384]{1,0:T(8,128)(2,1)S(1)}, bf16[1536,384]{1,0:T(8,128)(2,1)}, u32[]{:S(2)}) %copy-start.1) | copy-done | bytes 1179672
  95.5 0.0 copy-start.2
  95.5 0.0 copy-start.3
  95.5 4.3 %shard_map.41.r0 = bf16[1536,384]{1,0:T(8,128)(2,1)S(1)} custom-call(s32[6]{0:T(128)S(1)} %stack.27.pos, bf16[2,1536,384]{2,1,0:T(8,128)(2,1)} %w_own.3, bf16[1536,384]{1,0:T(8,128)(2,1)S(1)} %copy-done.1, bf16[2,1024,384]{2,1,0:T(8,128)(2,1)} %get-tuple-element.112.factor, bf16[2560,256]{1,0:T(8,128)(2,1)S(1)} %collective-permute-done.4.refs_0_.refs_1_), custom_call_target="tpu_custom_call" | custom-call | tf_op jit(solution)/shard_map/pallas_call | solution.py:211
  99.8 0.0 collective-permute-done.15.refs_2_
  99.8 6.0 %collective-permute-done.14.w_pair = bf16[1536,384]{1,0:T(8,128)(2,1)S(1)} collective-permute-done((bf16[1536,384]{1,0:T(8,128)(2,1)}, bf16[1536,384]{1,0:T(8,128)(2,1)S(1)}, u32[]{:S(2)}, u32[]{:S(2)}) %collective-permute-start.14) | collective-permute-done | bytes 1179680 | tf_op jit(solution)/shard_map/ppermute | solution.py:259
  105.8 0.0 copy-done.2
  105.8 0.0 copy-done.3
  105.8 3.5 %shard_map.42.r1 = bf16[1536,384]{1,0:T(8,128)(2,1)S(1)} custom-call(s32[6]{0:T(128)S(1)} %stack.27.pos, bf16[2,1536,384]{2,1,0:T(8,128)(2,1)S(1)} %copy-done.2, bf16[1536,384]{1,0:T(8,128)(2,1)S(1)} %collective-permute-done.14.w_pair, bf16[2,1024,384]{2,1,0:T(8,128)(2,1)S(1)} %copy-done.3, bf16[2560,256]{1,0:T(8,128)(2,1)S(1)} %collective-permute-done.4.refs_0_.refs_1_, ...), custom_call_target="tpu_custom_call" | custom-call | tf_op jit(solution)/shard_map/pallas_call | solution.py:211
  109.3 0.0 collective-permute-done.11.p1
  109.3 0.0 collective-permute-done.12.p2
  109.3 0.0 collective-permute-done.13.p3
  109.3 8.6 %shard_map.43 = bf16[2,1536,384]{2,1,0:T(8,128)(2,1)} custom-call(s32[6]{0:T(128)S(1)} %stack.27.pos, bf16[128,1920]{1,0:T(8,128)(2,1)S(1)} %pad_maximum_fusion.p0, bf16[128,1920]{1,0:T(8,128)(2,1)S(1)} %collective-permute-done.11.p1, bf16[128,1920]{1,0:T(8,128)(2,1)} %collective-permute-done.12.p2, bf16[128,1920]{1,0:T(8,128)(2,1)} %collective-permute-done.13.p3, ...), custom_call_target="tpu_custom_call" | custom-call | tf_op jit(solution)/shard_map/pallas_call | solution.py:211
  (5 shorter events, 0.1 us)
Async XLA Ops:
  3.4 49.7 %collective-permute-start.4 = (bf16[2560,256]{1,0:T(8,128)(2,1)}, bf16[2560,256]{1,0:T(8,128)(2,1)S(1)}, u32[]{:S(2)}, u32[]{:S(2)}) collective-permute-start(bf16[2560,256]{1,0:T(8,128)(2,1)} %get-tuple-element.70), channel_id=1, source_target_pairs={{16,32},{32,16},{17,33},{33,17},{18,34},{34,18},{19,35},{35,19},{2... | collective-permute-start | bytes 3932168 | tf_op jit(solution)/shard_map/ppermute | solution.py:260
  4.1 48.9 %collective-permute-start.3 = (bf16[1536,384]{1,0:T(8,128)(2,1)}, bf16[1536,384]{1,0:T(8,128)(2,1)S(1)}, u32[]{:S(2)}, u32[]{:S(2)}) collective-permute-start(bf16[1536,384]{1,0:T(8,128)(2,1)} %get-tuple-element.69), channel_id=1, source_target_pairs={{0,16},{16,0},{32,48},{48,32},{1,17},{17,1},{33,49},{49,33},{2,18}... | collective-permute-start | bytes 3538952 | tf_op jit(solution)/shard_map/ppermute | solution.py:259
  14.7 12.1 %all-to-all-start = ((bf16[4,32,1920]{2,1,0:T(8,128)(2,1)}), bf16[4,32,1920]{2,1,0:T(8,128)(2,1)}, u32[]{:S(2)}, u32[]{:S(2)}) async-start(bf16[4,32,1920]{2,1,0:T(8,128)(2,1)} %bitcast.17), calls=%async_computation | async-start | bytes 983040 | tf_op jit(solution)/shard_map/cond/branch_1_fun/all_to_all | solution.py:290
  26.9 24.3 %collective-permute-start = (bf16[128,1920]{1,0:T(8,128)(2,1)}, bf16[128,1920]{1,0:T(8,128)(2,1)S(1)}, u32[]{:S(2)}, u32[]{:S(2)}) collective-permute-start(bf16[128,1920]{1,0:T(8,128)(2,1)} %get-tuple-element.61), channel_id=1, source_target_pairs={{0,64},{64,128},{128,192},{192,0},{1,65},{65,129},{129,193},{193,1... | collective-permute-start | bytes 1474568 | tf_op jit(solution)/shard_map/ppermute | solution.py:251
  28.2 23.0 %collective-permute-start.1 = (bf16[128,1920]{1,0:T(8,128)(2,1)}, bf16[128,1920]{1,0:T(8,128)(2,1)}, u32[]{:S(2)}, u32[]{:S(2)}) collective-permute-start(bf16[128,1920]{1,0:T(8,128)(2,1)} %get-tuple-element.62), channel_id=1, source_target_pairs={{0,128},{64,192},{128,0},{192,64},{1,129},{65,193},{129,1},{193,65... | collective-permute-start | bytes 1474568 | tf_op jit(solution)/shard_map/ppermute | solution.py:251
  30.4 21.2 %collective-permute-start.2 = (bf16[128,1920]{1,0:T(8,128)(2,1)}, bf16[128,1920]{1,0:T(8,128)(2,1)}, u32[]{:S(2)}, u32[]{:S(2)}) collective-permute-start(bf16[128,1920]{1,0:T(8,128)(2,1)} %get-tuple-element.63), channel_id=1, source_target_pairs={{0,192},{64,0},{128,64},{192,128},{1,193},{65,1},{129,65},{193,129... | collective-permute-start | bytes 1474568 | tf_op jit(solution)/shard_map/ppermute | solution.py:251
  44.9 35.6 %all-to-all-start.3 = ((bf16[8,16,2560]{2,1,0:T(8,128)(2,1)}), bf16[8,16,2560]{2,1,0:T(8,128)(2,1)}, u32[]{:S(2)}, u32[]{:S(2)}) async-start(bf16[8,16,2560]{2,1,0:T(8,128)(2,1)} %bitcast.12), calls=%async_computation.3 | async-start | bytes 1310720 | tf_op jit(solution)/shard_map/all_to_all | solution.py:308
  53.0 2.9 %copy-start = (bf16[1536,384]{1,0:T(8,128)(2,1)}, bf16[1536,384]{1,0:T(8,128)(2,1)S(1)}, u32[]{:S(2)}) copy-start(bf16[1536,384]{1,0:T(8,128)(2,1)S(1)} %collective-permute-done.3.w_pair) | copy-start | bytes 3538948
  53.2 8.6 %collective-permute-start.5 = (bf16[32,1920]{1,0:T(8,128)(2,1)S(1)}, bf16[32,1920]{1,0:T(8,128)(2,1)S(1)}, u32[]{:S(2)}, u32[]{:S(2)}) collective-permute-start(bf16[32,1920]{1,0:T(8,128)(2,1)S(1)} %pad_maximum_fusion.1), channel_id=1, source_target_pairs={{0,16},{16,32},{32,48},{48,0},{1,17},{17,33},{33,49},{49,1},{2,18}... | collective-permute-start | bytes 368648 | tf_op jit(solution)/shard_map/ppermute | solution.py:251
  53.9 7.9 %collective-permute-start.6 = (bf16[32,1920]{1,0:T(8,128)(2,1)S(1)}, bf16[32,1920]{1,0:T(8,128)(2,1)S(1)}, u32[]{:S(2)}, u32[]{:S(2)}) collective-permute-start(bf16[32,1920]{1,0:T(8,128)(2,1)S(1)} %pad_maximum_fusion.2), channel_id=1, source_target_pairs={{0,32},{16,48},{32,0},{48,16},{1,33},{17,49},{33,1},{49,17},{2,34}... | collective-permute-start | bytes 368648 | tf_op jit(solution)/shard_map/ppermute | solution.py:251
  56.0 6.5 %collective-permute-start.7 = (bf16[32,1920]{1,0:T(8,128)(2,1)S(1)}, bf16[32,1920]{1,0:T(8,128)(2,1)S(1)}, u32[]{:S(2)}, u32[]{:S(2)}) collective-permute-start(bf16[32,1920]{1,0:T(8,128)(2,1)S(1)} %pad_maximum_fusion.3), channel_id=1, source_target_pairs={{0,48},{16,0},{32,16},{48,32},{1,49},{17,1},{33,17},{49,33},{2,50}... | collective-permute-start | bytes 368648 | tf_op jit(solution)/shard_map/ppermute | solution.py:251
  62.5 5.2 %collective-permute-start.10 = (bf16[32,1920]{1,0:T(8,128)(2,1)S(1)}, bf16[32,1920]{1,0:T(8,128)(2,1)S(1)}, u32[]{:S(2)}, u32[]{:S(2)}) collective-permute-start(bf16[32,1920]{1,0:T(8,128)(2,1)S(1)} %multiply_convert_fusion), channel_id=1, source_target_pairs={{0,48},{16,0},{32,16},{48,32},{1,49},{17,1},{33,17},{49,33},{2,50}... | collective-permute-start | bytes 368648 | tf_op jit(solution)/shard_map/ppermute | solution.py:251
  65.3 8.1 %collective-permute-start.8 = (bf16[32,1920]{1,0:T(8,128)(2,1)S(1)}, bf16[32,1920]{1,0:T(8,128)(2,1)S(1)}, u32[]{:S(2)}, u32[]{:S(2)}) collective-permute-start(bf16[32,1920]{1,0:T(8,128)(2,1)S(1)} %multiply_convert_fusion), channel_id=1, source_target_pairs={{0,16},{16,32},{32,48},{48,0},{1,17},{17,33},{33,49},{49,1},{2,18}... | collective-permute-start | bytes 368648 | tf_op jit(solution)/shard_map/ppermute | solution.py:251
  65.3 8.1 %collective-permute-start.9 = (bf16[32,1920]{1,0:T(8,128)(2,1)S(1)}, bf16[32,1920]{1,0:T(8,128)(2,1)S(1)}, u32[]{:S(2)}, u32[]{:S(2)}) collective-permute-start(bf16[32,1920]{1,0:T(8,128)(2,1)S(1)} %multiply_convert_fusion), channel_id=1, source_target_pairs={{0,32},{16,48},{32,0},{48,16},{1,33},{17,49},{33,1},{49,17},{2,34}... | collective-permute-start | bytes 368648 | tf_op jit(solution)/shard_map/ppermute | solution.py:251
  73.4 35.8 %collective-permute-start.11 = (bf16[128,1920]{1,0:T(8,128)(2,1)S(1)}, bf16[128,1920]{1,0:T(8,128)(2,1)S(1)}, u32[]{:S(2)}, u32[]{:S(2)}) collective-permute-start(bf16[128,1920]{1,0:T(8,128)(2,1)S(1)} %pad_maximum_fusion.p0), channel_id=1, source_target_pairs={{0,64},{64,128},{128,192},{192,0},{1,65},{65,129},{129,193},{193,1... | collective-permute-start | bytes 1474568 | tf_op jit(solution)/shard_map/ppermute | solution.py:251
  73.5 35.7 %collective-permute-start.12 = (bf16[128,1920]{1,0:T(8,128)(2,1)S(1)}, bf16[128,1920]{1,0:T(8,128)(2,1)}, u32[]{:S(2)}, u32[]{:S(2)}) collective-permute-start(bf16[128,1920]{1,0:T(8,128)(2,1)S(1)} %pad_maximum_fusion.p0), channel_id=1, source_target_pairs={{0,128},{64,192},{128,0},{192,64},{1,129},{65,193},{129,1},{193,65... | collective-permute-start | bytes 1474568 | tf_op jit(solution)/shard_map/ppermute | solution.py:251
  76.7 32.6 %collective-permute-start.13 = (bf16[128,1920]{1,0:T(8,128)(2,1)S(1)}, bf16[128,1920]{1,0:T(8,128)(2,1)}, u32[]{:S(2)}, u32[]{:S(2)}) collective-permute-start(bf16[128,1920]{1,0:T(8,128)(2,1)S(1)} %pad_maximum_fusion.p0), channel_id=1, source_target_pairs={{0,192},{64,0},{128,64},{192,128},{1,193},{65,1},{129,65},{193,129... | collective-permute-start | bytes 1474568 | tf_op jit(solution)/shard_map/ppermute | solution.py:251
  79.2 26.6 %collective-permute-start.14 = (bf16[1536,384]{1,0:T(8,128)(2,1)}, bf16[1536,384]{1,0:T(8,128)(2,1)S(1)}, u32[]{:S(2)}, u32[]{:S(2)}) collective-permute-start(bf16[1536,384]{1,0:T(8,128)(2,1)} %get-tuple-element.77), channel_id=1, source_target_pairs={{0,16},{16,0},{32,48},{48,32},{1,17},{17,1},{33,49},{49,33},{2,18}... | collective-permute-start | bytes 3538952 | tf_op jit(solution)/shard_map/ppermute | solution.py:259
  79.2 20.6 %collective-permute-start.15 = (bf16[512,256]{1,0:T(8,128)(2,1)}, bf16[512,256]{1,0:T(8,128)(2,1)}, u32[]{:S(2)}, u32[]{:S(2)}) collective-permute-start(bf16[512,256]{1,0:T(8,128)(2,1)} %get-tuple-element.78), channel_id=1, source_target_pairs={{16,32},{32,16},{17,33},{33,17},{18,34},{34,18},{19,35},{35,19},{2... | collective-permute-start | bytes 786440 | tf_op jit(solution)/shard_map/ppermute | solution.py:260
  94.2 1.3 %copy-start.1 = (bf16[1536,384]{1,0:T(8,128)(2,1)S(1)}, bf16[1536,384]{1,0:T(8,128)(2,1)}, u32[]{:S(2)}) copy-start(bf16[1536,384]{1,0:T(8,128)(2,1)} %copy-done) | copy-start | bytes 3538948
  95.5 10.3 %copy-start.2 = (bf16[2,1536,384]{2,1,0:T(8,128)(2,1)S(1)}, bf16[2,1536,384]{2,1,0:T(8,128)(2,1)}, u32[]{:S(2)}) copy-start(bf16[2,1536,384]{2,1,0:T(8,128)(2,1)} %w_own.3) | copy-start | bytes 7077892
  95.5 10.3 %copy-start.3 = (bf16[2,1024,384]{2,1,0:T(8,128)(2,1)S(1)}, bf16[2,1024,384]{2,1,0:T(8,128)(2,1)}, u32[]{:S(2)}) copy-start(bf16[2,1024,384]{2,1,0:T(8,128)(2,1)} %get-tuple-element.112.factor) | copy-start | bytes 4718596

commit v9 on v8

--- a/solution.py
+++ b/solution.py
@@ -25,9 +25,19 @@
     return lax.dot_general(a, b, (((1,), (0,)), ((), ())), preferred_element_type=F32)
 
 
-def relay(copies, sems):
-    loads = [pltpu.make_async_copy(a, b, sems.at[0, n]) for n, (a, b, _) in enumerate(copies)]
-    stores = [pltpu.make_async_copy(b, c, sems.at[1, n]) for n, (_, b, c) in enumerate(copies)]
+def middle(pos):
+    return pl.ds(pl.multiple_of(jnp.where(pos[0] == 1, SUB, 0), SUB), 256)
+
+
+def late_kernel(pos, w, rest, out, mid, held_rest, held, held_mid, sems):
+    size = rest.shape[0]
+    sources = (
+        (w.at[0, pl.ds(w.shape[1] - size, size)], held_rest, rest),
+        (w.at[1], held, out),
+        (w.at[1, :, middle(pos)], held_mid, mid),
+    )
+    loads = [pltpu.make_async_copy(a, b, sems.at[0, n]) for n, (a, b, _) in enumerate(sources)]
+    stores = [pltpu.make_async_copy(b, c, sems.at[1, n]) for n, (_, b, c) in enumerate(sources)]
     for load in loads:
         load.start()
     for load, store in zip(loads, stores):
@@ -35,24 +45,6 @@
         store.start()
     for store in stores:
         store.wait()
-
-
-def middle(pos):
-    return pl.ds(pl.multiple_of(jnp.where(pos[0] == 1, SUB, 0), SUB), 256)
-
-
-def early_kernel(pos, w, whole0, mid0, held, held_mid, sems):
-    full, rest = w.shape[1], w.shape[1] - BLK
-    relay([
-        (w.at[0], held, whole0),
-        (w.at[0, :, middle(pos)], held_mid.at[pl.ds(0, full)], mid0.at[pl.ds(0, full)]),
-        (w.at[1, pl.ds(0, rest), middle(pos)], held_mid.at[pl.ds(full, rest)], mid0.at[pl.ds(full, rest)]),
-    ], sems)
-
-
-def late_kernel(pos, w, whole1, mid1, held, held_mid, sems):
-    rest = w.shape[1] - BLK
-    relay([(w.at[1], held, whole1), (w.at[1, pl.ds(rest, BLK), middle(pos)], held_mid, mid1)], sems)
 
 
 def cov_kernel(pos, grads, h0, h1, h2, h3, pack):
@@ -75,8 +67,23 @@
         send[64:128, :] = pack[1, pl.ds(at, 64), :]
 
 
-def side_kernel(pos, acts, out):
-    part = pos[3]
+def side_kernel(pos, acts, w, out, early, mid, held, held_mid, sems):
+    part, step = pos[3], pl.program_id(0)
+    sources = (w.at[0, pl.ds(0, early.shape[0])], held, early), (w.at[0, :, middle(pos)], held_mid, mid)
+    loads = [pltpu.make_async_copy(a, b, sems.at[0, n]) for n, (a, b, _) in enumerate(sources)]
+    stores = [pltpu.make_async_copy(b, c, sems.at[1, n]) for n, (_, b, c) in enumerate(sources)]
+
+    @pl.when(step == 0)
+    def _():
+        for load in loads:
+            load.start()
+
+    @pl.when(step == 2)
+    def _():
+        for load, store in zip(loads, stores):
+            load.wait()
+            store.start()
+
     k = lax.broadcasted_iota(jnp.int32, (BLK, 64), 0)
     m = lax.broadcasted_iota(jnp.int32, (BLK, 64), 1)
     select = jnp.where(k == m // 16 * SUB + part * 16 + m % 16, 1.0, 0.0).astype(BF16)
@@ -88,6 +95,11 @@
             s = 10 * b + i
             at = s // 15 * 16
             out[at:at + 16, s % 15 * SUB:(s % 15 + 1) * SUB] = cov[r * 16:(r + 1) * 16, c * SUB:(c + 1) * SUB]
+
+    @pl.when(step == 3)
+    def _():
+        for store in stores:
+            store.wait()
 
 
 def total_kernel(pos, parts, out):
@@ -142,17 +154,12 @@
     return nn_dot(iterate, residue).astype(BF16)
 
 
-def twice_kernel(pos, a, out):
-    out[0:128, :] = a[...]
-    out[128:256, :] = a[...]
-
-
-def factor_kernel(pos, both, out, pack, full, diag):
-    x = pos[0]
+def factor_kernel(pos, mine, other, out, pack, full, diag):
+    x, core = pos[0], pos[2]
     for z in range(8):
-        for core in range(2):
-            rows = 128 * core + 16 * z
-            pack[32 * z + 16 * core:32 * z + 16 * core + 16, :] = both[rows:rows + 16, :]
+        rows = slice(16 * z, 16 * z + 16)
+        pack[pl.ds(pl.multiple_of(32 * z + core * 16, 16), 16), :] = mine[rows, :]
+        pack[pl.ds(pl.multiple_of(32 * z + 16 - core * 16, 16), 16), :] = other[rows, :]
     base = x // 2 * BLK
     own = pl.multiple_of(x * 384 - base, SUB)
     pair = pl.multiple_of((x + 1 - 2 * (x % 2)) * 384 - base, SUB)
@@ -172,15 +179,15 @@
         out[layer, 768:1024, :] = diag[layer, pl.ds(mid, 256), columns]
 
 
-def right_kernel(pos, w_own, w_pair, factor, *refs):
+def right_kernel(pos, w_own, w_mid, factor, *refs):
     out, at = refs[-1], 0
-    for mid in refs[:-1]:
-        rows = slice(at, at + mid.shape[0])
+    for pair in refs[:-1]:
+        rows = slice(at, at + pair.shape[0])
         total = nn_dot(w_own[0, rows, :], factor[0, 0:384, :])
-        total += nn_dot(w_pair[rows, :], factor[0, 384:768, :])
-        total += nn_dot(mid[...], factor[0, 768:1024, :])
+        total += nn_dot(pair[...], factor[0, 384:768, :])
+        total += nn_dot(w_mid[rows, :], factor[0, 768:1024, :])
         out[rows, :] = total.astype(BF16)
-        at += mid.shape[0]
+        at += pair.shape[0]
 
 
 def left_kernel(pos, p0, p1, p2, p3, r0, r1, out, pack, full, ready, sems):
@@ -235,10 +242,6 @@
     return pl.BlockSpec((1,) + a.shape[1:], lambda i, p: (layer, 0, 0), pipeline_mode=ONCE)
 
 
-def part(rows, n):
-    return pl.BlockSpec((rows, 256), lambda i, p: (n, 0), pipeline_mode=ONCE)
-
-
 def shape(*dims):
     return jax.ShapeDtypeStruct(dims, BF16)
 
@@ -255,9 +258,12 @@
     return lax.dynamic_slice_in_dim(a, index % 4 * rows, rows, 0)
 
 
-def exchange(w, middle):
-    pair = lax.ppermute(w, "x", [(0, 1), (1, 0), (2, 3), (3, 2)])
-    return [pair, lax.ppermute(middle, "x", [(1, 2), (2, 1)])]
+def paired(w):
+    return lax.ppermute(w, "x", [(0, 1), (1, 0), (2, 3), (3, 2)])
+
+
+def crossed(w):
+    return lax.ppermute(w, "x", [(1, 2), (2, 1)])
 
 
 def body(acts, grads_out, weight_grad):
@@ -266,83 +272,71 @@
     rows, width = weight_grad.shape[1:]
     barrier = lax.optimization_barrier
 
-    def relayed(kernel, w, *shapes, **options):
-        return call(
-            kernel, pos, (w,), [ANYWHERE], list(shapes),
-            [VMEM(a.shape, BF16) for a in shapes] + [pltpu.SemaphoreType.DMA((2, 3))],
-            out_specs=[ANYWHERE] * 2, vmem=60, **options,
+    early, rest, mid = shape(rows - BLK, width), shape(BLK, width), shape(rows, 256)
+    side, *own = call(
+        side_kernel, pos, (acts, weight_grad),
+        [pl.BlockSpec((1, acts.shape[1], 3 * BLK), lambda i, p: (p[4], 0, i)), ANYWHERE],
+        [shape(128, LANES), early, mid],
+        [VMEM(early.shape, BF16), VMEM(mid.shape, BF16), pltpu.SemaphoreType.DMA((2, 2))],
+        out_specs=[pl.BlockSpec((32, LANES), lambda i, p: (i, 0)), ANYWHERE, ANYWHERE], vmem=60, grid=4,
+    )
+    pair0, mid0 = paired(own[0]), crossed(own[1])
+    side, grads_out = barrier((side, grads_out))
+    side = lax.all_to_all(side, "y", 0, 0, tiled=True)
+
+    covs = call(
+        cov_kernel, pos, (grads_out,), [whole(grads_out)], [shape(128, LANES)] * 4,
+        [VMEM((2, 256, LANES), BF16)], vmem=60, flops=12_000_000_000,
+    )
+    start = covs[0]
+    covs = spread(covs, "y")
+    side, pair0, mid0 = barrier((side, pair0, mid0))
+    side = call(total_kernel, pos, (side,), [whole(side)], [shape(128, LANES)], [], flops=60_000_000_000)[0]
+
+    def sum_side(operands):
+        pos, side, weight_grad, _ = operands
+        side = lax.all_to_all(side, "x", 0, 0, tiled=True)
+        late = [rest, shape(rows, width), mid]
+        late = call(
+            late_kernel, pos, (weight_grad,), [ANYWHERE], late,
+            [VMEM(a.shape, BF16) for a in late] + [pltpu.SemaphoreType.DMA((2, 3))],
+            out_specs=[ANYWHERE] * 3, vmem=60, flops=4_000_000_000,
         )
-
-    w_early = exchange(*relayed(early_kernel, weight_grad, shape(rows, width), shape(2 * rows - BLK, 256)))
-
-    def blocks(operands):
-        pos, acts, grads_out, weight_grad = operands
-        side = call(
-            side_kernel, pos, (acts,),
-            [pl.BlockSpec((1, acts.shape[1], 3 * BLK), lambda i, p: (p[4], 0, i))],
-            [shape(128, LANES)], [], out_specs=[pl.BlockSpec((32, LANES), lambda i, p: (i, 0))], vmem=60, grid=4,
-        )[0]
-        covs = call(
-            cov_kernel, pos, (grads_out,), [whole(grads_out)], [shape(128, LANES)] * 4,
-            [VMEM((2, 256, LANES), BF16)], vmem=60, flops=10_000_000_000,
-        )
-        w_late = relayed(late_kernel, weight_grad, shape(rows, width), shape(BLK, 256), flops=5_000_000_000)
-        return lax.all_to_all(side, "y", 0, 0, tiled=True), *w_late, *covs
-
-    always = x + y + z + c < 64
-    late = (rows, width), (BLK, 256)
-    side, *covs = lax.cond(
-        always, blocks, lambda operands: tuple(jnp.zeros(n, BF16) for n in ((128, LANES), *late, *((128, LANES),) * 4)),
-        (pos, acts, grads_out, weight_grad),
-    )
-    w_late, covs = covs[:2], covs[2:]
-    covs = spread(covs, "y")
-
-    def sum_side(operands):
-        pos, side, _ = operands
-        side = call(total_kernel, pos, (side,), [whole(side)], [shape(128, LANES)], [])[0]
-        side = lax.all_to_all(side, "x", 0, 0, tiled=True)
-        return call(chosen_kernel, pos, (side,), [whole(side)], [shape(128, 2560)], [])[0]
-
-    side = lax.cond(always, sum_side, lambda operands: jnp.zeros((128, 2560), BF16), (pos, side, covs[0]))
+        return call(chosen_kernel, pos, (side,), [whole(side)], [shape(128, 2560)], [])[0], *late
+
+    side, rest, pair1, mid1 = lax.cond(
+        x + y + z + c < 64, sum_side,
+        lambda operands: tuple(
+            jnp.zeros(n, BF16) for n in ((128, 2560), rest.shape, (rows, width), mid.shape)
+        ),
+        (pos, side, weight_grad, start),
+    )
+    rest = paired(rest)
     mine = lax.all_to_all(side, "z", 0, 0, tiled=True)
-    *covs, _ = barrier((*covs, side))
+    *covs, _, rest = barrier((*covs, side, rest))
     quarter = add(covs).astype(BF16)
-    quarter, w_early = barrier((quarter, w_early))
 
     sends = [
         jnp.concatenate([chunk(quarter[:64], x + d, 16), chunk(quarter[64:], x + d, 16)], axis=0) for d in range(4)
     ]
     own = (add(spread(sends, "x")) * (1.0 / TOKENS)).astype(BF16)
     quarter = jnp.concatenate(spread([own] * 4, "x"), axis=0)
-    quarter, w_late = barrier((quarter, w_late))
-    w_late = exchange(*w_late)
+    quarter, pair1, mid1, mine = barrier((quarter, pair1, mid1, mine))
+    pair1, mid1 = paired(pair1), crossed(mid1)
     parts = spread([quarter] * 4, "y")
-
-    twice = call(twice_kernel, pos, (mine,), [whole(mine)], [shape(256, 2560)], [], flops=60_000_000_000)[0]
-
-    def invert_side(operands):
-        pos, twice, _ = operands
-        both = lax.all_to_all(twice, "c", 0, 0, tiled=True)
-        return call(
-            factor_kernel, pos, (both,), [whole(both)], [shape(2, 1024, 384)],
-            [VMEM((256, 2560), BF16), VMEM((2, 2, BLK, BLK), F32), VMEM((2, 1024, 1024), BF16)],
+    other = lax.ppermute(mine, "c", [(0, 1), (1, 0)])
+    factor = call(
+        factor_kernel, pos, (mine, other), [whole(mine), whole(other)], [shape(2, 1024, 384)],
+        [VMEM((256, 2560), BF16), VMEM((2, 2, BLK, BLK), F32), VMEM((2, 1024, 1024), BF16)], flops=10_000_000_000,
+    )[0]
+    rights = [
+        call(
+            right_kernel, pos, (weight_grad, mid, factor, *pairs),
+            [of_layer(weight_grad, layer), whole(mid), of_layer(factor, layer), *(whole(a) for a in pairs)],
+            [shape(rows, width)], [],
         )[0]
-
-    factor = lax.cond(
-        always, invert_side, lambda operands: jnp.zeros((2, 1024, 384), BF16), (pos, twice, parts[0])
-    )
-    block = rows // BLK
-    rights = []
-    for layer, pair in enumerate((w_early[0], w_late[0])):
-        mids = [(w_early[1], part(rows, 0))] if layer == 0 else [
-            (w_early[1], part(BLK, n)) for n in range(block, 2 * block - 1)
-        ] + [(w_late[1], whole(w_late[1]))]
-        rights.append(call(
-            right_kernel, pos, (weight_grad, pair, factor, *(m[0] for m in mids)),
-            [of_layer(weight_grad, layer), whole(pair), of_layer(factor, layer), *(m[1] for m in mids)],
-            [shape(rows, width)], [],
-        )[0])
+        for layer, (mid, pairs) in enumerate(((mid0, (pair0, rest)), (mid1, (pair1,))))
+    ]
     return call(
         left_kernel, pos, (*parts, *rights), [whole(a) for a in (*parts, *rights)],
         [shape(*weight_grad.shape)],

time: 119 us -> 115 us (0.966)
  the two profiles are of different devices: /device:TPU:200 before, /device:TPU:1 now
where the time goes in v9:
time: 115 us; the launch traced here: 113 us
  starting transfers between devices  48.3 us (42%)
  Pallas kernels  33.2 us (29%)
  waiting for transfers between devices  29.7 us (26%)
  other arithmetic  1.72 us (1%)
    pallas_call x9, Pallas kernels, call(): pl.pallas_call(kernel, grid_spec=pltpu.PrefetchScalarGridSpec(num_scalar_...  33.2 us
    ppermute x12, starting transfers between devices, spread(): lax.ppermute(parts[d], axis, [(i, (i + d) % 4) for i in range(4)])  18 us
    ppermute x3, waiting for transfers between devices, paired(): return lax.ppermute(w, 'x', [(0, 1), (1, 0), (2, 3), (3, 2)])  17.7 us
    all_to_all x1, starting transfers between devices, body(): mine = lax.all_to_all(side, 'z', 0, 0, tiled=True)  8.21 us
    ppermute x12, waiting for transfers between devices, spread(): lax.ppermute(parts[d], axis, [(i, (i + d) % 4) for i in range(4)])  8.04 us
    all_to_all x1, starting transfers between devices, sum_side(): side = lax.all_to_all(side, 'x', 0, 0, tiled=True)  7.75 us
    ppermute x1, starting transfers between devices, body(): other = lax.ppermute(mine, 'c', [(0, 1), (1, 0)])  6.3 us
    all_to_all x1, starting transfers between devices, body(): side = lax.all_to_all(side, 'y', 0, 0, tiled=True)  4.2 us
  transfers between devices with their start and end apart: 21, of which 9 were waited for; matrix products, arithmetic and copies ran while one was open for 2% of the time, Pallas kernels for 17%

profile of v9, /device:TPU:1, one launch (start us, length us, event | category | flops | bytes accessed | tf_op | source)
XLA Modules:
  0.0 113.4 jit_solution(749246084938872371)
XLA Ops:
  0.0 0.1 stack.27.pos
  0.1 6.5 %shard_map.37 = (bf16[128,1920]{1,0:T(8,128)(2,1)}, bf16[1024,384]{1,0:T(8,128)(2,1)}, bf16[1536,256]{1,0:T(8,128)(2,1)}) custom-call(s32[6]{0:T(128)S(1)} %stack.27.pos, bf16[2,256,6144]{2,1,0:T(8,128)(2,1)} %acts.1, bf16[2,1536,384]{2,1,0:T(8,128)(2,1)} %w_own.3), custom_call_target="tpu_custom_call" | custom-call | tf_op jit(solution)/shard_map/pallas_call | solution.py:218
  6.6 2.1 %collective-permute-start.3 = (bf16[1024,384]{1,0:T(8,128)(2,1)}, bf16[1024,384]{1,0:T(8,128)(2,1)S(1)}, u32[]{:S(2)}, u32[]{:S(2)}) collective-permute-start(bf16[1024,384]{1,0:T(8,128)(2,1)} %get-tuple-element.49), channel_id=1, source_target_pairs={{0,16},{16,0},{32,48},{48,32},{1,17},{17,1},{33,49},{49,33},{2,18}... | collective-permute-start | bytes 2359304 | tf_op jit(solution)/shard_map/ppermute | solution.py:262
  8.7 0.7 collective-permute-start.4
  9.4 4.2 %all-to-all-start.1 = ((bf16[4,32,1920]{2,1,0:T(8,128)(2,1)}), bf16[4,32,1920]{2,1,0:T(8,128)(2,1)S(1)}, u32[]{:S(2)}, u32[]{:S(2)}) async-start(bf16[4,32,1920]{2,1,0:T(8,128)(2,1)} %bitcast.16), calls=%async_computation.1 | async-start | bytes 983040 | tf_op jit(solution)/shard_map/all_to_all | solution.py:285
  13.6 4.1 %shard_map.38 = (bf16[128,1920]{1,0:T(8,128)(2,1)}, bf16[128,1920]{1,0:T(8,128)(2,1)}, bf16[128,1920]{1,0:T(8,128)(2,1)}, bf16[128,1920]{1,0:T(8,128)(2,1)}) custom-call(s32[6]{0:T(128)S(1)} %stack.27.pos, bf16[2,256,1536]{2,1,0:T(8,128)(2,1)} %grads), custom_call_target="tpu_custom_call" | custom-call | flops 12000000000 | tf_op jit(solution)/shard_map/pallas_call | solution.py:218
  17.7 1.5 %collective-permute-start = (bf16[128,1920]{1,0:T(8,128)(2,1)}, bf16[128,1920]{1,0:T(8,128)(2,1)}, u32[]{:S(2)}, u32[]{:S(2)}) collective-permute-start(bf16[128,1920]{1,0:T(8,128)(2,1)} %get-tuple-element.45), channel_id=1, source_target_pairs={{0,64},{64,128},{128,192},{192,0},{1,65},{65,129},{129,193},{193,1... | collective-permute-start | bytes 1474568 | tf_op jit(solution)/shard_map/ppermute | solution.py:254
  19.1 2.4 %collective-permute-start.1 = (bf16[128,1920]{1,0:T(8,128)(2,1)}, bf16[128,1920]{1,0:T(8,128)(2,1)}, u32[]{:S(2)}, u32[]{:S(2)}) collective-permute-start(bf16[128,1920]{1,0:T(8,128)(2,1)} %get-tuple-element.46), channel_id=1, source_target_pairs={{0,128},{64,192},{128,0},{192,64},{1,129},{65,193},{129,1},{193,65... | collective-permute-start | bytes 1474568 | tf_op jit(solution)/shard_map/ppermute | solution.py:254
  21.5 1.2 %collective-permute-start.2 = (bf16[128,1920]{1,0:T(8,128)(2,1)}, bf16[128,1920]{1,0:T(8,128)(2,1)}, u32[]{:S(2)}, u32[]{:S(2)}) collective-permute-start(bf16[128,1920]{1,0:T(8,128)(2,1)} %get-tuple-element.47), channel_id=1, source_target_pairs={{0,192},{64,0},{128,64},{192,128},{1,193},{65,1},{129,65},{193,129... | collective-permute-start | bytes 1474568 | tf_op jit(solution)/shard_map/ppermute | solution.py:254
  22.7 0.0 all-to-all-done.1
  22.7 2.2 %collective-permute-done.3.refs_0_ = bf16[1024,384]{1,0:T(8,128)(2,1)S(1)} collective-permute-done((bf16[1024,384]{1,0:T(8,128)(2,1)}, bf16[1024,384]{1,0:T(8,128)(2,1)S(1)}, u32[]{:S(2)}, u32[]{:S(2)}) %collective-permute-start.3) | collective-permute-done | bytes 786464 | tf_op jit(solution)/shard_map/ppermute | solution.py:262
  24.9 0.0 collective-permute-done.4.w_mid
  24.9 1.4 %shard_map.39 = bf16[128,1920]{1,0:T(8,128)(2,1)} custom-call(s32[6]{0:T(128)S(1)} %stack.27.pos, bf16[128,1920]{1,0:T(8,128)(2,1)S(1)} %bitcast.15), custom_call_target="tpu_custom_call" | custom-call | flops 60000002048 | tf_op jit(solution)/shard_map/pallas_call | solution.py:218
  26.4 16.5 %conditional.1 = (bf16[128,2560]{1,0:T(8,128)(2,1)}, bf16[512,384]{1,0:T(8,128)(2,1)S(1)}, bf16[1536,384]{1,0:T(8,128)(2,1)}, bf16[1536,256]{1,0:T(8,128)(2,1)}) conditional(s32[]{:T(128)} %convert_element_type.33, () %tuple.18, (bf16[128,1920]{1,0:T(8,128)(2,1)}, s32[6]{0:T(128)S(1)}, bf16[2,1536,384]{2,1,0:T(8,128)(2,1)}) %tuple.20), branch_computations={%region_0.1_spmd, %region_1.2_spmd} | conditional | flops 4000000000 | bytes 3014696 | solution.py:307
  26.4 7.7 %all-to-all-start = ((bf16[4,32,1920]{2,1,0:T(8,128)(2,1)}), bf16[4,32,1920]{2,1,0:T(8,128)(2,1)S(1)}, u32[]{:S(2)}, u32[]{:S(2)}) async-start(bf16[4,32,1920]{2,1,0:T(8,128)(2,1)} %bitcast), calls=%async_computation | async-start | bytes 983040 | tf_op jit(solution)/shard_map/cond/branch_1_fun/all_to_all | solution.py:298
  34.1 3.3 %branch_1_fun.3 = (bf16[512,384]{1,0:T(8,128)(2,1)S(1)}, bf16[1536,384]{1,0:T(8,128)(2,1)}, bf16[1536,256]{1,0:T(8,128)(2,1)}) custom-call(s32[6]{0:T(128)S(1)} %get-tuple-element.11.pos, bf16[2,1536,384]{2,1,0:T(8,128)(2,1)} %get-tuple-element.13.w), custom_call_target="tpu_custom_call" | custom-call | flops 4000000000 | tf_op jit(solution)/shard_map/cond/branch_1_fun/pallas_call | solution.py:218
  37.4 3.9 %all-to-all-done = bf16[4,32,1920]{2,1,0:T(8,128)(2,1)S(1)} async-done(((bf16[4,32,1920]{2,1,0:T(8,128)(2,1)}), bf16[4,32,1920]{2,1,0:T(8,128)(2,1)S(1)}, u32[]{:S(2)}, u32[]{:S(2)}) %all-to-all-start) | async-done | bytes 491552 | tf_op jit(solution)/shard_map/cond/branch_1_fun/all_to_all | solution.py:298
  41.3 1.5 %branch_1_fun.2 = bf16[128,2560]{1,0:T(8,128)(2,1)} custom-call(s32[6]{0:T(128)S(1)} %get-tuple-element.11.pos, bf16[128,1920]{1,0:T(8,128)(2,1)S(1)} %bitcast.12), custom_call_target="tpu_custom_call" | custom-call | tf_op jit(solution)/shard_map/cond/branch_1_fun/pallas_call | solution.py:218
  42.9 0.0 copy-start.1
  42.9 0.3 collective-permute-start.5
  43.2 8.2 %all-to-all-start.2 = ((bf16[8,16,2560]{2,1,0:T(8,128)(2,1)}), bf16[8,16,2560]{2,1,0:T(8,128)(2,1)S(1)}, u32[]{:S(2)}, u32[]{:S(2)}) async-start(bf16[8,16,2560]{2,1,0:T(8,128)(2,1)} %bitcast.10), calls=%async_computation.2 | async-start | bytes 1310720 | tf_op jit(solution)/shard_map/all_to_all | solution.py:315
  51.4 0.0 collective-permute-done
  51.4 0.0 collective-permute-done.1
  51.4 0.0 collective-permute-done.2
  51.4 0.0 collective-permute-done.5.refs_1_
  51.4 0.0 copy-done.1
  51.4 1.6 %add_convert_fusion = bf16[128,1920]{1,0:T(8,128)(2,1)S(1)} fusion(bf16[128,1920]{1,0:T(8,128)(2,1)} %collective-permute-done.2, bf16[128,1920]{1,0:T(8,128)(2,1)} %collective-permute-done.1, bf16[128,1920]{1,0:T(8,128)(2,1)} %collective-permute-done, bf16[128,1920]{1,0:T(8,128)(2,1)S(1)} %copy-done.1), kind=kLoop, calls=%fused_computation | loop fusion | flops 1966080 | bytes 2457600 | tf_op jit(solution)/shard_map/convert_element_type | solution.py:317
  53.0 0.1 constant_dynamic-slice_fusion.6
  53.1 1.3 %collective-permute-start.6 = (bf16[32,1920]{1,0:T(8,128)(2,1)S(1)}, bf16[32,1920]{1,0:T(8,128)(2,1)S(1)}, u32[]{:S(2)}, u32[]{:S(2)}) collective-permute-start(bf16[32,1920]{1,0:T(8,128)(2,1)S(1)} %pad_maximum_fusion.1), channel_id=1, source_target_pairs={{0,16},{16,32},{32,48},{48,0},{1,17},{17,33},{33,49},{49,1},{2,18}... | collective-permute-start | bytes 368648 | tf_op jit(solution)/shard_map/ppermute | solution.py:254
  54.4 0.9 collective-permute-start.7
  55.3 2.0 %collective-permute-start.8 = (bf16[32,1920]{1,0:T(8,128)(2,1)S(1)}, bf16[32,1920]{1,0:T(8,128)(2,1)S(1)}, u32[]{:S(2)}, u32[]{:S(2)}) collective-permute-start(bf16[32,1920]{1,0:T(8,128)(2,1)S(1)} %pad_maximum_fusion.3), channel_id=1, source_target_pairs={{0,48},{16,0},{32,16},{48,32},{1,49},{17,1},{33,17},{49,33},{2,50}... | collective-permute-start | bytes 368648 | tf_op jit(solution)/shard_map/ppermute | solution.py:254
  57.3 0.8 collective-permute-done.6
  58.1 1.6 %collective-permute-done.7 = bf16[32,1920]{1,0:T(8,128)(2,1)S(1)} collective-permute-done((bf16[32,1920]{1,0:T(8,128)(2,1)S(1)}, bf16[32,1920]{1,0:T(8,128)(2,1)S(1)}, u32[]{:S(2)}, u32[]{:S(2)}) %collective-permute-start.7) | collective-permute-done | bytes 122912 | tf_op jit(solution)/shard_map/ppermute | solution.py:254
  59.7 0.7 collective-permute-done.8
  60.4 0.1 multiply_convert_fusion
  60.5 2.0 %collective-permute-start.10 = (bf16[32,1920]{1,0:T(8,128)(2,1)S(1)}, bf16[32,1920]{1,0:T(8,128)(2,1)S(1)}, u32[]{:S(2)}, u32[]{:S(2)}) collective-permute-start(bf16[32,1920]{1,0:T(8,128)(2,1)S(1)} %multiply_convert_fusion), channel_id=1, source_target_pairs={{0,32},{16,48},{32,0},{48,16},{1,33},{17,49},{33,1},{49,17},{2,34}... | collective-permute-start | bytes 368648 | tf_op jit(solution)/shard_map/ppermute | solution.py:254
  62.5 1.8 %collective-permute-start.11 = (bf16[32,1920]{1,0:T(8,128)(2,1)S(1)}, bf16[32,1920]{1,0:T(8,128)(2,1)S(1)}, u32[]{:S(2)}, u32[]{:S(2)}) collective-permute-start(bf16[32,1920]{1,0:T(8,128)(2,1)S(1)} %multiply_convert_fusion), channel_id=1, source_target_pairs={{0,48},{16,0},{32,16},{48,32},{1,49},{17,1},{33,17},{49,33},{2,50}... | collective-permute-start | bytes 368648 | tf_op jit(solution)/shard_map/ppermute | solution.py:254
  64.3 0.0 collective-permute-start.9
  64.3 1.9 %collective-permute-done.10 = bf16[32,1920]{1,0:T(8,128)(2,1)S(1)} collective-permute-done((bf16[32,1920]{1,0:T(8,128)(2,1)S(1)}, bf16[32,1920]{1,0:T(8,128)(2,1)S(1)}, u32[]{:S(2)}, u32[]{:S(2)}) %collective-permute-start.10) | collective-permute-done | bytes 122912 | tf_op jit(solution)/shard_map/ppermute | solution.py:254
  66.1 1.1 collective-permute-done.11
  67.2 2.0 %collective-permute-done.9 = bf16[32,1920]{1,0:T(8,128)(2,1)S(1)} collective-permute-done((bf16[32,1920]{1,0:T(8,128)(2,1)S(1)}, bf16[32,1920]{1,0:T(8,128)(2,1)S(1)}, u32[]{:S(2)}, u32[]{:S(2)}) %collective-permute-start.9) | collective-permute-done | bytes 122912 | tf_op jit(solution)/shard_map/ppermute | solution.py:254
  69.2 0.0 all-to-all-done.2
  69.2 6.3 %collective-permute-start.15 = (bf16[128,2560]{1,0:T(8,128)(2,1)S(1)}, bf16[128,2560]{1,0:T(8,128)(2,1)S(1)}, u32[]{:S(2)}, u32[]{:S(2)}) collective-permute-start(bf16[128,2560]{1,0:T(8,128)(2,1)S(1)} %bitcast.13), channel_id=1, source_target_pairs={{0,1},{1,0},{2,3},{3,2},{4,5},{5,4},{6,7},{7,6},{8,9},{9,8},{10,11... | collective-permute-start | bytes 1966088 | tf_op jit(solution)/shard_map/ppermute | solution.py:327
  75.6 0.0 collective-permute-start.17
  75.6 1.4 %collective-permute-start.12 = (bf16[128,1920]{1,0:T(8,128)(2,1)S(1)}, bf16[128,1920]{1,0:T(8,128)(2,1)S(1)}, u32[]{:S(2)}, u32[]{:S(2)}) collective-permute-start(bf16[128,1920]{1,0:T(8,128)(2,1)S(1)} %pad_maximum_fusion.p0), channel_id=1, source_target_pairs={{0,64},{64,128},{128,192},{192,0},{1,65},{65,129},{129,193},{193,1... | collective-permute-start | bytes 1474568 | tf_op jit(solution)/shard_map/ppermute | solution.py:254
  76.9 2.6 %collective-permute-start.13 = (bf16[128,1920]{1,0:T(8,128)(2,1)S(1)}, bf16[128,1920]{1,0:T(8,128)(2,1)S(1)}, u32[]{:S(2)}, u32[]{:S(2)}) collective-permute-start(bf16[128,1920]{1,0:T(8,128)(2,1)S(1)} %pad_maximum_fusion.p0), channel_id=1, source_target_pairs={{0,128},{64,192},{128,0},{192,64},{1,129},{65,193},{129,1},{193,65... | collective-permute-start | bytes 1474568 | tf_op jit(solution)/shard_map/ppermute | solution.py:254
  79.5 1.1 collective-permute-start.14
  80.6 0.0 collective-permute-done.15.other
  80.6 0.7 collective-permute-start.16
  81.3 0.0 copy-start
  81.3 3.9 %shard_map.40.factor = bf16[2,1024,384]{2,1,0:T(8,128)(2,1)S(1)} custom-call(s32[6]{0:T(128)S(1)} %stack.27.pos, bf16[128,2560]{1,0:T(8,128)(2,1)S(1)} %bitcast.14, bf16[128,2560]{1,0:T(8,128)(2,1)S(1)} %collective-permute-done.15.other), custom_call_target="tpu_custom_call" | custom-call | flops 10000000000 | tf_op jit(solution)/shard_map/pallas_call | solution.py:218
  85.3 0.0 copy-done
  85.3 2.5 %shard_map.41.r0 = bf16[1536,384]{1,0:T(8,128)(2,1)S(1)} custom-call(s32[6]{0:T(128)S(1)} %stack.27.pos, bf16[2,1536,384]{2,1,0:T(8,128)(2,1)S(1)} %copy-done, bf16[1536,256]{1,0:T(8,128)(2,1)S(1)} %collective-permute-done.4.w_mid, bf16[2,1024,384]{2,1,0:T(8,128)(2,1)S(1)} %shard_map.40.factor, bf16[1024,384]{1,0:T(8,128)(2,1)S(1)} %collective-permute-done.3.refs_0_, ...), custom_call_target="tpu_custom_call" | custom-call | tf_op jit(solution)/shard_map/pallas_call | solution.py:218
  87.8 0.0 collective-permute-done.16.w_mid
  87.8 15.4 %collective-permute-done.17.refs_0_ = bf16[1536,384]{1,0:T(8,128)(2,1)S(1)} collective-permute-done((bf16[1536,384]{1,0:T(8,128)(2,1)}, bf16[1536,384]{1,0:T(8,128)(2,1)S(1)}, u32[]{:S(2)}, u32[]{:S(2)}) %collective-permute-start.17) | collective-permute-done | bytes 1179680 | tf_op jit(solution)/shard_map/ppermute | solution.py:262
  103.3 2.5 %shard_map.42.r1 = bf16[1536,384]{1,0:T(8,128)(2,1)S(1)} custom-call(s32[6]{0:T(128)S(1)} %stack.27.pos, bf16[2,1536,384]{2,1,0:T(8,128)(2,1)S(1)} %copy-done, bf16[1536,256]{1,0:T(8,128)(2,1)S(1)} %collective-permute-done.16.w_mid, bf16[2,1024,384]{2,1,0:T(8,128)(2,1)S(1)} %shard_map.40.factor, bf16[1536,384]{1,0:T(8,128)(2,1)S(1)} %collective-permute-done.17.refs_0_), custom_call_target="tpu_custom_call" | custom-call | tf_op jit(solution)/shard_map/pallas_call | solution.py:218
  105.8 0.0 collective-permute-done.12.p1
  105.8 0.0 collective-permute-done.13.p2
  105.8 0.0 collective-permute-done.14.p3
  105.9 7.4 %shard_map.43 = bf16[2,1536,384]{2,1,0:T(8,128)(2,1)} custom-call(s32[6]{0:T(128)S(1)} %stack.27.pos, bf16[128,1920]{1,0:T(8,128)(2,1)S(1)} %pad_maximum_fusion.p0, bf16[128,1920]{1,0:T(8,128)(2,1)S(1)} %collective-permute-done.12.p1, bf16[128,1920]{1,0:T(8,128)(2,1)S(1)} %collective-permute-done.13.p2, bf16[128,1920]{1,0:T(8,128)(2,1)S(1)} %collective-permute-done.14.p3, ...), custom_call_target="tpu_custom_call" | custom-call | tf_op jit(solution)/shard_map/pallas_call | solution.py:218
  (5 shorter events, 0.1 us)
Async XLA Ops:
  6.6 18.4 %collective-permute-start.3 = (bf16[1024,384]{1,0:T(8,128)(2,1)}, bf16[1024,384]{1,0:T(8,128)(2,1)S(1)}, u32[]{:S(2)}, u32[]{:S(2)}) collective-permute-start(bf16[1024,384]{1,0:T(8,128)(2,1)} %get-tuple-element.49), channel_id=1, source_target_pairs={{0,16},{16,0},{32,48},{48,32},{1,17},{17,1},{33,49},{49,33},{2,18}... | collective-permute-start | bytes 2359304 | tf_op jit(solution)/shard_map/ppermute | solution.py:262
  8.7 16.2 %collective-permute-start.4 = (bf16[1536,256]{1,0:T(8,128)(2,1)}, bf16[1536,256]{1,0:T(8,128)(2,1)S(1)}, u32[]{:S(2)}, u32[]{:S(2)}) collective-permute-start(bf16[1536,256]{1,0:T(8,128)(2,1)} %get-tuple-element.50), channel_id=1, source_target_pairs={{16,32},{32,16},{17,33},{33,17},{18,34},{34,18},{19,35},{35,19},{2... | collective-permute-start | bytes 2359304 | tf_op jit(solution)/shard_map/ppermute | solution.py:266
  9.4 13.3 %all-to-all-start.1 = ((bf16[4,32,1920]{2,1,0:T(8,128)(2,1)}), bf16[4,32,1920]{2,1,0:T(8,128)(2,1)S(1)}, u32[]{:S(2)}, u32[]{:S(2)}) async-start(bf16[4,32,1920]{2,1,0:T(8,128)(2,1)} %bitcast.16), calls=%async_computation.1 | async-start | bytes 983040 | tf_op jit(solution)/shard_map/all_to_all | solution.py:285
  17.7 33.7 %collective-permute-start = (bf16[128,1920]{1,0:T(8,128)(2,1)}, bf16[128,1920]{1,0:T(8,128)(2,1)}, u32[]{:S(2)}, u32[]{:S(2)}) collective-permute-start(bf16[128,1920]{1,0:T(8,128)(2,1)} %get-tuple-element.45), channel_id=1, source_target_pairs={{0,64},{64,128},{128,192},{192,0},{1,65},{65,129},{129,193},{193,1... | collective-permute-start | bytes 1474568 | tf_op jit(solution)/shard_map/ppermute | solution.py:254
  19.1 32.3 %collective-permute-start.1 = (bf16[128,1920]{1,0:T(8,128)(2,1)}, bf16[128,1920]{1,0:T(8,128)(2,1)}, u32[]{:S(2)}, u32[]{:S(2)}) collective-permute-start(bf16[128,1920]{1,0:T(8,128)(2,1)} %get-tuple-element.46), channel_id=1, source_target_pairs={{0,128},{64,192},{128,0},{192,64},{1,129},{65,193},{129,1},{193,65... | collective-permute-start | bytes 1474568 | tf_op jit(solution)/shard_map/ppermute | solution.py:254
  21.5 29.9 %collective-permute-start.2 = (bf16[128,1920]{1,0:T(8,128)(2,1)}, bf16[128,1920]{1,0:T(8,128)(2,1)}, u32[]{:S(2)}, u32[]{:S(2)}) collective-permute-start(bf16[128,1920]{1,0:T(8,128)(2,1)} %get-tuple-element.47), channel_id=1, source_target_pairs={{0,192},{64,0},{128,64},{192,128},{1,193},{65,1},{129,65},{193,129... | collective-permute-start | bytes 1474568 | tf_op jit(solution)/shard_map/ppermute | solution.py:254
  26.4 15.0 %all-to-all-start = ((bf16[4,32,1920]{2,1,0:T(8,128)(2,1)}), bf16[4,32,1920]{2,1,0:T(8,128)(2,1)S(1)}, u32[]{:S(2)}, u32[]{:S(2)}) async-start(bf16[4,32,1920]{2,1,0:T(8,128)(2,1)} %bitcast), calls=%async_computation | async-start | bytes 983040 | tf_op jit(solution)/shard_map/cond/branch_1_fun/all_to_all | solution.py:298
  42.9 8.5 %copy-start.1 = (bf16[128,1920]{1,0:T(8,128)(2,1)S(1)}, bf16[128,1920]{1,0:T(8,128)(2,1)}, u32[]{:S(2)}) copy-start(bf16[128,1920]{1,0:T(8,128)(2,1)} %get-tuple-element.54) | copy-start | bytes 1474564
  42.9 8.5 %collective-permute-start.5 = (bf16[512,384]{1,0:T(8,128)(2,1)S(1)}, bf16[512,384]{1,0:T(8,128)(2,1)S(1)}, u32[]{:S(2)}, u32[]{:S(2)}) collective-permute-start(bf16[512,384]{1,0:T(8,128)(2,1)S(1)} %get-tuple-element.53), channel_id=1, source_target_pairs={{0,16},{16,0},{32,48},{48,32},{1,17},{17,1},{33,49},{49,33},{2,18}... | collective-permute-start | bytes 1179656 | tf_op jit(solution)/shard_map/ppermute | solution.py:262
  43.2 26.1 %all-to-all-start.2 = ((bf16[8,16,2560]{2,1,0:T(8,128)(2,1)}), bf16[8,16,2560]{2,1,0:T(8,128)(2,1)S(1)}, u32[]{:S(2)}, u32[]{:S(2)}) async-start(bf16[8,16,2560]{2,1,0:T(8,128)(2,1)} %bitcast.10), calls=%async_computation.2 | async-start | bytes 1310720 | tf_op jit(solution)/shard_map/all_to_all | solution.py:315
  53.1 5.0 %collective-permute-start.6 = (bf16[32,1920]{1,0:T(8,128)(2,1)S(1)}, bf16[32,1920]{1,0:T(8,128)(2,1)S(1)}, u32[]{:S(2)}, u32[]{:S(2)}) collective-permute-start(bf16[32,1920]{1,0:T(8,128)(2,1)S(1)} %pad_maximum_fusion.1), channel_id=1, source_target_pairs={{0,16},{16,32},{32,48},{48,0},{1,17},{17,33},{33,49},{49,1},{2,18}... | collective-permute-start | bytes 368648 | tf_op jit(solution)/shard_map/ppermute | solution.py:254
  54.4 5.3 %collective-permute-start.7 = (bf16[32,1920]{1,0:T(8,128)(2,1)S(1)}, bf16[32,1920]{1,0:T(8,128)(2,1)S(1)}, u32[]{:S(2)}, u32[]{:S(2)}) collective-permute-start(bf16[32,1920]{1,0:T(8,128)(2,1)S(1)} %pad_maximum_fusion.2), channel_id=1, source_target_pairs={{0,32},{16,48},{32,0},{48,16},{1,33},{17,49},{33,1},{49,17},{2,34}... | collective-permute-start | bytes 368648 | tf_op jit(solution)/shard_map/ppermute | solution.py:254
  55.3 5.1 %collective-permute-start.8 = (bf16[32,1920]{1,0:T(8,128)(2,1)S(1)}, bf16[32,1920]{1,0:T(8,128)(2,1)S(1)}, u32[]{:S(2)}, u32[]{:S(2)}) collective-permute-start(bf16[32,1920]{1,0:T(8,128)(2,1)S(1)} %pad_maximum_fusion.3), channel_id=1, source_target_pairs={{0,48},{16,0},{32,16},{48,32},{1,49},{17,1},{33,17},{49,33},{2,50}... | collective-permute-start | bytes 368648 | tf_op jit(solution)/shard_map/ppermute | solution.py:254
  60.5 5.6 %collective-permute-start.10 = (bf16[32,1920]{1,0:T(8,128)(2,1)S(1)}, bf16[32,1920]{1,0:T(8,128)(2,1)S(1)}, u32[]{:S(2)}, u32[]{:S(2)}) collective-permute-start(bf16[32,1920]{1,0:T(8,128)(2,1)S(1)} %multiply_convert_fusion), channel_id=1, source_target_pairs={{0,32},{16,48},{32,0},{48,16},{1,33},{17,49},{33,1},{49,17},{2,34}... | collective-permute-start | bytes 368648 | tf_op jit(solution)/shard_map/ppermute | solution.py:254
  62.5 4.7 %collective-permute-start.11 = (bf16[32,1920]{1,0:T(8,128)(2,1)S(1)}, bf16[32,1920]{1,0:T(8,128)(2,1)S(1)}, u32[]{:S(2)}, u32[]{:S(2)}) collective-permute-start(bf16[32,1920]{1,0:T(8,128)(2,1)S(1)} %multiply_convert_fusion), channel_id=1, source_target_pairs={{0,48},{16,0},{32,16},{48,32},{1,49},{17,1},{33,17},{49,33},{2,50}... | collective-permute-start | bytes 368648 | tf_op jit(solution)/shard_map/ppermute | solution.py:254
  64.3 4.9 %collective-permute-start.9 = (bf16[32,1920]{1,0:T(8,128)(2,1)S(1)}, bf16[32,1920]{1,0:T(8,128)(2,1)S(1)}, u32[]{:S(2)}, u32[]{:S(2)}) collective-permute-start(bf16[32,1920]{1,0:T(8,128)(2,1)S(1)} %multiply_convert_fusion), channel_id=1, source_target_pairs={{0,16},{16,32},{32,48},{48,0},{1,17},{17,33},{33,49},{49,1},{2,18}... | collective-permute-start | bytes 368648 | tf_op jit(solution)/shard_map/ppermute | solution.py:254
  69.2 11.4 %collective-permute-start.15 = (bf16[128,2560]{1,0:T(8,128)(2,1)S(1)}, bf16[128,2560]{1,0:T(8,128)(2,1)S(1)}, u32[]{:S(2)}, u32[]{:S(2)}) collective-permute-start(bf16[128,2560]{1,0:T(8,128)(2,1)S(1)} %bitcast.13), channel_id=1, source_target_pairs={{0,1},{1,0},{2,3},{3,2},{4,5},{5,4},{6,7},{7,6},{8,9},{9,8},{10,11... | collective-permute-start | bytes 1966088 | tf_op jit(solution)/shard_map/ppermute | solution.py:327
  75.6 27.7 %collective-permute-start.17 = (bf16[1536,384]{1,0:T(8,128)(2,1)}, bf16[1536,384]{1,0:T(8,128)(2,1)S(1)}, u32[]{:S(2)}, u32[]{:S(2)}) collective-permute-start(bf16[1536,384]{1,0:T(8,128)(2,1)} %get-tuple-element.66), channel_id=1, source_target_pairs={{0,16},{16,0},{32,48},{48,32},{1,17},{17,1},{33,49},{49,33},{2,18}... | collective-permute-start | bytes 3538952 | tf_op jit(solution)/shard_map/ppermute | solution.py:262
  75.6 30.3 %collective-permute-start.12 = (bf16[128,1920]{1,0:T(8,128)(2,1)S(1)}, bf16[128,1920]{1,0:T(8,128)(2,1)S(1)}, u32[]{:S(2)}, u32[]{:S(2)}) collective-permute-start(bf16[128,1920]{1,0:T(8,128)(2,1)S(1)} %pad_maximum_fusion.p0), channel_id=1, source_target_pairs={{0,64},{64,128},{128,192},{192,0},{1,65},{65,129},{129,193},{193,1... | collective-permute-start | bytes 1474568 | tf_op jit(solution)/shard_map/ppermute | solution.py:254
  76.9 28.9 %collective-permute-start.13 = (bf16[128,1920]{1,0:T(8,128)(2,1)S(1)}, bf16[128,1920]{1,0:T(8,128)(2,1)S(1)}, u32[]{:S(2)}, u32[]{:S(2)}) collective-permute-start(bf16[128,1920]{1,0:T(8,128)(2,1)S(1)} %pad_maximum_fusion.p0), channel_id=1, source_target_pairs={{0,128},{64,192},{128,0},{192,64},{1,129},{65,193},{129,1},{193,65... | collective-permute-start | bytes 1474568 | tf_op jit(solution)/shard_map/ppermute | solution.py:254
  79.5 26.3 %collective-permute-start.14 = (bf16[128,1920]{1,0:T(8,128)(2,1)S(1)}, bf16[128,1920]{1,0:T(8,128)(2,1)S(1)}, u32[]{:S(2)}, u32[]{:S(2)}) collective-permute-start(bf16[128,1920]{1,0:T(8,128)(2,1)S(1)} %pad_maximum_fusion.p0), channel_id=1, source_target_pairs={{0,192},{64,0},{128,64},{192,128},{1,193},{65,1},{129,65},{193,129... | collective-permute-start | bytes 1474568 | tf_op jit(solution)/shard_map/ppermute | solution.py:254
  80.6 7.2 %collective-permute-start.16 = (bf16[1536,256]{1,0:T(8,128)(2,1)}, bf16[1536,256]{1,0:T(8,128)(2,1)S(1)}, u32[]{:S(2)}, u32[]{:S(2)}) collective-permute-start(bf16[1536,256]{1,0:T(8,128)(2,1)} %get-tuple-element.65), channel_id=1, source_target_pairs={{16,32},{32,16},{17,33},{33,17},{18,34},{34,18},{19,35},{35,19},{2... | collective-permute-start | bytes 2359304 | tf_op jit(solution)/shard_map/ppermute | solution.py:266
  81.3 4.0 %copy-start = (bf16[2,1536,384]{2,1,0:T(8,128)(2,1)S(1)}, bf16[2,1536,384]{2,1,0:T(8,128)(2,1)}, u32[]{:S(2)}) copy-start(bf16[2,1536,384]{2,1,0:T(8,128)(2,1)} %w_own.3) | copy-start | bytes 7077892

commit v10 on v9

--- a/solution.py
+++ b/solution.py
@@ -1,3 +1,5 @@
+import functools
+
 import jax
 import jax.numpy as jnp
 from jax import lax
@@ -15,6 +17,7 @@
 
 PAIRS = [(r, c) for r in range(4) for c in range(r, 4)]
 LANES = 15 * SUB
+PARTS = 1024, 448, 64
 
 
 def tn_dot(a, b):
@@ -30,10 +33,11 @@
 
 
 def late_kernel(pos, w, rest, out, mid, held_rest, held, held_mid, sems):
-    size = rest.shape[0]
+    last = PARTS[2]
     sources = (
-        (w.at[0, pl.ds(w.shape[1] - size, size)], held_rest, rest),
-        (w.at[1], held, out),
+        (w.at[0, pl.ds(w.shape[1] - last, last)], held_rest.at[pl.ds(0, last)], rest.at[pl.ds(0, last)]),
+        (w.at[1, pl.ds(0, BLK)], held_rest.at[pl.ds(last, BLK)], rest.at[pl.ds(last, BLK)]),
+        (w.at[1, pl.ds(BLK, out.shape[0])], held, out),
         (w.at[1, :, middle(pos)], held_mid, mid),
     )
     loads = [pltpu.make_async_copy(a, b, sems.at[0, n]) for n, (a, b, _) in enumerate(sources)]
@@ -67,9 +71,13 @@
         send[64:128, :] = pack[1, pl.ds(at, 64), :]
 
 
-def side_kernel(pos, acts, w, out, early, mid, held, held_mid, sems):
+def side_kernel(pos, acts, w, out, early, following, mid, held, held_next, held_mid, sems):
     part, step = pos[3], pl.program_id(0)
-    sources = (w.at[0, pl.ds(0, early.shape[0])], held, early), (w.at[0, :, middle(pos)], held_mid, mid)
+    sources = (
+        (w.at[0, pl.ds(0, PARTS[0])], held, early),
+        (w.at[0, pl.ds(PARTS[0], PARTS[1])], held_next, following),
+        (w.at[0, :, middle(pos)], held_mid, mid),
+    )
     loads = [pltpu.make_async_copy(a, b, sems.at[0, n]) for n, (a, b, _) in enumerate(sources)]
     stores = [pltpu.make_async_copy(b, c, sems.at[1, n]) for n, (_, b, c) in enumerate(sources)]
 
@@ -179,15 +187,15 @@
         out[layer, 768:1024, :] = diag[layer, pl.ds(mid, 256), columns]
 
 
-def right_kernel(pos, w_own, w_mid, factor, *refs):
+def right_kernel(parts, pos, w_own, w_mid, factor, *refs):
     out, at = refs[-1], 0
-    for pair in refs[:-1]:
-        rows = slice(at, at + pair.shape[0])
+    for pair, (first, count) in zip(refs[:-1], parts):
+        rows = slice(at, at + count)
         total = nn_dot(w_own[0, rows, :], factor[0, 0:384, :])
-        total += nn_dot(pair[...], factor[0, 384:768, :])
+        total += nn_dot(pair[first:first + count, :], factor[0, 384:768, :])
         total += nn_dot(w_mid[rows, :], factor[0, 768:1024, :])
         out[rows, :] = total.astype(BF16)
-        at += pair.shape[0]
+        at += count
 
 
 def left_kernel(pos, p0, p1, p2, p3, r0, r1, out, pack, full, ready, sems):
@@ -272,15 +280,16 @@
     rows, width = weight_grad.shape[1:]
     barrier = lax.optimization_barrier
 
-    early, rest, mid = shape(rows - BLK, width), shape(BLK, width), shape(rows, 256)
+    early, following, mid = shape(PARTS[0], width), shape(PARTS[1], width), shape(rows, 256)
+    rest, late = shape(PARTS[2] + BLK, width), shape(rows - BLK, width)
     side, *own = call(
         side_kernel, pos, (acts, weight_grad),
         [pl.BlockSpec((1, acts.shape[1], 3 * BLK), lambda i, p: (p[4], 0, i)), ANYWHERE],
-        [shape(128, LANES), early, mid],
-        [VMEM(early.shape, BF16), VMEM(mid.shape, BF16), pltpu.SemaphoreType.DMA((2, 2))],
-        out_specs=[pl.BlockSpec((32, LANES), lambda i, p: (i, 0)), ANYWHERE, ANYWHERE], vmem=60, grid=4,
-    )
-    pair0, mid0 = paired(own[0]), crossed(own[1])
+        [shape(128, LANES), early, following, mid],
+        [VMEM(a.shape, BF16) for a in (early, following, mid)] + [pltpu.SemaphoreType.DMA((2, 3))],
+        out_specs=[pl.BlockSpec((32, LANES), lambda i, p: (i, 0))] + [ANYWHERE] * 3, vmem=60, grid=4,
+    )
+    early, following, mid0 = paired(own[0]), paired(own[1]), crossed(own[2])
     side, grads_out = barrier((side, grads_out))
     side = lax.all_to_all(side, "y", 0, 0, tiled=True)
 
@@ -290,27 +299,28 @@
     )
     start = covs[0]
     covs = spread(covs, "y")
-    side, pair0, mid0 = barrier((side, pair0, mid0))
+    side, early, mid0 = barrier((side, early, mid0))
     side = call(total_kernel, pos, (side,), [whole(side)], [shape(128, LANES)], [], flops=60_000_000_000)[0]
 
     def sum_side(operands):
         pos, side, weight_grad, _ = operands
         side = lax.all_to_all(side, "x", 0, 0, tiled=True)
-        late = [rest, shape(rows, width), mid]
-        late = call(
-            late_kernel, pos, (weight_grad,), [ANYWHERE], late,
-            [VMEM(a.shape, BF16) for a in late] + [pltpu.SemaphoreType.DMA((2, 3))],
+        outs = [rest, late, mid]
+        outs = call(
+            late_kernel, pos, (weight_grad,), [ANYWHERE], outs,
+            [VMEM(a.shape, BF16) for a in outs] + [pltpu.SemaphoreType.DMA((2, 4))],
             out_specs=[ANYWHERE] * 3, vmem=60, flops=4_000_000_000,
         )
-        return call(chosen_kernel, pos, (side,), [whole(side)], [shape(128, 2560)], [])[0], *late
-
-    side, rest, pair1, mid1 = lax.cond(
+        return call(chosen_kernel, pos, (side,), [whole(side)], [shape(128, 2560)], [])[0], *outs
+
+    side, rest, late, mid1 = lax.cond(
         x + y + z + c < 64, sum_side,
         lambda operands: tuple(
-            jnp.zeros(n, BF16) for n in ((128, 2560), rest.shape, (rows, width), mid.shape)
+            jnp.zeros(n, BF16) for n in ((128, 2560), rest.shape, late.shape, mid.shape)
         ),
         (pos, side, weight_grad, start),
     )
+    side, rest, following = barrier((side, rest, following))
     rest = paired(rest)
     mine = lax.all_to_all(side, "z", 0, 0, tiled=True)
     *covs, _, rest = barrier((*covs, side, rest))
@@ -321,8 +331,8 @@
     ]
     own = (add(spread(sends, "x")) * (1.0 / TOKENS)).astype(BF16)
     quarter = jnp.concatenate(spread([own] * 4, "x"), axis=0)
-    quarter, pair1, mid1, mine = barrier((quarter, pair1, mid1, mine))
-    pair1, mid1 = paired(pair1), crossed(mid1)
+    quarter, late, mid1, mine = barrier((quarter, late, mid1, mine))
+    late, mid1 = paired(late), crossed(mid1)
     parts = spread([quarter] * 4, "y")
     other = lax.ppermute(mine, "c", [(0, 1), (1, 0)])
     factor = call(
@@ -331,11 +341,14 @@
     )[0]
     rights = [
         call(
-            right_kernel, pos, (weight_grad, mid, factor, *pairs),
+            functools.partial(right_kernel, parts_of), pos, (weight_grad, mid, factor, *pairs),
             [of_layer(weight_grad, layer), whole(mid), of_layer(factor, layer), *(whole(a) for a in pairs)],
             [shape(rows, width)], [],
         )[0]
-        for layer, (mid, pairs) in enumerate(((mid0, (pair0, rest)), (mid1, (pair1,))))
+        for layer, (mid, pairs, parts_of) in enumerate((
+            (mid0, (early, following, rest), ((0, PARTS[0]), (0, PARTS[1]), (0, PARTS[2]))),
+            (mid1, (rest, late), ((PARTS[2], BLK), (0, rows - BLK))),
+        ))
     ]
     return call(
         left_kernel, pos, (*parts, *rights), [whole(a) for a in (*parts, *rights)],

time: 115 us -> 110 us (0.957)
  waiting for transfers between devices: 29.7 us -> 22.8 us
  starting transfers between devices: 48.3 us -> 51.4 us
  Pallas kernels: 33.2 us -> 31.4 us
  local copies, waits for them, and re-layouts: 0.19 us -> 1.46 us
    ppermute x3 -> x4, waiting for transfers between devices: 17.7 us -> 10.5 us  [paired(): return lax.ppermute(w, 'x', [(0, 1), (1, 0), (2, 3), (3, 2)])]
    ppermute x3 -> x4, starting transfers between devices: 2.42 us -> 8.02 us  [paired(): return lax.ppermute(w, 'x', [(0, 1), (1, 0), (2, 3), (3, 2)])]
    all_to_all x1, starting transfers between devices: 7.75 us -> 4.12 us  [sum_side(): side = lax.all_to_all(side, 'x', 0, 0, tiled=True)]
    pallas_call x9, Pallas kernels: 33.2 us -> 31.4 us  [call(): pl.pallas_call(kernel, grid_spec=pltpu.PrefetchScalarGridSpec(num_scalar_...]
    ppermute x1, starting transfers between devices: 6.3 us -> 7.61 us  [body(): other = lax.ppermute(mine, 'c', [(0, 1), (1, 0)])]
  transfers between devices with their start and end apart: 21 -> 22, of which waited for: 9 -> 9; matrix products, arithmetic and copies ran while one was open for 2% -> 2% of each run, Pallas kernels for 17% -> 16%
where the time goes in v10:
time: 110 us; the launch traced here: 109 us
  starting transfers between devices  51.4 us (47%)
  Pallas kernels  31.4 us (29%)
  waiting for transfers between devices  22.8 us (21%)
  other arithmetic  1.72 us (2%)
  local copies, waits for them, and re-layouts  1.46 us (1%)
    pallas_call x9, Pallas kernels, call(): pl.pallas_call(kernel, grid_spec=pltpu.PrefetchScalarGridSpec(num_scalar_...  31.4 us
    ppermute x12, starting transfers between devices, spread(): lax.ppermute(parts[d], axis, [(i, (i + d) % 4) for i in range(4)])  17.9 us
    ppermute x4, waiting for transfers between devices, paired(): return lax.ppermute(w, 'x', [(0, 1), (1, 0), (2, 3), (3, 2)])  10.5 us
    all_to_all x1, starting transfers between devices, body(): mine = lax.all_to_all(side, 'z', 0, 0, tiled=True)  8.18 us
    ppermute x4, starting transfers between devices, paired(): return lax.ppermute(w, 'x', [(0, 1), (1, 0), (2, 3), (3, 2)])  8.02 us
    ppermute x1, starting transfers between devices, body(): other = lax.ppermute(mine, 'c', [(0, 1), (1, 0)])  7.61 us
    ppermute x12, waiting for transfers between devices, spread(): lax.ppermute(parts[d], axis, [(i, (i + d) % 4) for i in range(4)])  7.1 us
    all_to_all x1, starting transfers between devices, body(): side = lax.all_to_all(side, 'y', 0, 0, tiled=True)  4.19 us
  transfers between devices with their start and end apart: 22, of which 9 were waited for; matrix products, arithmetic and copies ran while one was open for 2% of the time, Pallas kernels for 16%

profile of v10, /device:TPU:1, one launch (start us, length us, event | category | flops | bytes accessed | tf_op | source)
XLA Modules:
  0.0 109.2 jit_solution(18174283379105816385)
XLA Ops:
  0.0 0.1 stack.27.pos
  0.1 6.5 %shard_map.37 = (bf16[128,1920]{1,0:T(8,128)(2,1)}, bf16[1024,384]{1,0:T(8,128)(2,1)}, bf16[448,384]{1,0:T(8,128)(2,1)}, bf16[1536,256]{1,0:T(8,128)(2,1)}) custom-call(s32[6]{0:T(128)S(1)} %stack.27.pos, bf16[2,256,6144]{2,1,0:T(8,128)(2,1)} %acts.1, bf16[2,1536,384]{2,1,0:T(8,128)(2,1)} %w_own.3), custom_call_target="tpu_custom_call" | custom-call | tf_op jit(solution)/shard_map/pallas_call | solution.py:226
  6.6 2.1 %collective-permute-start.3 = (bf16[1024,384]{1,0:T(8,128)(2,1)}, bf16[1024,384]{1,0:T(8,128)(2,1)S(1)}, u32[]{:S(2)}, u32[]{:S(2)}) collective-permute-start(bf16[1024,384]{1,0:T(8,128)(2,1)} %get-tuple-element.53), channel_id=1, source_target_pairs={{0,16},{16,0},{32,48},{48,32},{1,17},{17,1},{33,49},{49,33},{2,18}... | collective-permute-start | bytes 2359304 | tf_op jit(solution)/shard_map/ppermute | solution.py:270
  8.8 0.7 collective-permute-start.4
  9.5 4.2 %all-to-all-start.1 = ((bf16[4,32,1920]{2,1,0:T(8,128)(2,1)}), bf16[4,32,1920]{2,1,0:T(8,128)(2,1)S(1)}, u32[]{:S(2)}, u32[]{:S(2)}) async-start(bf16[4,32,1920]{2,1,0:T(8,128)(2,1)} %bitcast.17), calls=%async_computation.1 | async-start | bytes 983040 | tf_op jit(solution)/shard_map/all_to_all | solution.py:294
  13.7 3.3 %collective-permute-start.5 = (bf16[448,384]{1,0:T(8,128)(2,1)}, bf16[448,384]{1,0:T(8,128)(2,1)S(1)}, u32[]{:S(2)}, u32[]{:S(2)}) collective-permute-start(bf16[448,384]{1,0:T(8,128)(2,1)} %get-tuple-element.58), channel_id=1, source_target_pairs={{0,16},{16,0},{32,48},{48,32},{1,17},{17,1},{33,49},{49,33},{2,18}... | collective-permute-start | bytes 1032200 | tf_op jit(solution)/shard_map/ppermute | solution.py:270
  17.0 4.1 %shard_map.38 = (bf16[128,1920]{1,0:T(8,128)(2,1)}, bf16[128,1920]{1,0:T(8,128)(2,1)}, bf16[128,1920]{1,0:T(8,128)(2,1)}, bf16[128,1920]{1,0:T(8,128)(2,1)}) custom-call(s32[6]{0:T(128)S(1)} %stack.27.pos, bf16[2,256,1536]{2,1,0:T(8,128)(2,1)} %grads), custom_call_target="tpu_custom_call" | custom-call | flops 12000000000 | tf_op jit(solution)/shard_map/pallas_call | solution.py:226
  21.1 1.5 %collective-permute-start = (bf16[128,1920]{1,0:T(8,128)(2,1)}, bf16[128,1920]{1,0:T(8,128)(2,1)}, u32[]{:S(2)}, u32[]{:S(2)}) collective-permute-start(bf16[128,1920]{1,0:T(8,128)(2,1)} %get-tuple-element.49), channel_id=1, source_target_pairs={{0,64},{64,128},{128,192},{192,0},{1,65},{65,129},{129,193},{193,1... | collective-permute-start | bytes 1474568 | tf_op jit(solution)/shard_map/ppermute | solution.py:262
  22.5 2.4 %collective-permute-start.1 = (bf16[128,1920]{1,0:T(8,128)(2,1)}, bf16[128,1920]{1,0:T(8,128)(2,1)}, u32[]{:S(2)}, u32[]{:S(2)}) collective-permute-start(bf16[128,1920]{1,0:T(8,128)(2,1)} %get-tuple-element.50), channel_id=1, source_target_pairs={{0,128},{64,192},{128,0},{192,64},{1,129},{65,193},{129,1},{193,65... | collective-permute-start | bytes 1474568 | tf_op jit(solution)/shard_map/ppermute | solution.py:262
  24.9 0.1 collective-permute-done.3.refs_0_
  25.0 3.9 %collective-permute-start.2 = (bf16[128,1920]{1,0:T(8,128)(2,1)}, bf16[128,1920]{1,0:T(8,128)(2,1)}, u32[]{:S(2)}, u32[]{:S(2)}) collective-permute-start(bf16[128,1920]{1,0:T(8,128)(2,1)} %get-tuple-element.51), channel_id=1, source_target_pairs={{0,192},{64,0},{128,64},{192,128},{1,193},{65,1},{129,65},{193,129... | collective-permute-start | bytes 1474568 | tf_op jit(solution)/shard_map/ppermute | solution.py:262
  28.9 0.0 all-to-all-done.1
  28.9 0.0 collective-permute-done.4.w_mid
  28.9 0.6 shard_map.39
  29.5 12.8 %conditional.1 = (bf16[128,2560]{1,0:T(8,128)(2,1)S(1)}, bf16[576,384]{1,0:T(8,128)(2,1)}, bf16[1024,384]{1,0:T(8,128)(2,1)}, bf16[1536,256]{1,0:T(8,128)(2,1)}) conditional(s32[]{:T(128)} %convert_element_type.33, () %tuple.19, (bf16[128,1920]{1,0:T(8,128)(2,1)S(1)}, s32[6]{0:T(128)S(1)}, bf16[2,1536,384]{2,1,0:T(8,128)(2,1)}) %tuple.21), branch_computations={%region_0.1_spmd, %region_1.2_spmd} | conditional | flops 4000000000 | bytes 3440732 | solution.py:316
  29.5 0.0 copy-start.3
  29.5 0.8 copy-done.3
  30.3 4.1 %all-to-all-start = ((bf16[4,32,1920]{2,1,0:T(8,128)(2,1)}), bf16[4,32,1920]{2,1,0:T(8,128)(2,1)S(1)}, u32[]{:S(2)}, u32[]{:S(2)}) async-start(bf16[4,32,1920]{2,1,0:T(8,128)(2,1)} %bitcast.18), calls=%async_computation | async-start | bytes 983040 | tf_op jit(solution)/shard_map/cond/branch_1_fun/all_to_all | solution.py:307
  34.5 3.0 %branch_1_fun.3 = (bf16[576,384]{1,0:T(8,128)(2,1)}, bf16[1024,384]{1,0:T(8,128)(2,1)}, bf16[1536,256]{1,0:T(8,128)(2,1)}) custom-call(s32[6]{0:T(128)S(1)} %get-tuple-element.11.pos, bf16[2,1536,384]{2,1,0:T(8,128)(2,1)} %get-tuple-element.13.w), custom_call_target="tpu_custom_call" | custom-call | flops 4000000000 | tf_op jit(solution)/shard_map/cond/branch_1_fun/pallas_call | solution.py:226
  37.5 4.1 %all-to-all-done = bf16[4,32,1920]{2,1,0:T(8,128)(2,1)S(1)} async-done(((bf16[4,32,1920]{2,1,0:T(8,128)(2,1)}), bf16[4,32,1920]{2,1,0:T(8,128)(2,1)S(1)}, u32[]{:S(2)}, u32[]{:S(2)}) %all-to-all-start) | async-done | bytes 491552 | tf_op jit(solution)/shard_map/cond/branch_1_fun/all_to_all | solution.py:307
  41.6 0.7 branch_1_fun.2
  42.3 0.0 copy-start.1
  42.3 0.0 collective-permute-done.5.refs_1_
  42.3 0.4 collective-permute-start.6
  42.7 0.5 copy-done.1
  43.2 8.2 %all-to-all-start.2 = ((bf16[8,16,2560]{2,1,0:T(8,128)(2,1)}), bf16[8,16,2560]{2,1,0:T(8,128)(2,1)S(1)}, u32[]{:S(2)}, u32[]{:S(2)}) async-start(bf16[8,16,2560]{2,1,0:T(8,128)(2,1)} %bitcast.16), calls=%async_computation.2 | async-start | bytes 1310720 | tf_op jit(solution)/shard_map/all_to_all | solution.py:325
  51.4 0.0 collective-permute-done
  51.4 0.0 collective-permute-done.1
  51.4 0.0 collective-permute-done.2
  51.4 0.0 collective-permute-done.6.refs_2_.refs_0_
  51.4 0.0 copy-done.2
  51.4 1.6 %add_convert_fusion = bf16[128,1920]{1,0:T(8,128)(2,1)S(1)} fusion(bf16[128,1920]{1,0:T(8,128)(2,1)} %collective-permute-done.2, bf16[128,1920]{1,0:T(8,128)(2,1)} %collective-permute-done.1, bf16[128,1920]{1,0:T(8,128)(2,1)} %collective-permute-done, bf16[128,1920]{1,0:T(8,128)(2,1)S(1)} %copy-done.2), kind=kLoop, calls=%fused_computation | loop fusion | flops 1966080 | bytes 2457600 | tf_op jit(solution)/shard_map/convert_element_type | solution.py:327
  53.0 0.1 constant_dynamic-slice_fusion.6
  53.1 0.8 collective-permute-start.7
  53.9 1.5 %collective-permute-start.8 = (bf16[32,1920]{1,0:T(8,128)(2,1)S(1)}, bf16[32,1920]{1,0:T(8,128)(2,1)S(1)}, u32[]{:S(2)}, u32[]{:S(2)}) collective-permute-start(bf16[32,1920]{1,0:T(8,128)(2,1)S(1)} %pad_maximum_fusion.2), channel_id=1, source_target_pairs={{0,32},{16,48},{32,0},{48,16},{1,33},{17,49},{33,1},{49,17},{2,34}... | collective-permute-start | bytes 368648 | tf_op jit(solution)/shard_map/ppermute | solution.py:262
  55.4 1.4 %collective-permute-start.9 = (bf16[32,1920]{1,0:T(8,128)(2,1)S(1)}, bf16[32,1920]{1,0:T(8,128)(2,1)S(1)}, u32[]{:S(2)}, u32[]{:S(2)}) collective-permute-start(bf16[32,1920]{1,0:T(8,128)(2,1)S(1)} %pad_maximum_fusion.3), channel_id=1, source_target_pairs={{0,48},{16,0},{32,16},{48,32},{1,49},{17,1},{33,17},{49,33},{2,50}... | collective-permute-start | bytes 368648 | tf_op jit(solution)/shard_map/ppermute | solution.py:262
  56.8 2.7 %collective-permute-done.7 = bf16[32,1920]{1,0:T(8,128)(2,1)S(1)} collective-permute-done((bf16[32,1920]{1,0:T(8,128)(2,1)S(1)}, bf16[32,1920]{1,0:T(8,128)(2,1)S(1)}, u32[]{:S(2)}, u32[]{:S(2)}) %collective-permute-start.7) | collective-permute-done | bytes 122912 | tf_op jit(solution)/shard_map/ppermute | solution.py:262
  59.4 0.0 collective-permute-done.8
  59.4 0.7 collective-permute-done.9
  60.1 0.1 multiply_convert_fusion
  60.2 0.8 collective-permute-start.10
  61.0 3.0 %collective-permute-start.11 = (bf16[32,1920]{1,0:T(8,128)(2,1)S(1)}, bf16[32,1920]{1,0:T(8,128)(2,1)S(1)}, u32[]{:S(2)}, u32[]{:S(2)}) collective-permute-start(bf16[32,1920]{1,0:T(8,128)(2,1)S(1)} %multiply_convert_fusion), channel_id=1, source_target_pairs={{0,32},{16,48},{32,0},{48,16},{1,33},{17,49},{33,1},{49,17},{2,34}... | collective-permute-start | bytes 368648 | tf_op jit(solution)/shard_map/ppermute | solution.py:262
  64.0 0.0 collective-permute-start.12
  64.0 2.0 %collective-permute-done.10 = bf16[32,1920]{1,0:T(8,128)(2,1)S(1)} collective-permute-done((bf16[32,1920]{1,0:T(8,128)(2,1)S(1)}, bf16[32,1920]{1,0:T(8,128)(2,1)S(1)}, u32[]{:S(2)}, u32[]{:S(2)}) %collective-permute-start.10) | collective-permute-done | bytes 122912 | tf_op jit(solution)/shard_map/ppermute | solution.py:262
  66.0 1.6 %collective-permute-done.11 = bf16[32,1920]{1,0:T(8,128)(2,1)S(1)} collective-permute-done((bf16[32,1920]{1,0:T(8,128)(2,1)S(1)}, bf16[32,1920]{1,0:T(8,128)(2,1)S(1)}, u32[]{:S(2)}, u32[]{:S(2)}) %collective-permute-start.11) | collective-permute-done | bytes 122912 | tf_op jit(solution)/shard_map/ppermute | solution.py:262
  67.6 0.1 collective-permute-done.12
  67.8 1.1 all-to-all-done.2
  68.8 7.6 %collective-permute-start.16 = (bf16[128,2560]{1,0:T(8,128)(2,1)S(1)}, bf16[128,2560]{1,0:T(8,128)(2,1)S(1)}, u32[]{:S(2)}, u32[]{:S(2)}) collective-permute-start(bf16[128,2560]{1,0:T(8,128)(2,1)S(1)} %bitcast.13), channel_id=1, source_target_pairs={{0,1},{1,0},{2,3},{3,2},{4,5},{5,4},{6,7},{7,6},{8,9},{9,8},{10,11... | collective-permute-start | bytes 1966088 | tf_op jit(solution)/shard_map/ppermute | solution.py:337
  76.4 0.0 collective-permute-start.13
  76.4 1.6 %collective-permute-start.14 = (bf16[128,1920]{1,0:T(8,128)(2,1)S(1)}, bf16[128,1920]{1,0:T(8,128)(2,1)S(1)}, u32[]{:S(2)}, u32[]{:S(2)}) collective-permute-start(bf16[128,1920]{1,0:T(8,128)(2,1)S(1)} %pad_maximum_fusion.p0), channel_id=1, source_target_pairs={{0,128},{64,192},{128,0},{192,64},{1,129},{65,193},{129,1},{193,65... | collective-permute-start | bytes 1474568 | tf_op jit(solution)/shard_map/ppermute | solution.py:262
  78.0 1.1 %collective-permute-start.15 = (bf16[128,1920]{1,0:T(8,128)(2,1)S(1)}, bf16[128,1920]{1,0:T(8,128)(2,1)S(1)}, u32[]{:S(2)}, u32[]{:S(2)}) collective-permute-start(bf16[128,1920]{1,0:T(8,128)(2,1)S(1)} %pad_maximum_fusion.p0), channel_id=1, source_target_pairs={{0,192},{64,0},{128,64},{192,128},{1,193},{65,1},{129,65},{193,129... | collective-permute-start | bytes 1474568 | tf_op jit(solution)/shard_map/ppermute | solution.py:262
  79.1 0.7 collective-permute-start.17
  79.8 0.0 collective-permute-done.16.other
  79.9 2.2 %collective-permute-start.18 = (bf16[1024,384]{1,0:T(8,128)(2,1)}, bf16[1024,384]{1,0:T(8,128)(2,1)S(1)}, u32[]{:S(2)}, u32[]{:S(2)}) collective-permute-start(bf16[1024,384]{1,0:T(8,128)(2,1)} %get-tuple-element.74), channel_id=1, source_target_pairs={{0,16},{16,0},{32,48},{48,32},{1,17},{17,1},{33,49},{49,33},{2,18}... | collective-permute-start | bytes 2359304 | tf_op jit(solution)/shard_map/ppermute | solution.py:270
  82.0 3.9 %shard_map.40.factor = bf16[2,1024,384]{2,1,0:T(8,128)(2,1)S(1)} custom-call(s32[6]{0:T(128)S(1)} %stack.27.pos, bf16[128,2560]{1,0:T(8,128)(2,1)S(1)} %bitcast.14, bf16[128,2560]{1,0:T(8,128)(2,1)S(1)} %collective-permute-done.16.other), custom_call_target="tpu_custom_call" | custom-call | flops 10000000000 | tf_op jit(solution)/shard_map/pallas_call | solution.py:226
  86.0 0.0 copy-done
  86.0 2.6 %shard_map.41.r0 = bf16[1536,384]{1,0:T(8,128)(2,1)S(1)} custom-call(s32[6]{0:T(128)S(1)} %stack.27.pos, bf16[2,1536,384]{2,1,0:T(8,128)(2,1)S(1)} %copy-done, bf16[1536,256]{1,0:T(8,128)(2,1)S(1)} %collective-permute-done.4.w_mid, bf16[2,1024,384]{2,1,0:T(8,128)(2,1)S(1)} %shard_map.40.factor, bf16[1024,384]{1,0:T(8,128)(2,1)S(1)} %collective-permute-done.3.refs_0_, ...), custom_call_target="tpu_custom_call" | custom-call | tf_op jit(solution)/shard_map/pallas_call | solution.py:226
  88.6 0.0 collective-permute-done.17.w_mid
  88.6 10.4 %collective-permute-done.18.refs_1_ = bf16[1024,384]{1,0:T(8,128)(2,1)S(1)} collective-permute-done((bf16[1024,384]{1,0:T(8,128)(2,1)}, bf16[1024,384]{1,0:T(8,128)(2,1)S(1)}, u32[]{:S(2)}, u32[]{:S(2)}) %collective-permute-start.18) | collective-permute-done | bytes 786464 | tf_op jit(solution)/shard_map/ppermute | solution.py:270
  99.0 2.5 %shard_map.42.r1 = bf16[1536,384]{1,0:T(8,128)(2,1)S(1)} custom-call(s32[6]{0:T(128)S(1)} %stack.27.pos, bf16[2,1536,384]{2,1,0:T(8,128)(2,1)S(1)} %copy-done, bf16[1536,256]{1,0:T(8,128)(2,1)S(1)} %collective-permute-done.17.w_mid, bf16[2,1024,384]{2,1,0:T(8,128)(2,1)S(1)} %shard_map.40.factor, bf16[576,384]{1,0:T(8,128)(2,1)S(1)} %collective-permute-done.6.refs_2_.refs_0_, ...), custom_call_target="tpu_custom_call" | custom-call | tf_op jit(solution)/shard_map/pallas_call | solution.py:226
  101.6 0.0 collective-permute-done.13.p1
  101.6 0.0 collective-permute-done.14.p2
  101.6 0.0 collective-permute-done.15.p3
  101.6 7.4 %shard_map.43 = bf16[2,1536,384]{2,1,0:T(8,128)(2,1)} custom-call(s32[6]{0:T(128)S(1)} %stack.27.pos, bf16[128,1920]{1,0:T(8,128)(2,1)S(1)} %pad_maximum_fusion.p0, bf16[128,1920]{1,0:T(8,128)(2,1)S(1)} %collective-permute-done.13.p1, bf16[128,1920]{1,0:T(8,128)(2,1)S(1)} %collective-permute-done.14.p2, bf16[128,1920]{1,0:T(8,128)(2,1)S(1)} %collective-permute-done.15.p3, ...), custom_call_target="tpu_custom_call" | custom-call | tf_op jit(solution)/shard_map/pallas_call | solution.py:226
  (7 shorter events, 0.1 us)
Async XLA Ops:
  6.6 18.4 %collective-permute-start.3 = (bf16[1024,384]{1,0:T(8,128)(2,1)}, bf16[1024,384]{1,0:T(8,128)(2,1)S(1)}, u32[]{:S(2)}, u32[]{:S(2)}) collective-permute-start(bf16[1024,384]{1,0:T(8,128)(2,1)} %get-tuple-element.53), channel_id=1, source_target_pairs={{0,16},{16,0},{32,48},{48,32},{1,17},{17,1},{33,49},{49,33},{2,18}... | collective-permute-start | bytes 2359304 | tf_op jit(solution)/shard_map/ppermute | solution.py:270
  8.8 20.1 %collective-permute-start.4 = (bf16[1536,256]{1,0:T(8,128)(2,1)}, bf16[1536,256]{1,0:T(8,128)(2,1)S(1)}, u32[]{:S(2)}, u32[]{:S(2)}) collective-permute-start(bf16[1536,256]{1,0:T(8,128)(2,1)} %get-tuple-element.54), channel_id=1, source_target_pairs={{16,32},{32,16},{17,33},{33,17},{18,34},{34,18},{19,35},{35,19},{2... | collective-permute-start | bytes 2359304 | tf_op jit(solution)/shard_map/ppermute | solution.py:274
  9.5 19.4 %all-to-all-start.1 = ((bf16[4,32,1920]{2,1,0:T(8,128)(2,1)}), bf16[4,32,1920]{2,1,0:T(8,128)(2,1)S(1)}, u32[]{:S(2)}, u32[]{:S(2)}) async-start(bf16[4,32,1920]{2,1,0:T(8,128)(2,1)} %bitcast.17), calls=%async_computation.1 | async-start | bytes 983040 | tf_op jit(solution)/shard_map/all_to_all | solution.py:294
  13.7 28.7 %collective-permute-start.5 = (bf16[448,384]{1,0:T(8,128)(2,1)}, bf16[448,384]{1,0:T(8,128)(2,1)S(1)}, u32[]{:S(2)}, u32[]{:S(2)}) collective-permute-start(bf16[448,384]{1,0:T(8,128)(2,1)} %get-tuple-element.58), channel_id=1, source_target_pairs={{0,16},{16,0},{32,48},{48,32},{1,17},{17,1},{33,49},{49,33},{2,18}... | collective-permute-start | bytes 1032200 | tf_op jit(solution)/shard_map/ppermute | solution.py:270
  21.1 30.3 %collective-permute-start = (bf16[128,1920]{1,0:T(8,128)(2,1)}, bf16[128,1920]{1,0:T(8,128)(2,1)}, u32[]{:S(2)}, u32[]{:S(2)}) collective-permute-start(bf16[128,1920]{1,0:T(8,128)(2,1)} %get-tuple-element.49), channel_id=1, source_target_pairs={{0,64},{64,128},{128,192},{192,0},{1,65},{65,129},{129,193},{193,1... | collective-permute-start | bytes 1474568 | tf_op jit(solution)/shard_map/ppermute | solution.py:262
  22.5 28.9 %collective-permute-start.1 = (bf16[128,1920]{1,0:T(8,128)(2,1)}, bf16[128,1920]{1,0:T(8,128)(2,1)}, u32[]{:S(2)}, u32[]{:S(2)}) collective-permute-start(bf16[128,1920]{1,0:T(8,128)(2,1)} %get-tuple-element.50), channel_id=1, source_target_pairs={{0,128},{64,192},{128,0},{192,64},{1,129},{65,193},{129,1},{193,65... | collective-permute-start | bytes 1474568 | tf_op jit(solution)/shard_map/ppermute | solution.py:262
  25.0 26.4 %collective-permute-start.2 = (bf16[128,1920]{1,0:T(8,128)(2,1)}, bf16[128,1920]{1,0:T(8,128)(2,1)}, u32[]{:S(2)}, u32[]{:S(2)}) collective-permute-start(bf16[128,1920]{1,0:T(8,128)(2,1)} %get-tuple-element.51), channel_id=1, source_target_pairs={{0,192},{64,0},{128,64},{192,128},{1,193},{65,1},{129,65},{193,129... | collective-permute-start | bytes 1474568 | tf_op jit(solution)/shard_map/ppermute | solution.py:262
  29.5 0.8 copy-start.3
  30.3 11.3 %all-to-all-start = ((bf16[4,32,1920]{2,1,0:T(8,128)(2,1)}), bf16[4,32,1920]{2,1,0:T(8,128)(2,1)S(1)}, u32[]{:S(2)}, u32[]{:S(2)}) async-start(bf16[4,32,1920]{2,1,0:T(8,128)(2,1)} %bitcast.18), calls=%async_computation | async-start | bytes 983040 | tf_op jit(solution)/shard_map/cond/branch_1_fun/all_to_all | solution.py:307
  42.3 0.9 copy-start.1
  42.3 9.1 %copy-start.2 = (bf16[128,1920]{1,0:T(8,128)(2,1)S(1)}, bf16[128,1920]{1,0:T(8,128)(2,1)}, u32[]{:S(2)}) copy-start(bf16[128,1920]{1,0:T(8,128)(2,1)} %get-tuple-element.61) | copy-start | bytes 1474564
  42.3 9.1 %collective-permute-start.6 = (bf16[576,384]{1,0:T(8,128)(2,1)}, bf16[576,384]{1,0:T(8,128)(2,1)S(1)}, u32[]{:S(2)}, u32[]{:S(2)}) collective-permute-start(bf16[576,384]{1,0:T(8,128)(2,1)} %get-tuple-element.60), channel_id=1, source_target_pairs={{0,16},{16,0},{32,48},{48,32},{1,17},{17,1},{33,49},{49,33},{2,18}... | collective-permute-start | bytes 1327112 | tf_op jit(solution)/shard_map/ppermute | solution.py:270
  43.2 25.7 %all-to-all-start.2 = ((bf16[8,16,2560]{2,1,0:T(8,128)(2,1)}), bf16[8,16,2560]{2,1,0:T(8,128)(2,1)S(1)}, u32[]{:S(2)}, u32[]{:S(2)}) async-start(bf16[8,16,2560]{2,1,0:T(8,128)(2,1)} %bitcast.16), calls=%async_computation.2 | async-start | bytes 1310720 | tf_op jit(solution)/shard_map/all_to_all | solution.py:325
  53.1 6.3 %collective-permute-start.7 = (bf16[32,1920]{1,0:T(8,128)(2,1)S(1)}, bf16[32,1920]{1,0:T(8,128)(2,1)S(1)}, u32[]{:S(2)}, u32[]{:S(2)}) collective-permute-start(bf16[32,1920]{1,0:T(8,128)(2,1)S(1)} %pad_maximum_fusion.1), channel_id=1, source_target_pairs={{0,16},{16,32},{32,48},{48,0},{1,17},{17,33},{33,49},{49,1},{2,18}... | collective-permute-start | bytes 368648 | tf_op jit(solution)/shard_map/ppermute | solution.py:262
  53.9 5.5 %collective-permute-start.8 = (bf16[32,1920]{1,0:T(8,128)(2,1)S(1)}, bf16[32,1920]{1,0:T(8,128)(2,1)S(1)}, u32[]{:S(2)}, u32[]{:S(2)}) collective-permute-start(bf16[32,1920]{1,0:T(8,128)(2,1)S(1)} %pad_maximum_fusion.2), channel_id=1, source_target_pairs={{0,32},{16,48},{32,0},{48,16},{1,33},{17,49},{33,1},{49,17},{2,34}... | collective-permute-start | bytes 368648 | tf_op jit(solution)/shard_map/ppermute | solution.py:262
  55.4 4.7 %collective-permute-start.9 = (bf16[32,1920]{1,0:T(8,128)(2,1)S(1)}, bf16[32,1920]{1,0:T(8,128)(2,1)S(1)}, u32[]{:S(2)}, u32[]{:S(2)}) collective-permute-start(bf16[32,1920]{1,0:T(8,128)(2,1)S(1)} %pad_maximum_fusion.3), channel_id=1, source_target_pairs={{0,48},{16,0},{32,16},{48,32},{1,49},{17,1},{33,17},{49,33},{2,50}... | collective-permute-start | bytes 368648 | tf_op jit(solution)/shard_map/ppermute | solution.py:262
  60.2 5.8 %collective-permute-start.10 = (bf16[32,1920]{1,0:T(8,128)(2,1)S(1)}, bf16[32,1920]{1,0:T(8,128)(2,1)S(1)}, u32[]{:S(2)}, u32[]{:S(2)}) collective-permute-start(bf16[32,1920]{1,0:T(8,128)(2,1)S(1)} %multiply_convert_fusion), channel_id=1, source_target_pairs={{0,16},{16,32},{32,48},{48,0},{1,17},{17,33},{33,49},{49,1},{2,18}... | collective-permute-start | bytes 368648 | tf_op jit(solution)/shard_map/ppermute | solution.py:262
  61.0 6.6 %collective-permute-start.11 = (bf16[32,1920]{1,0:T(8,128)(2,1)S(1)}, bf16[32,1920]{1,0:T(8,128)(2,1)S(1)}, u32[]{:S(2)}, u32[]{:S(2)}) collective-permute-start(bf16[32,1920]{1,0:T(8,128)(2,1)S(1)} %multiply_convert_fusion), channel_id=1, source_target_pairs={{0,32},{16,48},{32,0},{48,16},{1,33},{17,49},{33,1},{49,17},{2,34}... | collective-permute-start | bytes 368648 | tf_op jit(solution)/shard_map/ppermute | solution.py:262
  64.0 3.7 %collective-permute-start.12 = (bf16[32,1920]{1,0:T(8,128)(2,1)S(1)}, bf16[32,1920]{1,0:T(8,128)(2,1)S(1)}, u32[]{:S(2)}, u32[]{:S(2)}) collective-permute-start(bf16[32,1920]{1,0:T(8,128)(2,1)S(1)} %multiply_convert_fusion), channel_id=1, source_target_pairs={{0,48},{16,0},{32,16},{48,32},{1,49},{17,1},{33,17},{49,33},{2,50}... | collective-permute-start | bytes 368648 | tf_op jit(solution)/shard_map/ppermute | solution.py:262
  68.8 11.0 %collective-permute-start.16 = (bf16[128,2560]{1,0:T(8,128)(2,1)S(1)}, bf16[128,2560]{1,0:T(8,128)(2,1)S(1)}, u32[]{:S(2)}, u32[]{:S(2)}) collective-permute-start(bf16[128,2560]{1,0:T(8,128)(2,1)S(1)} %bitcast.13), channel_id=1, source_target_pairs={{0,1},{1,0},{2,3},{3,2},{4,5},{5,4},{6,7},{7,6},{8,9},{9,8},{10,11... | collective-permute-start | bytes 1966088 | tf_op jit(solution)/shard_map/ppermute | solution.py:337
  76.4 25.1 %collective-permute-start.13 = (bf16[128,1920]{1,0:T(8,128)(2,1)S(1)}, bf16[128,1920]{1,0:T(8,128)(2,1)S(1)}, u32[]{:S(2)}, u32[]{:S(2)}) collective-permute-start(bf16[128,1920]{1,0:T(8,128)(2,1)S(1)} %pad_maximum_fusion.p0), channel_id=1, source_target_pairs={{0,64},{64,128},{128,192},{192,0},{1,65},{65,129},{129,193},{193,1... | collective-permute-start | bytes 1474568 | tf_op jit(solution)/shard_map/ppermute | solution.py:262
  76.4 25.1 %collective-permute-start.14 = (bf16[128,1920]{1,0:T(8,128)(2,1)S(1)}, bf16[128,1920]{1,0:T(8,128)(2,1)S(1)}, u32[]{:S(2)}, u32[]{:S(2)}) collective-permute-start(bf16[128,1920]{1,0:T(8,128)(2,1)S(1)} %pad_maximum_fusion.p0), channel_id=1, source_target_pairs={{0,128},{64,192},{128,0},{192,64},{1,129},{65,193},{129,1},{193,65... | collective-permute-start | bytes 1474568 | tf_op jit(solution)/shard_map/ppermute | solution.py:262
  78.0 23.6 %collective-permute-start.15 = (bf16[128,1920]{1,0:T(8,128)(2,1)S(1)}, bf16[128,1920]{1,0:T(8,128)(2,1)S(1)}, u32[]{:S(2)}, u32[]{:S(2)}) collective-permute-start(bf16[128,1920]{1,0:T(8,128)(2,1)S(1)} %pad_maximum_fusion.p0), channel_id=1, source_target_pairs={{0,192},{64,0},{128,64},{192,128},{1,193},{65,1},{129,65},{193,129... | collective-permute-start | bytes 1474568 | tf_op jit(solution)/shard_map/ppermute | solution.py:262
  79.1 9.4 %collective-permute-start.17 = (bf16[1536,256]{1,0:T(8,128)(2,1)}, bf16[1536,256]{1,0:T(8,128)(2,1)S(1)}, u32[]{:S(2)}, u32[]{:S(2)}) collective-permute-start(bf16[1536,256]{1,0:T(8,128)(2,1)} %get-tuple-element.73), channel_id=1, source_target_pairs={{16,32},{32,16},{17,33},{33,17},{18,34},{34,18},{19,35},{35,19},{2... | collective-permute-start | bytes 2359304 | tf_op jit(solution)/shard_map/ppermute | solution.py:274
  79.9 19.2 %collective-permute-start.18 = (bf16[1024,384]{1,0:T(8,128)(2,1)}, bf16[1024,384]{1,0:T(8,128)(2,1)S(1)}, u32[]{:S(2)}, u32[]{:S(2)}) collective-permute-start(bf16[1024,384]{1,0:T(8,128)(2,1)} %get-tuple-element.74), channel_id=1, source_target_pairs={{0,16},{16,0},{32,48},{48,32},{1,17},{17,1},{33,49},{49,33},{2,18}... | collective-permute-start | bytes 2359304 | tf_op jit(solution)/shard_map/ppermute | solution.py:270
  82.0 3.9 %copy-start = (bf16[2,1536,384]{2,1,0:T(8,128)(2,1)S(1)}, bf16[2,1536,384]{2,1,0:T(8,128)(2,1)}, u32[]{:S(2)}) copy-start(bf16[2,1536,384]{2,1,0:T(8,128)(2,1)} %w_own.3) | copy-start | bytes 7077892

commit v11 on v10

--- a/solution.py
+++ b/solution.py
@@ -17,7 +17,9 @@
 
 PAIRS = [(r, c) for r in range(4) for c in range(r, 4)]
 LANES = 15 * SUB
-PARTS = 1024, 448, 64
+ABOVE = [(r, c) for r in range(4) for c in range(r + 1, 4)]
+DENSE = 13 * SUB
+PARTS = 1024, 496, 16
 
 
 def tn_dot(a, b):
@@ -53,18 +55,31 @@
 
 def cov_kernel(pos, grads, h0, h1, h2, h3, pack):
     y = pos[1]
+    row = lax.broadcasted_iota(jnp.int32, (SUB, SUB), 0)
+    column = lax.broadcasted_iota(jnp.int32, (SUB, SUB), 1)
     for layer in range(2):
+        def store(s, tile):
+            at = slice(s // 13 * SUB, (s // 13 + 1) * SUB), slice(s % 13 * SUB, (s % 13 + 1) * SUB)
+            pack[layer, at[0], at[1]] = tile.astype(BF16)
+
+        diagonals = jnp.zeros((SUB, SUB), F32)
         for b in range(3):
             rows = grads[layer, :, b * BLK:(b + 1) * BLK]
-            top = tn_dot(rows[:, :256], rows).astype(BF16)
-            low = tn_dot(rows[:, 256:], rows[:, 256:]).astype(BF16)
-            for i, (r, c) in enumerate(PAIRS):
-                s = 10 * b + i
-                if r < 2:
-                    piece = top[r * SUB:(r + 1) * SUB, c * SUB:(c + 1) * SUB]
-                else:
-                    piece = low[(r - 2) * SUB:(r - 1) * SUB, (c - 2) * SUB:(c - 1) * SUB]
-                pack[layer, s // 15 * SUB:(s // 15 + 1) * SUB, s % 15 * SUB:(s % 15 + 1) * SUB] = piece
+            halves = tn_dot(rows[:, :256], rows), tn_dot(rows[:, 256:], rows[:, 256:])
+
+            def tile(r, c):
+                first = r // 2 * 2
+                return halves[r // 2][(r - first) * SUB:(r - first + 1) * SUB, (c - first) * SUB:(c - first + 1) * SUB]
+
+            for i, (r, c) in enumerate(ABOVE):
+                store(8 * b + i, tile(r, c))
+            for k in range(2):
+                lower = tile(2 * k + 1, 2 * k + 1)
+                store(8 * b + 6 + k, jnp.where(row <= column, tile(2 * k, 2 * k), lower))
+                line = jnp.sum(jnp.where(row == column, lower, 0.0), axis=1, keepdims=True)
+                diagonals = jnp.where(column == 2 * b + k, line, diagonals)
+        store(24, diagonals)
+        store(25, jnp.zeros((SUB, SUB), F32))
     for d, send in enumerate((h0, h1, h2, h3)):
         at = pl.multiple_of((y + d) % 4 * 64, 64)
         send[0:64, :] = pack[0, pl.ds(at, 64), :]
@@ -144,6 +159,23 @@
         full[r * SUB:(r + 1) * SUB, c * SUB:(c + 1) * SUB] = tile.astype(full.dtype)
         if r != c:
             full[c * SUB:(c + 1) * SUB, r * SUB:(r + 1) * SUB] = tile.T.astype(full.dtype)
+
+
+def unpack_dense(b, tile, full):
+    row = lax.broadcasted_iota(jnp.int32, (SUB, SUB), 0)
+    column = lax.broadcasted_iota(jnp.int32, (SUB, SUB), 1)
+    at = [slice(n * SUB, (n + 1) * SUB) for n in range(4)]
+    for i, (r, c) in enumerate(ABOVE):
+        piece = tile(8 * b + i)
+        full[at[r], at[c]] = piece
+        full[at[c], at[r]] = piece.T
+    diagonals = tile(24)
+    for k in range(2):
+        piece = tile(8 * b + 6 + k)
+        turned = piece.T
+        line = jnp.sum(jnp.where(column == 2 * b + k, diagonals, 0.0), axis=1, keepdims=True)
+        full[at[2 * k], at[2 * k]] = jnp.where(row <= column, piece, turned)
+        full[at[2 * k + 1], at[2 * k + 1]] = jnp.where(row > column, piece, jnp.where(row == column, line, turned))
 
 
 def invert(full):
@@ -207,12 +239,11 @@
                 at = (y + 4 - d) % 4 * 64 + (x + 4 - e) % 4 * 16
                 rows = 32 * e + 16 * layer
                 pack[layer, pl.ds(pl.multiple_of(at, 16), 16), :] = part[rows:rows + 16, :]
+        def tile(s):
+            return pack[layer, s // 13 * SUB:(s // 13 + 1) * SUB, s % 13 * SUB:(s % 13 + 1) * SUB].astype(F32)
+
         for b in range(3):
-            def piece(i):
-                s = 10 * b + i
-                return pack[layer, s // 15 * SUB:(s // 15 + 1) * SUB, s % 15 * SUB:(s % 15 + 1) * SUB].astype(F32)
-
-            unpack(piece, full.at[layer, b])
+            unpack_dense(b, tile, full.at[layer, b])
             at = b * BLK
             n = 3 * layer + b
             ready[n] = nn_dot(invert(full.at[layer, b]), right[at:at + BLK, :]).astype(BF16)
@@ -294,8 +325,8 @@
     side = lax.all_to_all(side, "y", 0, 0, tiled=True)
 
     covs = call(
-        cov_kernel, pos, (grads_out,), [whole(grads_out)], [shape(128, LANES)] * 4,
-        [VMEM((2, 256, LANES), BF16)], vmem=60, flops=12_000_000_000,
+        cov_kernel, pos, (grads_out,), [whole(grads_out)], [shape(128, DENSE)] * 4,
+        [VMEM((2, 256, DENSE), BF16)], vmem=60, flops=12_000_000_000,
     )
     start = covs[0]
     covs = spread(covs, "y")
@@ -354,7 +385,7 @@
         left_kernel, pos, (*parts, *rights), [whole(a) for a in (*parts, *rights)],
         [shape(*weight_grad.shape)],
         [
-            VMEM((2, 256, LANES), BF16), VMEM((2, 3, BLK, BLK), F32), VMEM((6, BLK, width), BF16),
+            VMEM((2, 256, DENSE), BF16), VMEM((2, 3, BLK, BLK), F32), VMEM((6, BLK, width), BF16),
             pltpu.SemaphoreType.DMA((6,)),
         ],
         out_specs=[ANYWHERE],

time: 110 us -> 110 us (level)
  transfers between devices with their start and end apart: 22 -> 22, of which waited for: 9 -> 10; matrix products, arithmetic and copies ran while one was open for 2% -> 2% of each run, Pallas kernels for 16% -> 16%
where the time goes in v11:
time: 110 us; the launch traced here: 109 us
  starting transfers between devices  50.6 us (46%)
  Pallas kernels  31.6 us (29%)
  waiting for transfers between devices  22.9 us (21%)
  other arithmetic  1.62 us (1%)
  local copies, waits for them, and re-layouts  1.46 us (1%)
    pallas_call x9, Pallas kernels, call(): pl.pallas_call(kernel, grid_spec=pltpu.PrefetchScalarGridSpec(num_scalar_...  31.6 us
    ppermute x12, starting transfers between devices, spread(): lax.ppermute(parts[d], axis, [(i, (i + d) % 4) for i in range(4)])  17.7 us
    ppermute x4, waiting for transfers between devices, paired(): return lax.ppermute(w, 'x', [(0, 1), (1, 0), (2, 3), (3, 2)])  10.4 us
    all_to_all x1, starting transfers between devices, body(): mine = lax.all_to_all(side, 'z', 0, 0, tiled=True)  8.17 us
    ppermute x4, starting transfers between devices, paired(): return lax.ppermute(w, 'x', [(0, 1), (1, 0), (2, 3), (3, 2)])  8.01 us
    ppermute x1, starting transfers between devices, body(): other = lax.ppermute(mine, 'c', [(0, 1), (1, 0)])  6.98 us
    ppermute x12, waiting for transfers between devices, spread(): lax.ppermute(parts[d], axis, [(i, (i + d) % 4) for i in range(4)])  6.87 us
    all_to_all x1, starting transfers between devices, body(): side = lax.all_to_all(side, 'y', 0, 0, tiled=True)  4.2 us
  transfers between devices with their start and end apart: 22, of which 10 were waited for; matrix products, arithmetic and copies ran while one was open for 2% of the time, Pallas kernels for 16%

profile of v11, /device:TPU:1, one launch (start us, length us, event | category | flops | bytes accessed | tf_op | source)
XLA Modules:
  0.0 108.5 jit_solution(11305775571289783331)
XLA Ops:
  0.0 0.1 stack.27.pos
  0.1 6.5 %shard_map.37 = (bf16[128,1920]{1,0:T(8,128)(2,1)}, bf16[1024,384]{1,0:T(8,128)(2,1)}, bf16[496,384]{1,0:T(8,128)(2,1)}, bf16[1536,256]{1,0:T(8,128)(2,1)}) custom-call(s32[6]{0:T(128)S(1)} %stack.27.pos, bf16[2,256,6144]{2,1,0:T(8,128)(2,1)} %acts.1, bf16[2,1536,384]{2,1,0:T(8,128)(2,1)} %w_own.3), custom_call_target="tpu_custom_call" | custom-call | tf_op jit(solution)/shard_map/pallas_call | solution.py:257
  6.6 2.1 %collective-permute-start.3 = (bf16[1024,384]{1,0:T(8,128)(2,1)}, bf16[1024,384]{1,0:T(8,128)(2,1)S(1)}, u32[]{:S(2)}, u32[]{:S(2)}) collective-permute-start(bf16[1024,384]{1,0:T(8,128)(2,1)} %get-tuple-element.53), channel_id=1, source_target_pairs={{0,16},{16,0},{32,48},{48,32},{1,17},{17,1},{33,49},{49,33},{2,18}... | collective-permute-start | bytes 2359304 | tf_op jit(solution)/shard_map/ppermute | solution.py:301
  8.8 0.7 collective-permute-start.4
  9.5 4.2 %all-to-all-start.1 = ((bf16[4,32,1920]{2,1,0:T(8,128)(2,1)}), bf16[4,32,1920]{2,1,0:T(8,128)(2,1)S(1)}, u32[]{:S(2)}, u32[]{:S(2)}) async-start(bf16[4,32,1920]{2,1,0:T(8,128)(2,1)} %bitcast.17), calls=%async_computation.1 | async-start | bytes 983040 | tf_op jit(solution)/shard_map/all_to_all | solution.py:325
  13.7 3.3 %collective-permute-start.5 = (bf16[496,384]{1,0:T(8,128)(2,1)}, bf16[496,384]{1,0:T(8,128)(2,1)S(1)}, u32[]{:S(2)}, u32[]{:S(2)}) collective-permute-start(bf16[496,384]{1,0:T(8,128)(2,1)} %get-tuple-element.58), channel_id=1, source_target_pairs={{0,16},{16,0},{32,48},{48,32},{1,17},{17,1},{33,49},{49,33},{2,18}... | collective-permute-start | bytes 1142792 | tf_op jit(solution)/shard_map/ppermute | solution.py:301
  17.0 4.1 %shard_map.38 = (bf16[128,1664]{1,0:T(8,128)(2,1)}, bf16[128,1664]{1,0:T(8,128)(2,1)}, bf16[128,1664]{1,0:T(8,128)(2,1)}, bf16[128,1664]{1,0:T(8,128)(2,1)}) custom-call(s32[6]{0:T(128)S(1)} %stack.27.pos, bf16[2,256,1536]{2,1,0:T(8,128)(2,1)} %grads), custom_call_target="tpu_custom_call" | custom-call | flops 12000000000 | tf_op jit(solution)/shard_map/pallas_call | solution.py:257
  21.0 1.5 %collective-permute-start = (bf16[128,1664]{1,0:T(8,128)(2,1)}, bf16[128,1664]{1,0:T(8,128)(2,1)}, u32[]{:S(2)}, u32[]{:S(2)}) collective-permute-start(bf16[128,1664]{1,0:T(8,128)(2,1)} %get-tuple-element.49), channel_id=1, source_target_pairs={{0,64},{64,128},{128,192},{192,0},{1,65},{65,129},{129,193},{193,1... | collective-permute-start | bytes 1277960 | tf_op jit(solution)/shard_map/ppermute | solution.py:293
  22.5 2.4 %collective-permute-start.1 = (bf16[128,1664]{1,0:T(8,128)(2,1)}, bf16[128,1664]{1,0:T(8,128)(2,1)}, u32[]{:S(2)}, u32[]{:S(2)}) collective-permute-start(bf16[128,1664]{1,0:T(8,128)(2,1)} %get-tuple-element.50), channel_id=1, source_target_pairs={{0,128},{64,192},{128,0},{192,64},{1,129},{65,193},{129,1},{193,65... | collective-permute-start | bytes 1277960 | tf_op jit(solution)/shard_map/ppermute | solution.py:293
  24.9 0.1 collective-permute-done.3.refs_0_
  25.0 3.9 %collective-permute-start.2 = (bf16[128,1664]{1,0:T(8,128)(2,1)}, bf16[128,1664]{1,0:T(8,128)(2,1)}, u32[]{:S(2)}, u32[]{:S(2)}) collective-permute-start(bf16[128,1664]{1,0:T(8,128)(2,1)} %get-tuple-element.51), channel_id=1, source_target_pairs={{0,192},{64,0},{128,64},{192,128},{1,193},{65,1},{129,65},{193,129... | collective-permute-start | bytes 1277960 | tf_op jit(solution)/shard_map/ppermute | solution.py:293
  28.9 0.0 all-to-all-done.1
  28.9 0.0 collective-permute-done.4.w_mid
  28.9 0.6 shard_map.39
  29.5 12.8 %conditional.1 = (bf16[128,2560]{1,0:T(8,128)(2,1)S(1)}, bf16[528,384]{1,0:T(8,128)(2,1)}, bf16[1024,384]{1,0:T(8,128)(2,1)}, bf16[1536,256]{1,0:T(8,128)(2,1)}) conditional(s32[]{:T(128)} %convert_element_type.33, () %tuple.19, (bf16[128,1920]{1,0:T(8,128)(2,1)S(1)}, s32[6]{0:T(128)S(1)}, bf16[2,1536,384]{2,1,0:T(8,128)(2,1)}) %tuple.21), branch_computations={%region_0.1_spmd, %region_1.2_spmd} | conditional | flops 4000000000 | bytes 3440732 | solution.py:347
  29.5 0.0 copy-start.2
  29.5 0.8 copy-done.2
  30.3 4.1 %all-to-all-start = ((bf16[4,32,1920]{2,1,0:T(8,128)(2,1)}), bf16[4,32,1920]{2,1,0:T(8,128)(2,1)S(1)}, u32[]{:S(2)}, u32[]{:S(2)}) async-start(bf16[4,32,1920]{2,1,0:T(8,128)(2,1)} %bitcast.18), calls=%async_computation | async-start | bytes 983040 | tf_op jit(solution)/shard_map/cond/branch_1_fun/all_to_all | solution.py:338
  34.5 3.0 %branch_1_fun.3 = (bf16[528,384]{1,0:T(8,128)(2,1)}, bf16[1024,384]{1,0:T(8,128)(2,1)}, bf16[1536,256]{1,0:T(8,128)(2,1)}) custom-call(s32[6]{0:T(128)S(1)} %get-tuple-element.11.pos, bf16[2,1536,384]{2,1,0:T(8,128)(2,1)} %get-tuple-element.13.w), custom_call_target="tpu_custom_call" | custom-call | flops 4000000000 | tf_op jit(solution)/shard_map/cond/branch_1_fun/pallas_call | solution.py:257
  37.5 4.1 %all-to-all-done = bf16[4,32,1920]{2,1,0:T(8,128)(2,1)S(1)} async-done(((bf16[4,32,1920]{2,1,0:T(8,128)(2,1)}), bf16[4,32,1920]{2,1,0:T(8,128)(2,1)S(1)}, u32[]{:S(2)}, u32[]{:S(2)}) %all-to-all-start) | async-done | bytes 491552 | tf_op jit(solution)/shard_map/cond/branch_1_fun/all_to_all | solution.py:338
  41.6 0.7 branch_1_fun.2
  42.3 0.0 copy-start.1
  42.3 0.0 copy-start.3
  42.3 0.0 collective-permute-done.5.refs_1_
  42.3 0.4 collective-permute-start.6
  42.7 0.5 copy-done.1
  43.2 8.2 %all-to-all-start.2 = ((bf16[8,16,2560]{2,1,0:T(8,128)(2,1)}), bf16[8,16,2560]{2,1,0:T(8,128)(2,1)S(1)}, u32[]{:S(2)}, u32[]{:S(2)}) async-start(bf16[8,16,2560]{2,1,0:T(8,128)(2,1)} %bitcast.16), calls=%async_computation.2 | async-start | bytes 1310720 | tf_op jit(solution)/shard_map/all_to_all | solution.py:356
  51.4 0.0 collective-permute-done
  51.4 0.0 collective-permute-done.1
  51.4 0.0 collective-permute-done.2
  51.4 0.0 collective-permute-done.6.refs_2_.refs_0_
  51.4 0.0 copy-done.3
  51.4 1.5 %add_convert_fusion = bf16[128,1664]{1,0:T(8,128)(2,1)S(1)} fusion(bf16[128,1664]{1,0:T(8,128)(2,1)} %collective-permute-done.2, bf16[128,1664]{1,0:T(8,128)(2,1)} %collective-permute-done.1, bf16[128,1664]{1,0:T(8,128)(2,1)} %collective-permute-done, bf16[128,1664]{1,0:T(8,128)(2,1)S(1)} %copy-done.3), kind=kLoop, calls=%fused_computation | loop fusion | flops 1703936 | bytes 2129920 | tf_op jit(solution)/shard_map/convert_element_type | solution.py:358
  52.9 0.1 constant_dynamic-slice_fusion.6
  53.0 0.8 collective-permute-start.7
  53.8 1.4 %collective-permute-start.8 = (bf16[32,1664]{1,0:T(8,128)(2,1)S(1)}, bf16[32,1664]{1,0:T(8,128)(2,1)S(1)}, u32[]{:S(2)}, u32[]{:S(2)}) collective-permute-start(bf16[32,1664]{1,0:T(8,128)(2,1)S(1)} %pad_maximum_fusion.2), channel_id=1, source_target_pairs={{0,32},{16,48},{32,0},{48,16},{1,33},{17,49},{33,1},{49,17},{2,34}... | collective-permute-start | bytes 319496 | tf_op jit(solution)/shard_map/ppermute | solution.py:293
  55.3 1.4 %collective-permute-start.9 = (bf16[32,1664]{1,0:T(8,128)(2,1)S(1)}, bf16[32,1664]{1,0:T(8,128)(2,1)S(1)}, u32[]{:S(2)}, u32[]{:S(2)}) collective-permute-start(bf16[32,1664]{1,0:T(8,128)(2,1)S(1)} %pad_maximum_fusion.3), channel_id=1, source_target_pairs={{0,48},{16,0},{32,16},{48,32},{1,49},{17,1},{33,17},{49,33},{2,50}... | collective-permute-start | bytes 319496 | tf_op jit(solution)/shard_map/ppermute | solution.py:293
  56.7 1.2 %collective-permute-done.7 = bf16[32,1664]{1,0:T(8,128)(2,1)S(1)} collective-permute-done((bf16[32,1664]{1,0:T(8,128)(2,1)S(1)}, bf16[32,1664]{1,0:T(8,128)(2,1)S(1)}, u32[]{:S(2)}, u32[]{:S(2)}) %collective-permute-start.7) | collective-permute-done | bytes 106528 | tf_op jit(solution)/shard_map/ppermute | solution.py:293
  57.9 1.1 %collective-permute-done.8 = bf16[32,1664]{1,0:T(8,128)(2,1)S(1)} collective-permute-done((bf16[32,1664]{1,0:T(8,128)(2,1)S(1)}, bf16[32,1664]{1,0:T(8,128)(2,1)S(1)}, u32[]{:S(2)}, u32[]{:S(2)}) %collective-permute-start.8) | collective-permute-done | bytes 106528 | tf_op jit(solution)/shard_map/ppermute | solution.py:293
  59.0 0.7 collective-permute-done.9
  59.7 0.1 multiply_convert_fusion
  59.7 0.8 collective-permute-start.10
  60.5 2.9 %collective-permute-start.11 = (bf16[32,1664]{1,0:T(8,128)(2,1)S(1)}, bf16[32,1664]{1,0:T(8,128)(2,1)S(1)}, u32[]{:S(2)}, u32[]{:S(2)}) collective-permute-start(bf16[32,1664]{1,0:T(8,128)(2,1)S(1)} %multiply_convert_fusion), channel_id=1, source_target_pairs={{0,32},{16,48},{32,0},{48,16},{1,33},{17,49},{33,1},{49,17},{2,34}... | collective-permute-start | bytes 319496 | tf_op jit(solution)/shard_map/ppermute | solution.py:293
  63.4 0.0 collective-permute-start.12
  63.4 2.2 %collective-permute-done.10 = bf16[32,1664]{1,0:T(8,128)(2,1)S(1)} collective-permute-done((bf16[32,1664]{1,0:T(8,128)(2,1)S(1)}, bf16[32,1664]{1,0:T(8,128)(2,1)S(1)}, u32[]{:S(2)}, u32[]{:S(2)}) %collective-permute-start.10) | collective-permute-done | bytes 106528 | tf_op jit(solution)/shard_map/ppermute | solution.py:293
  65.6 1.3 %collective-permute-done.11 = bf16[32,1664]{1,0:T(8,128)(2,1)S(1)} collective-permute-done((bf16[32,1664]{1,0:T(8,128)(2,1)S(1)}, bf16[32,1664]{1,0:T(8,128)(2,1)S(1)}, u32[]{:S(2)}, u32[]{:S(2)}) %collective-permute-start.11) | collective-permute-done | bytes 106528 | tf_op jit(solution)/shard_map/ppermute | solution.py:293
  66.9 0.3 collective-permute-done.12
  67.3 1.5 %all-to-all-done.2 = bf16[8,16,2560]{2,1,0:T(8,128)(2,1)S(1)} async-done(((bf16[8,16,2560]{2,1,0:T(8,128)(2,1)}), bf16[8,16,2560]{2,1,0:T(8,128)(2,1)S(1)}, u32[]{:S(2)}, u32[]{:S(2)}) %all-to-all-start.2) | async-done | bytes 655392 | tf_op jit(solution)/shard_map/all_to_all | solution.py:356
  68.8 7.0 %collective-permute-start.16 = (bf16[128,2560]{1,0:T(8,128)(2,1)S(1)}, bf16[128,2560]{1,0:T(8,128)(2,1)S(1)}, u32[]{:S(2)}, u32[]{:S(2)}) collective-permute-start(bf16[128,2560]{1,0:T(8,128)(2,1)S(1)} %bitcast.13), channel_id=1, source_target_pairs={{0,1},{1,0},{2,3},{3,2},{4,5},{5,4},{6,7},{7,6},{8,9},{9,8},{10,11... | collective-permute-start | bytes 1966088 | tf_op jit(solution)/shard_map/ppermute | solution.py:368
  75.8 0.0 collective-permute-start.13
  75.8 1.3 %collective-permute-start.14 = (bf16[128,1664]{1,0:T(8,128)(2,1)S(1)}, bf16[128,1664]{1,0:T(8,128)(2,1)S(1)}, u32[]{:S(2)}, u32[]{:S(2)}) collective-permute-start(bf16[128,1664]{1,0:T(8,128)(2,1)S(1)} %pad_maximum_fusion.p0), channel_id=1, source_target_pairs={{0,128},{64,192},{128,0},{192,64},{1,129},{65,193},{129,1},{193,65... | collective-permute-start | bytes 1277960 | tf_op jit(solution)/shard_map/ppermute | solution.py:293
  77.1 1.4 %collective-permute-start.15 = (bf16[128,1664]{1,0:T(8,128)(2,1)S(1)}, bf16[128,1664]{1,0:T(8,128)(2,1)S(1)}, u32[]{:S(2)}, u32[]{:S(2)}) collective-permute-start(bf16[128,1664]{1,0:T(8,128)(2,1)S(1)} %pad_maximum_fusion.p0), channel_id=1, source_target_pairs={{0,192},{64,0},{128,64},{192,128},{1,193},{65,1},{129,65},{193,129... | collective-permute-start | bytes 1277960 | tf_op jit(solution)/shard_map/ppermute | solution.py:293
  78.5 0.7 collective-permute-start.17
  79.2 0.0 collective-permute-done.16.other
  79.2 2.2 %collective-permute-start.18 = (bf16[1024,384]{1,0:T(8,128)(2,1)}, bf16[1024,384]{1,0:T(8,128)(2,1)S(1)}, u32[]{:S(2)}, u32[]{:S(2)}) collective-permute-start(bf16[1024,384]{1,0:T(8,128)(2,1)} %get-tuple-element.74), channel_id=1, source_target_pairs={{0,16},{16,0},{32,48},{48,32},{1,17},{17,1},{33,49},{49,33},{2,18}... | collective-permute-start | bytes 2359304 | tf_op jit(solution)/shard_map/ppermute | solution.py:301
  81.4 4.0 %shard_map.40.factor = bf16[2,1024,384]{2,1,0:T(8,128)(2,1)S(1)} custom-call(s32[6]{0:T(128)S(1)} %stack.27.pos, bf16[128,2560]{1,0:T(8,128)(2,1)S(1)} %bitcast.14, bf16[128,2560]{1,0:T(8,128)(2,1)S(1)} %collective-permute-done.16.other), custom_call_target="tpu_custom_call" | custom-call | flops 10000000000 | tf_op jit(solution)/shard_map/pallas_call | solution.py:257
  85.3 2.7 %shard_map.41.r0 = bf16[1536,384]{1,0:T(8,128)(2,1)S(1)} custom-call(s32[6]{0:T(128)S(1)} %stack.27.pos, bf16[2,1536,384]{2,1,0:T(8,128)(2,1)S(1)} %copy-done, bf16[1536,256]{1,0:T(8,128)(2,1)S(1)} %collective-permute-done.4.w_mid, bf16[2,1024,384]{2,1,0:T(8,128)(2,1)S(1)} %shard_map.40.factor, bf16[1024,384]{1,0:T(8,128)(2,1)S(1)} %collective-permute-done.3.refs_0_, ...), custom_call_target="tpu_custom_call" | custom-call | tf_op jit(solution)/shard_map/pallas_call | solution.py:257
  88.1 0.0 collective-permute-done.17.w_mid
  88.1 10.3 %collective-permute-done.18.refs_1_ = bf16[1024,384]{1,0:T(8,128)(2,1)S(1)} collective-permute-done((bf16[1024,384]{1,0:T(8,128)(2,1)}, bf16[1024,384]{1,0:T(8,128)(2,1)S(1)}, u32[]{:S(2)}, u32[]{:S(2)}) %collective-permute-start.18) | collective-permute-done | bytes 786464 | tf_op jit(solution)/shard_map/ppermute | solution.py:301
  98.3 2.5 %shard_map.42.r1 = bf16[1536,384]{1,0:T(8,128)(2,1)S(1)} custom-call(s32[6]{0:T(128)S(1)} %stack.27.pos, bf16[2,1536,384]{2,1,0:T(8,128)(2,1)S(1)} %copy-done, bf16[1536,256]{1,0:T(8,128)(2,1)S(1)} %collective-permute-done.17.w_mid, bf16[2,1024,384]{2,1,0:T(8,128)(2,1)S(1)} %shard_map.40.factor, bf16[528,384]{1,0:T(8,128)(2,1)S(1)} %collective-permute-done.6.refs_2_.refs_0_, ...), custom_call_target="tpu_custom_call" | custom-call | tf_op jit(solution)/shard_map/pallas_call | solution.py:257
  100.9 0.0 collective-permute-done.13.p1
  100.9 0.0 collective-permute-done.14.p2
  100.9 0.0 collective-permute-done.15.p3
  100.9 7.5 %shard_map.43 = bf16[2,1536,384]{2,1,0:T(8,128)(2,1)} custom-call(s32[6]{0:T(128)S(1)} %stack.27.pos, bf16[128,1664]{1,0:T(8,128)(2,1)S(1)} %pad_maximum_fusion.p0, bf16[128,1664]{1,0:T(8,128)(2,1)S(1)} %collective-permute-done.13.p1, bf16[128,1664]{1,0:T(8,128)(2,1)S(1)} %collective-permute-done.14.p2, bf16[128,1664]{1,0:T(8,128)(2,1)S(1)} %collective-permute-done.15.p3, ...), custom_call_target="tpu_custom_call" | custom-call | tf_op jit(solution)/shard_map/pallas_call | solution.py:257
  (7 shorter events, 0.1 us)
Async XLA Ops:
  6.6 18.4 %collective-permute-start.3 = (bf16[1024,384]{1,0:T(8,128)(2,1)}, bf16[1024,384]{1,0:T(8,128)(2,1)S(1)}, u32[]{:S(2)}, u32[]{:S(2)}) collective-permute-start(bf16[1024,384]{1,0:T(8,128)(2,1)} %get-tuple-element.53), channel_id=1, source_target_pairs={{0,16},{16,0},{32,48},{48,32},{1,17},{17,1},{33,49},{49,33},{2,18}... | collective-permute-start | bytes 2359304 | tf_op jit(solution)/shard_map/ppermute | solution.py:301
  8.8 20.2 %collective-permute-start.4 = (bf16[1536,256]{1,0:T(8,128)(2,1)}, bf16[1536,256]{1,0:T(8,128)(2,1)S(1)}, u32[]{:S(2)}, u32[]{:S(2)}) collective-permute-start(bf16[1536,256]{1,0:T(8,128)(2,1)} %get-tuple-element.54), channel_id=1, source_target_pairs={{16,32},{32,16},{17,33},{33,17},{18,34},{34,18},{19,35},{35,19},{2... | collective-permute-start | bytes 2359304 | tf_op jit(solution)/shard_map/ppermute | solution.py:305
  9.5 19.4 %all-to-all-start.1 = ((bf16[4,32,1920]{2,1,0:T(8,128)(2,1)}), bf16[4,32,1920]{2,1,0:T(8,128)(2,1)S(1)}, u32[]{:S(2)}, u32[]{:S(2)}) async-start(bf16[4,32,1920]{2,1,0:T(8,128)(2,1)} %bitcast.17), calls=%async_computation.1 | async-start | bytes 983040 | tf_op jit(solution)/shard_map/all_to_all | solution.py:325
  13.7 28.7 %collective-permute-start.5 = (bf16[496,384]{1,0:T(8,128)(2,1)}, bf16[496,384]{1,0:T(8,128)(2,1)S(1)}, u32[]{:S(2)}, u32[]{:S(2)}) collective-permute-start(bf16[496,384]{1,0:T(8,128)(2,1)} %get-tuple-element.58), channel_id=1, source_target_pairs={{0,16},{16,0},{32,48},{48,32},{1,17},{17,1},{33,49},{49,33},{2,18}... | collective-permute-start | bytes 1142792 | tf_op jit(solution)/shard_map/ppermute | solution.py:301
  21.0 30.3 %collective-permute-start = (bf16[128,1664]{1,0:T(8,128)(2,1)}, bf16[128,1664]{1,0:T(8,128)(2,1)}, u32[]{:S(2)}, u32[]{:S(2)}) collective-permute-start(bf16[128,1664]{1,0:T(8,128)(2,1)} %get-tuple-element.49), channel_id=1, source_target_pairs={{0,64},{64,128},{128,192},{192,0},{1,65},{65,129},{129,193},{193,1... | collective-permute-start | bytes 1277960 | tf_op jit(solution)/shard_map/ppermute | solution.py:293
  22.5 28.9 %collective-permute-start.1 = (bf16[128,1664]{1,0:T(8,128)(2,1)}, bf16[128,1664]{1,0:T(8,128)(2,1)}, u32[]{:S(2)}, u32[]{:S(2)}) collective-permute-start(bf16[128,1664]{1,0:T(8,128)(2,1)} %get-tuple-element.50), channel_id=1, source_target_pairs={{0,128},{64,192},{128,0},{192,64},{1,129},{65,193},{129,1},{193,65... | collective-permute-start | bytes 1277960 | tf_op jit(solution)/shard_map/ppermute | solution.py:293
  25.0 26.4 %collective-permute-start.2 = (bf16[128,1664]{1,0:T(8,128)(2,1)}, bf16[128,1664]{1,0:T(8,128)(2,1)}, u32[]{:S(2)}, u32[]{:S(2)}) collective-permute-start(bf16[128,1664]{1,0:T(8,128)(2,1)} %get-tuple-element.51), channel_id=1, source_target_pairs={{0,192},{64,0},{128,64},{192,128},{1,193},{65,1},{129,65},{193,129... | collective-permute-start | bytes 1277960 | tf_op jit(solution)/shard_map/ppermute | solution.py:293
  29.5 0.8 copy-start.2
  30.3 11.3 %all-to-all-start = ((bf16[4,32,1920]{2,1,0:T(8,128)(2,1)}), bf16[4,32,1920]{2,1,0:T(8,128)(2,1)S(1)}, u32[]{:S(2)}, u32[]{:S(2)}) async-start(bf16[4,32,1920]{2,1,0:T(8,128)(2,1)} %bitcast.18), calls=%async_computation | async-start | bytes 983040 | tf_op jit(solution)/shard_map/cond/branch_1_fun/all_to_all | solution.py:338
  42.3 0.9 copy-start.1
  42.3 9.1 %copy-start.3 = (bf16[128,1664]{1,0:T(8,128)(2,1)S(1)}, bf16[128,1664]{1,0:T(8,128)(2,1)}, u32[]{:S(2)}) copy-start(bf16[128,1664]{1,0:T(8,128)(2,1)} %get-tuple-element.61) | copy-start | bytes 1277956
  42.3 9.0 %collective-permute-start.6 = (bf16[528,384]{1,0:T(8,128)(2,1)}, bf16[528,384]{1,0:T(8,128)(2,1)S(1)}, u32[]{:S(2)}, u32[]{:S(2)}) collective-permute-start(bf16[528,384]{1,0:T(8,128)(2,1)} %get-tuple-element.60), channel_id=1, source_target_pairs={{0,16},{16,0},{32,48},{48,32},{1,17},{17,1},{33,49},{49,33},{2,18}... | collective-permute-start | bytes 1216520 | tf_op jit(solution)/shard_map/ppermute | solution.py:301
  43.2 25.6 %all-to-all-start.2 = ((bf16[8,16,2560]{2,1,0:T(8,128)(2,1)}), bf16[8,16,2560]{2,1,0:T(8,128)(2,1)S(1)}, u32[]{:S(2)}, u32[]{:S(2)}) async-start(bf16[8,16,2560]{2,1,0:T(8,128)(2,1)} %bitcast.16), calls=%async_computation.2 | async-start | bytes 1310720 | tf_op jit(solution)/shard_map/all_to_all | solution.py:356
  53.0 4.9 %collective-permute-start.7 = (bf16[32,1664]{1,0:T(8,128)(2,1)S(1)}, bf16[32,1664]{1,0:T(8,128)(2,1)S(1)}, u32[]{:S(2)}, u32[]{:S(2)}) collective-permute-start(bf16[32,1664]{1,0:T(8,128)(2,1)S(1)} %pad_maximum_fusion.1), channel_id=1, source_target_pairs={{0,16},{16,32},{32,48},{48,0},{1,17},{17,33},{33,49},{49,1},{2,18}... | collective-permute-start | bytes 319496 | tf_op jit(solution)/shard_map/ppermute | solution.py:293
  53.8 5.2 %collective-permute-start.8 = (bf16[32,1664]{1,0:T(8,128)(2,1)S(1)}, bf16[32,1664]{1,0:T(8,128)(2,1)S(1)}, u32[]{:S(2)}, u32[]{:S(2)}) collective-permute-start(bf16[32,1664]{1,0:T(8,128)(2,1)S(1)} %pad_maximum_fusion.2), channel_id=1, source_target_pairs={{0,32},{16,48},{32,0},{48,16},{1,33},{17,49},{33,1},{49,17},{2,34}... | collective-permute-start | bytes 319496 | tf_op jit(solution)/shard_map/ppermute | solution.py:293
  55.3 4.4 %collective-permute-start.9 = (bf16[32,1664]{1,0:T(8,128)(2,1)S(1)}, bf16[32,1664]{1,0:T(8,128)(2,1)S(1)}, u32[]{:S(2)}, u32[]{:S(2)}) collective-permute-start(bf16[32,1664]{1,0:T(8,128)(2,1)S(1)} %pad_maximum_fusion.3), channel_id=1, source_target_pairs={{0,48},{16,0},{32,16},{48,32},{1,49},{17,1},{33,17},{49,33},{2,50}... | collective-permute-start | bytes 319496 | tf_op jit(solution)/shard_map/ppermute | solution.py:293
  59.7 5.9 %collective-permute-start.10 = (bf16[32,1664]{1,0:T(8,128)(2,1)S(1)}, bf16[32,1664]{1,0:T(8,128)(2,1)S(1)}, u32[]{:S(2)}, u32[]{:S(2)}) collective-permute-start(bf16[32,1664]{1,0:T(8,128)(2,1)S(1)} %multiply_convert_fusion), channel_id=1, source_target_pairs={{0,16},{16,32},{32,48},{48,0},{1,17},{17,33},{33,49},{49,1},{2,18}... | collective-permute-start | bytes 319496 | tf_op jit(solution)/shard_map/ppermute | solution.py:293
  60.5 6.4 %collective-permute-start.11 = (bf16[32,1664]{1,0:T(8,128)(2,1)S(1)}, bf16[32,1664]{1,0:T(8,128)(2,1)S(1)}, u32[]{:S(2)}, u32[]{:S(2)}) collective-permute-start(bf16[32,1664]{1,0:T(8,128)(2,1)S(1)} %multiply_convert_fusion), channel_id=1, source_target_pairs={{0,32},{16,48},{32,0},{48,16},{1,33},{17,49},{33,1},{49,17},{2,34}... | collective-permute-start | bytes 319496 | tf_op jit(solution)/shard_map/ppermute | solution.py:293
  63.4 3.9 %collective-permute-start.12 = (bf16[32,1664]{1,0:T(8,128)(2,1)S(1)}, bf16[32,1664]{1,0:T(8,128)(2,1)S(1)}, u32[]{:S(2)}, u32[]{:S(2)}) collective-permute-start(bf16[32,1664]{1,0:T(8,128)(2,1)S(1)} %multiply_convert_fusion), channel_id=1, source_target_pairs={{0,48},{16,0},{32,16},{48,32},{1,49},{17,1},{33,17},{49,33},{2,50}... | collective-permute-start | bytes 319496 | tf_op jit(solution)/shard_map/ppermute | solution.py:293
  68.8 10.4 %collective-permute-start.16 = (bf16[128,2560]{1,0:T(8,128)(2,1)S(1)}, bf16[128,2560]{1,0:T(8,128)(2,1)S(1)}, u32[]{:S(2)}, u32[]{:S(2)}) collective-permute-start(bf16[128,2560]{1,0:T(8,128)(2,1)S(1)} %bitcast.13), channel_id=1, source_target_pairs={{0,1},{1,0},{2,3},{3,2},{4,5},{5,4},{6,7},{7,6},{8,9},{9,8},{10,11... | collective-permute-start | bytes 1966088 | tf_op jit(solution)/shard_map/ppermute | solution.py:368
  75.8 25.1 %collective-permute-start.13 = (bf16[128,1664]{1,0:T(8,128)(2,1)S(1)}, bf16[128,1664]{1,0:T(8,128)(2,1)S(1)}, u32[]{:S(2)}, u32[]{:S(2)}) collective-permute-start(bf16[128,1664]{1,0:T(8,128)(2,1)S(1)} %pad_maximum_fusion.p0), channel_id=1, source_target_pairs={{0,64},{64,128},{128,192},{192,0},{1,65},{65,129},{129,193},{193,1... | collective-permute-start | bytes 1277960 | tf_op jit(solution)/shard_map/ppermute | solution.py:293
  75.8 25.1 %collective-permute-start.14 = (bf16[128,1664]{1,0:T(8,128)(2,1)S(1)}, bf16[128,1664]{1,0:T(8,128)(2,1)S(1)}, u32[]{:S(2)}, u32[]{:S(2)}) collective-permute-start(bf16[128,1664]{1,0:T(8,128)(2,1)S(1)} %pad_maximum_fusion.p0), channel_id=1, source_target_pairs={{0,128},{64,192},{128,0},{192,64},{1,129},{65,193},{129,1},{193,65... | collective-permute-start | bytes 1277960 | tf_op jit(solution)/shard_map/ppermute | solution.py:293
  77.1 23.8 %collective-permute-start.15 = (bf16[128,1664]{1,0:T(8,128)(2,1)S(1)}, bf16[128,1664]{1,0:T(8,128)(2,1)S(1)}, u32[]{:S(2)}, u32[]{:S(2)}) collective-permute-start(bf16[128,1664]{1,0:T(8,128)(2,1)S(1)} %pad_maximum_fusion.p0), channel_id=1, source_target_pairs={{0,192},{64,0},{128,64},{192,128},{1,193},{65,1},{129,65},{193,129... | collective-permute-start | bytes 1277960 | tf_op jit(solution)/shard_map/ppermute | solution.py:293
  78.5 9.6 %collective-permute-start.17 = (bf16[1536,256]{1,0:T(8,128)(2,1)}, bf16[1536,256]{1,0:T(8,128)(2,1)S(1)}, u32[]{:S(2)}, u32[]{:S(2)}) collective-permute-start(bf16[1536,256]{1,0:T(8,128)(2,1)} %get-tuple-element.73), channel_id=1, source_target_pairs={{16,32},{32,16},{17,33},{33,17},{18,34},{34,18},{19,35},{35,19},{2... | collective-permute-start | bytes 2359304 | tf_op jit(solution)/shard_map/ppermute | solution.py:305
  79.2 19.2 %collective-permute-start.18 = (bf16[1024,384]{1,0:T(8,128)(2,1)}, bf16[1024,384]{1,0:T(8,128)(2,1)S(1)}, u32[]{:S(2)}, u32[]{:S(2)}) collective-permute-start(bf16[1024,384]{1,0:T(8,128)(2,1)} %get-tuple-element.74), channel_id=1, source_target_pairs={{0,16},{16,0},{32,48},{48,32},{1,17},{17,1},{33,49},{49,33},{2,18}... | collective-permute-start | bytes 2359304 | tf_op jit(solution)/shard_map/ppermute | solution.py:301
  81.4 4.0 %copy-start = (bf16[2,1536,384]{2,1,0:T(8,128)(2,1)S(1)}, bf16[2,1536,384]{2,1,0:T(8,128)(2,1)}, u32[]{:S(2)}) copy-start(bf16[2,1536,384]{2,1,0:T(8,128)(2,1)} %w_own.3) | copy-start | bytes 7077892

commit v12 on v11

--- a/solution.py
+++ b/solution.py
@@ -19,7 +19,7 @@
 LANES = 15 * SUB
 ABOVE = [(r, c) for r in range(4) for c in range(r + 1, 4)]
 DENSE = 13 * SUB
-PARTS = 1024, 496, 16
+PARTS = 1024, (512, 96), 528, 912
 
 
 def tn_dot(a, b):
@@ -35,11 +35,10 @@
 
 
 def late_kernel(pos, w, rest, out, mid, held_rest, held, held_mid, sems):
-    last = PARTS[2]
+    first = PARTS[1][1]
     sources = (
-        (w.at[0, pl.ds(w.shape[1] - last, last)], held_rest.at[pl.ds(0, last)], rest.at[pl.ds(0, last)]),
-        (w.at[1, pl.ds(0, BLK)], held_rest.at[pl.ds(last, BLK)], rest.at[pl.ds(last, BLK)]),
-        (w.at[1, pl.ds(BLK, out.shape[0])], held, out),
+        (w.at[1, pl.ds(first, PARTS[2])], held_rest, rest),
+        (w.at[1, pl.ds(first + PARTS[2], PARTS[3])], held, out),
         (w.at[1, :, middle(pos)], held_mid, mid),
     )
     loads = [pltpu.make_async_copy(a, b, sems.at[0, n]) for n, (a, b, _) in enumerate(sources)]
@@ -88,9 +87,11 @@
 
 def side_kernel(pos, acts, w, out, early, following, mid, held, held_next, held_mid, sems):
     part, step = pos[3], pl.program_id(0)
+    upper, lower = PARTS[1]
     sources = (
         (w.at[0, pl.ds(0, PARTS[0])], held, early),
-        (w.at[0, pl.ds(PARTS[0], PARTS[1])], held_next, following),
+        (w.at[0, pl.ds(PARTS[0], upper)], held_next.at[pl.ds(0, upper)], following.at[pl.ds(0, upper)]),
+        (w.at[1, pl.ds(0, lower)], held_next.at[pl.ds(upper, lower)], following.at[pl.ds(upper, lower)]),
         (w.at[0, :, middle(pos)], held_mid, mid),
     )
     loads = [pltpu.make_async_copy(a, b, sems.at[0, n]) for n, (a, b, _) in enumerate(sources)]
@@ -311,13 +312,13 @@
     rows, width = weight_grad.shape[1:]
     barrier = lax.optimization_barrier
 
-    early, following, mid = shape(PARTS[0], width), shape(PARTS[1], width), shape(rows, 256)
-    rest, late = shape(PARTS[2] + BLK, width), shape(rows - BLK, width)
+    early, following, mid = shape(PARTS[0], width), shape(sum(PARTS[1]), width), shape(rows, 256)
+    rest, late = shape(PARTS[2], width), shape(PARTS[3], width)
     side, *own = call(
         side_kernel, pos, (acts, weight_grad),
         [pl.BlockSpec((1, acts.shape[1], 3 * BLK), lambda i, p: (p[4], 0, i)), ANYWHERE],
         [shape(128, LANES), early, following, mid],
-        [VMEM(a.shape, BF16) for a in (early, following, mid)] + [pltpu.SemaphoreType.DMA((2, 3))],
+        [VMEM(a.shape, BF16) for a in (early, following, mid)] + [pltpu.SemaphoreType.DMA((2, 4))],
         out_specs=[pl.BlockSpec((32, LANES), lambda i, p: (i, 0))] + [ANYWHERE] * 3, vmem=60, grid=4,
     )
     early, following, mid0 = paired(own[0]), paired(own[1]), crossed(own[2])
@@ -377,8 +378,8 @@
             [shape(rows, width)], [],
         )[0]
         for layer, (mid, pairs, parts_of) in enumerate((
-            (mid0, (early, following, rest), ((0, PARTS[0]), (0, PARTS[1]), (0, PARTS[2]))),
-            (mid1, (rest, late), ((PARTS[2], BLK), (0, rows - BLK))),
+            (mid0, (early, following), ((0, PARTS[0]), (0, PARTS[1][0]))),
+            (mid1, (following, rest, late), (PARTS[1], (0, PARTS[2]), (0, PARTS[3]))),
         ))
     ]
     return call(

time: 110 us -> 110 us (level)
    ppermute x1, starting transfers between devices: 6.98 us -> 4.77 us  [body(): other = lax.ppermute(mine, 'c', [(0, 1), (1, 0)])]
    ppermute x12, starting transfers between devices: 17.7 us -> 19.8 us  [spread(): lax.ppermute(parts[d], axis, [(i, (i + d) % 4) for i in range(4)])]
    ppermute x4, waiting for transfers between devices: 10.4 us -> 8.34 us  [paired(): return lax.ppermute(w, 'x', [(0, 1), (1, 0), (2, 3), (3, 2)])]
where the time goes in v12:
time: 110 us; the launch traced here: 108 us
  starting transfers between devices  50.2 us (46%)
  Pallas kernels  31.6 us (29%)
  waiting for transfers between devices  22 us (20%)
  other arithmetic  1.78 us (2%)
  local copies, waits for them, and re-layouts  1.69 us (2%)
    pallas_call x9, Pallas kernels, call(): pl.pallas_call(kernel, grid_spec=pltpu.PrefetchScalarGridSpec(num_scalar_...  31.6 us
    ppermute x12, starting transfers between devices, spread(): lax.ppermute(parts[d], axis, [(i, (i + d) % 4) for i in range(4)])  19.8 us
    ppermute x4, waiting for transfers between devices, paired(): return lax.ppermute(w, 'x', [(0, 1), (1, 0), (2, 3), (3, 2)])  8.34 us
    all_to_all x1, starting transfers between devices, body(): mine = lax.all_to_all(side, 'z', 0, 0, tiled=True)  8.18 us
    ppermute x4, starting transfers between devices, paired(): return lax.ppermute(w, 'x', [(0, 1), (1, 0), (2, 3), (3, 2)])  7.73 us
    ppermute x12, waiting for transfers between devices, spread(): lax.ppermute(parts[d], axis, [(i, (i + d) % 4) for i in range(4)])  7.12 us
    all_to_all x1, waiting for transfers between devices, sum_side(): side = lax.all_to_all(side, 'x', 0, 0, tiled=True)  4.83 us
    ppermute x1, starting transfers between devices, body(): other = lax.ppermute(mine, 'c', [(0, 1), (1, 0)])  4.77 us
  transfers between devices with their start and end apart: 22, of which 10 were waited for; matrix products, arithmetic and copies ran while one was open for 2% of the time, Pallas kernels for 16%

profile of v12, /device:TPU:1, one launch (start us, length us, event | category | flops | bytes accessed | tf_op | source)
XLA Modules:
  0.0 107.8 jit_solution(12766622893734124895)
XLA Ops:
  0.0 0.1 stack.27.pos
  0.1 6.6 %shard_map.37 = (bf16[128,1920]{1,0:T(8,128)(2,1)}, bf16[1024,384]{1,0:T(8,128)(2,1)}, bf16[608,384]{1,0:T(8,128)(2,1)}, bf16[1536,256]{1,0:T(8,128)(2,1)}) custom-call(s32[6]{0:T(128)S(1)} %stack.27.pos, bf16[2,256,6144]{2,1,0:T(8,128)(2,1)} %acts.1, bf16[2,1536,384]{2,1,0:T(8,128)(2,1)} %w_own.3), custom_call_target="tpu_custom_call" | custom-call | tf_op jit(solution)/shard_map/pallas_call | solution.py:258
  6.7 2.1 %collective-permute-start.3 = (bf16[1024,384]{1,0:T(8,128)(2,1)}, bf16[1024,384]{1,0:T(8,128)(2,1)S(1)}, u32[]{:S(2)}, u32[]{:S(2)}) collective-permute-start(bf16[1024,384]{1,0:T(8,128)(2,1)} %get-tuple-element.53), channel_id=1, source_target_pairs={{0,16},{16,0},{32,48},{48,32},{1,17},{17,1},{33,49},{49,33},{2,18}... | collective-permute-start | bytes 2359304 | tf_op jit(solution)/shard_map/ppermute | solution.py:302
  8.8 0.7 collective-permute-start.4
  9.5 4.2 %all-to-all-start.1 = ((bf16[4,32,1920]{2,1,0:T(8,128)(2,1)}), bf16[4,32,1920]{2,1,0:T(8,128)(2,1)S(1)}, u32[]{:S(2)}, u32[]{:S(2)}) async-start(bf16[4,32,1920]{2,1,0:T(8,128)(2,1)} %bitcast.17), calls=%async_computation.1 | async-start | bytes 983040 | tf_op jit(solution)/shard_map/all_to_all | solution.py:326
  13.7 3.3 %collective-permute-start.5 = (bf16[608,384]{1,0:T(8,128)(2,1)}, bf16[608,384]{1,0:T(8,128)(2,1)S(1)}, u32[]{:S(2)}, u32[]{:S(2)}) collective-permute-start(bf16[608,384]{1,0:T(8,128)(2,1)} %get-tuple-element.58), channel_id=1, source_target_pairs={{0,16},{16,0},{32,48},{48,32},{1,17},{17,1},{33,49},{49,33},{2,18}... | collective-permute-start | bytes 1400840 | tf_op jit(solution)/shard_map/ppermute | solution.py:302
  17.0 4.1 %shard_map.38 = (bf16[128,1664]{1,0:T(8,128)(2,1)}, bf16[128,1664]{1,0:T(8,128)(2,1)}, bf16[128,1664]{1,0:T(8,128)(2,1)}, bf16[128,1664]{1,0:T(8,128)(2,1)}) custom-call(s32[6]{0:T(128)S(1)} %stack.27.pos, bf16[2,256,1536]{2,1,0:T(8,128)(2,1)} %grads), custom_call_target="tpu_custom_call" | custom-call | flops 12000000000 | tf_op jit(solution)/shard_map/pallas_call | solution.py:258
  21.1 1.5 %collective-permute-start = (bf16[128,1664]{1,0:T(8,128)(2,1)}, bf16[128,1664]{1,0:T(8,128)(2,1)}, u32[]{:S(2)}, u32[]{:S(2)}) collective-permute-start(bf16[128,1664]{1,0:T(8,128)(2,1)} %get-tuple-element.49), channel_id=1, source_target_pairs={{0,64},{64,128},{128,192},{192,0},{1,65},{65,129},{129,193},{193,1... | collective-permute-start | bytes 1277960 | tf_op jit(solution)/shard_map/ppermute | solution.py:294
  22.6 2.4 %collective-permute-start.1 = (bf16[128,1664]{1,0:T(8,128)(2,1)}, bf16[128,1664]{1,0:T(8,128)(2,1)}, u32[]{:S(2)}, u32[]{:S(2)}) collective-permute-start(bf16[128,1664]{1,0:T(8,128)(2,1)} %get-tuple-element.50), channel_id=1, source_target_pairs={{0,128},{64,192},{128,0},{192,64},{1,129},{65,193},{129,1},{193,65... | collective-permute-start | bytes 1277960 | tf_op jit(solution)/shard_map/ppermute | solution.py:294
  25.0 0.1 collective-permute-done.3.refs_0_
  25.0 3.9 %collective-permute-start.2 = (bf16[128,1664]{1,0:T(8,128)(2,1)}, bf16[128,1664]{1,0:T(8,128)(2,1)}, u32[]{:S(2)}, u32[]{:S(2)}) collective-permute-start(bf16[128,1664]{1,0:T(8,128)(2,1)} %get-tuple-element.51), channel_id=1, source_target_pairs={{0,192},{64,0},{128,64},{192,128},{1,193},{65,1},{129,65},{193,129... | collective-permute-start | bytes 1277960 | tf_op jit(solution)/shard_map/ppermute | solution.py:294
  28.9 0.0 all-to-all-done.1
  28.9 0.0 collective-permute-done.4.w_mid
  28.9 0.6 shard_map.39
  29.6 13.4 %conditional.1 = (bf16[128,2560]{1,0:T(8,128)(2,1)S(1)}, bf16[528,384]{1,0:T(8,128)(2,1)}, bf16[912,384]{1,0:T(8,128)(2,1)}, bf16[1536,256]{1,0:T(8,128)(2,1)}) conditional(s32[]{:T(128)} %convert_element_type.33, () %tuple.19, (bf16[128,1920]{1,0:T(8,128)(2,1)S(1)}, s32[6]{0:T(128)S(1)}, bf16[2,1536,384]{2,1,0:T(8,128)(2,1)}) %tuple.21), branch_computations={%region_0.1_spmd, %region_1.2_spmd} | conditional | flops 4000000000 | bytes 3440732 | solution.py:348
  29.6 0.0 copy-start.4
  29.6 0.8 copy-done.4
  30.4 4.1 %all-to-all-start = ((bf16[4,32,1920]{2,1,0:T(8,128)(2,1)}), bf16[4,32,1920]{2,1,0:T(8,128)(2,1)S(1)}, u32[]{:S(2)}, u32[]{:S(2)}) async-start(bf16[4,32,1920]{2,1,0:T(8,128)(2,1)} %bitcast.18), calls=%async_computation | async-start | bytes 983040 | tf_op jit(solution)/shard_map/cond/branch_1_fun/all_to_all | solution.py:339
  34.5 3.0 %branch_1_fun.3 = (bf16[528,384]{1,0:T(8,128)(2,1)}, bf16[912,384]{1,0:T(8,128)(2,1)}, bf16[1536,256]{1,0:T(8,128)(2,1)}) custom-call(s32[6]{0:T(128)S(1)} %get-tuple-element.11.pos, bf16[2,1536,384]{2,1,0:T(8,128)(2,1)} %get-tuple-element.13.w), custom_call_target="tpu_custom_call" | custom-call | flops 4000000000 | tf_op jit(solution)/shard_map/cond/branch_1_fun/pallas_call | solution.py:258
  37.5 4.8 %all-to-all-done = bf16[4,32,1920]{2,1,0:T(8,128)(2,1)S(1)} async-done(((bf16[4,32,1920]{2,1,0:T(8,128)(2,1)}), bf16[4,32,1920]{2,1,0:T(8,128)(2,1)S(1)}, u32[]{:S(2)}, u32[]{:S(2)}) %all-to-all-start) | async-done | bytes 491552 | tf_op jit(solution)/shard_map/cond/branch_1_fun/all_to_all | solution.py:339
  42.3 0.7 branch_1_fun.2
  43.0 0.0 copy-start.3
  43.0 0.0 copy-start.5
  43.0 0.0 collective-permute-done.5.refs_1_.refs_0_
  43.0 0.1 collective-permute-start.6
  43.2 0.7 copy-done.3
  43.9 8.2 %all-to-all-start.2 = ((bf16[8,16,2560]{2,1,0:T(8,128)(2,1)}), bf16[8,16,2560]{2,1,0:T(8,128)(2,1)S(1)}, u32[]{:S(2)}, u32[]{:S(2)}) async-start(bf16[8,16,2560]{2,1,0:T(8,128)(2,1)} %bitcast.16), calls=%async_computation.2 | async-start | bytes 1310720 | tf_op jit(solution)/shard_map/all_to_all | solution.py:357
  52.0 0.0 collective-permute-done
  52.0 0.0 collective-permute-done.1
  52.0 0.0 collective-permute-done.2
  52.1 0.0 collective-permute-done.6.refs_1_
  52.1 0.0 copy-start
  52.1 1.6 %add_convert_fusion = bf16[128,1664]{1,0:T(8,128)(2,1)S(1)} fusion(bf16[128,1664]{1,0:T(8,128)(2,1)} %collective-permute-done.2, bf16[128,1664]{1,0:T(8,128)(2,1)} %collective-permute-done.1, bf16[128,1664]{1,0:T(8,128)(2,1)} %collective-permute-done, bf16[128,1664]{1,0:T(8,128)(2,1)S(1)} %copy-done.5), kind=kLoop, calls=%fused_computation | loop fusion | flops 1703936 | bytes 2129920 | tf_op jit(solution)/shard_map/convert_element_type | solution.py:359
  53.8 0.1 constant_dynamic-slice_fusion.6
  53.9 0.8 collective-permute-start.7
  54.7 1.0 collective-permute-start.8
  55.7 1.6 %collective-permute-start.9 = (bf16[32,1664]{1,0:T(8,128)(2,1)S(1)}, bf16[32,1664]{1,0:T(8,128)(2,1)S(1)}, u32[]{:S(2)}, u32[]{:S(2)}) collective-permute-start(bf16[32,1664]{1,0:T(8,128)(2,1)S(1)} %pad_maximum_fusion.3), channel_id=1, source_target_pairs={{0,48},{16,0},{32,16},{48,32},{1,49},{17,1},{33,17},{49,33},{2,50}... | collective-permute-start | bytes 319496 | tf_op jit(solution)/shard_map/ppermute | solution.py:294
  57.3 1.4 %collective-permute-done.7 = bf16[32,1664]{1,0:T(8,128)(2,1)S(1)} collective-permute-done((bf16[32,1664]{1,0:T(8,128)(2,1)S(1)}, bf16[32,1664]{1,0:T(8,128)(2,1)S(1)}, u32[]{:S(2)}, u32[]{:S(2)}) %collective-permute-start.7) | collective-permute-done | bytes 106528 | tf_op jit(solution)/shard_map/ppermute | solution.py:294
  58.7 1.1 %collective-permute-done.8 = bf16[32,1664]{1,0:T(8,128)(2,1)S(1)} collective-permute-done((bf16[32,1664]{1,0:T(8,128)(2,1)S(1)}, bf16[32,1664]{1,0:T(8,128)(2,1)S(1)}, u32[]{:S(2)}, u32[]{:S(2)}) %collective-permute-start.8) | collective-permute-done | bytes 106528 | tf_op jit(solution)/shard_map/ppermute | solution.py:294
  59.8 1.0 collective-permute-done.9
  60.8 0.1 multiply_convert_fusion
  60.9 0.5 collective-permute-start.10
  61.4 3.1 %collective-permute-start.11 = (bf16[32,1664]{1,0:T(8,128)(2,1)S(1)}, bf16[32,1664]{1,0:T(8,128)(2,1)S(1)}, u32[]{:S(2)}, u32[]{:S(2)}) collective-permute-start(bf16[32,1664]{1,0:T(8,128)(2,1)S(1)} %multiply_convert_fusion), channel_id=1, source_target_pairs={{0,32},{16,48},{32,0},{48,16},{1,33},{17,49},{33,1},{49,17},{2,34}... | collective-permute-start | bytes 319496 | tf_op jit(solution)/shard_map/ppermute | solution.py:294
  64.5 0.0 collective-permute-start.12
  64.5 1.5 %collective-permute-done.10 = bf16[32,1664]{1,0:T(8,128)(2,1)S(1)} collective-permute-done((bf16[32,1664]{1,0:T(8,128)(2,1)S(1)}, bf16[32,1664]{1,0:T(8,128)(2,1)S(1)}, u32[]{:S(2)}, u32[]{:S(2)}) %collective-permute-start.10) | collective-permute-done | bytes 106528 | tf_op jit(solution)/shard_map/ppermute | solution.py:294
  66.0 1.8 %collective-permute-done.11 = bf16[32,1664]{1,0:T(8,128)(2,1)S(1)} collective-permute-done((bf16[32,1664]{1,0:T(8,128)(2,1)S(1)}, bf16[32,1664]{1,0:T(8,128)(2,1)S(1)}, u32[]{:S(2)}, u32[]{:S(2)}) %collective-permute-start.11) | collective-permute-done | bytes 106528 | tf_op jit(solution)/shard_map/ppermute | solution.py:294
  67.9 0.2 collective-permute-done.12
  68.1 1.7 %all-to-all-done.2 = bf16[8,16,2560]{2,1,0:T(8,128)(2,1)S(1)} async-done(((bf16[8,16,2560]{2,1,0:T(8,128)(2,1)}), bf16[8,16,2560]{2,1,0:T(8,128)(2,1)S(1)}, u32[]{:S(2)}, u32[]{:S(2)}) %all-to-all-start.2) | async-done | bytes 655392 | tf_op jit(solution)/shard_map/all_to_all | solution.py:357
  69.9 4.8 %collective-permute-start.16 = (bf16[128,2560]{1,0:T(8,128)(2,1)S(1)}, bf16[128,2560]{1,0:T(8,128)(2,1)S(1)}, u32[]{:S(2)}, u32[]{:S(2)}) collective-permute-start(bf16[128,2560]{1,0:T(8,128)(2,1)S(1)} %bitcast.13), channel_id=1, source_target_pairs={{0,1},{1,0},{2,3},{3,2},{4,5},{5,4},{6,7},{7,6},{8,9},{9,8},{10,11... | collective-permute-start | bytes 1966088 | tf_op jit(solution)/shard_map/ppermute | solution.py:369
  74.6 1.3 %collective-permute-start.13 = (bf16[128,1664]{1,0:T(8,128)(2,1)S(1)}, bf16[128,1664]{1,0:T(8,128)(2,1)S(1)}, u32[]{:S(2)}, u32[]{:S(2)}) collective-permute-start(bf16[128,1664]{1,0:T(8,128)(2,1)S(1)} %pad_maximum_fusion.p0), channel_id=1, source_target_pairs={{0,64},{64,128},{128,192},{192,0},{1,65},{65,129},{129,193},{193,1... | collective-permute-start | bytes 1277960 | tf_op jit(solution)/shard_map/ppermute | solution.py:294
  76.0 2.6 %collective-permute-start.14 = (bf16[128,1664]{1,0:T(8,128)(2,1)S(1)}, bf16[128,1664]{1,0:T(8,128)(2,1)S(1)}, u32[]{:S(2)}, u32[]{:S(2)}) collective-permute-start(bf16[128,1664]{1,0:T(8,128)(2,1)S(1)} %pad_maximum_fusion.p0), channel_id=1, source_target_pairs={{0,128},{64,192},{128,0},{192,64},{1,129},{65,193},{129,1},{193,65... | collective-permute-start | bytes 1277960 | tf_op jit(solution)/shard_map/ppermute | solution.py:294
  78.6 1.1 collective-permute-start.15
  79.6 0.7 collective-permute-start.17
  80.4 0.0 collective-permute-done.16.other
  80.4 2.2 %collective-permute-start.18 = (bf16[912,384]{1,0:T(8,128)(2,1)}, bf16[912,384]{1,0:T(8,128)(2,1)S(1)}, u32[]{:S(2)}, u32[]{:S(2)}) collective-permute-start(bf16[912,384]{1,0:T(8,128)(2,1)} %get-tuple-element.74), channel_id=1, source_target_pairs={{0,16},{16,0},{32,48},{48,32},{1,17},{17,1},{33,49},{49,33},{2,18}... | collective-permute-start | bytes 2101256 | tf_op jit(solution)/shard_map/ppermute | solution.py:302
  82.6 4.0 %shard_map.40.factor = bf16[2,1024,384]{2,1,0:T(8,128)(2,1)S(1)} custom-call(s32[6]{0:T(128)S(1)} %stack.27.pos, bf16[128,2560]{1,0:T(8,128)(2,1)S(1)} %bitcast.14, bf16[128,2560]{1,0:T(8,128)(2,1)S(1)} %collective-permute-done.16.other), custom_call_target="tpu_custom_call" | custom-call | flops 10000000000 | tf_op jit(solution)/shard_map/pallas_call | solution.py:258
  86.5 2.6 %shard_map.41.r0 = bf16[1536,384]{1,0:T(8,128)(2,1)S(1)} custom-call(s32[6]{0:T(128)S(1)} %stack.27.pos, bf16[2,1536,384]{2,1,0:T(8,128)(2,1)S(1)} %copy-done.2, bf16[1536,256]{1,0:T(8,128)(2,1)S(1)} %collective-permute-done.4.w_mid, bf16[2,1024,384]{2,1,0:T(8,128)(2,1)S(1)} %shard_map.40.factor, bf16[1024,384]{1,0:T(8,128)(2,1)S(1)} %collective-permute-done.3.refs_0_, ...), custom_call_target="tpu_custom_call" | custom-call | tf_op jit(solution)/shard_map/pallas_call | solution.py:258
  89.1 8.3 %collective-permute-done.18.refs_2_ = bf16[912,384]{1,0:T(8,128)(2,1)S(1)} collective-permute-done((bf16[912,384]{1,0:T(8,128)(2,1)}, bf16[912,384]{1,0:T(8,128)(2,1)S(1)}, u32[]{:S(2)}, u32[]{:S(2)}) %collective-permute-start.18) | collective-permute-done | bytes 700448 | tf_op jit(solution)/shard_map/ppermute | solution.py:302
  97.4 0.0 collective-permute-done.17.w_mid
  97.4 2.7 %shard_map.42.r1 = bf16[1536,384]{1,0:T(8,128)(2,1)S(1)} custom-call(s32[6]{0:T(128)S(1)} %stack.27.pos, bf16[2,1536,384]{2,1,0:T(8,128)(2,1)S(1)} %copy-done.2, bf16[1536,256]{1,0:T(8,128)(2,1)S(1)} %collective-permute-done.17.w_mid, bf16[2,1024,384]{2,1,0:T(8,128)(2,1)S(1)} %shard_map.40.factor, ...), custom_call_target="tpu_custom_call" | custom-call | tf_op jit(solution)/shard_map/pallas_call | solution.py:258
  100.1 0.0 collective-permute-done.13.p1
  100.1 0.0 collective-permute-done.14.p2
  100.2 0.0 collective-permute-done.15.p3
  100.2 7.5 %shard_map.43 = bf16[2,1536,384]{2,1,0:T(8,128)(2,1)} custom-call(s32[6]{0:T(128)S(1)} %stack.27.pos, bf16[128,1664]{1,0:T(8,128)(2,1)S(1)} %pad_maximum_fusion.p0, bf16[128,1664]{1,0:T(8,128)(2,1)S(1)} %collective-permute-done.13.p1, bf16[128,1664]{1,0:T(8,128)(2,1)S(1)} %collective-permute-done.14.p2, bf16[128,1664]{1,0:T(8,128)(2,1)S(1)} %collective-permute-done.15.p3, ...), custom_call_target="tpu_custom_call" | custom-call | tf_op jit(solution)/shard_map/pallas_call | solution.py:258
  (11 shorter events, 0.1 us)
Async XLA Ops:
  6.7 18.4 %collective-permute-start.3 = (bf16[1024,384]{1,0:T(8,128)(2,1)}, bf16[1024,384]{1,0:T(8,128)(2,1)S(1)}, u32[]{:S(2)}, u32[]{:S(2)}) collective-permute-start(bf16[1024,384]{1,0:T(8,128)(2,1)} %get-tuple-element.53), channel_id=1, source_target_pairs={{0,16},{16,0},{32,48},{48,32},{1,17},{17,1},{33,49},{49,33},{2,18}... | collective-permute-start | bytes 2359304 | tf_op jit(solution)/shard_map/ppermute | solution.py:302
  8.8 20.2 %collective-permute-start.4 = (bf16[1536,256]{1,0:T(8,128)(2,1)}, bf16[1536,256]{1,0:T(8,128)(2,1)S(1)}, u32[]{:S(2)}, u32[]{:S(2)}) collective-permute-start(bf16[1536,256]{1,0:T(8,128)(2,1)} %get-tuple-element.54), channel_id=1, source_target_pairs={{16,32},{32,16},{17,33},{33,17},{18,34},{34,18},{19,35},{35,19},{2... | collective-permute-start | bytes 2359304 | tf_op jit(solution)/shard_map/ppermute | solution.py:306
  9.5 19.4 %all-to-all-start.1 = ((bf16[4,32,1920]{2,1,0:T(8,128)(2,1)}), bf16[4,32,1920]{2,1,0:T(8,128)(2,1)S(1)}, u32[]{:S(2)}, u32[]{:S(2)}) async-start(bf16[4,32,1920]{2,1,0:T(8,128)(2,1)} %bitcast.17), calls=%async_computation.1 | async-start | bytes 983040 | tf_op jit(solution)/shard_map/all_to_all | solution.py:326
  13.7 29.3 %collective-permute-start.5 = (bf16[608,384]{1,0:T(8,128)(2,1)}, bf16[608,384]{1,0:T(8,128)(2,1)S(1)}, u32[]{:S(2)}, u32[]{:S(2)}) collective-permute-start(bf16[608,384]{1,0:T(8,128)(2,1)} %get-tuple-element.58), channel_id=1, source_target_pairs={{0,16},{16,0},{32,48},{48,32},{1,17},{17,1},{33,49},{49,33},{2,18}... | collective-permute-start | bytes 1400840 | tf_op jit(solution)/shard_map/ppermute | solution.py:302
  21.1 30.9 %collective-permute-start = (bf16[128,1664]{1,0:T(8,128)(2,1)}, bf16[128,1664]{1,0:T(8,128)(2,1)}, u32[]{:S(2)}, u32[]{:S(2)}) collective-permute-start(bf16[128,1664]{1,0:T(8,128)(2,1)} %get-tuple-element.49), channel_id=1, source_target_pairs={{0,64},{64,128},{128,192},{192,0},{1,65},{65,129},{129,193},{193,1... | collective-permute-start | bytes 1277960 | tf_op jit(solution)/shard_map/ppermute | solution.py:294
  22.6 29.5 %collective-permute-start.1 = (bf16[128,1664]{1,0:T(8,128)(2,1)}, bf16[128,1664]{1,0:T(8,128)(2,1)}, u32[]{:S(2)}, u32[]{:S(2)}) collective-permute-start(bf16[128,1664]{1,0:T(8,128)(2,1)} %get-tuple-element.50), channel_id=1, source_target_pairs={{0,128},{64,192},{128,0},{192,64},{1,129},{65,193},{129,1},{193,65... | collective-permute-start | bytes 1277960 | tf_op jit(solution)/shard_map/ppermute | solution.py:294
  25.0 27.0 %collective-permute-start.2 = (bf16[128,1664]{1,0:T(8,128)(2,1)}, bf16[128,1664]{1,0:T(8,128)(2,1)}, u32[]{:S(2)}, u32[]{:S(2)}) collective-permute-start(bf16[128,1664]{1,0:T(8,128)(2,1)} %get-tuple-element.51), channel_id=1, source_target_pairs={{0,192},{64,0},{128,64},{192,128},{1,193},{65,1},{129,65},{193,129... | collective-permute-start | bytes 1277960 | tf_op jit(solution)/shard_map/ppermute | solution.py:294
  29.6 0.8 copy-start.4
  30.4 11.9 %all-to-all-start = ((bf16[4,32,1920]{2,1,0:T(8,128)(2,1)}), bf16[4,32,1920]{2,1,0:T(8,128)(2,1)S(1)}, u32[]{:S(2)}, u32[]{:S(2)}) async-start(bf16[4,32,1920]{2,1,0:T(8,128)(2,1)} %bitcast.18), calls=%async_computation | async-start | bytes 983040 | tf_op jit(solution)/shard_map/cond/branch_1_fun/all_to_all | solution.py:339
  43.0 0.9 copy-start.3
  43.0 9.1 %copy-start.5 = (bf16[128,1664]{1,0:T(8,128)(2,1)S(1)}, bf16[128,1664]{1,0:T(8,128)(2,1)}, u32[]{:S(2)}) copy-start(bf16[128,1664]{1,0:T(8,128)(2,1)} %get-tuple-element.61) | copy-start | bytes 1277956
  43.0 9.0 %collective-permute-start.6 = (bf16[528,384]{1,0:T(8,128)(2,1)}, bf16[528,384]{1,0:T(8,128)(2,1)S(1)}, u32[]{:S(2)}, u32[]{:S(2)}) collective-permute-start(bf16[528,384]{1,0:T(8,128)(2,1)} %get-tuple-element.60), channel_id=1, source_target_pairs={{0,16},{16,0},{32,48},{48,32},{1,17},{17,1},{33,49},{49,33},{2,18}... | collective-permute-start | bytes 1216520 | tf_op jit(solution)/shard_map/ppermute | solution.py:302
  43.9 26.0 %all-to-all-start.2 = ((bf16[8,16,2560]{2,1,0:T(8,128)(2,1)}), bf16[8,16,2560]{2,1,0:T(8,128)(2,1)S(1)}, u32[]{:S(2)}, u32[]{:S(2)}) async-start(bf16[8,16,2560]{2,1,0:T(8,128)(2,1)} %bitcast.16), calls=%async_computation.2 | async-start | bytes 1310720 | tf_op jit(solution)/shard_map/all_to_all | solution.py:357
  52.1 1.8 %copy-start = (bf16[528,384]{1,0:T(8,128)(2,1)}, bf16[528,384]{1,0:T(8,128)(2,1)S(1)}, u32[]{:S(2)}) copy-start(bf16[528,384]{1,0:T(8,128)(2,1)S(1)} %collective-permute-done.6.refs_1_) | copy-start | bytes 1216516
  53.9 4.9 %collective-permute-start.7 = (bf16[32,1664]{1,0:T(8,128)(2,1)S(1)}, bf16[32,1664]{1,0:T(8,128)(2,1)S(1)}, u32[]{:S(2)}, u32[]{:S(2)}) collective-permute-start(bf16[32,1664]{1,0:T(8,128)(2,1)S(1)} %pad_maximum_fusion.1), channel_id=1, source_target_pairs={{0,16},{16,32},{32,48},{48,0},{1,17},{17,33},{33,49},{49,1},{2,18}... | collective-permute-start | bytes 319496 | tf_op jit(solution)/shard_map/ppermute | solution.py:294
  54.7 5.2 %collective-permute-start.8 = (bf16[32,1664]{1,0:T(8,128)(2,1)S(1)}, bf16[32,1664]{1,0:T(8,128)(2,1)S(1)}, u32[]{:S(2)}, u32[]{:S(2)}) collective-permute-start(bf16[32,1664]{1,0:T(8,128)(2,1)S(1)} %pad_maximum_fusion.2), channel_id=1, source_target_pairs={{0,32},{16,48},{32,0},{48,16},{1,33},{17,49},{33,1},{49,17},{2,34}... | collective-permute-start | bytes 319496 | tf_op jit(solution)/shard_map/ppermute | solution.py:294
  55.7 5.1 %collective-permute-start.9 = (bf16[32,1664]{1,0:T(8,128)(2,1)S(1)}, bf16[32,1664]{1,0:T(8,128)(2,1)S(1)}, u32[]{:S(2)}, u32[]{:S(2)}) collective-permute-start(bf16[32,1664]{1,0:T(8,128)(2,1)S(1)} %pad_maximum_fusion.3), channel_id=1, source_target_pairs={{0,48},{16,0},{32,16},{48,32},{1,49},{17,1},{33,17},{49,33},{2,50}... | collective-permute-start | bytes 319496 | tf_op jit(solution)/shard_map/ppermute | solution.py:294
  60.9 5.1 %collective-permute-start.10 = (bf16[32,1664]{1,0:T(8,128)(2,1)S(1)}, bf16[32,1664]{1,0:T(8,128)(2,1)S(1)}, u32[]{:S(2)}, u32[]{:S(2)}) collective-permute-start(bf16[32,1664]{1,0:T(8,128)(2,1)S(1)} %multiply_convert_fusion), channel_id=1, source_target_pairs={{0,16},{16,32},{32,48},{48,0},{1,17},{17,33},{33,49},{49,1},{2,18}... | collective-permute-start | bytes 319496 | tf_op jit(solution)/shard_map/ppermute | solution.py:294
  61.4 6.4 %collective-permute-start.11 = (bf16[32,1664]{1,0:T(8,128)(2,1)S(1)}, bf16[32,1664]{1,0:T(8,128)(2,1)S(1)}, u32[]{:S(2)}, u32[]{:S(2)}) collective-permute-start(bf16[32,1664]{1,0:T(8,128)(2,1)S(1)} %multiply_convert_fusion), channel_id=1, source_target_pairs={{0,32},{16,48},{32,0},{48,16},{1,33},{17,49},{33,1},{49,17},{2,34}... | collective-permute-start | bytes 319496 | tf_op jit(solution)/shard_map/ppermute | solution.py:294
  64.5 3.6 %collective-permute-start.12 = (bf16[32,1664]{1,0:T(8,128)(2,1)S(1)}, bf16[32,1664]{1,0:T(8,128)(2,1)S(1)}, u32[]{:S(2)}, u32[]{:S(2)}) collective-permute-start(bf16[32,1664]{1,0:T(8,128)(2,1)S(1)} %multiply_convert_fusion), channel_id=1, source_target_pairs={{0,48},{16,0},{32,16},{48,32},{1,49},{17,1},{33,17},{49,33},{2,50}... | collective-permute-start | bytes 319496 | tf_op jit(solution)/shard_map/ppermute | solution.py:294
  69.9 10.5 %collective-permute-start.16 = (bf16[128,2560]{1,0:T(8,128)(2,1)S(1)}, bf16[128,2560]{1,0:T(8,128)(2,1)S(1)}, u32[]{:S(2)}, u32[]{:S(2)}) collective-permute-start(bf16[128,2560]{1,0:T(8,128)(2,1)S(1)} %bitcast.13), channel_id=1, source_target_pairs={{0,1},{1,0},{2,3},{3,2},{4,5},{5,4},{6,7},{7,6},{8,9},{9,8},{10,11... | collective-permute-start | bytes 1966088 | tf_op jit(solution)/shard_map/ppermute | solution.py:369
  74.6 25.5 %collective-permute-start.13 = (bf16[128,1664]{1,0:T(8,128)(2,1)S(1)}, bf16[128,1664]{1,0:T(8,128)(2,1)S(1)}, u32[]{:S(2)}, u32[]{:S(2)}) collective-permute-start(bf16[128,1664]{1,0:T(8,128)(2,1)S(1)} %pad_maximum_fusion.p0), channel_id=1, source_target_pairs={{0,64},{64,128},{128,192},{192,0},{1,65},{65,129},{129,193},{193,1... | collective-permute-start | bytes 1277960 | tf_op jit(solution)/shard_map/ppermute | solution.py:294
  76.0 24.2 %collective-permute-start.14 = (bf16[128,1664]{1,0:T(8,128)(2,1)S(1)}, bf16[128,1664]{1,0:T(8,128)(2,1)S(1)}, u32[]{:S(2)}, u32[]{:S(2)}) collective-permute-start(bf16[128,1664]{1,0:T(8,128)(2,1)S(1)} %pad_maximum_fusion.p0), channel_id=1, source_target_pairs={{0,128},{64,192},{128,0},{192,64},{1,129},{65,193},{129,1},{193,65... | collective-permute-start | bytes 1277960 | tf_op jit(solution)/shard_map/ppermute | solution.py:294
  78.6 21.6 %collective-permute-start.15 = (bf16[128,1664]{1,0:T(8,128)(2,1)S(1)}, bf16[128,1664]{1,0:T(8,128)(2,1)S(1)}, u32[]{:S(2)}, u32[]{:S(2)}) collective-permute-start(bf16[128,1664]{1,0:T(8,128)(2,1)S(1)} %pad_maximum_fusion.p0), channel_id=1, source_target_pairs={{0,192},{64,0},{128,64},{192,128},{1,193},{65,1},{129,65},{193,129... | collective-permute-start | bytes 1277960 | tf_op jit(solution)/shard_map/ppermute | solution.py:294
  79.6 17.7 %collective-permute-start.17 = (bf16[1536,256]{1,0:T(8,128)(2,1)}, bf16[1536,256]{1,0:T(8,128)(2,1)S(1)}, u32[]{:S(2)}, u32[]{:S(2)}) collective-permute-start(bf16[1536,256]{1,0:T(8,128)(2,1)} %get-tuple-element.72), channel_id=1, source_target_pairs={{16,32},{32,16},{17,33},{33,17},{18,34},{34,18},{19,35},{35,19},{2... | collective-permute-start | bytes 2359304 | tf_op jit(solution)/shard_map/ppermute | solution.py:306
  80.4 17.0 %collective-permute-start.18 = (bf16[912,384]{1,0:T(8,128)(2,1)}, bf16[912,384]{1,0:T(8,128)(2,1)S(1)}, u32[]{:S(2)}, u32[]{:S(2)}) collective-permute-start(bf16[912,384]{1,0:T(8,128)(2,1)} %get-tuple-element.74), channel_id=1, source_target_pairs={{0,16},{16,0},{32,48},{48,32},{1,17},{17,1},{33,49},{49,33},{2,18}... | collective-permute-start | bytes 2101256 | tf_op jit(solution)/shard_map/ppermute | solution.py:302
  82.6 4.0 %copy-start.2 = (bf16[2,1536,384]{2,1,0:T(8,128)(2,1)S(1)}, bf16[2,1536,384]{2,1,0:T(8,128)(2,1)}, u32[]{:S(2)}) copy-start(bf16[2,1536,384]{2,1,0:T(8,128)(2,1)} %w_own.3) | copy-start | bytes 7077892
  86.5 10.9 %copy-start.1 = (bf16[528,384]{1,0:T(8,128)(2,1)S(1)}, bf16[528,384]{1,0:T(8,128)(2,1)}, u32[]{:S(2)}) copy-start(bf16[528,384]{1,0:T(8,128)(2,1)} %copy-done) | copy-start | bytes 1216516
